TPU v7x, 256 devices: a whole 4x4x8 slice. The times are simulated.
256 devices in a mesh: span: 4 (over y_lo, core), lat: 8 (over x, y_hi), rad: 8 (over z).
Axes of the slice: x: 4, y: 4 (y_hi: 2, y_lo: 2; y = y_hi * 2 + y_lo), z: 8, core: 2. Of those that a mesh axis runs over, the one named last changes fastest.
Arguments:
- current: float32 [3, 32, 128, 512], P(None, 'rad', 'lat', 'span'), may hold values from -6 to 6
- previous: float32 [3, 32, 128, 512], P(None, 'rad', 'lat', 'span'), may hold values from -6 to 6
- moduli: float32 [4, 32, 128, 512], P(None, 'rad', 'lat', 'span'), may hold values from 0.5 to 1.5
- density: float32 [32, 128, 512], P('rad', 'lat', 'span'), may hold values from 0.8 to 1.2
- traces: float32 [32768, 3, 512], P(('span', 'lat', 'rad')), may hold values from -12 to 12
- receivers: int32 [32768], P(('span', 'lat', 'rad')), may hold values from 0 to 8191
- owners: int32 [32768, 1], P(('span', 'lat', 'rad')), may hold values from 0 to 63; in each aligned block of 128 rows (0 to 127, 128 to 255, ...) at most 4 rows name the same one
- offsets: int32 [32768], P(('span', 'lat', 'rad')), may hold values from 0 to 508
Outputs:
- final: float32 [3, 32, 128, 512], P(None, 'rad', 'lat', 'span')
- before_final: float32 [3, 32, 128, 512], P(None, 'rad', 'lat', 'span')
Inputs may be any that keep to these rules, and one draw needn't show every extreme that they name: `owners`: o identifies the owner lat * 8 + rad among the devices of the station's own face set; in the stations of one device no owner is named by more than 4 rows, and exactly 4 in some devices. `receivers`: index (r * 16 + l) * 128 + e of the cell on its owner.
All inputs are finite; a program needn't handle non-finite values.
Results may differ from a plain program's by a relative error of at most 0.00002.
Values sent between devices are 32-bit elements; how exact they have to be, the bound alone decides.
No kernel may reach another device: no remote copies, remote signals or barrier semaphores. Data moves between devices by JAX's collectives and lax.ppermute only.
A program may use at most 64 MiB of HBM per device.

v0:
```python
import jax
import jax.numpy as jnp
from jax import lax
from jax.sharding import PartitionSpec as P

STEPS = 4


step_square = 0.16
modulus_table = ((0, 2, 2), (2, 1, 3), (2, 3, 1))


def padded(block, sides, width, periodic):
    for axis, dim in sides:
        count = lax.axis_size(axis)
        forward = [(i, i + 1) for i in range(count - 1)]
        if periodic:
            forward.append((count - 1, 0))
        backward = [(target, source) for source, target in forward]
        low = lax.ppermute(
            lax.slice_in_dim(block, block.shape[dim] - width, None, axis=dim), axis, forward
        )
        high = lax.ppermute(lax.slice_in_dim(block, 0, width, axis=dim), axis, backward)
        block = jnp.concatenate([low, block, high], axis=dim)
    return block


def face_flux(centre, centre_mod, upper, lower, upper_mod, lower_mod):
    return 0.5 * (centre_mod + upper_mod) * (upper - centre) + 0.5 * (centre_mod + lower_mod) * (
        lower - centre
    )


def forces(current, moduli, current_near, moduli_near):
    pieces = []
    for component in range(3):
        running = jnp.zeros_like(current[component])
        for direction in range(3):
            pick_mod = modulus_table[component][direction]
            running = running + face_flux(
                current[component],
                moduli[pick_mod],
                current_near[direction][0][component],
                current_near[direction][1][component],
                moduli_near[direction][0][pick_mod],
                moduli_near[direction][1][pick_mod],
            )
        pieces.append(running)
    return jnp.stack(pieces)


def rims(stacked):
    loop_pad = padded(stacked, (("span", 3),), 1, True)
    shell_pad = padded(stacked, (("lat", 2), ("rad", 1)), 1, False)
    return (
        (shell_pad[:, 2:, 1:-1], shell_pad[:, :-2, 1:-1]),
        (shell_pad[:, 1:-1, 2:], shell_pad[:, 1:-1, :-2]),
        (loop_pad[..., 2:], loop_pad[..., :-2]),
    )


def on_device(current, previous, moduli, density, traces, receivers, owners, offsets):
    lat_count = lax.axis_size("lat")
    rad_count = lax.axis_size("rad")
    groups = lat_count * rad_count
    station_count = traces.shape[0]
    capacity = max(2, 2 * station_count // groups)
    owner_ids = owners[:, 0]
    same_owner = owner_ids[:, None] == owner_ids[None, :]
    earlier = jnp.arange(station_count)[None, :] < jnp.arange(station_count)[:, None]
    slot_rank = jnp.sum(same_owner & earlier, axis=1)
    slot_index = owner_ids * capacity + slot_rank
    sample_picks = offsets[:, None] + jnp.arange(STEPS, dtype=jnp.int32)[None, :]
    sample_picks = jnp.broadcast_to(sample_picks[:, None, :], (station_count, 3, STEPS))
    payload = jnp.take_along_axis(traces, sample_picks, axis=2)
    labels = receivers[:, None]
    tail = payload.shape[1:]
    send_values = jnp.zeros((groups * capacity,) + tail, jnp.float32).at[slot_index].set(payload)
    send_labels = (
        jnp.zeros((groups * capacity, labels.shape[1]), jnp.int32).at[slot_index].set(labels)
    )
    got_values, got_labels = (
        lax.all_to_all(
            send_values.reshape((groups, capacity) + tail),
            ("lat", "rad"),
            split_axis=0,
            concat_axis=0,
            tiled=True,
        ),
        lax.all_to_all(
            send_labels.reshape(groups, capacity, labels.shape[1]),
            ("lat", "rad"),
            split_axis=0,
            concat_axis=0,
            tiled=True,
        ),
    )
    got_values = got_values.reshape((groups * capacity,) + tail)
    got_labels = got_labels.reshape(groups * capacity, labels.shape[1])
    cell_index = got_labels[:, 0]
    moduli_near = rims(moduli)
    for step_index in range(STEPS):
        forcing = forces(current, moduli, rims(current), moduli_near)
        forcing = (
            forcing.reshape(3, -1)
            .at[:, cell_index]
            .add(got_values[:, :, step_index].T)
            .reshape(forcing.shape)
        )
        following = 2.0 * current - previous + step_square * forcing / density
        previous, current = (current, following)
    return (current, previous)


def solution(mesh):
    in_specs = (
        P(None, "rad", "lat", "span"),
        P(None, "rad", "lat", "span"),
        P(None, "rad", "lat", "span"),
        P("rad", "lat", "span"),
        P(("span", "lat", "rad"), None, None),
        P(("span", "lat", "rad")),
        P(("span", "lat", "rad"), None),
        P(("span", "lat", "rad")),
    )
    out_specs = (P(None, "rad", "lat", "span"), P(None, "rad", "lat", "span"))
    return jax.shard_map(
        on_device, mesh=mesh, in_specs=in_specs, out_specs=out_specs, check_vma=False
    )
```

profile of v0, /device:TPU:1, one launch (start us, length us, event | category | flops | bytes accessed | tf_op | source)
XLA Modules:
  0.0 234.3 jit_solution(10987002734939590601)
XLA Ops:
  2.9 6.3 %collective-permute-start.3 = (f32[3,4,1,128]{3,2,1,0:T(1,128)S(1)}, f32[3,4,1,128]{3,2,1,0:T(1,128)S(1)}, u32[]{:S(2)}, u32[]{:S(2)}) collective-permute-start(f32[3,4,1,128]{3,2,1,0:T(1,128)S(1)} %get-tuple-element.50), channel_id=1, source_target_pairs={{0,8},{8,16},{16,24},{24,32},{32,40},{40,48},{48,56},{1,9},{9,17},... | collective-permute-start | bytes 18440 | tf_op jit(solution)/shard_map/ppermute | solution.py:20
  10.0 5.8 %collective-permute-start = (f32[4,4,1,128]{3,2,1,0:T(1,128)S(1)}, f32[4,4,1,128]{3,2,1,0:T(1,128)S(1)}, u32[]{:S(2)}, u32[]{:S(2)}) collective-permute-start(f32[4,4,1,128]{3,2,1,0:T(1,128)S(1)} %get-tuple-element.27), channel_id=1, source_target_pairs={{0,8},{8,16},{16,24},{24,32},{32,40},{40,48},{48,56},{1,9},{9,17},... | collective-permute-start | bytes 24584 | tf_op jit(solution)/shard_map/ppermute | solution.py:20
  23.2 15.2 %all-to-all-start = ((s32[64,4,1]{1,2,0:T(1,128)}), s32[64,4,1]{1,2,0:T(1,128)S(1)}, u32[]{:S(2)}, u32[]{:S(2)}) async-start(s32[64,4,1]{1,2,0:T(1,128)} %bitcast.6), calls=%async_computation | async-start | bytes 65536 | tf_op jit(solution)/shard_map/all_to_all | solution.py:90
  42.5 14.6 %gather_fusion = f32[1536]{0:T(1024)S(1)} fusion(f32[128,3,512]{2,0,1:T(8,128)S(1)} %copy-done, s32[1536]{0:T(1024)S(1)} %reshape.101), kind=kCustom, calls=%fused_computation | custom fusion | bytes 30720 | tf_op jit(solution)/shard_map/jit(take_along_axis)/gather | solution.py:75
  57.7 4.3 %scatter_fusion = f32[256,3,4]{2,1,0:T(4,128)S(1)} fusion(f32[256,3,4]{2,1,0:T(4,128)S(1)} %broadcast_in_dim.45, s32[128]{0:T(128)S(1)} %fusion.187, f32[128,3,4]{2,1,0:T(4,128)S(1)} %fusion.1), kind=kCustom, calls=%fused_computation.2 | custom fusion | bytes 18944 | tf_op jit(solution)/shard_map/scatter | solution.py:78
  67.3 12.2 %all-to-all-start.1 = ((f32[64,4,3,4]{3,1,2,0:T(4,128)}), f32[64,4,3,4]{3,1,2,0:T(4,128)S(1)}, u32[]{:S(2)}, u32[]{:S(2)}) async-start(f32[64,4,3,4]{3,1,2,0:T(4,128)} %copy.79), calls=%async_computation.1 | async-start | bytes 786432 | tf_op jit(solution)/shard_map/all_to_all | solution.py:83
  88.8 6.3 %all-to-all-done.1 = f32[64,4,3,4]{3,1,2,0:T(4,128)S(1)} async-done(((f32[64,4,3,4]{3,1,2,0:T(4,128)}), f32[64,4,3,4]{3,1,2,0:T(4,128)S(1)}, u32[]{:S(2)}, u32[]{:S(2)}) %all-to-all-start.1) | async-done | bytes 12320 | tf_op jit(solution)/shard_map/all_to_all | solution.py:83
  104.5 5.9 %scatter_custom_fusion.2 = f32[3,8192]{0,1:T(8,128)} fusion(f32[3,8192]{0,1:T(8,128)} %copy.81, s32[256]{0:T(256)S(1)} %bitcast.62, f32[256,3,1]{1,0,2:T(8,128)S(1)} %copy.93), kind=kCustom, calls=%fused_computation.25 | custom fusion | flops 768 | bytes 229376 | tf_op jit(solution)/shard_map/scatter-add | solution.py:107
  110.4 4.6 %broadcast_multiply_fusion.3 = f32[3,8192]{0,1:T(8,128)} fusion(f32[3,8192]{0,1:T(8,128)} %scatter_custom_fusion.2), kind=kLoop, calls=%fused_computation.10 | loop fusion | flops 24576 | bytes 196608 | tf_op jit(solution)/shard_map/mul | solution.py:110
  121.0 4.6 %collective-permute-done.13 = f32[3,4,1,128]{3,2,1,0:T(1,128)S(1)} collective-permute-done((f32[3,4,1,128]{3,2,1,0:T(1,128)S(1)}, f32[3,4,1,128]{3,2,1,0:T(1,128)S(1)}, u32[]{:S(2)}, u32[]{:S(2)}) %collective-permute-start.13) | collective-permute-done | bytes 6176 | tf_op jit(solution)/shard_map/ppermute | solution.py:23
  126.9 4.3 %collective-permute-start.15 = (f32[3,1,18,128]{3,2,1,0:T(8,128)S(1)}, f32[3,1,18,128]{3,2,1,0:T(8,128)S(1)}, u32[]{:S(2)}, u32[]{:S(2)}) collective-permute-start(f32[3,1,18,128]{3,2,1,0:T(8,128)S(1)} %get-tuple-element.34), channel_id=1, source_target_pairs={{0,1},{1,2},{2,3},{3,4},{4,5},{5,6},{6,7},{8,9},{9,10},{10,11},{11... | collective-permute-start | bytes 82952 | tf_op jit(solution)/shard_map/ppermute | solution.py:20
  131.3 5.6 %collective-permute-start.16 = (f32[3,4,16,1]{3,2,1,0:T(8,128)S(1)}, f32[3,4,16,1]{3,2,1,0:T(8,128)S(1)}, u32[]{:S(2)}, u32[]{:S(2)}) collective-permute-start(f32[3,4,16,1]{3,2,1,0:T(8,128)S(1)} %get-tuple-element.47), channel_id=1, source_target_pairs={{64,0},{128,64},{192,128},{0,192},{65,1},{129,65},{193,129},{1,193... | collective-permute-start | bytes 2312 | tf_op jit(solution)/shard_map/ppermute | solution.py:23
  143.1 5.9 %scatter_custom_fusion.3 = f32[3,8192]{0,1:T(8,128)} fusion(f32[3,8192]{0,1:T(8,128)} %copy.84, s32[256]{0:T(256)S(1)} %bitcast.63, f32[256,3,1]{1,0,2:T(8,128)S(1)} %copy.94), kind=kCustom, calls=%fused_computation.23 | custom fusion | flops 768 | bytes 229376 | tf_op jit(solution)/shard_map/scatter-add | solution.py:107
  149.1 4.6 %broadcast_multiply_fusion.2 = f32[3,8192]{0,1:T(8,128)} fusion(f32[3,8192]{0,1:T(8,128)} %scatter_custom_fusion.3), kind=kLoop, calls=%fused_computation.9 | loop fusion | flops 24576 | bytes 196608 | tf_op jit(solution)/shard_map/mul | solution.py:110
  156.6 5.9 %collective-permute-start.18 = (f32[3,4,1,128]{3,2,1,0:T(1,128)S(1)}, f32[3,4,1,128]{3,2,1,0:T(1,128)S(1)}, u32[]{:S(2)}, u32[]{:S(2)}) collective-permute-start(f32[3,4,1,128]{3,2,1,0:T(1,128)S(1)} %get-tuple-element.42), channel_id=1, source_target_pairs={{0,8},{8,16},{16,24},{24,32},{32,40},{40,48},{48,56},{1,9},{9,17},... | collective-permute-start | bytes 18440 | tf_op jit(solution)/shard_map/ppermute | solution.py:20
  163.8 4.6 %collective-permute-done.19 = f32[3,4,1,128]{3,2,1,0:T(1,128)S(1)} collective-permute-done((f32[3,4,1,128]{3,2,1,0:T(1,128)S(1)}, f32[3,4,1,128]{3,2,1,0:T(1,128)S(1)}, u32[]{:S(2)}, u32[]{:S(2)}) %collective-permute-start.19) | collective-permute-done | bytes 6176 | tf_op jit(solution)/shard_map/ppermute | solution.py:23
  169.7 4.3 %collective-permute-start.21 = (f32[3,1,18,128]{3,2,1,0:T(8,128)S(1)}, f32[3,1,18,128]{3,2,1,0:T(8,128)S(1)}, u32[]{:S(2)}, u32[]{:S(2)}) collective-permute-start(f32[3,1,18,128]{3,2,1,0:T(8,128)S(1)} %get-tuple-element.32), channel_id=1, source_target_pairs={{0,1},{1,2},{2,3},{3,4},{4,5},{5,6},{6,7},{8,9},{9,10},{10,11},{11... | collective-permute-start | bytes 82952 | tf_op jit(solution)/shard_map/ppermute | solution.py:20
  182.0 5.9 %scatter_custom_fusion.4 = f32[3,8192]{0,1:T(8,128)} fusion(f32[3,8192]{0,1:T(8,128)} %copy.87, s32[256]{0:T(256)S(1)} %bitcast.64, f32[256,3,1]{1,0,2:T(8,128)S(1)} %copy.95), kind=kCustom, calls=%fused_computation.21 | custom fusion | flops 768 | bytes 229376 | tf_op jit(solution)/shard_map/scatter-add | solution.py:107
  188.0 4.6 %broadcast_multiply_fusion.1 = f32[3,8192]{0,1:T(8,128)} fusion(f32[3,8192]{0,1:T(8,128)} %scatter_custom_fusion.4), kind=kLoop, calls=%fused_computation.8 | loop fusion | flops 24576 | bytes 196608 | tf_op jit(solution)/shard_map/mul | solution.py:110
  195.4 5.6 %collective-permute-start.24 = (f32[3,4,1,128]{3,2,1,0:T(1,128)S(1)}, f32[3,4,1,128]{3,2,1,0:T(1,128)S(1)}, u32[]{:S(2)}, u32[]{:S(2)}) collective-permute-start(f32[3,4,1,128]{3,2,1,0:T(1,128)S(1)} %get-tuple-element.38), channel_id=1, source_target_pairs={{0,8},{8,16},{16,24},{24,32},{32,40},{40,48},{48,56},{1,9},{9,17},... | collective-permute-start | bytes 18440 | tf_op jit(solution)/shard_map/ppermute | solution.py:20
  202.4 4.6 %collective-permute-done.25 = f32[3,4,1,128]{3,2,1,0:T(1,128)S(1)} collective-permute-done((f32[3,4,1,128]{3,2,1,0:T(1,128)S(1)}, f32[3,4,1,128]{3,2,1,0:T(1,128)S(1)}, u32[]{:S(2)}, u32[]{:S(2)}) %collective-permute-start.25) | collective-permute-done | bytes 6176 | tf_op jit(solution)/shard_map/ppermute | solution.py:23
  208.2 4.2 %collective-permute-start.27 = (f32[3,1,18,128]{3,2,1,0:T(8,128)S(1)}, f32[3,1,18,128]{3,2,1,0:T(8,128)S(1)}, u32[]{:S(2)}, u32[]{:S(2)}) collective-permute-start(f32[3,1,18,128]{3,2,1,0:T(8,128)S(1)} %get-tuple-element.30), channel_id=1, source_target_pairs={{0,1},{1,2},{2,3},{3,4},{4,5},{5,6},{6,7},{8,9},{9,10},{10,11},{11... | collective-permute-start | bytes 82952 | tf_op jit(solution)/shard_map/ppermute | solution.py:20
  220.3 5.9 %scatter_custom_fusion.5 = f32[3,8192]{0,1:T(8,128)} fusion(f32[3,8192]{0,1:T(8,128)} %copy.90, s32[256]{0:T(256)S(1)} %bitcast.65, f32[256,3,1]{1,0,2:T(8,128)S(1)} %copy.96), kind=kCustom, calls=%fused_computation.19 | custom fusion | flops 768 | bytes 229376 | tf_op jit(solution)/shard_map/scatter-add | solution.py:107
  226.2 4.6 %broadcast_multiply_fusion = f32[3,8192]{0,1:T(8,128)} fusion(f32[3,8192]{0,1:T(8,128)} %scatter_custom_fusion.5), kind=kLoop, calls=%fused_computation.7 | loop fusion | flops 24576 | bytes 196608 | tf_op jit(solution)/shard_map/mul | solution.py:110
  (138 shorter events, 82.7 us)
Async XLA Ops:
  1.6 79.3 %collective-permute-start.4 = (f32[3,4,1,128]{3,2,1,0:T(1,128)S(1)}, f32[3,4,1,128]{3,2,1,0:T(1,128)S(1)}, u32[]{:S(2)}, u32[]{:S(2)}) collective-permute-start(f32[3,4,1,128]{3,2,1,0:T(1,128)S(1)} %get-tuple-element.49), channel_id=1, source_target_pairs={{8,0},{16,8},{24,16},{32,24},{40,32},{48,40},{56,48},{9,1},{17,9},... | collective-permute-start | bytes 18440 | tf_op jit(solution)/shard_map/ppermute | solution.py:23
  2.9 79.2 %collective-permute-start.3 = (f32[3,4,1,128]{3,2,1,0:T(1,128)S(1)}, f32[3,4,1,128]{3,2,1,0:T(1,128)S(1)}, u32[]{:S(2)}, u32[]{:S(2)}) collective-permute-start(f32[3,4,1,128]{3,2,1,0:T(1,128)S(1)} %get-tuple-element.50), channel_id=1, source_target_pairs={{0,8},{8,16},{16,24},{24,32},{32,40},{40,48},{48,56},{1,9},{9,17},... | collective-permute-start | bytes 18440 | tf_op jit(solution)/shard_map/ppermute | solution.py:20
  10.0 73.4 %collective-permute-start = (f32[4,4,1,128]{3,2,1,0:T(1,128)S(1)}, f32[4,4,1,128]{3,2,1,0:T(1,128)S(1)}, u32[]{:S(2)}, u32[]{:S(2)}) collective-permute-start(f32[4,4,1,128]{3,2,1,0:T(1,128)S(1)} %get-tuple-element.27), channel_id=1, source_target_pairs={{0,8},{8,16},{16,24},{24,32},{32,40},{40,48},{48,56},{1,9},{9,17},... | collective-permute-start | bytes 24584 | tf_op jit(solution)/shard_map/ppermute | solution.py:20
  15.8 71.6 %collective-permute-start.1 = (f32[4,4,1,128]{3,2,1,0:T(1,128)S(1)}, f32[4,4,1,128]{3,2,1,0:T(1,128)S(1)}, u32[]{:S(2)}, u32[]{:S(2)}) collective-permute-start(f32[4,4,1,128]{3,2,1,0:T(1,128)S(1)} %get-tuple-element.28), channel_id=1, source_target_pairs={{8,0},{16,8},{24,16},{32,24},{40,32},{48,40},{56,48},{9,1},{17,9},... | collective-permute-start | bytes 24584 | tf_op jit(solution)/shard_map/ppermute | solution.py:23
  18.2 44.7 %collective-permute-start.9 = (f32[3,4,16,1]{3,2,1,0:T(8,128)S(1)}, f32[3,4,16,1]{3,2,1,0:T(8,128)S(1)}, u32[]{:S(2)}, u32[]{:S(2)}) collective-permute-start(f32[3,4,16,1]{3,2,1,0:T(8,128)S(1)} %get-tuple-element.53), channel_id=1, source_target_pairs={{64,0},{128,64},{192,128},{0,192},{65,1},{129,65},{193,129},{1,193... | collective-permute-start | bytes 2312 | tf_op jit(solution)/shard_map/ppermute | solution.py:23
  23.2 44.1 %all-to-all-start = ((s32[64,4,1]{1,2,0:T(1,128)}), s32[64,4,1]{1,2,0:T(1,128)S(1)}, u32[]{:S(2)}, u32[]{:S(2)}) async-start(s32[64,4,1]{1,2,0:T(1,128)} %bitcast.6), calls=%async_computation | async-start | bytes 65536 | tf_op jit(solution)/shard_map/all_to_all | solution.py:90
  67.3 33.1 %collective-permute-start.10 = (f32[4,4,16,1]{3,2,1,0:T(8,128)S(1)}, f32[4,4,16,1]{3,2,1,0:T(8,128)S(1)}, u32[]{:S(2)}, u32[]{:S(2)}) collective-permute-start(f32[4,4,16,1]{3,2,1,0:T(8,128)S(1)} %get-tuple-element.23), channel_id=1, source_target_pairs={{0,64},{64,128},{128,192},{192,0},{1,65},{65,129},{129,193},{193,1... | collective-permute-start | bytes 3080 | tf_op jit(solution)/shard_map/ppermute | solution.py:20
  67.3 27.8 %all-to-all-start.1 = ((f32[64,4,3,4]{3,1,2,0:T(4,128)}), f32[64,4,3,4]{3,1,2,0:T(4,128)S(1)}, u32[]{:S(2)}, u32[]{:S(2)}) async-start(f32[64,4,3,4]{3,1,2,0:T(4,128)} %copy.79), calls=%async_computation.1 | async-start | bytes 786432 | tf_op jit(solution)/shard_map/all_to_all | solution.py:83
  80.9 15.9 %collective-permute-start.11 = (f32[3,4,16,1]{3,2,1,0:T(8,128)S(1)}, f32[3,4,16,1]{3,2,1,0:T(8,128)S(1)}, u32[]{:S(2)}, u32[]{:S(2)}) collective-permute-start(f32[3,4,16,1]{3,2,1,0:T(8,128)S(1)} %get-tuple-element.54), channel_id=1, source_target_pairs={{0,64},{64,128},{128,192},{192,0},{1,65},{65,129},{129,193},{193,1... | collective-permute-start | bytes 2312 | tf_op jit(solution)/shard_map/ppermute | solution.py:20
  82.0 18.4 %collective-permute-start.5 = (f32[3,1,18,128]{3,2,1,0:T(8,128)S(1)}, f32[3,1,18,128]{3,2,1,0:T(8,128)S(1)}, u32[]{:S(2)}, u32[]{:S(2)}) collective-permute-start(f32[3,1,18,128]{3,2,1,0:T(8,128)S(1)} %get-tuple-element.35), channel_id=1, source_target_pairs={{1,0},{2,1},{3,2},{4,3},{5,4},{6,5},{7,6},{9,8},{10,9},{11,10},{12... | collective-permute-start | bytes 82952 | tf_op jit(solution)/shard_map/ppermute | solution.py:23
  83.4 17.0 %collective-permute-start.7 = (f32[3,1,18,128]{3,2,1,0:T(8,128)S(1)}, f32[3,1,18,128]{3,2,1,0:T(8,128)S(1)}, u32[]{:S(2)}, u32[]{:S(2)}) collective-permute-start(f32[3,1,18,128]{3,2,1,0:T(8,128)S(1)} %get-tuple-element.36), channel_id=1, source_target_pairs={{0,1},{1,2},{2,3},{3,4},{4,5},{5,6},{6,7},{8,9},{9,10},{10,11},{11... | collective-permute-start | bytes 82952 | tf_op jit(solution)/shard_map/ppermute | solution.py:20
  87.4 13.0 %collective-permute-start.2 = (f32[4,1,18,128]{3,2,1,0:T(8,128)S(1)}, f32[4,1,18,128]{3,2,1,0:T(8,128)S(1)}, u32[]{:S(2)}, u32[]{:S(2)}) collective-permute-start(f32[4,1,18,128]{3,2,1,0:T(8,128)S(1)} %get-tuple-element.22), channel_id=1, source_target_pairs={{1,0},{2,1},{3,2},{4,3},{5,4},{6,5},{7,6},{9,8},{10,9},{11,10},{12... | collective-permute-start | bytes 110600 | tf_op jit(solution)/shard_map/ppermute | solution.py:23
  119.7 5.9 %collective-permute-start.13 = (f32[3,4,1,128]{3,2,1,0:T(1,128)S(1)}, f32[3,4,1,128]{3,2,1,0:T(1,128)S(1)}, u32[]{:S(2)}, u32[]{:S(2)}) collective-permute-start(f32[3,4,1,128]{3,2,1,0:T(1,128)S(1)} %get-tuple-element.45), channel_id=1, source_target_pairs={{8,0},{16,8},{24,16},{32,24},{40,32},{48,40},{56,48},{9,1},{17,9},... | collective-permute-start | bytes 18440 | tf_op jit(solution)/shard_map/ppermute | solution.py:23
  125.6 14.4 %collective-permute-start.14 = (f32[3,1,18,128]{3,2,1,0:T(8,128)S(1)}, f32[3,1,18,128]{3,2,1,0:T(8,128)S(1)}, u32[]{:S(2)}, u32[]{:S(2)}) collective-permute-start(f32[3,1,18,128]{3,2,1,0:T(8,128)S(1)} %get-tuple-element.33), channel_id=1, source_target_pairs={{1,0},{2,1},{3,2},{4,3},{5,4},{6,5},{7,6},{9,8},{10,9},{11,10},{12... | collective-permute-start | bytes 82952 | tf_op jit(solution)/shard_map/ppermute | solution.py:23
  126.9 13.1 %collective-permute-start.15 = (f32[3,1,18,128]{3,2,1,0:T(8,128)S(1)}, f32[3,1,18,128]{3,2,1,0:T(8,128)S(1)}, u32[]{:S(2)}, u32[]{:S(2)}) collective-permute-start(f32[3,1,18,128]{3,2,1,0:T(8,128)S(1)} %get-tuple-element.34), channel_id=1, source_target_pairs={{0,1},{1,2},{2,3},{3,4},{4,5},{5,6},{6,7},{8,9},{9,10},{10,11},{11... | collective-permute-start | bytes 82952 | tf_op jit(solution)/shard_map/ppermute | solution.py:20
  131.3 8.7 %collective-permute-start.16 = (f32[3,4,16,1]{3,2,1,0:T(8,128)S(1)}, f32[3,4,16,1]{3,2,1,0:T(8,128)S(1)}, u32[]{:S(2)}, u32[]{:S(2)}) collective-permute-start(f32[3,4,16,1]{3,2,1,0:T(8,128)S(1)} %get-tuple-element.47), channel_id=1, source_target_pairs={{64,0},{128,64},{192,128},{0,192},{65,1},{129,65},{193,129},{1,193... | collective-permute-start | bytes 2312 | tf_op jit(solution)/shard_map/ppermute | solution.py:23
  156.6 7.2 %collective-permute-start.18 = (f32[3,4,1,128]{3,2,1,0:T(1,128)S(1)}, f32[3,4,1,128]{3,2,1,0:T(1,128)S(1)}, u32[]{:S(2)}, u32[]{:S(2)}) collective-permute-start(f32[3,4,1,128]{3,2,1,0:T(1,128)S(1)} %get-tuple-element.42), channel_id=1, source_target_pairs={{0,8},{8,16},{16,24},{24,32},{32,40},{40,48},{48,56},{1,9},{9,17},... | collective-permute-start | bytes 18440 | tf_op jit(solution)/shard_map/ppermute | solution.py:20
  162.5 5.9 %collective-permute-start.19 = (f32[3,4,1,128]{3,2,1,0:T(1,128)S(1)}, f32[3,4,1,128]{3,2,1,0:T(1,128)S(1)}, u32[]{:S(2)}, u32[]{:S(2)}) collective-permute-start(f32[3,4,1,128]{3,2,1,0:T(1,128)S(1)} %get-tuple-element.41), channel_id=1, source_target_pairs={{8,0},{16,8},{24,16},{32,24},{40,32},{48,40},{56,48},{9,1},{17,9},... | collective-permute-start | bytes 18440 | tf_op jit(solution)/shard_map/ppermute | solution.py:23
  168.4 10.5 %collective-permute-start.20 = (f32[3,1,18,128]{3,2,1,0:T(8,128)S(1)}, f32[3,1,18,128]{3,2,1,0:T(8,128)S(1)}, u32[]{:S(2)}, u32[]{:S(2)}) collective-permute-start(f32[3,1,18,128]{3,2,1,0:T(8,128)S(1)} %get-tuple-element.31), channel_id=1, source_target_pairs={{1,0},{2,1},{3,2},{4,3},{5,4},{6,5},{7,6},{9,8},{10,9},{11,10},{12... | collective-permute-start | bytes 82952 | tf_op jit(solution)/shard_map/ppermute | solution.py:23
  169.7 9.2 %collective-permute-start.21 = (f32[3,1,18,128]{3,2,1,0:T(8,128)S(1)}, f32[3,1,18,128]{3,2,1,0:T(8,128)S(1)}, u32[]{:S(2)}, u32[]{:S(2)}) collective-permute-start(f32[3,1,18,128]{3,2,1,0:T(8,128)S(1)} %get-tuple-element.32), channel_id=1, source_target_pairs={{0,1},{1,2},{2,3},{3,4},{4,5},{5,6},{6,7},{8,9},{9,10},{10,11},{11... | collective-permute-start | bytes 82952 | tf_op jit(solution)/shard_map/ppermute | solution.py:20
  195.4 6.9 %collective-permute-start.24 = (f32[3,4,1,128]{3,2,1,0:T(1,128)S(1)}, f32[3,4,1,128]{3,2,1,0:T(1,128)S(1)}, u32[]{:S(2)}, u32[]{:S(2)}) collective-permute-start(f32[3,4,1,128]{3,2,1,0:T(1,128)S(1)} %get-tuple-element.38), channel_id=1, source_target_pairs={{0,8},{8,16},{16,24},{24,32},{32,40},{40,48},{48,56},{1,9},{9,17},... | collective-permute-start | bytes 18440 | tf_op jit(solution)/shard_map/ppermute | solution.py:20
  201.1 5.9 %collective-permute-start.25 = (f32[3,4,1,128]{3,2,1,0:T(1,128)S(1)}, f32[3,4,1,128]{3,2,1,0:T(1,128)S(1)}, u32[]{:S(2)}, u32[]{:S(2)}) collective-permute-start(f32[3,4,1,128]{3,2,1,0:T(1,128)S(1)} %get-tuple-element.37), channel_id=1, source_target_pairs={{8,0},{16,8},{24,16},{32,24},{40,32},{48,40},{56,48},{9,1},{17,9},... | collective-permute-start | bytes 18440 | tf_op jit(solution)/shard_map/ppermute | solution.py:23
  206.9 10.3 %collective-permute-start.26 = (f32[3,1,18,128]{3,2,1,0:T(8,128)S(1)}, f32[3,1,18,128]{3,2,1,0:T(8,128)S(1)}, u32[]{:S(2)}, u32[]{:S(2)}) collective-permute-start(f32[3,1,18,128]{3,2,1,0:T(8,128)S(1)} %get-tuple-element.29), channel_id=1, source_target_pairs={{1,0},{2,1},{3,2},{4,3},{5,4},{6,5},{7,6},{9,8},{10,9},{11,10},{12... | collective-permute-start | bytes 82952 | tf_op jit(solution)/shard_map/ppermute | solution.py:23
  208.2 9.0 %collective-permute-start.27 = (f32[3,1,18,128]{3,2,1,0:T(8,128)S(1)}, f32[3,1,18,128]{3,2,1,0:T(8,128)S(1)}, u32[]{:S(2)}, u32[]{:S(2)}) collective-permute-start(f32[3,1,18,128]{3,2,1,0:T(8,128)S(1)} %get-tuple-element.30), channel_id=1, source_target_pairs={{0,1},{1,2},{2,3},{3,4},{4,5},{5,6},{6,7},{8,9},{9,10},{10,11},{11... | collective-permute-start | bytes 82952 | tf_op jit(solution)/shard_map/ppermute | solution.py:20
  (14 other events, 160.1 us)
where the time goes:
time: 238 us; the launch traced here: 234 us
  starting transfers between devices  99.6 us (42%)
  local copies, waits for them, and re-layouts  52.9 us (22%)
  other arithmetic  48.3 us (20%)
  waiting for transfers between devices  32.2 us (14%)
    ppermute x15, starting transfers between devices, padded(): lax.ppermute(lax.slice_in_dim(block, block.shape[dim] - width, None, axis...  47 us
    ppermute x15, starting transfers between devices, padded(): lax.ppermute(lax.slice_in_dim(block, 0, width, axis=dim), axis, backward)  25.1 us
    ppermute x15, waiting for transfers between devices, padded(): lax.ppermute(lax.slice_in_dim(block, 0, width, axis=dim), axis, backward)  24.3 us
    scatter-add x4, other arithmetic, on_device(): forcing = forcing.reshape(3, -1).at[:, cell_index].add(got_values[:, :, s...  23.7 us
    mul x4, other arithmetic, on_device(): following = 2.0 * current - previous + step_square * forcing / density  18.3 us
    all_to_all x1, starting transfers between devices, on_device(): lax.all_to_all(send_labels.reshape(groups, capacity, labels.shape[1]), ('...  15.2 us
    gather x4, local copies, waits for them, and re-layouts, on_device(): payload = jnp.take_along_axis(traces, sample_picks, axis=2)  15.2 us
    all_to_all x1, starting transfers between devices, on_device(): lax.all_to_all(send_values.reshape((groups, capacity) + tail), ('lat', 'r...  12.2 us
  transfers between devices with their start and end apart: 32, of which 11 were waited for; matrix products, arithmetic and copies ran while one was open for 14% of the time, Pallas kernels for 0%

commit v1 on v0

v1 whole, which is shorter than its diff:
```python
import jax
import jax.numpy as jnp
from jax import lax
from jax.experimental import pallas as pl
from jax.experimental.pallas import tpu as pltpu
from jax.sharding import PartitionSpec as P

STEPS = 4
STEP_SQUARE = 0.16
TABLE = ((0, 2, 2), (2, 1, 3), (2, 3, 1))
CR, CL, CE = 4, 16, 128
HALO = 4
ROWS = CL + 2 * HALO
CAP = 4
SLOTS = 6
STATIONS = 128
F32 = jnp.float32
I32 = jnp.int32


def iota(shape, dim):
    return lax.broadcasted_iota(I32, shape, dim)


def fold(tiles, at):
    lane, sub = iota((8, 128), 1), iota((8, 128), 0)
    rows = []
    for start in range(0, len(tiles), 16):
        gathered = jnp.zeros((8, 128), F32)
        for i, tile in enumerate(tiles[start : start + 16]):
            column = jnp.broadcast_to(tile[:, at : at + 1], (8, 128))
            gathered = jnp.where(lane == i * 8 + sub, column, gathered)
        rows.append(jnp.sum(gathered, axis=0, keepdims=True))
    return rows


def unfold(ref, first_row, tile):
    row = first_row + tile // 16
    spread = jnp.broadcast_to(ref[row : row + 1, :], (8, 128))
    return jnp.take_along_axis(spread, (tile % 16) * 8 + iota((8, 128), 0), axis=1)


def column(ref, first_row, k, r):
    first = (k * CR + r) * (ROWS // 8)
    return jnp.concatenate([unfold(ref, first_row, first + i) for i in range(ROWS // 8)], axis=0)


def tiles_of(ref, count, first=0):
    return [
        ref[first + k, r, 8 * i : 8 * i + 8, :]
        for k in range(count)
        for r in range(CR)
        for i in range(ROWS // 8)
    ]


def put_columns(tiles, left_ref, right_ref, first_row):
    for ref, at in ((left_ref, 0), (right_ref, CE - 1)):
        for i, row in enumerate(fold(tiles, at)):
            ref[first_row + i : first_row + i + 1, :] = row


def put_faces(u_ref, down_ref, up_ref, left_ref, right_ref):
    for k in range(3):
        down_ref[k] = u_ref[k, 0]
        up_ref[k] = u_ref[k, CR - 1]
    left_ref[...] = jnp.zeros_like(left_ref)
    right_ref[...] = jnp.zeros_like(right_ref)
    put_columns(tiles_of(u_ref, 3), left_ref, right_ref, 0)


def edges_kernel(cur, prv, mod, den, low, high):
    fields = (
        [cur.at[k] for k in range(3)]
        + [prv.at[k] for k in range(3)]
        + [mod.at[k] for k in range(4)]
        + [den]
    )
    for f, ref in enumerate(fields):
        for r in range(CR):
            spot = slice(HALO * (r % 2), HALO * (r % 2) + HALO)
            low[f, r // 2, spot, :] = ref[r, 0:HALO, :]
            high[f, r // 2, spot, :] = ref[r, CL - HALO : CL, :]


def pack_kernel(offsets, receivers, owners, traces, out, window):
    lane, sub = iota((8, 128), 1), iota((8, 128), 0)
    pattern = (lane // 8) % STEPS
    mine = (lane // 32) == sub
    for s in range(STATIONS):
        offset = offsets[s]
        tile = offset // 128
        inside = offset % 128
        first = traces[s, :, pl.ds(pl.multiple_of(tile * 128, 128), 128)]
        second = traces[
            s, :, pl.ds(pl.multiple_of(jnp.minimum(tile + 1, 3) * 128, 128), 128)
        ]
        merged = jnp.where(lane[:3] >= inside, first, second)
        picked = jnp.take_along_axis(merged, (inside + pattern[:3]) % 128, axis=1)
        window[s : s + 1, :] = jnp.sum(
            jnp.where(mine[:3], picked, 0.0), axis=0, keepdims=True
        )

    owner_row = owners[...]
    q = receivers[...]
    r, l, e = q // 2048, (q // 128) % CL, q % 128
    wide_sub, wide_lane = iota((128, 128), 0), iota((128, 128), 1)
    owner_cols = jnp.transpose(jnp.broadcast_to(owner_row.astype(F32), (128, 128)))
    same = (owner_cols.astype(I32) == owner_row) & (wide_sub < wide_lane)
    rank = jnp.sum(jnp.where(same, 1.0, 0.0), axis=0, keepdims=True).astype(I32)

    lefts, rights = [], []
    for shift in (-1, 0, 1):
        slot = (shift + 1) * CAP + rank
        half, j = slot // SLOTS, slot % SLOTS
        if shift == 0:
            row, near = l, l >= 0
        elif shift == -1:
            row, near = CL + l, l <= HALO - 2
        else:
            row, near = l + HALO + HALO, l >= CL - HALO + 1
        target = owner_row + 8 * shift
        ok = near & (target >= 0) & (target < 64)
        place = jnp.where(ok, half * 64 + target, -1)
        lefts.append(jnp.where(wide_sub == place, 1.0, 0.0))
        sheet = jnp.transpose(
            jnp.concatenate(
                [
                    j.astype(F32),
                    (r * ROWS + row).astype(F32),
                    e.astype(F32),
                    jnp.zeros((5, 128), F32),
                ],
                axis=0,
            )
        )
        words = jnp.where(
            wide_lane < 96,
            window[...],
            jnp.where(
                wide_lane < 104,
                jnp.broadcast_to(sheet[:, 1:2], (128, 128)),
                jnp.broadcast_to(sheet[:, 2:3], (128, 128)),
            ),
        )
        slots = jnp.broadcast_to(sheet[:, 0:1], (128, 128)).astype(I32)
        rights.append(jnp.where((wide_lane % 8 == slots) & (wide_lane < 112), words, 0.0))
    packed = lax.dot_general(
        jnp.concatenate(lefts, axis=1),
        jnp.concatenate(rights, axis=0),
        (((1,), (0,)), ((), ())),
        precision=lax.Precision.HIGHEST,
        preferred_element_type=F32,
    )
    out[:, :128] = packed[:64]
    out[:, 128:] = packed[64:]


def widen_kernel(
    cur, prv, mod, den, from_low, from_high, u, v, m, c, down, up, left, right
):
    lat = lax.axis_index("lat")
    has_low, has_high = lat > 0, lat < lax.axis_size("lat") - 1

    def ghosts(f, r):
        spot = slice(HALO * (r % 2), HALO * (r % 2) + HALO)
        return jnp.concatenate(
            [
                jnp.where(has_high, from_high[f, r // 2, spot, :], 0.0),
                jnp.where(has_low, from_low[f, r // 2, spot, :], 0.0),
            ],
            axis=0,
        )

    for r in range(CR):
        for k in range(3):
            u[k, r, 0:CL, :] = cur[k, r]
            u[k, r, CL:ROWS, :] = ghosts(k, r)
            v[k, r, 0:CL, :] = prv[k, r]
            v[k, r, CL:ROWS, :] = ghosts(3 + k, r)
        for j in range(4):
            m[j, r, 0:CL, :] = mod[j, r]
            m[j, r, CL:ROWS, :] = ghosts(6 + j, r)
        c[r, 0:CL, :] = STEP_SQUARE / den[r]
        spot = slice(HALO * (r % 2), HALO * (r % 2) + HALO)
        outer = STEP_SQUARE / jnp.concatenate(
            [from_high[10, r // 2, spot, :], from_low[10, r // 2, spot, :]], axis=0
        )
        present = jnp.where(iota((8, 128), 0) < HALO, has_high.astype(I32), has_low.astype(I32))
        c[r, CL:ROWS, :] = jnp.where(present > 0, outer, 0.0)
    for k in range(3):
        down[k] = u[k, 0]
        up[k] = u[k, CR - 1]
    for i, j in enumerate((0, 2)):
        down[3 + i] = m[j, 0]
        up[3 + i] = m[j, CR - 1]
    left[...] = jnp.zeros_like(left)
    right[...] = jnp.zeros_like(right)
    put_columns(tiles_of(u, 3), left, right, 0)
    put_columns(tiles_of(m, 3, 1), left, right, 3)


def force(k, r, u, low, high, at_left, at_right, ar, al, au, ad):
    jr, jl, je = TABLE[k]
    here = u[k, r]
    below = u[k, r - 1] if r > 0 else low[k]
    above = u[k, r + 1] if r < CR - 1 else high[k]
    total = ar[jr // 2, r + 1] * (above - here) - ar[jr // 2, r] * (here - below)
    flux = al[jl - 1, r] * (pltpu.roll(here, ROWS - 1, 0) - here)
    total = total + (flux - pltpu.roll(flux, 1, 0))
    lane = iota((ROWS, CE), 1)
    after = jnp.where(lane == CE - 1, column(at_right, 0, k, r), pltpu.roll(here, CE - 1, 1))
    before = jnp.where(lane == 0, column(at_left, 0, k, r), pltpu.roll(here, 1, 1))
    return total + (au[je - 1, r] * (after - here) + ad[je - 1, r] * (before - here))


def radial_ends(low, high, count):
    rad = lax.axis_index("rad")
    lows = [jnp.where(rad > 0, low[k], 0.0) for k in range(count)]
    highs = [
        jnp.where(rad < lax.axis_size("rad") - 1, high[k], 0.0) for k in range(count)
    ]
    return lows, highs


def prepare_kernel(u, v, m, c, low, high, at_left, at_right, ar, al, au, ad, following):
    lows, highs = radial_ends(low, high, 5)
    lane = iota((ROWS, CE), 1)
    for i, j in enumerate((0, 2)):
        layers = [lows[3 + i]] + [m[j, r] for r in range(CR)] + [highs[3 + i]]
        for face in range(CR + 1):
            ar[i, face] = 0.5 * (layers[face] + layers[face + 1])
    for j in (1, 2, 3):
        for r in range(CR):
            here = m[j, r]
            al[j - 1, r] = 0.5 * (here + pltpu.roll(here, ROWS - 1, 0))
            after = jnp.where(
                lane == CE - 1, column(at_right, 3, j - 1, r), pltpu.roll(here, CE - 1, 1)
            )
            before = jnp.where(lane == 0, column(at_left, 3, j - 1, r), pltpu.roll(here, 1, 1))
            au[j - 1, r] = 0.5 * (here + after)
            ad[j - 1, r] = 0.5 * (here + before)
    for k in range(3):
        for r in range(CR):
            total = force(k, r, u, lows, highs, at_left, at_right, ar, al, au, ad)
            following[k, r] = 2.0 * u[k, r] - v[k, r] + c[r] * total


def scatter_kernel(got, free, c, first, sources, down, up, left, right, weights, picks):
    turned = jnp.transpose(jnp.concatenate([got[:, :128], got[:, 128:]], axis=0))
    cell_rows, cell_lanes = iota((CR * ROWS, 128), 0), iota((CE, 128), 0)
    for j in range(SLOTS):
        span = slice(128 * j, 128 * j + 128)
        place = turned[96 + j : 97 + j].astype(I32)
        around = turned[104 + j : 105 + j].astype(I32)
        picks[:, span] = jnp.where(cell_lanes == around, 1.0, 0.0)
        here = cell_rows == place
        for w in range(3 * STEPS):
            weights[w * CR * ROWS : (w + 1) * CR * ROWS, span] = jnp.where(
                here, turned[w * 8 + j : w * 8 + j + 1], 0.0
            )
    summed = lax.dot_general(
        weights[...],
        picks[...],
        (((1,), (1,)), ((), ())),
        precision=lax.Precision.HIGHEST,
        preferred_element_type=F32,
    )
    for k in range(3):
        for r in range(CR):
            for t in range(STEPS):
                at = ((k * STEPS + t) * CR + r) * ROWS
                value = summed[at : at + ROWS] * c[r]
                if t == 0:
                    first[k, r] = free[k, r] + value
                else:
                    sources[t - 1, k, r] = value
    put_faces(first, down, up, left, right)


def step_kernel(t, u, v, c, sources, low, high, at_left, at_right, ar, al, au, ad, *outs):
    lows, highs = radial_ends(low, high, 3)
    following = outs[0]
    last = t == STEPS - 1
    for k in range(3):
        for r in range(CR):
            total = force(k, r, u, lows, highs, at_left, at_right, ar, al, au, ad)
            value = 2.0 * u[k, r] - v[k, r] + c[r] * total + sources[t - 1, k, r]
            if last:
                following[k, r] = value[:CL]
                outs[1][k, r] = u[k, r, 0:CL, :]
            else:
                following[k, r] = value
    if not last:
        put_faces(following, *outs[1:])


def call(kernel, outs, args, scratch=(), smem=0):
    vmem = pl.BlockSpec(memory_space=pltpu.VMEM)
    specs = [pl.BlockSpec(memory_space=pltpu.SMEM)] * smem + [vmem] * (len(args) - smem)
    return pl.pallas_call(
        kernel,
        out_shape=[jax.ShapeDtypeStruct(shape, F32) for shape in outs],
        in_specs=specs,
        out_specs=[vmem] * len(outs),
        scratch_shapes=[pltpu.VMEM(shape, F32) for shape in scratch],
        compiler_params=pltpu.CompilerParams(vmem_limit_bytes=32 * 1024 * 1024),
    )(*args)


def shifted(block, axis, by):
    count = lax.axis_size(axis)
    return lax.ppermute(block, axis, [(i, (i + by) % count) for i in range(count)])


def swap_faces(down, up, left, right):
    low = shifted(up, "rad", 1)
    high = shifted(down, "rad", -1)
    at_left = shifted(right, "span", 1)
    at_right = shifted(left, "span", -1)
    return low, high, at_left, at_right


def on_device(current, previous, moduli, density, traces, receivers, owners, offsets):
    wide = (3, CR, ROWS, CE)
    edge = (11, 2, 8, CE)
    faces = [(3, ROWS, CE), (3, ROWS, CE), (8, CE), (8, CE)]

    low_rows, high_rows = call(
        edges_kernel, [edge, edge], (current, previous, moduli, density)
    )
    from_low = shifted(high_rows, "lat", 1)
    from_high = shifted(low_rows, "lat", -1)

    (packed,) = call(
        pack_kernel,
        [(64, 256)],
        (offsets, receivers.reshape(1, 128), owners.reshape(1, 128), traces),
        scratch=[(STATIONS, 128)],
        smem=1,
    )
    got = lax.all_to_all(packed, ("lat", "rad"), 0, 0, tiled=True)

    u, v, m, c, *ends = call(
        widen_kernel,
        [wide, wide, (4, CR, ROWS, CE), (CR, ROWS, CE)]
        + [(5, ROWS, CE), (5, ROWS, CE), (8, CE), (8, CE)],
        (current, previous, moduli, density, from_low, from_high),
    )
    *coefficients, free = call(
        prepare_kernel,
        [(2, CR + 1, ROWS, CE), wide, wide, wide, wide],
        (u, v, m, c, *swap_faces(*ends)),
    )
    first, sources, *ends = call(
        scatter_kernel,
        [wide, (STEPS - 1,) + wide] + faces,
        (got, free, c),
        scratch=[(3 * STEPS * CR * ROWS, 128 * SLOTS), (CE, 128 * SLOTS)],
    )
    v, u = u, first
    for t in range(1, STEPS):
        args = (u, v, c, sources, *swap_faces(*ends), *coefficients)

        def kernel(*refs, t=t):
            step_kernel(t, *refs)

        if t == STEPS - 1:
            return tuple(call(kernel, [(3, CR, CL, CE)] * 2, args))
        following, *ends = call(kernel, [wide] + faces, args)
        v, u = u, following


def solution(mesh):
    in_specs = (
        P(None, "rad", "lat", "span"),
        P(None, "rad", "lat", "span"),
        P(None, "rad", "lat", "span"),
        P("rad", "lat", "span"),
        P(("span", "lat", "rad"), None, None),
        P(("span", "lat", "rad")),
        P(("span", "lat", "rad"), None),
        P(("span", "lat", "rad")),
    )
    out_specs = (P(None, "rad", "lat", "span"), P(None, "rad", "lat", "span"))
    return jax.shard_map(
        on_device, mesh=mesh, in_specs=in_specs, out_specs=out_specs, check_vma=False
    )
```

time: 238 us -> 67.2 us (0.28); the launches traced: 234 us -> 66.9 us
  starting transfers between devices: 99.6 us -> 36.6 us
  other arithmetic: 48.3 us -> 0 us
  local copies, waits for them, and re-layouts: 52.9 us -> 6.5 us
  waiting for transfers between devices: 32.2 us -> 14.7 us
  Pallas kernels: 0 us -> 8.26 us
    ppermute x30 -> x18, starting transfers between devices: 72.1 us -> 24.4 us  [shifted(): lax.ppermute(block, axis, [(i, (i + by) % count) for i in range(count)])]
    scatter-add x4 -> x0, other arithmetic: 23.7 us -> none  [on_device(): forcing = forcing.reshape(3, -1).at[:, cell_index].add(got_values[:, :, s...]
    mul x4 -> x0, other arithmetic: 18.3 us -> none  [on_device(): following = 2.0 * current - previous + step_square * forcing / density]
    ppermute x30 -> x18, waiting for transfers between devices: 26 us -> 9.12 us  [shifted(): lax.ppermute(block, axis, [(i, (i + by) % count) for i in range(count)])]
    all_to_all x2 -> x1, starting transfers between devices: 27.4 us -> 12.2 us  [on_device(): got = lax.all_to_all(packed, ('lat', 'rad'), 0, 0, tiled=True)]
    gather x4 -> x0, local copies, waits for them, and re-layouts: 15.2 us -> none  [on_device(): payload = jnp.take_along_axis(traces, sample_picks, axis=2)]
    mul x4 -> x0, local copies, waits for them, and re-layouts: 11.4 us -> none  [on_device(): following = 2.0 * current - previous + step_square * forcing / density]
    another operation x5 -> x0, local copies, waits for them, and re-layouts: 10.8 us -> none  [the longest x4 10.7 us: forces(): return jnp.stack(pieces)]
  transfers between devices with their start and end apart: 32 -> 19, of which waited for: 11 -> 7; matrix products, arithmetic and copies ran while one was open for 14% -> 4% of each run, Pallas kernels for 0% -> 4%
where the time goes in v1:
time: 67.2 us; the launch traced here: 66.9 us
  starting transfers between devices  36.6 us (54%)
  waiting for transfers between devices  14.7 us (22%)
  Pallas kernels  8.26 us (12%)
  local copies, waits for them, and re-layouts  6.5 us (10%)
  between operations  0.83 us (1%)
    ppermute x18, starting transfers between devices, shifted(): lax.ppermute(block, axis, [(i, (i + by) % count) for i in range(count)])  24.4 us
    all_to_all x1, starting transfers between devices, on_device(): got = lax.all_to_all(packed, ('lat', 'rad'), 0, 0, tiled=True)  12.2 us
    ppermute x18, waiting for transfers between devices, shifted(): lax.ppermute(block, axis, [(i, (i + by) % count) for i in range(count)])  9.12 us
    pallas_call x8, Pallas kernels, call(): pl.pallas_call(kernel, out_shape=[jax.ShapeDtypeStruct(shape, F32) for sh...  8.26 us
    unnamed x24, local copies, waits for them, and re-layouts  5.81 us
    all_to_all x1, waiting for transfers between devices, on_device(): got = lax.all_to_all(packed, ('lat', 'rad'), 0, 0, tiled=True)  5.56 us
  transfers between devices with their start and end apart: 19, of which 7 were waited for; matrix products, arithmetic and copies ran while one was open for 4% of the time, Pallas kernels for 4%

profile of v1, /device:TPU:1, one launch (start us, length us, event | category | flops | bytes accessed | tf_op | source)
XLA Modules:
  0.0 66.9 jit_solution(6669824501138657984)
XLA Ops:
  0.6 0.9 %copy-done = f32[4,4,16,128]{3,2,1,0:T(8,128)S(1)} copy-done((f32[4,4,16,128]{3,2,1,0:T(8,128)S(1)}, f32[4,4,16,128]{3,2,1,0:T(8,128)}, u32[]{:S(2)}) %copy-start) | copy-done | bytes 131096
  1.5 0.9 %copy-done.2 = f32[3,4,16,128]{3,2,1,0:T(8,128)S(1)} copy-done((f32[3,4,16,128]{3,2,1,0:T(8,128)S(1)}, f32[3,4,16,128]{3,2,1,0:T(8,128)}, u32[]{:S(2)}) %copy-start.2) | copy-done | bytes 98328
  2.4 0.9 %copy-done.4 = f32[3,4,16,128]{3,2,1,0:T(8,128)S(1)} copy-done((f32[3,4,16,128]{3,2,1,0:T(8,128)S(1)}, f32[3,4,16,128]{3,2,1,0:T(8,128)}, u32[]{:S(2)}) %copy-start.4) | copy-done | bytes 98328
  3.3 0.8 %copy-done.6 = f32[4,16,128]{2,1,0:T(8,128)S(1)} copy-done((f32[4,16,128]{2,1,0:T(8,128)S(1)}, f32[4,16,128]{2,1,0:T(8,128)}, u32[]{:S(2)}) %copy-start.6) | copy-done | bytes 32792
  4.1 3.8 %collective-permute-start = (f32[11,2,8,128]{3,2,1,0:T(8,128)S(1)}, f32[11,2,8,128]{3,2,1,0:T(8,128)S(1)}, u32[]{:S(2)}, u32[]{:S(2)}) collective-permute-start(f32[11,2,8,128]{3,2,1,0:T(8,128)S(1)} %get-tuple-element.33), channel_id=1, source_target_pairs={{0,8},{8,16},{16,24},{24,32},{32,40},{40,48},{48,56},{56,0},{1,9},... | collective-permute-start | bytes 270344 | tf_op jit(solution)/shard_map/ppermute | solution.py:313
  7.9 2.3 %collective-permute-start.1 = (f32[11,2,8,128]{3,2,1,0:T(8,128)S(1)}, f32[11,2,8,128]{3,2,1,0:T(8,128)S(1)}, u32[]{:S(2)}, u32[]{:S(2)}) collective-permute-start(f32[11,2,8,128]{3,2,1,0:T(8,128)S(1)} %get-tuple-element.34), channel_id=1, source_target_pairs={{0,56},{8,0},{16,8},{24,16},{32,24},{40,32},{48,40},{56,48},{1,57}... | collective-permute-start | bytes 270344 | tf_op jit(solution)/shard_map/ppermute | solution.py:313
  10.2 1.7 %copy.11.traces = f32[128,3,512]{2,1,0:T(4,128)S(1)} copy(f32[128,3,512]{2,0,1:T(8,128)} %param.12) | data formatting | bytes 1572864 | tf_op args[4]
  12.6 2.3 %shard_map.95 = f32[64,256]{1,0:T(8,128)S(1)} custom-call(s32[128]{0:T(128)S(1)} %copy-done.8, s32[1,128]{1,0:T(1,128)S(1)} %bitcast.8, s32[1,128]{1,0:T(1,128)S(1)} %bitcast.9, f32[128,3,512]{2,1,0:T(4,128)S(1)} %copy.11.traces), custom_call_target="tpu_custom_call" | custom-call | tf_op jit(solution)/shard_map/pallas_call | solution.py:301
  15.6 12.2 %all-to-all-start = ((f32[64,1,256]{2,1,0:T(1,128)}), f32[64,1,256]{2,1,0:T(1,128)S(1)}, u32[]{:S(2)}, u32[]{:S(2)}) async-start(f32[64,1,256]{2,1,0:T(1,128)} %copy.12), calls=%async_computation | async-start | bytes 131072 | tf_op jit(solution)/shard_map/all_to_all | solution.py:342
  28.1 1.1 %collective-permute-start.2 = (f32[5,24,128]{2,1,0:T(8,128)S(1)}, f32[5,24,128]{2,1,0:T(8,128)S(1)}, u32[]{:S(2)}, u32[]{:S(2)}) collective-permute-start(f32[5,24,128]{2,1,0:T(8,128)S(1)} %get-tuple-element.39), channel_id=1, source_target_pairs={{0,1},{1,2},{2,3},{3,4},{4,5},{5,6},{6,7},{7,0},{8,9},{9,10},{10,1... | collective-permute-start | bytes 184328 | tf_op jit(solution)/shard_map/ppermute | solution.py:313
  29.2 1.7 %collective-permute-start.3 = (f32[5,24,128]{2,1,0:T(8,128)S(1)}, f32[5,24,128]{2,1,0:T(8,128)S(1)}, u32[]{:S(2)}, u32[]{:S(2)}) collective-permute-start(f32[5,24,128]{2,1,0:T(8,128)S(1)} %get-tuple-element.40), channel_id=1, source_target_pairs={{0,7},{1,0},{2,1},{3,2},{4,3},{5,4},{6,5},{7,6},{8,15},{9,8},{10,9... | collective-permute-start | bytes 184328 | tf_op jit(solution)/shard_map/ppermute | solution.py:313
  30.9 2.4 %collective-permute-start.4 = (f32[8,128]{1,0:T(8,128)S(1)}, f32[8,128]{1,0:T(8,128)S(1)}, u32[]{:S(2)}, u32[]{:S(2)}) collective-permute-start(f32[8,128]{1,0:T(8,128)S(1)} %get-tuple-element.41), channel_id=1, source_target_pairs={{0,64},{64,128},{128,192},{192,0},{1,65},{65,129},{129,193},{193,1... | collective-permute-start | bytes 12296 | tf_op jit(solution)/shard_map/ppermute | solution.py:313
  33.2 5.6 %all-to-all-done = f32[64,1,256]{2,1,0:T(1,128)S(1)} async-done(((f32[64,1,256]{2,1,0:T(1,128)}), f32[64,1,256]{2,1,0:T(1,128)S(1)}, u32[]{:S(2)}, u32[]{:S(2)}) %all-to-all-start) | async-done | bytes 65568 | tf_op jit(solution)/shard_map/all_to_all | solution.py:342
  39.5 3.2 %shard_map.99 = (f32[3,4,24,128]{3,2,1,0:T(8,128)S(1)}, f32[3,3,4,24,128]{4,3,2,1,0:T(8,128)S(1)}, f32[3,24,128]{2,1,0:T(8,128)S(1)}, f32[3,24,128]{2,1,0:T(8,12...) custom-call(f32[64,256]{1,0:T(8,128)S(1)} %bitcast.7, f32[3,4,24,128]{3,2,1,0:T(8,128)S(1)} %get-tuple-element.43.free, ...), custom_call_target="tpu_custom_call" | custom-call | tf_op jit(solution)/shard_map/pallas_call | solution.py:301
  43.4 2.2 %collective-permute-start.7 = (f32[3,24,128]{2,1,0:T(8,128)S(1)}, f32[3,24,128]{2,1,0:T(8,128)S(1)}, u32[]{:S(2)}, u32[]{:S(2)}) collective-permute-start(f32[3,24,128]{2,1,0:T(8,128)S(1)} %get-tuple-element.47), channel_id=1, source_target_pairs={{0,7},{1,0},{2,1},{3,2},{4,3},{5,4},{6,5},{7,6},{8,15},{9,8},{10,9... | collective-permute-start | bytes 110600 | tf_op jit(solution)/shard_map/ppermute | solution.py:313
  45.6 3.5 %collective-permute-start.8 = (f32[8,128]{1,0:T(8,128)S(1)}, f32[8,128]{1,0:T(8,128)S(1)}, u32[]{:S(2)}, u32[]{:S(2)}) collective-permute-start(f32[8,128]{1,0:T(8,128)S(1)} %get-tuple-element.48), channel_id=1, source_target_pairs={{0,64},{64,128},{128,192},{192,0},{1,65},{65,129},{129,193},{193,1... | collective-permute-start | bytes 12296 | tf_op jit(solution)/shard_map/ppermute | solution.py:313
  49.2 0.8 %collective-permute-done.8.refs_6_ = f32[8,128]{1,0:T(8,128)S(1)} collective-permute-done((f32[8,128]{1,0:T(8,128)S(1)}, f32[8,128]{1,0:T(8,128)S(1)}, u32[]{:S(2)}, u32[]{:S(2)}) %collective-permute-start.8) | collective-permute-done | bytes 4128 | tf_op jit(solution)/shard_map/ppermute | solution.py:313
  49.9 2.3 %collective-permute-done.9.refs_7_ = f32[8,128]{1,0:T(8,128)S(1)} collective-permute-done((f32[8,128]{1,0:T(8,128)S(1)}, f32[8,128]{1,0:T(8,128)S(1)}, u32[]{:S(2)}, u32[]{:S(2)}) %collective-permute-start.9) | collective-permute-done | bytes 4128 | tf_op jit(solution)/shard_map/ppermute | solution.py:313
  52.8 2.7 %collective-permute-start.11 = (f32[3,24,128]{2,1,0:T(8,128)S(1)}, f32[3,24,128]{2,1,0:T(8,128)S(1)}, u32[]{:S(2)}, u32[]{:S(2)}) collective-permute-start(f32[3,24,128]{2,1,0:T(8,128)S(1)} %get-tuple-element.56), channel_id=1, source_target_pairs={{0,7},{1,0},{2,1},{3,2},{4,3},{5,4},{6,5},{7,6},{8,15},{9,8},{10,9... | collective-permute-start | bytes 110600 | tf_op jit(solution)/shard_map/ppermute | solution.py:313
  56.0 0.8 %collective-permute-done.12.refs_6_ = f32[8,128]{1,0:T(8,128)S(1)} collective-permute-done((f32[8,128]{1,0:T(8,128)S(1)}, f32[8,128]{1,0:T(8,128)S(1)}, u32[]{:S(2)}, u32[]{:S(2)}) %collective-permute-start.12) | collective-permute-done | bytes 4128 | tf_op jit(solution)/shard_map/ppermute | solution.py:313
  56.8 2.3 %collective-permute-done.13.refs_7_ = f32[8,128]{1,0:T(8,128)S(1)} collective-permute-done((f32[8,128]{1,0:T(8,128)S(1)}, f32[8,128]{1,0:T(8,128)S(1)}, u32[]{:S(2)}, u32[]{:S(2)}) %collective-permute-start.13) | collective-permute-done | bytes 4128 | tf_op jit(solution)/shard_map/ppermute | solution.py:313
  59.7 2.7 %collective-permute-start.15 = (f32[3,24,128]{2,1,0:T(8,128)S(1)}, f32[3,24,128]{2,1,0:T(8,128)S(1)}, u32[]{:S(2)}, u32[]{:S(2)}) collective-permute-start(f32[3,24,128]{2,1,0:T(8,128)S(1)} %get-tuple-element.61), channel_id=1, source_target_pairs={{0,7},{1,0},{2,1},{3,2},{4,3},{5,4},{6,5},{7,6},{8,15},{9,8},{10,9... | collective-permute-start | bytes 110600 | tf_op jit(solution)/shard_map/ppermute | solution.py:313
  63.7 2.3 %collective-permute-done.17.refs_7_ = f32[8,128]{1,0:T(8,128)S(1)} collective-permute-done((f32[8,128]{1,0:T(8,128)S(1)}, f32[8,128]{1,0:T(8,128)S(1)}, u32[]{:S(2)}, u32[]{:S(2)}) %collective-permute-start.17) | collective-permute-done | bytes 4128 | tf_op jit(solution)/shard_map/ppermute | solution.py:313
  66.0 0.9 %shard_map.102 = (f32[3,4,16,128]{3,2,1,0:T(8,128)}, f32[3,4,16,128]{3,2,1,0:T(8,128)}) custom-call(f32[3,4,24,128]{3,2,1,0:T(8,128)S(1)} %get-tuple-element.59.refs_0_, f32[3,4,24,128]{3,2,1,0:T(8,128)S(1)} %get-tuple-element.54.refs_0_.refs_1_, f32[4,24,128]{2,1,0:T(8,128)S(1)} %get-tuple-element.38.c.refs_2_, ...), custom_call_target="tpu_custom_call" | custom-call | tf_op jit(solution)/shard_map/pallas_call | solution.py:301
  (47 shorter events, 6.1 us)
Async XLA Ops:
  0.6 0.9 %copy-start = (f32[4,4,16,128]{3,2,1,0:T(8,128)S(1)}, f32[4,4,16,128]{3,2,1,0:T(8,128)}, u32[]{:S(2)}) copy-start(f32[4,4,16,128]{3,2,1,0:T(8,128)} %mod.3) | copy-start | bytes 393220
  4.1 23.7 %collective-permute-start = (f32[11,2,8,128]{3,2,1,0:T(8,128)S(1)}, f32[11,2,8,128]{3,2,1,0:T(8,128)S(1)}, u32[]{:S(2)}, u32[]{:S(2)}) collective-permute-start(f32[11,2,8,128]{3,2,1,0:T(8,128)S(1)} %get-tuple-element.33), channel_id=1, source_target_pairs={{0,8},{8,16},{16,24},{24,32},{32,40},{40,48},{48,56},{56,0},{1,9},... | collective-permute-start | bytes 270344 | tf_op jit(solution)/shard_map/ppermute | solution.py:313
  7.9 19.9 %collective-permute-start.1 = (f32[11,2,8,128]{3,2,1,0:T(8,128)S(1)}, f32[11,2,8,128]{3,2,1,0:T(8,128)S(1)}, u32[]{:S(2)}, u32[]{:S(2)}) collective-permute-start(f32[11,2,8,128]{3,2,1,0:T(8,128)S(1)} %get-tuple-element.34), channel_id=1, source_target_pairs={{0,56},{8,0},{16,8},{24,16},{32,24},{40,32},{48,40},{56,48},{1,57}... | collective-permute-start | bytes 270344 | tf_op jit(solution)/shard_map/ppermute | solution.py:313
  12.6 15.2 %copy-start.5 = (f32[3,4,16,128]{3,2,1,0:T(8,128)S(1)}, f32[3,4,16,128]{3,2,1,0:T(8,128)}, u32[]{:S(2)}) copy-start(f32[3,4,16,128]{3,2,1,0:T(8,128)} %prv.3) | copy-start | bytes 294916
  14.9 13.0 %copy-start.1 = (f32[4,4,16,128]{3,2,1,0:T(8,128)S(1)}, f32[4,4,16,128]{3,2,1,0:T(8,128)}, u32[]{:S(2)}) copy-start(f32[4,4,16,128]{3,2,1,0:T(8,128)} %mod.3) | copy-start | bytes 393220
  14.9 13.0 %copy-start.3 = (f32[3,4,16,128]{3,2,1,0:T(8,128)S(1)}, f32[3,4,16,128]{3,2,1,0:T(8,128)}, u32[]{:S(2)}) copy-start(f32[3,4,16,128]{3,2,1,0:T(8,128)} %cur.3) | copy-start | bytes 294916
  15.6 12.3 %copy-start.7 = (f32[4,16,128]{2,1,0:T(8,128)S(1)}, f32[4,16,128]{2,1,0:T(8,128)}, u32[]{:S(2)}) copy-start(f32[4,16,128]{2,1,0:T(8,128)} %den.3) | copy-start | bytes 98308
  15.6 23.2 %all-to-all-start = ((f32[64,1,256]{2,1,0:T(1,128)}), f32[64,1,256]{2,1,0:T(1,128)S(1)}, u32[]{:S(2)}, u32[]{:S(2)}) async-start(f32[64,1,256]{2,1,0:T(1,128)} %copy.12), calls=%async_computation | async-start | bytes 131072 | tf_op jit(solution)/shard_map/all_to_all | solution.py:342
  28.1 10.7 %collective-permute-start.2 = (f32[5,24,128]{2,1,0:T(8,128)S(1)}, f32[5,24,128]{2,1,0:T(8,128)S(1)}, u32[]{:S(2)}, u32[]{:S(2)}) collective-permute-start(f32[5,24,128]{2,1,0:T(8,128)S(1)} %get-tuple-element.39), channel_id=1, source_target_pairs={{0,1},{1,2},{2,3},{3,4},{4,5},{5,6},{6,7},{7,0},{8,9},{9,10},{10,1... | collective-permute-start | bytes 184328 | tf_op jit(solution)/shard_map/ppermute | solution.py:313
  29.2 9.6 %collective-permute-start.3 = (f32[5,24,128]{2,1,0:T(8,128)S(1)}, f32[5,24,128]{2,1,0:T(8,128)S(1)}, u32[]{:S(2)}, u32[]{:S(2)}) collective-permute-start(f32[5,24,128]{2,1,0:T(8,128)S(1)} %get-tuple-element.40), channel_id=1, source_target_pairs={{0,7},{1,0},{2,1},{3,2},{4,3},{5,4},{6,5},{7,6},{8,15},{9,8},{10,9... | collective-permute-start | bytes 184328 | tf_op jit(solution)/shard_map/ppermute | solution.py:313
  30.9 7.9 %collective-permute-start.4 = (f32[8,128]{1,0:T(8,128)S(1)}, f32[8,128]{1,0:T(8,128)S(1)}, u32[]{:S(2)}, u32[]{:S(2)}) collective-permute-start(f32[8,128]{1,0:T(8,128)S(1)} %get-tuple-element.41), channel_id=1, source_target_pairs={{0,64},{64,128},{128,192},{192,0},{1,65},{65,129},{129,193},{193,1... | collective-permute-start | bytes 12296 | tf_op jit(solution)/shard_map/ppermute | solution.py:313
  33.2 5.6 %collective-permute-start.5 = (f32[8,128]{1,0:T(8,128)S(1)}, f32[8,128]{1,0:T(8,128)S(1)}, u32[]{:S(2)}, u32[]{:S(2)}) collective-permute-start(f32[8,128]{1,0:T(8,128)S(1)} %get-tuple-element.42), channel_id=1, source_target_pairs={{0,192},{64,0},{128,64},{192,128},{1,193},{65,1},{129,65},{193,129... | collective-permute-start | bytes 12296 | tf_op jit(solution)/shard_map/ppermute | solution.py:313
  42.7 9.5 %collective-permute-start.6 = (f32[3,24,128]{2,1,0:T(8,128)S(1)}, f32[3,24,128]{2,1,0:T(8,128)S(1)}, u32[]{:S(2)}, u32[]{:S(2)}) collective-permute-start(f32[3,24,128]{2,1,0:T(8,128)S(1)} %get-tuple-element.46), channel_id=1, source_target_pairs={{0,1},{1,2},{2,3},{3,4},{4,5},{5,6},{6,7},{7,0},{8,9},{9,10},{10,1... | collective-permute-start | bytes 110600 | tf_op jit(solution)/shard_map/ppermute | solution.py:313
  43.4 8.8 %collective-permute-start.7 = (f32[3,24,128]{2,1,0:T(8,128)S(1)}, f32[3,24,128]{2,1,0:T(8,128)S(1)}, u32[]{:S(2)}, u32[]{:S(2)}) collective-permute-start(f32[3,24,128]{2,1,0:T(8,128)S(1)} %get-tuple-element.47), channel_id=1, source_target_pairs={{0,7},{1,0},{2,1},{3,2},{4,3},{5,4},{6,5},{7,6},{8,15},{9,8},{10,9... | collective-permute-start | bytes 110600 | tf_op jit(solution)/shard_map/ppermute | solution.py:313
  45.6 4.3 %collective-permute-start.8 = (f32[8,128]{1,0:T(8,128)S(1)}, f32[8,128]{1,0:T(8,128)S(1)}, u32[]{:S(2)}, u32[]{:S(2)}) collective-permute-start(f32[8,128]{1,0:T(8,128)S(1)} %get-tuple-element.48), channel_id=1, source_target_pairs={{0,64},{64,128},{128,192},{192,0},{1,65},{65,129},{129,193},{193,1... | collective-permute-start | bytes 12296 | tf_op jit(solution)/shard_map/ppermute | solution.py:313
  49.2 3.0 %collective-permute-start.9 = (f32[8,128]{1,0:T(8,128)S(1)}, f32[8,128]{1,0:T(8,128)S(1)}, u32[]{:S(2)}, u32[]{:S(2)}) collective-permute-start(f32[8,128]{1,0:T(8,128)S(1)} %get-tuple-element.49), channel_id=1, source_target_pairs={{0,192},{64,0},{128,64},{192,128},{1,193},{65,1},{129,65},{193,129... | collective-permute-start | bytes 12296 | tf_op jit(solution)/shard_map/ppermute | solution.py:313
  52.7 6.4 %collective-permute-start.10 = (f32[3,24,128]{2,1,0:T(8,128)S(1)}, f32[3,24,128]{2,1,0:T(8,128)S(1)}, u32[]{:S(2)}, u32[]{:S(2)}) collective-permute-start(f32[3,24,128]{2,1,0:T(8,128)S(1)} %get-tuple-element.55), channel_id=1, source_target_pairs={{0,1},{1,2},{2,3},{3,4},{4,5},{5,6},{6,7},{7,0},{8,9},{9,10},{10,1... | collective-permute-start | bytes 110600 | tf_op jit(solution)/shard_map/ppermute | solution.py:313
  52.8 6.3 %collective-permute-start.11 = (f32[3,24,128]{2,1,0:T(8,128)S(1)}, f32[3,24,128]{2,1,0:T(8,128)S(1)}, u32[]{:S(2)}, u32[]{:S(2)}) collective-permute-start(f32[3,24,128]{2,1,0:T(8,128)S(1)} %get-tuple-element.56), channel_id=1, source_target_pairs={{0,7},{1,0},{2,1},{3,2},{4,3},{5,4},{6,5},{7,6},{8,15},{9,8},{10,9... | collective-permute-start | bytes 110600 | tf_op jit(solution)/shard_map/ppermute | solution.py:313
  55.4 1.4 %collective-permute-start.12 = (f32[8,128]{1,0:T(8,128)S(1)}, f32[8,128]{1,0:T(8,128)S(1)}, u32[]{:S(2)}, u32[]{:S(2)}) collective-permute-start(f32[8,128]{1,0:T(8,128)S(1)} %get-tuple-element.57), channel_id=1, source_target_pairs={{0,64},{64,128},{128,192},{192,0},{1,65},{65,129},{129,193},{193,1... | collective-permute-start | bytes 12296 | tf_op jit(solution)/shard_map/ppermute | solution.py:313
  56.0 3.0 %collective-permute-start.13 = (f32[8,128]{1,0:T(8,128)S(1)}, f32[8,128]{1,0:T(8,128)S(1)}, u32[]{:S(2)}, u32[]{:S(2)}) collective-permute-start(f32[8,128]{1,0:T(8,128)S(1)} %get-tuple-element.58), channel_id=1, source_target_pairs={{0,192},{64,0},{128,64},{192,128},{1,193},{65,1},{129,65},{193,129... | collective-permute-start | bytes 12296 | tf_op jit(solution)/shard_map/ppermute | solution.py:313
  59.6 6.4 %collective-permute-start.14 = (f32[3,24,128]{2,1,0:T(8,128)S(1)}, f32[3,24,128]{2,1,0:T(8,128)S(1)}, u32[]{:S(2)}, u32[]{:S(2)}) collective-permute-start(f32[3,24,128]{2,1,0:T(8,128)S(1)} %get-tuple-element.60), channel_id=1, source_target_pairs={{0,1},{1,2},{2,3},{3,4},{4,5},{5,6},{6,7},{7,0},{8,9},{9,10},{10,1... | collective-permute-start | bytes 110600 | tf_op jit(solution)/shard_map/ppermute | solution.py:313
  59.7 6.3 %collective-permute-start.15 = (f32[3,24,128]{2,1,0:T(8,128)S(1)}, f32[3,24,128]{2,1,0:T(8,128)S(1)}, u32[]{:S(2)}, u32[]{:S(2)}) collective-permute-start(f32[3,24,128]{2,1,0:T(8,128)S(1)} %get-tuple-element.61), channel_id=1, source_target_pairs={{0,7},{1,0},{2,1},{3,2},{4,3},{5,4},{6,5},{7,6},{8,15},{9,8},{10,9... | collective-permute-start | bytes 110600 | tf_op jit(solution)/shard_map/ppermute | solution.py:313
  62.3 1.4 %collective-permute-start.16 = (f32[8,128]{1,0:T(8,128)S(1)}, f32[8,128]{1,0:T(8,128)S(1)}, u32[]{:S(2)}, u32[]{:S(2)}) collective-permute-start(f32[8,128]{1,0:T(8,128)S(1)} %get-tuple-element.62), channel_id=1, source_target_pairs={{0,64},{64,128},{128,192},{192,0},{1,65},{65,129},{129,193},{193,1... | collective-permute-start | bytes 12296 | tf_op jit(solution)/shard_map/ppermute | solution.py:313
  62.9 3.0 %collective-permute-start.17 = (f32[8,128]{1,0:T(8,128)S(1)}, f32[8,128]{1,0:T(8,128)S(1)}, u32[]{:S(2)}, u32[]{:S(2)}) collective-permute-start(f32[8,128]{1,0:T(8,128)S(1)} %get-tuple-element.63), channel_id=1, source_target_pairs={{0,192},{64,0},{128,64},{192,128},{1,193},{65,1},{129,65},{193,129... | collective-permute-start | bytes 12296 | tf_op jit(solution)/shard_map/ppermute | solution.py:313
  (6 other events, 4.5 us)

commit v2 on v1

--- a/solution.py
+++ b/solution.py
@@ -69,47 +69,64 @@
     put_columns(tiles_of(u_ref, 3), left_ref, right_ref, 0)
 
 
-def edges_kernel(cur, prv, mod, den, low, high):
-    fields = (
-        [cur.at[k] for k in range(3)]
-        + [prv.at[k] for k in range(3)]
-        + [mod.at[k] for k in range(4)]
-        + [den]
-    )
-    for f, ref in enumerate(fields):
-        for r in range(CR):
-            spot = slice(HALO * (r % 2), HALO * (r % 2) + HALO)
-            low[f, r // 2, spot, :] = ref[r, 0:HALO, :]
-            high[f, r // 2, spot, :] = ref[r, CL - HALO : CL, :]
-
-
-def pack_kernel(offsets, receivers, owners, traces, out, window):
-    lane, sub = iota((8, 128), 1), iota((8, 128), 0)
-    pattern = (lane // 8) % STEPS
-    mine = (lane // 32) == sub
-    for s in range(STATIONS):
-        offset = offsets[s]
-        tile = offset // 128
-        inside = offset % 128
-        first = traces[s, :, pl.ds(pl.multiple_of(tile * 128, 128), 128)]
-        second = traces[
-            s, :, pl.ds(pl.multiple_of(jnp.minimum(tile + 1, 3) * 128, 128), 128)
-        ]
-        merged = jnp.where(lane[:3] >= inside, first, second)
-        picked = jnp.take_along_axis(merged, (inside + pattern[:3]) % 128, axis=1)
-        window[s : s + 1, :] = jnp.sum(
-            jnp.where(mine[:3], picked, 0.0), axis=0, keepdims=True
-        )
-
-    owner_row = owners[...]
-    q = receivers[...]
+def edge_rows(start, fields, out, room, sems):
+    first, copies = 0, []
+    for i, ref in enumerate(fields):
+        count = ref.shape[0]
+        copies.append(
+            pltpu.make_async_copy(
+                ref.at[:, :, pl.ds(start, 8), :], room.at[pl.ds(first, count)], sems.at[i]
+            )
+        )
+        first += count
+    for copy in copies:
+        copy.start()
+
+    def finish():
+        for copy in copies:
+            copy.wait()
+        inner = slice(0, HALO) if start == 0 else slice(8 - HALO, 8)
+        for f in range(first):
+            for r in range(CR):
+                spot = slice(HALO * (r % 2), HALO * (r % 2) + HALO)
+                out[f, r // 2, spot, :] = room[f, r, inner, :]
+
+    return finish
+
+
+def high_kernel(cur, prv, mod, den, high, room, sems):
+    edge_rows(CL - 8, (cur, prv, mod, den), high, room, sems)()
+
+
+def pack_kernel(
+    offsets_in, receivers_in, owners_in, traces_in, cur, prv, mod, den, out, low,
+    room, sems, traces, words_in, trace_sem, word_sems,
+):
+    copy = pltpu.make_async_copy(traces_in, traces, trace_sem)
+    copy.start()
+    small = [
+        pltpu.make_async_copy(ref, words_in.at[pl.ds(i, 1)], word_sems.at[i])
+        for i, ref in enumerate((offsets_in, receivers_in, owners_in))
+    ]
+    for one in small:
+        one.start()
+    finish_low = edge_rows(0, (cur, prv, mod, den), low, room, sems)
+    for one in small:
+        one.wait()
+    offset_row, q, owner_row = words_in[0:1], words_in[1:2], words_in[2:3]
     r, l, e = q // 2048, (q // 128) % CL, q % 128
     wide_sub, wide_lane = iota((128, 128), 0), iota((128, 128), 1)
-    owner_cols = jnp.transpose(jnp.broadcast_to(owner_row.astype(F32), (128, 128)))
-    same = (owner_cols.astype(I32) == owner_row) & (wide_sub < wide_lane)
+    sheet = jnp.transpose(
+        jnp.concatenate(
+            [owner_row.astype(F32), offset_row.astype(F32), jnp.zeros((6, 128), F32)], axis=0
+        )
+    )
+    owner_cols = jnp.broadcast_to(sheet[:, 0:1], (128, 128)).astype(I32)
+    offsets = jnp.broadcast_to(sheet[:, 1:2], (128, 128)).astype(I32)
+    same = (owner_cols == owner_row) & (wide_sub < wide_lane)
     rank = jnp.sum(jnp.where(same, 1.0, 0.0), axis=0, keepdims=True).astype(I32)
 
-    lefts, rights = [], []
+    lefts, lines = [], [e.astype(F32)]
     for shift in (-1, 0, 1):
         slot = (shift + 1) * CAP + rank
         half, j = slot // SLOTS, slot % SLOTS
@@ -123,27 +140,29 @@
         ok = near & (target >= 0) & (target < 64)
         place = jnp.where(ok, half * 64 + target, -1)
         lefts.append(jnp.where(wide_sub == place, 1.0, 0.0))
-        sheet = jnp.transpose(
-            jnp.concatenate(
-                [
-                    j.astype(F32),
-                    (r * ROWS + row).astype(F32),
-                    e.astype(F32),
-                    jnp.zeros((5, 128), F32),
-                ],
-                axis=0,
-            )
-        )
-        words = jnp.where(
-            wide_lane < 96,
-            window[...],
-            jnp.where(
-                wide_lane < 104,
-                jnp.broadcast_to(sheet[:, 1:2], (128, 128)),
-                jnp.broadcast_to(sheet[:, 2:3], (128, 128)),
-            ),
-        )
-        slots = jnp.broadcast_to(sheet[:, 0:1], (128, 128)).astype(I32)
+        lines += [j.astype(F32), (r * ROWS + row).astype(F32)]
+    sheet = jnp.transpose(jnp.concatenate(lines + [jnp.zeros((1, 128), F32)], axis=0))
+    finish_low()
+
+    inside = offsets % 128
+    tile = offsets // 128 + jnp.where(wide_lane < inside, 1, 0)
+    index = (inside + (wide_lane // 8) % STEPS) % 128
+    copy.wait()
+    window = jnp.broadcast_to(sheet[:, 0:1], (128, 128))
+    for k in range(3):
+        parts = [traces[k, :, 128 * i : 128 * i + 128] for i in range(4)]
+        merged = jnp.where(
+            tile == 0,
+            parts[0],
+            jnp.where(tile == 1, parts[1], jnp.where(tile == 2, parts[2], parts[3])),
+        )
+        picked = jnp.take_along_axis(merged, index, axis=1)
+        window = jnp.where(wide_lane // 32 == k, picked, window)
+    rights = []
+    for i in range(3):
+        slots = jnp.broadcast_to(sheet[:, 2 * i + 1 : 2 * i + 2], (128, 128)).astype(I32)
+        cells = jnp.broadcast_to(sheet[:, 2 * i + 2 : 2 * i + 3], (128, 128))
+        words = jnp.where((wide_lane >= 96) & (wide_lane < 104), cells, window)
         rights.append(jnp.where((wide_lane % 8 == slots) & (wide_lane < 112), words, 0.0))
     packed = lax.dot_general(
         jnp.concatenate(lefts, axis=1),
@@ -152,8 +171,8 @@
         precision=lax.Precision.HIGHEST,
         preferred_element_type=F32,
     )
-    out[:, :128] = packed[:64]
-    out[:, 128:] = packed[64:]
+    out[:, 0, :128] = packed[:64]
+    out[:, 0, 128:] = packed[64:]
 
 
 def widen_kernel(
@@ -246,8 +265,8 @@
             following[k, r] = 2.0 * u[k, r] - v[k, r] + c[r] * total
 
 
-def scatter_kernel(got, free, c, first, sources, down, up, left, right, weights, picks):
-    turned = jnp.transpose(jnp.concatenate([got[:, :128], got[:, 128:]], axis=0))
+def gather_sources(steps, got, weights, picks):
+    turned = jnp.transpose(jnp.concatenate([got[:, 0, :128], got[:, 0, 128:]], axis=0))
     cell_rows, cell_lanes = iota((CR * ROWS, 128), 0), iota((CE, 128), 0)
     for j in range(SLOTS):
         span = slice(128 * j, 128 * j + 128)
@@ -255,27 +274,36 @@
         around = turned[104 + j : 105 + j].astype(I32)
         picks[:, span] = jnp.where(cell_lanes == around, 1.0, 0.0)
         here = cell_rows == place
-        for w in range(3 * STEPS):
-            weights[w * CR * ROWS : (w + 1) * CR * ROWS, span] = jnp.where(
-                here, turned[w * 8 + j : w * 8 + j + 1], 0.0
-            )
-    summed = lax.dot_general(
+        for i, t in enumerate(steps):
+            for k in range(3):
+                line = (k * STEPS + t) * 8 + j
+                at = (i * 3 + k) * CR * ROWS
+                weights[at : at + CR * ROWS, span] = jnp.where(here, turned[line : line + 1], 0.0)
+    return lax.dot_general(
         weights[...],
         picks[...],
         (((1,), (1,)), ((), ())),
         precision=lax.Precision.HIGHEST,
         preferred_element_type=F32,
     )
+
+
+def first_kernel(got, free, c, first, down, up, left, right, weights, picks):
+    summed = gather_sources((0,), got, weights, picks)
     for k in range(3):
         for r in range(CR):
-            for t in range(STEPS):
-                at = ((k * STEPS + t) * CR + r) * ROWS
-                value = summed[at : at + ROWS] * c[r]
-                if t == 0:
-                    first[k, r] = free[k, r] + value
-                else:
-                    sources[t - 1, k, r] = value
+            at = (k * CR + r) * ROWS
+            first[k, r] = free[k, r] + summed[at : at + ROWS] * c[r]
     put_faces(first, down, up, left, right)
+
+
+def sources_kernel(got, c, sources, weights, picks):
+    summed = gather_sources(range(1, STEPS), got, weights, picks)
+    for t in range(STEPS - 1):
+        for k in range(3):
+            for r in range(CR):
+                at = ((t * 3 + k) * CR + r) * ROWS
+                sources[t, k, r] = summed[at : at + ROWS] * c[r]
 
 
 def step_kernel(t, u, v, c, sources, low, high, at_left, at_right, ar, al, au, ad, *outs):
@@ -295,16 +323,19 @@
         put_faces(following, *outs[1:])
 
 
-def call(kernel, outs, args, scratch=(), smem=0):
+def call(kernel, outs, args, scratch=(), hbm=0, us=1.0):
     vmem = pl.BlockSpec(memory_space=pltpu.VMEM)
-    specs = [pl.BlockSpec(memory_space=pltpu.SMEM)] * smem + [vmem] * (len(args) - smem)
+    specs = [pl.BlockSpec(memory_space=pltpu.HBM)] * hbm + [vmem] * (len(args) - hbm)
     return pl.pallas_call(
         kernel,
         out_shape=[jax.ShapeDtypeStruct(shape, F32) for shape in outs],
         in_specs=specs,
         out_specs=[vmem] * len(outs),
-        scratch_shapes=[pltpu.VMEM(shape, F32) for shape in scratch],
-        compiler_params=pltpu.CompilerParams(vmem_limit_bytes=32 * 1024 * 1024),
+        scratch_shapes=[pltpu.VMEM(s, F32) if isinstance(s, tuple) else s for s in scratch],
+        cost_estimate=pl.CostEstimate(
+            flops=0, bytes_accessed=int(us * 3_000_000), transcendentals=0
+        ),
+        compiler_params=pltpu.CompilerParams(vmem_limit_bytes=(60 if hbm else 32) * 1024 * 1024),
     )(*args)
 
 
@@ -326,19 +357,31 @@
     edge = (11, 2, 8, CE)
     faces = [(3, ROWS, CE), (3, ROWS, CE), (8, CE), (8, CE)]
 
-    low_rows, high_rows = call(
-        edges_kernel, [edge, edge], (current, previous, moduli, density)
-    )
+    fields = (current, previous, moduli, density.reshape((1,) + density.shape))
+    rooms = [(11, CR, 8, CE), pltpu.SemaphoreType.DMA((4,))]
+    (high_rows,) = call(high_kernel, [edge], fields, scratch=rooms, hbm=4)
     from_low = shifted(high_rows, "lat", 1)
+    packed, low_rows = call(
+        pack_kernel,
+        [(64, 1, 256), edge],
+        (
+            offsets.reshape(1, 128),
+            receivers.reshape(1, 128),
+            owners.reshape(1, 128),
+            traces.transpose(1, 0, 2),
+        )
+        + fields,
+        scratch=rooms
+        + [
+            (3, STATIONS, 512),
+            pltpu.VMEM((8, 128), I32),
+            pltpu.SemaphoreType.DMA(()),
+            pltpu.SemaphoreType.DMA((3,)),
+        ],
+        hbm=8,
+        us=2.0,
+    )
     from_high = shifted(low_rows, "lat", -1)
-
-    (packed,) = call(
-        pack_kernel,
-        [(64, 256)],
-        (offsets, receivers.reshape(1, 128), owners.reshape(1, 128), traces),
-        scratch=[(STATIONS, 128)],
-        smem=1,
-    )
     got = lax.all_to_all(packed, ("lat", "rad"), 0, 0, tiled=True)
 
     u, v, m, c, *ends = call(
@@ -352,11 +395,19 @@
         [(2, CR + 1, ROWS, CE), wide, wide, wide, wide],
         (u, v, m, c, *swap_faces(*ends)),
     )
-    first, sources, *ends = call(
-        scatter_kernel,
-        [wide, (STEPS - 1,) + wide] + faces,
+    cells = CR * ROWS
+    first, *ends = call(
+        first_kernel,
+        [wide] + faces,
         (got, free, c),
-        scratch=[(3 * STEPS * CR * ROWS, 128 * SLOTS), (CE, 128 * SLOTS)],
+        scratch=[(3 * cells, 128 * SLOTS), (CE, 128 * SLOTS)],
+    )
+    (sources,) = call(
+        sources_kernel,
+        [(STEPS - 1,) + wide],
+        (got, c),
+        scratch=[(3 * (STEPS - 1) * cells, 128 * SLOTS), (CE, 128 * SLOTS)],
+        us=3.0,
     )
     v, u = u, first
     for t in range(1, STEPS):

time: 67.2 us -> 60.9 us (0.906)
  local copies, waits for them, and re-layouts: 6.5 us -> 0.02 us
  waiting for transfers between devices: 14.7 us -> 11.5 us
  Pallas kernels: 8.26 us -> 10.8 us
  starting transfers between devices: 36.6 us -> 37.6 us
    unnamed x24 -> x8, local copies, waits for them, and re-layouts: 5.81 us -> 0.02 us
    all_to_all x1, waiting for transfers between devices: 5.56 us -> 1.58 us  [on_device(): got = lax.all_to_all(packed, ('lat', 'rad'), 0, 0, tiled=True)]
    pallas_call x8 -> x9, Pallas kernels: 8.26 us -> 10.8 us  [call(): pl.pallas_call(kernel, out_shape=[jax.ShapeDtypeStruct(shape, F32) for sh...]
    ppermute x18, starting transfers between devices: 24.4 us -> 25.5 us  [shifted(): lax.ppermute(block, axis, [(i, (i + by) % count) for i in range(count)])]
    ppermute x18, waiting for transfers between devices: 9.12 us -> 9.96 us  [shifted(): lax.ppermute(block, axis, [(i, (i + by) % count) for i in range(count)])]
    all_to_all x1 -> x0, local copies, waits for them, and re-layouts: 0.7 us -> none  [on_device(): got = lax.all_to_all(packed, ('lat', 'rad'), 0, 0, tiled=True)]
  transfers between devices with their start and end apart: 19 -> 19, of which waited for: 7 -> 8; matrix products, arithmetic and copies ran while one was open for 4% -> 0% of each run, Pallas kernels for 4% -> 10%
where the time goes in v2:
time: 60.9 us; the launch traced here: 60.7 us
  starting transfers between devices  37.6 us (62%)
  waiting for transfers between devices  11.5 us (19%)
  Pallas kernels  10.8 us (18%)
  between operations  0.78 us (1%)
    ppermute x18, starting transfers between devices, shifted(): lax.ppermute(block, axis, [(i, (i + by) % count) for i in range(count)])  25.5 us
    all_to_all x1, starting transfers between devices, on_device(): got = lax.all_to_all(packed, ('lat', 'rad'), 0, 0, tiled=True)  12.1 us
    pallas_call x9, Pallas kernels, call(): pl.pallas_call(kernel, out_shape=[jax.ShapeDtypeStruct(shape, F32) for sh...  10.8 us
    ppermute x18, waiting for transfers between devices, shifted(): lax.ppermute(block, axis, [(i, (i + by) % count) for i in range(count)])  9.96 us
    all_to_all x1, waiting for transfers between devices, on_device(): got = lax.all_to_all(packed, ('lat', 'rad'), 0, 0, tiled=True)  1.58 us
  transfers between devices with their start and end apart: 19, of which 8 were waited for; matrix products, arithmetic and copies ran while one was open for 0% of the time, Pallas kernels for 10%

profile of v2, /device:TPU:1, one launch (start us, length us, event | category | flops | bytes accessed | tf_op | source)
XLA Modules:
  0.0 60.7 jit_solution(8106176364132472103)
XLA Ops:
  0.6 1.6 %shard_map.96 = f32[11,2,8,128]{3,2,1,0:T(8,128)} custom-call(f32[3,4,16,128]{3,2,1,0:T(8,128)} %cur.5, f32[3,4,16,128]{3,2,1,0:T(8,128)} %prv.5, f32[4,4,16,128]{3,2,1,0:T(8,128)} %mod.5, f32[1,4,16,128]{3,2,1,0:T(8,128)} %bitcast.5), custom_call_target="tpu_custom_call" | custom-call | bytes 3000000 | tf_op jit(solution)/shard_map/pallas_call | solution.py:329
  2.2 3.8 %collective-permute-start = (f32[11,2,8,128]{3,2,1,0:T(8,128)}, f32[11,2,8,128]{3,2,1,0:T(8,128)S(1)}, u32[]{:S(2)}, u32[]{:S(2)}) collective-permute-start(f32[11,2,8,128]{3,2,1,0:T(8,128)} %shard_map.96), channel_id=1, source_target_pairs={{0,8},{8,16},{16,24},{24,32},{32,40},{40,48},{48,56},{56,0},{1,9},... | collective-permute-start | bytes 270344 | tf_op jit(solution)/shard_map/ppermute | solution.py:344
  6.1 2.8 %shard_map.95 = (f32[64,1,256]{2,1,0:T(1,128)}, f32[11,2,8,128]{3,2,1,0:T(8,128)}) custom-call(s32[1,128]{1,0:T(1,128)} %bitcast.8, s32[1,128]{1,0:T(1,128)} %bitcast.9, s32[1,128]{1,0:T(1,128)} %bitcast.10, f32[3,128,512]{2,1,0:T(8,128)} %bitcast.7, f32[3,4,16,128]{3,2,1,0:T(8,128)} %cur.5, f32[3,4,16,128]{3,2,1,0:T(8,128)} %prv.5, f32[4,4,16,128]{3,2,1,0:T(8,128)} %mod.5, ...), custom_call_target="tpu_custom_call" | custom-call | bytes 6000000 | tf_op jit(solution)/shard_map/pallas_call | solution.py:329
  8.9 2.3 %collective-permute-start.1 = (f32[11,2,8,128]{3,2,1,0:T(8,128)}, f32[11,2,8,128]{3,2,1,0:T(8,128)S(1)}, u32[]{:S(2)}, u32[]{:S(2)}) collective-permute-start(f32[11,2,8,128]{3,2,1,0:T(8,128)} %get-tuple-element.33), channel_id=1, source_target_pairs={{0,56},{8,0},{16,8},{24,16},{32,24},{40,32},{48,40},{56,48},{1,57}... | collective-permute-start | bytes 270344 | tf_op jit(solution)/shard_map/ppermute | solution.py:344
  11.2 12.1 %all-to-all-start = ((f32[64,1,256]{2,1,0:T(1,128)}), f32[64,1,256]{2,1,0:T(1,128)S(1)}, u32[]{:S(2)}, u32[]{:S(2)}) async-start(f32[64,1,256]{2,1,0:T(1,128)} %get-tuple-element.32), calls=%async_computation | async-start | bytes 131072 | tf_op jit(solution)/shard_map/all_to_all | solution.py:385
  23.6 1.1 %collective-permute-start.2 = (f32[5,24,128]{2,1,0:T(8,128)S(1)}, f32[5,24,128]{2,1,0:T(8,128)S(1)}, u32[]{:S(2)}, u32[]{:S(2)}) collective-permute-start(f32[5,24,128]{2,1,0:T(8,128)S(1)} %get-tuple-element.38), channel_id=1, source_target_pairs={{0,1},{1,2},{2,3},{3,4},{4,5},{5,6},{6,7},{7,0},{8,9},{9,10},{10,1... | collective-permute-start | bytes 184328 | tf_op jit(solution)/shard_map/ppermute | solution.py:344
  24.7 1.7 %collective-permute-start.3 = (f32[5,24,128]{2,1,0:T(8,128)S(1)}, f32[5,24,128]{2,1,0:T(8,128)S(1)}, u32[]{:S(2)}, u32[]{:S(2)}) collective-permute-start(f32[5,24,128]{2,1,0:T(8,128)S(1)} %get-tuple-element.39), channel_id=1, source_target_pairs={{0,7},{1,0},{2,1},{3,2},{4,3},{5,4},{6,5},{7,6},{8,15},{9,8},{10,9... | collective-permute-start | bytes 184328 | tf_op jit(solution)/shard_map/ppermute | solution.py:344
  26.4 2.4 %collective-permute-start.4 = (f32[8,128]{1,0:T(8,128)S(1)}, f32[8,128]{1,0:T(8,128)S(1)}, u32[]{:S(2)}, u32[]{:S(2)}) collective-permute-start(f32[8,128]{1,0:T(8,128)S(1)} %get-tuple-element.40), channel_id=1, source_target_pairs={{0,64},{64,128},{128,192},{192,0},{1,65},{65,129},{129,193},{193,1... | collective-permute-start | bytes 12296 | tf_op jit(solution)/shard_map/ppermute | solution.py:344
  28.7 0.8 %collective-permute-done.4.at_left = f32[8,128]{1,0:T(8,128)S(1)} collective-permute-done((f32[8,128]{1,0:T(8,128)S(1)}, f32[8,128]{1,0:T(8,128)S(1)}, u32[]{:S(2)}, u32[]{:S(2)}) %collective-permute-start.4) | collective-permute-done | bytes 4128 | tf_op jit(solution)/shard_map/ppermute | solution.py:344
  29.5 2.6 %collective-permute-done.5.at_right = f32[8,128]{1,0:T(8,128)S(1)} collective-permute-done((f32[8,128]{1,0:T(8,128)S(1)}, f32[8,128]{1,0:T(8,128)S(1)}, u32[]{:S(2)}, u32[]{:S(2)}) %collective-permute-start.5) | collective-permute-done | bytes 4128 | tf_op jit(solution)/shard_map/ppermute | solution.py:344
  32.1 0.6 %shard_map.98 = (f32[2,5,24,128]{3,2,1,0:T(8,128)S(1)}, f32[3,4,24,128]{3,2,1,0:T(8,128)S(1)}, f32[3,4,24,128]{3,2,1,0:T(8,128)S(1)}, f32[3,4,24,128]{3,2,1,0:T(8,128)S(1)}, f32[3,4,24,128]{3,2,1,0:T(8,128)S(1)}) custom-call(f32[3,4,24,128]{3,2,1,0:T(8,128)S(1)} %get-tuple-element.34.u.refs_1_, f32[3,4,24,128]{3,2,1,0:T(8,128)S(1)} %get-tuple-element.35.v, ...), custom_call_target="tpu_custom_call" | custom-call | bytes 3000000 | tf_op jit(solution)/shard_map/pallas_call | solution.py:329
  32.7 1.6 %all-to-all-done.got = f32[64,1,256]{2,1,0:T(1,128)S(1)} async-done(((f32[64,1,256]{2,1,0:T(1,128)}), f32[64,1,256]{2,1,0:T(1,128)S(1)}, u32[]{:S(2)}, u32[]{:S(2)}) %all-to-all-start) | async-done | bytes 65568 | tf_op jit(solution)/shard_map/all_to_all | solution.py:385
  34.3 1.1 %shard_map.99 = (f32[3,4,24,128]{3,2,1,0:T(8,128)S(1)}, f32[3,24,128]{2,1,0:T(8,128)S(1)}, f32[3,24,128]{2,1,0:T(8,128)S(1)}, f32[8,128]{1,0:T(8,128)S(1)}, f32[8,128]{1,0:T(8,128)S(1)}) custom-call(f32[64,1,256]{2,1,0:T(1,128)S(1)} %all-to-all-done.got, f32[3,4,24,128]{3,2,1,0:T(8,128)S(1)} %get-tuple-element.42.free, ...), custom_call_target="tpu_custom_call" | custom-call | bytes 3000000 | tf_op jit(solution)/shard_map/pallas_call | solution.py:329
  36.0 2.2 %collective-permute-start.7 = (f32[3,24,128]{2,1,0:T(8,128)S(1)}, f32[3,24,128]{2,1,0:T(8,128)S(1)}, u32[]{:S(2)}, u32[]{:S(2)}) collective-permute-start(f32[3,24,128]{2,1,0:T(8,128)S(1)} %get-tuple-element.45), channel_id=1, source_target_pairs={{0,7},{1,0},{2,1},{3,2},{4,3},{5,4},{6,5},{7,6},{8,15},{9,8},{10,9... | collective-permute-start | bytes 110600 | tf_op jit(solution)/shard_map/ppermute | solution.py:344
  38.2 3.6 %collective-permute-start.8 = (f32[8,128]{1,0:T(8,128)S(1)}, f32[8,128]{1,0:T(8,128)S(1)}, u32[]{:S(2)}, u32[]{:S(2)}) collective-permute-start(f32[8,128]{1,0:T(8,128)S(1)} %get-tuple-element.46), channel_id=1, source_target_pairs={{0,64},{64,128},{128,192},{192,0},{1,65},{65,129},{129,193},{193,1... | collective-permute-start | bytes 12296 | tf_op jit(solution)/shard_map/ppermute | solution.py:344
  41.8 2.5 %shard_map.100.refs_3_ = f32[3,3,4,24,128]{4,3,2,1,0:T(8,128)S(1)} custom-call(f32[64,1,256]{2,1,0:T(1,128)S(1)} %all-to-all-done.got, f32[4,24,128]{2,1,0:T(8,128)S(1)} %get-tuple-element.37.c.refs_2_), custom_call_target="tpu_custom_call" | custom-call | bytes 9000000 | tf_op jit(solution)/shard_map/pallas_call | solution.py:329
  45.4 2.7 %collective-permute-start.11 = (f32[3,24,128]{2,1,0:T(8,128)S(1)}, f32[3,24,128]{2,1,0:T(8,128)S(1)}, u32[]{:S(2)}, u32[]{:S(2)}) collective-permute-start(f32[3,24,128]{2,1,0:T(8,128)S(1)} %get-tuple-element.54), channel_id=1, source_target_pairs={{0,7},{1,0},{2,1},{3,2},{4,3},{5,4},{6,5},{7,6},{8,15},{9,8},{10,9... | collective-permute-start | bytes 110600 | tf_op jit(solution)/shard_map/ppermute | solution.py:344
  48.1 1.8 %collective-permute-start.12 = (f32[8,128]{1,0:T(8,128)S(1)}, f32[8,128]{1,0:T(8,128)S(1)}, u32[]{:S(2)}, u32[]{:S(2)}) collective-permute-start(f32[8,128]{1,0:T(8,128)S(1)} %get-tuple-element.55), channel_id=1, source_target_pairs={{0,64},{64,128},{128,192},{192,0},{1,65},{65,129},{129,193},{193,1... | collective-permute-start | bytes 12296 | tf_op jit(solution)/shard_map/ppermute | solution.py:344
  49.8 0.8 %collective-permute-done.12.refs_6_ = f32[8,128]{1,0:T(8,128)S(1)} collective-permute-done((f32[8,128]{1,0:T(8,128)S(1)}, f32[8,128]{1,0:T(8,128)S(1)}, u32[]{:S(2)}, u32[]{:S(2)}) %collective-permute-start.12) | collective-permute-done | bytes 4128 | tf_op jit(solution)/shard_map/ppermute | solution.py:344
  50.6 2.3 %collective-permute-done.13.refs_7_ = f32[8,128]{1,0:T(8,128)S(1)} collective-permute-done((f32[8,128]{1,0:T(8,128)S(1)}, f32[8,128]{1,0:T(8,128)S(1)}, u32[]{:S(2)}, u32[]{:S(2)}) %collective-permute-start.13) | collective-permute-done | bytes 4128 | tf_op jit(solution)/shard_map/ppermute | solution.py:344
  53.5 2.7 %collective-permute-start.15 = (f32[3,24,128]{2,1,0:T(8,128)S(1)}, f32[3,24,128]{2,1,0:T(8,128)S(1)}, u32[]{:S(2)}, u32[]{:S(2)}) collective-permute-start(f32[3,24,128]{2,1,0:T(8,128)S(1)} %get-tuple-element.59), channel_id=1, source_target_pairs={{0,7},{1,0},{2,1},{3,2},{4,3},{5,4},{6,5},{7,6},{8,15},{9,8},{10,9... | collective-permute-start | bytes 110600 | tf_op jit(solution)/shard_map/ppermute | solution.py:344
  56.7 0.8 %collective-permute-done.16.refs_6_ = f32[8,128]{1,0:T(8,128)S(1)} collective-permute-done((f32[8,128]{1,0:T(8,128)S(1)}, f32[8,128]{1,0:T(8,128)S(1)}, u32[]{:S(2)}, u32[]{:S(2)}) %collective-permute-start.16) | collective-permute-done | bytes 4128 | tf_op jit(solution)/shard_map/ppermute | solution.py:344
  57.5 2.3 %collective-permute-done.17.refs_7_ = f32[8,128]{1,0:T(8,128)S(1)} collective-permute-done((f32[8,128]{1,0:T(8,128)S(1)}, f32[8,128]{1,0:T(8,128)S(1)}, u32[]{:S(2)}, u32[]{:S(2)}) %collective-permute-start.17) | collective-permute-done | bytes 4128 | tf_op jit(solution)/shard_map/ppermute | solution.py:344
  59.8 0.9 %shard_map.103 = (f32[3,4,16,128]{3,2,1,0:T(8,128)}, f32[3,4,16,128]{3,2,1,0:T(8,128)}) custom-call(f32[3,4,24,128]{3,2,1,0:T(8,128)S(1)} %get-tuple-element.57.refs_0_, f32[3,4,24,128]{3,2,1,0:T(8,128)S(1)} %get-tuple-element.52.refs_0_.refs_1_, f32[4,24,128]{2,1,0:T(8,128)S(1)} %get-tuple-element.37.c.refs_2_, ...), custom_call_target="tpu_custom_call" | custom-call | bytes 3000000 | tf_op jit(solution)/shard_map/pallas_call | solution.py:329
  (31 shorter events, 3.1 us)
Async XLA Ops:
  2.2 21.1 %collective-permute-start = (f32[11,2,8,128]{3,2,1,0:T(8,128)}, f32[11,2,8,128]{3,2,1,0:T(8,128)S(1)}, u32[]{:S(2)}, u32[]{:S(2)}) collective-permute-start(f32[11,2,8,128]{3,2,1,0:T(8,128)} %shard_map.96), channel_id=1, source_target_pairs={{0,8},{8,16},{16,24},{24,32},{32,40},{40,48},{48,56},{56,0},{1,9},... | collective-permute-start | bytes 270344 | tf_op jit(solution)/shard_map/ppermute | solution.py:344
  6.0 17.3 %copy-start.1 = (f32[3,4,16,128]{3,2,1,0:T(8,128)S(1)}, f32[3,4,16,128]{3,2,1,0:T(8,128)}, u32[]{:S(2)}) copy-start(f32[3,4,16,128]{3,2,1,0:T(8,128)} %cur.5) | copy-start | bytes 294916
  6.0 17.3 %copy-start.2 = (f32[3,4,16,128]{3,2,1,0:T(8,128)S(1)}, f32[3,4,16,128]{3,2,1,0:T(8,128)}, u32[]{:S(2)}) copy-start(f32[3,4,16,128]{3,2,1,0:T(8,128)} %prv.5) | copy-start | bytes 294916
  6.1 17.3 %copy-start.3 = (f32[4,16,128]{2,1,0:T(8,128)S(1)}, f32[4,16,128]{2,1,0:T(8,128)}, u32[]{:S(2)}) copy-start(f32[4,16,128]{2,1,0:T(8,128)} %den.1) | copy-start | bytes 98308
  8.9 14.5 %copy-start = (f32[4,4,16,128]{3,2,1,0:T(8,128)S(1)}, f32[4,4,16,128]{3,2,1,0:T(8,128)}, u32[]{:S(2)}) copy-start(f32[4,4,16,128]{3,2,1,0:T(8,128)} %mod.5) | copy-start | bytes 393220
  8.9 14.4 %collective-permute-start.1 = (f32[11,2,8,128]{3,2,1,0:T(8,128)}, f32[11,2,8,128]{3,2,1,0:T(8,128)S(1)}, u32[]{:S(2)}, u32[]{:S(2)}) collective-permute-start(f32[11,2,8,128]{3,2,1,0:T(8,128)} %get-tuple-element.33), channel_id=1, source_target_pairs={{0,56},{8,0},{16,8},{24,16},{32,24},{40,32},{48,40},{56,48},{1,57}... | collective-permute-start | bytes 270344 | tf_op jit(solution)/shard_map/ppermute | solution.py:344
  11.2 23.1 %all-to-all-start = ((f32[64,1,256]{2,1,0:T(1,128)}), f32[64,1,256]{2,1,0:T(1,128)S(1)}, u32[]{:S(2)}, u32[]{:S(2)}) async-start(f32[64,1,256]{2,1,0:T(1,128)} %get-tuple-element.32), calls=%async_computation | async-start | bytes 131072 | tf_op jit(solution)/shard_map/all_to_all | solution.py:385
  23.6 8.4 %collective-permute-start.2 = (f32[5,24,128]{2,1,0:T(8,128)S(1)}, f32[5,24,128]{2,1,0:T(8,128)S(1)}, u32[]{:S(2)}, u32[]{:S(2)}) collective-permute-start(f32[5,24,128]{2,1,0:T(8,128)S(1)} %get-tuple-element.38), channel_id=1, source_target_pairs={{0,1},{1,2},{2,3},{3,4},{4,5},{5,6},{6,7},{7,0},{8,9},{9,10},{10,1... | collective-permute-start | bytes 184328 | tf_op jit(solution)/shard_map/ppermute | solution.py:344
  24.7 7.4 %collective-permute-start.3 = (f32[5,24,128]{2,1,0:T(8,128)S(1)}, f32[5,24,128]{2,1,0:T(8,128)S(1)}, u32[]{:S(2)}, u32[]{:S(2)}) collective-permute-start(f32[5,24,128]{2,1,0:T(8,128)S(1)} %get-tuple-element.39), channel_id=1, source_target_pairs={{0,7},{1,0},{2,1},{3,2},{4,3},{5,4},{6,5},{7,6},{8,15},{9,8},{10,9... | collective-permute-start | bytes 184328 | tf_op jit(solution)/shard_map/ppermute | solution.py:344
  26.4 3.1 %collective-permute-start.4 = (f32[8,128]{1,0:T(8,128)S(1)}, f32[8,128]{1,0:T(8,128)S(1)}, u32[]{:S(2)}, u32[]{:S(2)}) collective-permute-start(f32[8,128]{1,0:T(8,128)S(1)} %get-tuple-element.40), channel_id=1, source_target_pairs={{0,64},{64,128},{128,192},{192,0},{1,65},{65,129},{129,193},{193,1... | collective-permute-start | bytes 12296 | tf_op jit(solution)/shard_map/ppermute | solution.py:344
  28.7 3.3 %collective-permute-start.5 = (f32[8,128]{1,0:T(8,128)S(1)}, f32[8,128]{1,0:T(8,128)S(1)}, u32[]{:S(2)}, u32[]{:S(2)}) collective-permute-start(f32[8,128]{1,0:T(8,128)S(1)} %get-tuple-element.41), channel_id=1, source_target_pairs={{0,192},{64,0},{128,64},{192,128},{1,193},{65,1},{129,65},{193,129... | collective-permute-start | bytes 12296 | tf_op jit(solution)/shard_map/ppermute | solution.py:344
  35.4 9.4 %collective-permute-start.6 = (f32[3,24,128]{2,1,0:T(8,128)S(1)}, f32[3,24,128]{2,1,0:T(8,128)S(1)}, u32[]{:S(2)}, u32[]{:S(2)}) collective-permute-start(f32[3,24,128]{2,1,0:T(8,128)S(1)} %get-tuple-element.44), channel_id=1, source_target_pairs={{0,1},{1,2},{2,3},{3,4},{4,5},{5,6},{6,7},{7,0},{8,9},{9,10},{10,1... | collective-permute-start | bytes 110600 | tf_op jit(solution)/shard_map/ppermute | solution.py:344
  36.0 8.8 %collective-permute-start.7 = (f32[3,24,128]{2,1,0:T(8,128)S(1)}, f32[3,24,128]{2,1,0:T(8,128)S(1)}, u32[]{:S(2)}, u32[]{:S(2)}) collective-permute-start(f32[3,24,128]{2,1,0:T(8,128)S(1)} %get-tuple-element.45), channel_id=1, source_target_pairs={{0,7},{1,0},{2,1},{3,2},{4,3},{5,4},{6,5},{7,6},{8,15},{9,8},{10,9... | collective-permute-start | bytes 110600 | tf_op jit(solution)/shard_map/ppermute | solution.py:344
  38.2 6.1 %collective-permute-start.8 = (f32[8,128]{1,0:T(8,128)S(1)}, f32[8,128]{1,0:T(8,128)S(1)}, u32[]{:S(2)}, u32[]{:S(2)}) collective-permute-start(f32[8,128]{1,0:T(8,128)S(1)} %get-tuple-element.46), channel_id=1, source_target_pairs={{0,64},{64,128},{128,192},{192,0},{1,65},{65,129},{129,193},{193,1... | collective-permute-start | bytes 12296 | tf_op jit(solution)/shard_map/ppermute | solution.py:344
  41.8 3.0 %collective-permute-start.9 = (f32[8,128]{1,0:T(8,128)S(1)}, f32[8,128]{1,0:T(8,128)S(1)}, u32[]{:S(2)}, u32[]{:S(2)}) collective-permute-start(f32[8,128]{1,0:T(8,128)S(1)} %get-tuple-element.47), channel_id=1, source_target_pairs={{0,192},{64,0},{128,64},{192,128},{1,193},{65,1},{129,65},{193,129... | collective-permute-start | bytes 12296 | tf_op jit(solution)/shard_map/ppermute | solution.py:344
  45.3 7.6 %collective-permute-start.10 = (f32[3,24,128]{2,1,0:T(8,128)S(1)}, f32[3,24,128]{2,1,0:T(8,128)S(1)}, u32[]{:S(2)}, u32[]{:S(2)}) collective-permute-start(f32[3,24,128]{2,1,0:T(8,128)S(1)} %get-tuple-element.53), channel_id=1, source_target_pairs={{0,1},{1,2},{2,3},{3,4},{4,5},{5,6},{6,7},{7,0},{8,9},{9,10},{10,1... | collective-permute-start | bytes 110600 | tf_op jit(solution)/shard_map/ppermute | solution.py:344
  45.4 7.5 %collective-permute-start.11 = (f32[3,24,128]{2,1,0:T(8,128)S(1)}, f32[3,24,128]{2,1,0:T(8,128)S(1)}, u32[]{:S(2)}, u32[]{:S(2)}) collective-permute-start(f32[3,24,128]{2,1,0:T(8,128)S(1)} %get-tuple-element.54), channel_id=1, source_target_pairs={{0,7},{1,0},{2,1},{3,2},{4,3},{5,4},{6,5},{7,6},{8,15},{9,8},{10,9... | collective-permute-start | bytes 110600 | tf_op jit(solution)/shard_map/ppermute | solution.py:344
  48.1 2.5 %collective-permute-start.12 = (f32[8,128]{1,0:T(8,128)S(1)}, f32[8,128]{1,0:T(8,128)S(1)}, u32[]{:S(2)}, u32[]{:S(2)}) collective-permute-start(f32[8,128]{1,0:T(8,128)S(1)} %get-tuple-element.55), channel_id=1, source_target_pairs={{0,64},{64,128},{128,192},{192,0},{1,65},{65,129},{129,193},{193,1... | collective-permute-start | bytes 12296 | tf_op jit(solution)/shard_map/ppermute | solution.py:344
  49.8 3.0 %collective-permute-start.13 = (f32[8,128]{1,0:T(8,128)S(1)}, f32[8,128]{1,0:T(8,128)S(1)}, u32[]{:S(2)}, u32[]{:S(2)}) collective-permute-start(f32[8,128]{1,0:T(8,128)S(1)} %get-tuple-element.56), channel_id=1, source_target_pairs={{0,192},{64,0},{128,64},{192,128},{1,193},{65,1},{129,65},{193,129... | collective-permute-start | bytes 12296 | tf_op jit(solution)/shard_map/ppermute | solution.py:344
  53.4 6.4 %collective-permute-start.14 = (f32[3,24,128]{2,1,0:T(8,128)S(1)}, f32[3,24,128]{2,1,0:T(8,128)S(1)}, u32[]{:S(2)}, u32[]{:S(2)}) collective-permute-start(f32[3,24,128]{2,1,0:T(8,128)S(1)} %get-tuple-element.58), channel_id=1, source_target_pairs={{0,1},{1,2},{2,3},{3,4},{4,5},{5,6},{6,7},{7,0},{8,9},{9,10},{10,1... | collective-permute-start | bytes 110600 | tf_op jit(solution)/shard_map/ppermute | solution.py:344
  53.5 6.3 %collective-permute-start.15 = (f32[3,24,128]{2,1,0:T(8,128)S(1)}, f32[3,24,128]{2,1,0:T(8,128)S(1)}, u32[]{:S(2)}, u32[]{:S(2)}) collective-permute-start(f32[3,24,128]{2,1,0:T(8,128)S(1)} %get-tuple-element.59), channel_id=1, source_target_pairs={{0,7},{1,0},{2,1},{3,2},{4,3},{5,4},{6,5},{7,6},{8,15},{9,8},{10,9... | collective-permute-start | bytes 110600 | tf_op jit(solution)/shard_map/ppermute | solution.py:344
  56.1 1.4 %collective-permute-start.16 = (f32[8,128]{1,0:T(8,128)S(1)}, f32[8,128]{1,0:T(8,128)S(1)}, u32[]{:S(2)}, u32[]{:S(2)}) collective-permute-start(f32[8,128]{1,0:T(8,128)S(1)} %get-tuple-element.60), channel_id=1, source_target_pairs={{0,64},{64,128},{128,192},{192,0},{1,65},{65,129},{129,193},{193,1... | collective-permute-start | bytes 12296 | tf_op jit(solution)/shard_map/ppermute | solution.py:344
  56.7 3.0 %collective-permute-start.17 = (f32[8,128]{1,0:T(8,128)S(1)}, f32[8,128]{1,0:T(8,128)S(1)}, u32[]{:S(2)}, u32[]{:S(2)}) collective-permute-start(f32[8,128]{1,0:T(8,128)S(1)} %get-tuple-element.61), channel_id=1, source_target_pairs={{0,192},{64,0},{128,64},{192,128},{1,193},{65,1},{129,65},{193,129... | collective-permute-start | bytes 12296 | tf_op jit(solution)/shard_map/ppermute | solution.py:344

commit v3 on v2

v3 whole, which is shorter than its diff:
```python
import jax
import jax.numpy as jnp
from jax import lax
from jax.experimental import pallas as pl
from jax.experimental.pallas import tpu as pltpu
from jax.sharding import PartitionSpec as P

STEPS = 4
STEP_SQUARE = 0.16
TABLE = ((0, 2, 2), (2, 1, 3), (2, 3, 1))
CR, CL, CE = 4, 16, 128
HALO = 4
ROWS = CL + 2 * HALO
CAP = 4
SLOTS = 6
STATIONS = 128
F32 = jnp.float32
I32 = jnp.int32


def iota(shape, dim):
    return lax.broadcasted_iota(I32, shape, dim)


LAYERS = CR + 2 * HALO
LEFT_PAD = 160


def radial_list(up):
    inner = range(1, CR) if up else range(CR - 1)
    full = range(CR)
    items = [("u", k, r) for k in range(3) for r in full]
    items += [("v", k, r) for k in range(3) for r in inner]
    items += [("c", 0, r) for r in inner]
    items += [("m", j, r) for j in (0, 2) for r in full]
    items += [("m", j, r) for j in (1, 3) for r in inner]
    return items


RADIAL = len(radial_list(True))


def column_list():
    items = [("u", k, r) for k in range(3) for r in range(1, LAYERS - 1)]
    items += [("v", k, r) for k in range(3) for r in range(2, LAYERS - 2)]
    items += [("c", 0, r) for r in range(2, LAYERS - 2)]
    items += [("m", j, r) for j in range(4) for r in range(1, LAYERS - 1)]
    for t in range(STEPS - 1):
        items += [("s%d" % t, k, r) for k in range(3) for r in range(t + 2, LAYERS - t - 2)]
    return items


def fold(layer, first):
    lane, sub = iota((8, 128), 1), iota((8, 128), 0)
    gathered = jnp.zeros((8, 128), F32)
    for i in range(ROWS // 8):
        part = jnp.take_along_axis(layer[8 * i : 8 * i + 8], first + lane % 4, axis=1)
        gathered = jnp.where(lane // 4 == 8 * i + sub, part, gathered)
    return jnp.sum(gathered, axis=0, keepdims=True)


def unfold(left, right):
    lane, sub = iota((8, 128), 1), iota((8, 128), 0)
    left, right = jnp.broadcast_to(left, (8, 128)), jnp.broadcast_to(right, (8, 128))
    parts = []
    for i in range(ROWS // 8):
        index = (8 * i + sub) * 4 + lane % 4
        parts.append(
            jnp.where(
                lane < 64,
                jnp.take_along_axis(right, index, axis=1),
                jnp.take_along_axis(left, index, axis=1),
            )
        )
    return jnp.concatenate(parts, axis=0)


def edge_rows(start, fields, out, room, sems):
    first, copies = 0, []
    for i, ref in enumerate(fields):
        count = ref.shape[0]
        copies.append(
            pltpu.make_async_copy(
                ref.at[:, :, pl.ds(start, 8), :], room.at[pl.ds(first, count)], sems.at[i]
            )
        )
        first += count
    for copy in copies:
        copy.start()

    def finish():
        for copy in copies:
            copy.wait()
        inner = slice(0, HALO) if start == 0 else slice(8 - HALO, 8)
        for f in range(first):
            for r in range(CR):
                spot = slice(HALO * (r % 2), HALO * (r % 2) + HALO)
                out[f, r // 2, spot, :] = room[f, r, inner, :]

    return finish


def high_kernel(cur, prv, mod, den, high, room, sems):
    edge_rows(CL - 8, (cur, prv, mod, den), high, room, sems)()


def pack_kernel(
    offsets_in, receivers_in, owners_in, traces_in, cur, prv, mod, den, out, low,
    room, sems, traces, words_in, trace_sem, word_sems,
):
    copy = pltpu.make_async_copy(traces_in, traces, trace_sem)
    copy.start()
    small = [
        pltpu.make_async_copy(ref, words_in.at[pl.ds(i, 1)], word_sems.at[i])
        for i, ref in enumerate((offsets_in, receivers_in, owners_in))
    ]
    for one in small:
        one.start()
    finish_low = edge_rows(0, (cur, prv, mod, den), low, room, sems)
    for one in small:
        one.wait()
    offset_row, q, owner_row = words_in[0:1], words_in[1:2], words_in[2:3]
    r, l, e = q // 2048, (q // 128) % CL, q % 128
    wide_sub, wide_lane = iota((128, 128), 0), iota((128, 128), 1)
    sheet = jnp.transpose(
        jnp.concatenate(
            [owner_row.astype(F32), offset_row.astype(F32), jnp.zeros((6, 128), F32)], axis=0
        )
    )
    owner_cols = jnp.broadcast_to(sheet[:, 0:1], (128, 128)).astype(I32)
    offsets = jnp.broadcast_to(sheet[:, 1:2], (128, 128)).astype(I32)
    same = (owner_cols == owner_row) & (wide_sub < wide_lane)
    rank = jnp.sum(jnp.where(same, 1.0, 0.0), axis=0, keepdims=True).astype(I32)

    lefts, lines = [], [e.astype(F32)]
    for shift in (-1, 0, 1):
        slot = (shift + 1) * CAP + rank
        half, j = slot // SLOTS, slot % SLOTS
        if shift == 0:
            row, near = l, l >= 0
        elif shift == -1:
            row, near = CL + l, l <= HALO - 2
        else:
            row, near = l + HALO + HALO, l >= CL - HALO + 1
        target = owner_row + 8 * shift
        ok = near & (target >= 0) & (target < 64)
        place = jnp.where(ok, half * 64 + target, -1)
        lefts.append(jnp.where(wide_sub == place, 1.0, 0.0))
        lines += [j.astype(F32), (r * ROWS + row).astype(F32)]
    sheet = jnp.transpose(jnp.concatenate(lines + [jnp.zeros((1, 128), F32)], axis=0))
    finish_low()

    inside = offsets % 128
    tile = offsets // 128 + jnp.where(wide_lane < inside, 1, 0)
    index = (inside + (wide_lane // 8) % STEPS) % 128
    copy.wait()
    window = jnp.broadcast_to(sheet[:, 0:1], (128, 128))
    for k in range(3):
        parts = [traces[k, :, 128 * i : 128 * i + 128] for i in range(4)]
        merged = jnp.where(
            tile == 0,
            parts[0],
            jnp.where(tile == 1, parts[1], jnp.where(tile == 2, parts[2], parts[3])),
        )
        picked = jnp.take_along_axis(merged, index, axis=1)
        window = jnp.where(wide_lane // 32 == k, picked, window)
    rights = []
    for i in range(3):
        slots = jnp.broadcast_to(sheet[:, 2 * i + 1 : 2 * i + 2], (128, 128)).astype(I32)
        cells = jnp.broadcast_to(sheet[:, 2 * i + 2 : 2 * i + 3], (128, 128))
        words = jnp.where((wide_lane >= 96) & (wide_lane < 104), cells, window)
        rights.append(jnp.where((wide_lane % 8 == slots) & (wide_lane < 112), words, 0.0))
    packed = lax.dot_general(
        jnp.concatenate(lefts, axis=1),
        jnp.concatenate(rights, axis=0),
        (((1,), (0,)), ((), ())),
        precision=lax.Precision.HIGHEST,
        preferred_element_type=F32,
    )
    out[:, 0, :128] = packed[:64]
    out[:, 0, 128:] = packed[64:]


def widen_kernel(cur, prv, mod, den, from_low, from_high, u, v, m, c, down, up):
    lat = lax.axis_index("lat")
    has_low, has_high = lat > 0, lat < lax.axis_size("lat") - 1

    def ghosts(f, r):
        spot = slice(HALO * (r % 2), HALO * (r % 2) + HALO)
        return jnp.concatenate(
            [
                jnp.where(has_high, from_high[f, r // 2, spot, :], 0.0),
                jnp.where(has_low, from_low[f, r // 2, spot, :], 0.0),
            ],
            axis=0,
        )

    for r in range(CR):
        for k in range(3):
            u[k, r, 0:CL, :] = cur[k, r]
            u[k, r, CL:ROWS, :] = ghosts(k, r)
            v[k, r, 0:CL, :] = prv[k, r]
            v[k, r, CL:ROWS, :] = ghosts(3 + k, r)
        for j in range(4):
            m[j, r, 0:CL, :] = mod[j, r]
            m[j, r, CL:ROWS, :] = ghosts(6 + j, r)
        c[0, r, 0:CL, :] = STEP_SQUARE / den[r]
        spot = slice(HALO * (r % 2), HALO * (r % 2) + HALO)
        outer = STEP_SQUARE / jnp.concatenate(
            [from_high[10, r // 2, spot, :], from_low[10, r // 2, spot, :]], axis=0
        )
        present = jnp.where(iota((8, 128), 0) < HALO, has_high.astype(I32), has_low.astype(I32))
        c[0, r, CL:ROWS, :] = jnp.where(present > 0, outer, 0.0)
    fields = dict(u=u, v=v, m=m, c=c)
    for message, is_up in ((down, False), (up, True)):
        for i, (name, k, r) in enumerate(radial_list(is_up)):
            message[i] = fields[name][k, r]


def turn_kernel(got, _, turned):
    turned[...] = jnp.transpose(jnp.concatenate([got[:, 0, :128], got[:, 0, 128:]], axis=0))


def thirds(x):
    high = x.astype(jnp.bfloat16).astype(F32)
    rest = x - high
    middle = rest.astype(jnp.bfloat16).astype(F32)
    return high, middle, rest - middle


def gather_sources(got, ranges, weights, picks):
    turned = got[...]
    parts = thirds(turned)
    cell_lanes = iota((CE, 128), 0)
    for j in range(SLOTS):
        place = turned[96 + j : 97 + j].astype(I32)
        around = turned[104 + j : 105 + j].astype(I32)
        pick = jnp.where(cell_lanes == around, 1.0, 0.0)
        for p in range(3):
            span = slice((p * SLOTS + j) * 128, (p * SLOTS + j + 1) * 128)
            picks[:, span] = pick
            at = 0
            for t, (low, high) in enumerate(ranges):
                count = (high - low) * ROWS
                here = iota((count, 128), 0) + low * ROWS == place
                for k in range(3):
                    line = (k * STEPS + t) * 8 + j
                    weights[at : at + count, span] = jnp.where(
                        here, parts[p][line : line + 1], 0.0
                    )
                    at += count
    return lax.dot_general(
        weights[...], picks[...], (((1,), (1,)), ((), ())), preferred_element_type=F32
    )


def own_kernel(got, c, *refs):
    sources, weights, picks = refs
    ranges = [(0, CR)] * STEPS
    summed = gather_sources(got, ranges, weights, picks)
    for t in range(STEPS):
        for k in range(3):
            for r in range(CR):
                at = ((t * 3 + k) * CR + r) * ROWS
                sources[t, k, r] = summed[at : at + ROWS] * c[0, r]


def source_span(t):
    return t + 1, LAYERS - t - 1


def assemble_kernel(
    u, v, m, c, own, low, high, low_list, high_list,
    wu, wv, wm, wc, ws, left, right, weights, picks,
):
    rad = lax.axis_index("rad")
    has_low, has_high = rad > 0, rad < lax.axis_size("rad") - 1
    pairs = dict(u=(u, wu), v=(v, wv), m=(m, wm), c=(c, wc))
    for narrow, wide in pairs.values():
        for k in range(narrow.shape[0]):
            for r in range(CR):
                wide[k, HALO + r] = narrow[k, r]
    for message, is_up, present in ((low, True, has_low), (high, False, has_high)):
        for i, (name, k, r) in enumerate(radial_list(is_up)):
            at = r if is_up else HALO + CR + r
            pairs[name][1][k, at] = jnp.where(present, message[i], 0.0)
    for t in range(STEPS):
        for k in range(3):
            for r in range(CR):
                ws[t, k, HALO + r] = own[t, k, r]
    lists = (
        (low_list, [(t + 1, CR) for t in range(STEPS - 1)], 0),
        (high_list, [(0, CR - 1 - t) for t in range(STEPS - 1)], HALO + CR),
    )
    for got, ranges, base in lists:
        summed = gather_sources(got, ranges, weights, picks)
        at = 0
        for t, (first, last) in enumerate(ranges):
            for k in range(3):
                for r in range(first, last):
                    ws[t, k, base + r] = summed[at : at + ROWS] * wc[0, base + r]
                    at += ROWS
    fields = dict(u=wu, v=wv, m=wm, c=wc)
    for t in range(STEPS):
        fields["s%d" % t] = ws.at[t]
    for i, (name, k, r) in enumerate(column_list()):
        layer = fields[name][k, r]
        left[i : i + 1, :] = fold(layer, 0)
        right[i : i + 1, :] = fold(layer, CE - 4)
    used = len(column_list())
    left[used:, :] = jnp.zeros((LEFT_PAD - used, 128), F32)
    right[used:, :] = jnp.zeros((LEFT_PAD - used, 128), F32)


def radial_faces(m, ar, first, last):
    for i, j in enumerate((0, 2)):
        for r in range(first, last + 1):
            ar[i, r] = 0.5 * (m[j, r - 1] + m[j, r])


def lateral_faces(m, al, first, last):
    for j in (1, 2, 3):
        for r in range(first, last + 1):
            al[j - 1, r] = 0.5 * (m[j, r] + pltpu.roll(m[j, r], ROWS - 1, 0))


def faces_kernel(m, ar, al):
    radial_faces(m, ar, 1, LAYERS - 1)
    lateral_faces(m, al, 1, LAYERS - 2)


def after(here, there):
    lane = iota((ROWS, CE), 1)
    a, b = pltpu.roll(here, CE - 1, 1), pltpu.roll(there, CE - 1, 1)
    return jnp.where(lane == CE - 1, b, a), jnp.where(lane == CE - 1, a, b)


def before(here, there):
    lane = iota((ROWS, CE), 1)
    a, b = pltpu.roll(here, 1, 1), pltpu.roll(there, 1, 1)
    return jnp.where(lane == 0, b, a), jnp.where(lane == 0, a, b)


def still(k, r, u, ar, al):
    jr, jl, _ = TABLE[k]
    here = u[k, r]
    total = ar[jr // 2, r + 1] * (u[k, r + 1] - here) - ar[jr // 2, r] * (here - u[k, r - 1])
    flux = al[jl - 1, r] * (pltpu.roll(here, ROWS - 1, 0) - here)
    return total + (flux - pltpu.roll(flux, 1, 0))


def steps_kernel(
    u, v, m, c, s, ar, al, at_left, at_right, final, before_final,
    gu, gv, gm, gc, gs, gar, gal, ae, gae, us, gus,
):
    ghosts = dict(u=gu, v=gv, m=gm, c=gc)
    for t in range(STEPS - 1):
        ghosts["s%d" % t] = gs.at[t]
    for i, (name, k, r) in enumerate(column_list()):
        ghosts[name][k, r] = unfold(at_left[i : i + 1, :], at_right[i : i + 1, :])
    radial_faces(gm, gar, 2, LAYERS - 2)
    lateral_faces(gm, gal, 2, LAYERS - 3)
    for j in (1, 2, 3):
        for r in range(1, LAYERS - 1):
            own, other = after(m[j, r], gm[j, r])
            ae[j - 1, r] = 0.5 * (m[j, r] + own)
            gae[j - 1, r] = 0.5 * (gm[j, r] + other)
    for t in range(STEPS):
        now, gnow = (u, gu) if t == 0 else (us.at[t - 1], gus.at[t - 1])
        old, gold = (v, gv) if t == 0 else (u, gu) if t == 1 else (us.at[t - 2], gus.at[t - 2])
        for k in range(3):
            je = TABLE[k][2] - 1
            for r in range(t + 1, LAYERS - t - 1):
                here, there = now[k, r], gnow[k, r]
                own, other = after(here, there)
                flux, gflux = ae[je, r] * (own - here), gae[je, r] * (other - there)
                own, other = before(flux, gflux)
                total = still(k, r, now, ar, al) + (flux - own)
                value = 2.0 * here - old[k, r] + c[0, r] * total + s[t, k, r]
                if t == STEPS - 1:
                    final[k, r - HALO] = value[:CL]
                    before_final[k, r - HALO] = here[:CL]
                    continue
                us[t, k, r] = value
                if t + 2 <= r < LAYERS - t - 2:
                    total = still(k, r, gnow, gar, gal) + (gflux - other)
                    gus[t, k, r] = 2.0 * there - gold[k, r] + gc[0, r] * total + gs[t, k, r]


def call(kernel, outs, args, scratch=(), hbm=0, us=1.0):
    vmem = pl.BlockSpec(memory_space=pltpu.VMEM)
    specs = [pl.BlockSpec(memory_space=pltpu.HBM)] * hbm + [vmem] * (len(args) - hbm)
    return pl.pallas_call(
        kernel,
        out_shape=[jax.ShapeDtypeStruct(shape, F32) for shape in outs],
        in_specs=specs,
        out_specs=[vmem] * len(outs),
        scratch_shapes=[pltpu.VMEM(s, F32) if isinstance(s, tuple) else s for s in scratch],
        cost_estimate=pl.CostEstimate(
            flops=0, bytes_accessed=int(us * 3_000_000), transcendentals=0
        ),
        compiler_params=pltpu.CompilerParams(vmem_limit_bytes=(60 if hbm else 32) * 1024 * 1024),
    )(*args)


def shifted(block, axis, by):
    count = lax.axis_size(axis)
    return lax.ppermute(block, axis, [(i, (i + by) % count) for i in range(count)])


def on_device(current, previous, moduli, density, traces, receivers, owners, offsets):
    edge = (11, 2, 8, CE)
    fields = (current, previous, moduli, density.reshape((1,) + density.shape))
    rooms = [(11, CR, 8, CE), pltpu.SemaphoreType.DMA((4,))]
    (high_rows,) = call(high_kernel, [edge], fields, scratch=rooms, hbm=4)
    from_low = shifted(high_rows, "lat", 1)
    packed, low_rows = call(
        pack_kernel,
        [(64, 1, 256), edge],
        (
            offsets.reshape(1, 128),
            receivers.reshape(1, 128),
            owners.reshape(1, 128),
            traces.transpose(1, 0, 2),
        )
        + fields,
        scratch=rooms
        + [
            (3, STATIONS, 512),
            pltpu.VMEM((8, 128), I32),
            pltpu.SemaphoreType.DMA(()),
            pltpu.SemaphoreType.DMA((3,)),
        ],
        hbm=8,
        us=2.0,
    )
    from_high = shifted(low_rows, "lat", -1)
    got = lax.all_to_all(packed, ("lat", "rad"), 0, 0, tiled=True)

    def block(*lead):
        return lead + (ROWS, CE)

    u, v, m, c, down, up = call(
        widen_kernel,
        [block(3, CR), block(3, CR), block(4, CR), block(1, CR), block(RADIAL), block(RADIAL)],
        (current, previous, moduli, density, from_low, from_high),
    )
    low = shifted(up, "rad", 1)
    high = shifted(down, "rad", -1)
    (got,) = call(turn_kernel, [(128, 128)], (got, c))
    low_list = shifted(got, "rad", 1)
    high_list = shifted(got, "rad", -1)
    lanes = 3 * SLOTS * 128
    (own,) = call(
        own_kernel,
        [block(STEPS, 3, CR)],
        (got, c),
        scratch=[(3 * STEPS * CR * ROWS, lanes), (CE, lanes)],
        us=3.0,
    )
    wu, wv, wm, wc, ws, left, right = call(
        assemble_kernel,
        [block(3, LAYERS), block(3, LAYERS), block(4, LAYERS), block(1, LAYERS)]
        + [block(STEPS, 3, LAYERS), (LEFT_PAD, 128), (LEFT_PAD, 128)],
        (u, v, m, c, own, low, high, low_list, high_list),
        scratch=[(3 * 6 * ROWS, lanes), (CE, lanes)],
        us=3.0,
    )
    at_left = shifted(right, "span", 1)
    at_right = shifted(left, "span", -1)
    ar, al = call(faces_kernel, [block(2, LAYERS), block(3, LAYERS)], (wm,))
    return tuple(
        call(
            steps_kernel,
            [(3, CR, CL, CE)] * 2,
            (wu, wv, wm, wc, ws, ar, al, at_left, at_right),
            scratch=[block(3, LAYERS), block(3, LAYERS), block(4, LAYERS), block(1, LAYERS)]
            + [block(STEPS - 1, 3, LAYERS), block(2, LAYERS), block(3, LAYERS)]
            + [block(3, LAYERS), block(3, LAYERS)]
            + [block(STEPS - 1, 3, LAYERS), block(STEPS - 1, 3, LAYERS)],
            us=5.0,
        )
    )


def solution(mesh):
    in_specs = (
        P(None, "rad", "lat", "span"),
        P(None, "rad", "lat", "span"),
        P(None, "rad", "lat", "span"),
        P("rad", "lat", "span"),
        P(("span", "lat", "rad"), None, None),
        P(("span", "lat", "rad")),
        P(("span", "lat", "rad"), None),
        P(("span", "lat", "rad")),
    )
    out_specs = (P(None, "rad", "lat", "span"), P(None, "rad", "lat", "span"))
    return jax.shard_map(
        on_device, mesh=mesh, in_specs=in_specs, out_specs=out_specs, check_vma=False
    )
```

time: 60.9 us -> 71.5 us (1.17)
  blocking collectives: 0 us -> 21.2 us
  starting transfers between devices: 37.6 us -> 20 us
  Pallas kernels: 10.8 us -> 17.3 us
  local copies, waits for them, and re-layouts: 0.02 us -> 3.45 us
  waiting for transfers between devices: 11.5 us -> 8.56 us
    all_to_all x0 -> x1, blocking collectives: none -> 21.2 us  [on_device(): got = lax.all_to_all(packed, ('lat', 'rad'), 0, 0, tiled=True)]
    all_to_all x1 -> x0, starting transfers between devices: 12.1 us -> none  [on_device(): got = lax.all_to_all(packed, ('lat', 'rad'), 0, 0, tiled=True)]
    pallas_call x9 -> x8, Pallas kernels: 10.8 us -> 17.3 us  [call(): pl.pallas_call(kernel, out_shape=[jax.ShapeDtypeStruct(shape, F32) for sh...]
    ppermute x18 -> x8, starting transfers between devices: 25.5 us -> 20 us  [shifted(): lax.ppermute(block, axis, [(i, (i + by) % count) for i in range(count)])]
    unnamed x8, local copies, waits for them, and re-layouts: 0.02 us -> 3.45 us
    all_to_all x1 -> x0, waiting for transfers between devices: 1.58 us -> none  [on_device(): got = lax.all_to_all(packed, ('lat', 'rad'), 0, 0, tiled=True)]
    ppermute x18 -> x8, waiting for transfers between devices: 9.96 us -> 8.56 us  [shifted(): lax.ppermute(block, axis, [(i, (i + by) % count) for i in range(count)])]
  transfers between devices with their start and end apart: 19 -> 8, of which waited for: 8 -> 5; matrix products, arithmetic and copies ran while one was open for 0% -> 0% of each run, Pallas kernels for 10% -> 6%
where the time goes in v3:
time: 71.5 us; the launch traced here: 71.1 us
  blocking collectives  21.2 us (30%)
  starting transfers between devices  20 us (28%)
  Pallas kernels  17.3 us (24%)
  waiting for transfers between devices  8.56 us (12%)
  local copies, waits for them, and re-layouts  3.45 us (5%)
    all_to_all x1, blocking collectives, on_device(): got = lax.all_to_all(packed, ('lat', 'rad'), 0, 0, tiled=True)  21.2 us
    ppermute x8, starting transfers between devices, shifted(): lax.ppermute(block, axis, [(i, (i + by) % count) for i in range(count)])  20 us
    pallas_call x8, Pallas kernels, call(): pl.pallas_call(kernel, out_shape=[jax.ShapeDtypeStruct(shape, F32) for sh...  17.3 us
    ppermute x8, waiting for transfers between devices, shifted(): lax.ppermute(block, axis, [(i, (i + by) % count) for i in range(count)])  8.56 us
    unnamed x8, local copies, waits for them, and re-layouts  3.45 us
  transfers between devices with their start and end apart: 8, of which 5 were waited for; matrix products, arithmetic and copies ran while one was open for 0% of the time, Pallas kernels for 6%

profile of v3, /device:TPU:1, one launch (start us, length us, event | category | flops | bytes accessed | tf_op | source)
XLA Modules:
  0.0 71.1 jit_solution(5220894865832175224)
XLA Ops:
  0.6 1.6 %shard_map.95 = f32[11,2,8,128]{3,2,1,0:T(8,128)} custom-call(f32[3,4,16,128]{3,2,1,0:T(8,128)} %cur.5, f32[3,4,16,128]{3,2,1,0:T(8,128)} %prv.5, f32[4,4,16,128]{3,2,1,0:T(8,128)} %mod.5, f32[1,4,16,128]{3,2,1,0:T(8,128)} %bitcast.5), custom_call_target="tpu_custom_call" | custom-call | bytes 3000000 | tf_op jit(solution)/shard_map/pallas_call | solution.py:393
  2.2 3.8 %collective-permute-start = (f32[11,2,8,128]{3,2,1,0:T(8,128)}, f32[11,2,8,128]{3,2,1,0:T(8,128)S(1)}, u32[]{:S(2)}, u32[]{:S(2)}) collective-permute-start(f32[11,2,8,128]{3,2,1,0:T(8,128)} %shard_map.95), channel_id=1, source_target_pairs={{0,8},{8,16},{16,24},{24,32},{32,40},{40,48},{48,56},{56,0},{1,9},... | collective-permute-start | bytes 270344 | tf_op jit(solution)/shard_map/ppermute | solution.py:408
  6.0 2.8 %shard_map.96 = (f32[64,1,256]{2,1,0:T(1,128)}, f32[11,2,8,128]{3,2,1,0:T(8,128)}) custom-call(s32[1,128]{1,0:T(1,128)} %bitcast.8, s32[1,128]{1,0:T(1,128)} %bitcast.9, s32[1,128]{1,0:T(1,128)} %bitcast.10, f32[3,128,512]{2,1,0:T(8,128)} %bitcast.7, f32[3,4,16,128]{3,2,1,0:T(8,128)} %cur.5, f32[3,4,16,128]{3,2,1,0:T(8,128)} %prv.5, f32[4,4,16,128]{3,2,1,0:T(8,128)} %mod.5, ...), custom_call_target="tpu_custom_call" | custom-call | bytes 6000000 | tf_op jit(solution)/shard_map/pallas_call | solution.py:393
  8.8 2.3 %collective-permute-start.1 = (f32[11,2,8,128]{3,2,1,0:T(8,128)}, f32[11,2,8,128]{3,2,1,0:T(8,128)S(1)}, u32[]{:S(2)}, u32[]{:S(2)}) collective-permute-start(f32[11,2,8,128]{3,2,1,0:T(8,128)} %get-tuple-element.19), channel_id=1, source_target_pairs={{0,56},{8,0},{16,8},{24,16},{32,24},{40,32},{48,40},{56,48},{1,57}... | collective-permute-start | bytes 270344 | tf_op jit(solution)/shard_map/ppermute | solution.py:408
  11.1 3.1 %collective-permute-done.1.from_high = f32[11,2,8,128]{3,2,1,0:T(8,128)S(1)} collective-permute-done((f32[11,2,8,128]{3,2,1,0:T(8,128)}, f32[11,2,8,128]{3,2,1,0:T(8,128)S(1)}, u32[]{:S(2)}, u32[]{:S(2)}) %collective-permute-start.1) | collective-permute-done | bytes 90144 | tf_op jit(solution)/shard_map/ppermute | solution.py:408
  14.2 0.9 %copy-done = f32[4,4,16,128]{3,2,1,0:T(8,128)S(1)} copy-done((f32[4,4,16,128]{3,2,1,0:T(8,128)S(1)}, f32[4,4,16,128]{3,2,1,0:T(8,128)}, u32[]{:S(2)}) %copy-start) | copy-done | bytes 131096
  15.1 0.9 %copy-done.1 = f32[3,4,16,128]{3,2,1,0:T(8,128)S(1)} copy-done((f32[3,4,16,128]{3,2,1,0:T(8,128)S(1)}, f32[3,4,16,128]{3,2,1,0:T(8,128)}, u32[]{:S(2)}) %copy-start.1) | copy-done | bytes 98328
  16.0 0.9 %copy-done.2 = f32[3,4,16,128]{3,2,1,0:T(8,128)S(1)} copy-done((f32[3,4,16,128]{3,2,1,0:T(8,128)S(1)}, f32[3,4,16,128]{3,2,1,0:T(8,128)}, u32[]{:S(2)}) %copy-start.2) | copy-done | bytes 98328
  16.9 0.8 %copy-done.3 = f32[4,16,128]{2,1,0:T(8,128)S(1)} copy-done((f32[4,16,128]{2,1,0:T(8,128)S(1)}, f32[4,16,128]{2,1,0:T(8,128)}, u32[]{:S(2)}) %copy-start.3) | copy-done | bytes 32792
  17.6 0.1 shard_map.97
  17.7 1.5 %collective-permute-start.2 = (f32[38,24,128]{2,1,0:T(8,128)S(1)}, f32[38,24,128]{2,1,0:T(8,128)S(1)}, u32[]{:S(2)}, u32[]{:S(2)}) collective-permute-start(f32[38,24,128]{2,1,0:T(8,128)S(1)} %get-tuple-element.25), channel_id=1, source_target_pairs={{0,1},{1,2},{2,3},{3,4},{4,5},{5,6},{6,7},{7,0},{8,9},{9,10},{10,1... | collective-permute-start | bytes 1400840 | tf_op jit(solution)/shard_map/ppermute | solution.py:408
  19.3 4.0 %collective-permute-start.3 = (f32[38,24,128]{2,1,0:T(8,128)S(1)}, f32[38,24,128]{2,1,0:T(8,128)S(1)}, u32[]{:S(2)}, u32[]{:S(2)}) collective-permute-start(f32[38,24,128]{2,1,0:T(8,128)S(1)} %get-tuple-element.26), channel_id=1, source_target_pairs={{0,7},{1,0},{2,1},{3,2},{4,3},{5,4},{6,5},{7,6},{8,15},{9,8},{10,9... | collective-permute-start | bytes 1400840 | tf_op jit(solution)/shard_map/ppermute | solution.py:408
  23.3 21.2 %all_to_all.5.got = f32[64,1,256]{2,1,0:T(1,128)S(1)} all-to-all(f32[64,1,256]{2,1,0:T(1,128)} %get-tuple-element.24), channel_id=1, replica_groups=mesh['span'=4,'lat'=8,'rad'=8] {'lat','rad'}, dimensions={0} | all-to-all | bytes 131072 | tf_op jit(solution)/shard_map/all_to_all | solution.py:438
  44.5 0.1 shard_map.98.got
  44.6 0.5 collective-permute-start.5
  45.1 1.1 %collective-permute-start.4 = (f32[128,128]{1,0:T(8,128)S(1)}, f32[128,128]{1,0:T(8,128)S(1)}, u32[]{:S(2)}, u32[]{:S(2)}) collective-permute-start(f32[128,128]{1,0:T(8,128)S(1)} %shard_map.98.got), channel_id=1, source_target_pairs={{0,1},{1,2},{2,3},{3,4},{4,5},{5,6},{6,7},{7,0},{8,9},{9,10},{10,1... | collective-permute-start | bytes 196616 | tf_op jit(solution)/shard_map/ppermute | solution.py:408
  46.2 1.5 %shard_map.99.own = f32[4,3,4,24,128]{4,3,2,1,0:T(8,128)S(1)} custom-call(f32[128,128]{1,0:T(8,128)S(1)} %shard_map.98.got, f32[1,4,24,128]{3,2,1,0:T(8,128)S(1)} %get-tuple-element.23._.c), custom_call_target="tpu_custom_call" | custom-call | bytes 9000000 | tf_op jit(solution)/shard_map/pallas_call | solution.py:393
  47.7 0.4 collective-permute-done.5.high_list
  48.1 1.3 %collective-permute-done.4.low_list = f32[128,128]{1,0:T(8,128)S(1)} collective-permute-done((f32[128,128]{1,0:T(8,128)S(1)}, f32[128,128]{1,0:T(8,128)S(1)}, u32[]{:S(2)}, u32[]{:S(2)}) %collective-permute-start.4) | collective-permute-done | bytes 65568 | tf_op jit(solution)/shard_map/ppermute | solution.py:408
  49.4 2.1 %shard_map.100 = (f32[3,12,24,128]{3,2,1,0:T(8,128)S(1)}, f32[3,12,24,128]{3,2,1,0:T(8,128)S(1)}, f32[4,12,24,128]{3,2,1,0:T(8,128)S(1)}, f32[1,12,24,128]{3,2,1...) custom-call(f32[3,4,24,128]{3,2,1,0:T(8,128)S(1)} %get-tuple-element.20.u, ...), custom_call_target="tpu_custom_call" | custom-call | bytes 9000000 | tf_op jit(solution)/shard_map/pallas_call | solution.py:393
  51.6 6.7 %collective-permute-start.6 = (f32[160,128]{1,0:T(8,128)S(1)}, f32[160,128]{1,0:T(8,128)S(1)}, u32[]{:S(2)}, u32[]{:S(2)}) collective-permute-start(f32[160,128]{1,0:T(8,128)S(1)} %get-tuple-element.34), channel_id=1, source_target_pairs={{0,64},{64,128},{128,192},{192,0},{1,65},{65,129},{129,193},{193,1... | collective-permute-start | bytes 245768 | tf_op jit(solution)/shard_map/ppermute | solution.py:408
  58.4 1.4 %collective-permute-done.6.at_left = f32[160,128]{1,0:T(8,128)S(1)} collective-permute-done((f32[160,128]{1,0:T(8,128)S(1)}, f32[160,128]{1,0:T(8,128)S(1)}, u32[]{:S(2)}, u32[]{:S(2)}) %collective-permute-start.6) | collective-permute-done | bytes 81952 | tf_op jit(solution)/shard_map/ppermute | solution.py:408
  59.8 2.4 %collective-permute-done.7.at_right = f32[160,128]{1,0:T(8,128)S(1)} collective-permute-done((f32[160,128]{1,0:T(8,128)S(1)}, f32[160,128]{1,0:T(8,128)S(1)}, u32[]{:S(2)}, u32[]{:S(2)}) %collective-permute-start.7) | collective-permute-done | bytes 81952 | tf_op jit(solution)/shard_map/ppermute | solution.py:408
  62.2 9.0 %shard_map.102 = (f32[3,4,16,128]{3,2,1,0:T(8,128)}, f32[3,4,16,128]{3,2,1,0:T(8,128)}) custom-call(f32[3,12,24,128]{3,2,1,0:T(8,128)S(1)} %get-tuple-element.27.u, f32[3,12,24,128]{3,2,1,0:T(8,128)S(1)} %get-tuple-element.28.v, f32[4,12,24,128]{3,2,1,0:T(8,128)S(1)} %get-tuple-element.29.m, f32[1,12,24,128]{3,2,1,0:T(8,128)S(1)} %get-tuple-element.30.c, ...), custom_call_target="tpu_custom_call" | custom-call | bytes 15000000 | tf_op jit(solution)/shard_map/pallas_call | solution.py:393
  (9 shorter events, 0.1 us)
Async XLA Ops:
  2.2 8.9 %collective-permute-start = (f32[11,2,8,128]{3,2,1,0:T(8,128)}, f32[11,2,8,128]{3,2,1,0:T(8,128)S(1)}, u32[]{:S(2)}, u32[]{:S(2)}) collective-permute-start(f32[11,2,8,128]{3,2,1,0:T(8,128)} %shard_map.95), channel_id=1, source_target_pairs={{0,8},{8,16},{16,24},{24,32},{32,40},{40,48},{48,56},{56,0},{1,9},... | collective-permute-start | bytes 270344 | tf_op jit(solution)/shard_map/ppermute | solution.py:408
  8.8 5.4 %collective-permute-start.1 = (f32[11,2,8,128]{3,2,1,0:T(8,128)}, f32[11,2,8,128]{3,2,1,0:T(8,128)S(1)}, u32[]{:S(2)}, u32[]{:S(2)}) collective-permute-start(f32[11,2,8,128]{3,2,1,0:T(8,128)} %get-tuple-element.19), channel_id=1, source_target_pairs={{0,56},{8,0},{16,8},{24,16},{32,24},{40,32},{48,40},{56,48},{1,57}... | collective-permute-start | bytes 270344 | tf_op jit(solution)/shard_map/ppermute | solution.py:408
  14.2 0.9 %copy-start = (f32[4,4,16,128]{3,2,1,0:T(8,128)S(1)}, f32[4,4,16,128]{3,2,1,0:T(8,128)}, u32[]{:S(2)}) copy-start(f32[4,4,16,128]{3,2,1,0:T(8,128)} %mod.5) | copy-start | bytes 393220
  15.1 0.9 %copy-start.1 = (f32[3,4,16,128]{3,2,1,0:T(8,128)S(1)}, f32[3,4,16,128]{3,2,1,0:T(8,128)}, u32[]{:S(2)}) copy-start(f32[3,4,16,128]{3,2,1,0:T(8,128)} %cur.5) | copy-start | bytes 294916
  16.0 0.9 %copy-start.2 = (f32[3,4,16,128]{3,2,1,0:T(8,128)S(1)}, f32[3,4,16,128]{3,2,1,0:T(8,128)}, u32[]{:S(2)}) copy-start(f32[3,4,16,128]{3,2,1,0:T(8,128)} %prv.5) | copy-start | bytes 294916
  16.9 0.8 %copy-start.3 = (f32[4,16,128]{2,1,0:T(8,128)S(1)}, f32[4,16,128]{2,1,0:T(8,128)}, u32[]{:S(2)}) copy-start(f32[4,16,128]{2,1,0:T(8,128)} %den.1) | copy-start | bytes 98308
  17.7 31.7 %collective-permute-start.2 = (f32[38,24,128]{2,1,0:T(8,128)S(1)}, f32[38,24,128]{2,1,0:T(8,128)S(1)}, u32[]{:S(2)}, u32[]{:S(2)}) collective-permute-start(f32[38,24,128]{2,1,0:T(8,128)S(1)} %get-tuple-element.25), channel_id=1, source_target_pairs={{0,1},{1,2},{2,3},{3,4},{4,5},{5,6},{6,7},{7,0},{8,9},{9,10},{10,1... | collective-permute-start | bytes 1400840 | tf_op jit(solution)/shard_map/ppermute | solution.py:408
  19.3 30.2 %collective-permute-start.3 = (f32[38,24,128]{2,1,0:T(8,128)S(1)}, f32[38,24,128]{2,1,0:T(8,128)S(1)}, u32[]{:S(2)}, u32[]{:S(2)}) collective-permute-start(f32[38,24,128]{2,1,0:T(8,128)S(1)} %get-tuple-element.26), channel_id=1, source_target_pairs={{0,7},{1,0},{2,1},{3,2},{4,3},{5,4},{6,5},{7,6},{8,15},{9,8},{10,9... | collective-permute-start | bytes 1400840 | tf_op jit(solution)/shard_map/ppermute | solution.py:408
  44.6 3.5 %collective-permute-start.5 = (f32[128,128]{1,0:T(8,128)S(1)}, f32[128,128]{1,0:T(8,128)S(1)}, u32[]{:S(2)}, u32[]{:S(2)}) collective-permute-start(f32[128,128]{1,0:T(8,128)S(1)} %shard_map.98.got), channel_id=1, source_target_pairs={{0,7},{1,0},{2,1},{3,2},{4,3},{5,4},{6,5},{7,6},{8,15},{9,8},{10,9... | collective-permute-start | bytes 196616 | tf_op jit(solution)/shard_map/ppermute | solution.py:408
  45.1 4.3 %collective-permute-start.4 = (f32[128,128]{1,0:T(8,128)S(1)}, f32[128,128]{1,0:T(8,128)S(1)}, u32[]{:S(2)}, u32[]{:S(2)}) collective-permute-start(f32[128,128]{1,0:T(8,128)S(1)} %shard_map.98.got), channel_id=1, source_target_pairs={{0,1},{1,2},{2,3},{3,4},{4,5},{5,6},{6,7},{7,0},{8,9},{9,10},{10,1... | collective-permute-start | bytes 196616 | tf_op jit(solution)/shard_map/ppermute | solution.py:408
  51.6 8.2 %collective-permute-start.6 = (f32[160,128]{1,0:T(8,128)S(1)}, f32[160,128]{1,0:T(8,128)S(1)}, u32[]{:S(2)}, u32[]{:S(2)}) collective-permute-start(f32[160,128]{1,0:T(8,128)S(1)} %get-tuple-element.34), channel_id=1, source_target_pairs={{0,64},{64,128},{128,192},{192,0},{1,65},{65,129},{129,193},{193,1... | collective-permute-start | bytes 245768 | tf_op jit(solution)/shard_map/ppermute | solution.py:408
  58.3 3.9 %collective-permute-start.7 = (f32[160,128]{1,0:T(8,128)S(1)}, f32[160,128]{1,0:T(8,128)S(1)}, u32[]{:S(2)}, u32[]{:S(2)}) collective-permute-start(f32[160,128]{1,0:T(8,128)S(1)} %get-tuple-element.35), channel_id=1, source_target_pairs={{0,192},{64,0},{128,64},{192,128},{1,193},{65,1},{129,65},{193,129... | collective-permute-start | bytes 245768 | tf_op jit(solution)/shard_map/ppermute | solution.py:408

commit v4 on v2

--- a/solution.py
+++ b/solution.py
@@ -60,10 +60,20 @@
             ref[first_row + i : first_row + i + 1, :] = row
 
 
-def put_faces(u_ref, down_ref, up_ref, left_ref, right_ref):
-    for k in range(3):
-        down_ref[k] = u_ref[k, 0]
-        up_ref[k] = u_ref[k, CR - 1]
+def rad_is_even():
+    return lax.axis_index("rad") % 2 == 0
+
+
+def put_layers(ref, ks, even_ref, odd_ref, first=0):
+    top = jnp.where(rad_is_even(), CR - 1, 0)
+    rows = even_ref.shape[1]
+    for i, k in enumerate(ks):
+        even_ref[first + i] = ref[k, top, :rows, :]
+        odd_ref[first + i] = ref[k, CR - 1 - top, :rows, :]
+
+
+def put_faces(u_ref, even_ref, odd_ref, left_ref, right_ref):
+    put_layers(u_ref, range(3), even_ref, odd_ref)
     left_ref[...] = jnp.zeros_like(left_ref)
     right_ref[...] = jnp.zeros_like(right_ref)
     put_columns(tiles_of(u_ref, 3), left_ref, right_ref, 0)
@@ -176,7 +186,7 @@
 
 
 def widen_kernel(
-    cur, prv, mod, den, from_low, from_high, u, v, m, c, down, up, left, right
+    cur, prv, mod, den, from_low, from_high, u, v, m, c, even, odd, left, right
 ):
     lat = lax.axis_index("lat")
     has_low, has_high = lat > 0, lat < lax.axis_size("lat") - 1
@@ -207,12 +217,8 @@
         )
         present = jnp.where(iota((8, 128), 0) < HALO, has_high.astype(I32), has_low.astype(I32))
         c[r, CL:ROWS, :] = jnp.where(present > 0, outer, 0.0)
-    for k in range(3):
-        down[k] = u[k, 0]
-        up[k] = u[k, CR - 1]
-    for i, j in enumerate((0, 2)):
-        down[3 + i] = m[j, 0]
-        up[3 + i] = m[j, CR - 1]
+    put_layers(u, range(3), even, odd)
+    put_layers(m, (0, 2), even, odd, 3)
     left[...] = jnp.zeros_like(left)
     right[...] = jnp.zeros_like(right)
     put_columns(tiles_of(u, 3), left, right, 0)
@@ -233,17 +239,19 @@
     return total + (au[je - 1, r] * (after - here) + ad[je - 1, r] * (before - here))
 
 
-def radial_ends(low, high, count):
-    rad = lax.axis_index("rad")
-    lows = [jnp.where(rad > 0, low[k], 0.0) for k in range(count)]
-    highs = [
-        jnp.where(rad < lax.axis_size("rad") - 1, high[k], 0.0) for k in range(count)
-    ]
+def radial_ends(even, odd, count):
+    rad, is_even = lax.axis_index("rad"), rad_is_even()
+    lows, highs = [], []
+    for k in range(count):
+        low = jnp.where(is_even, odd[k], even[k])
+        high = jnp.where(is_even, even[k], odd[k])
+        lows.append(jnp.where(rad > 0, low, 0.0))
+        highs.append(jnp.where(rad < lax.axis_size("rad") - 1, high, 0.0))
     return lows, highs
 
 
-def prepare_kernel(u, v, m, c, low, high, at_left, at_right, ar, al, au, ad, following):
-    lows, highs = radial_ends(low, high, 5)
+def prepare_kernel(u, v, m, c, even, odd, at_left, at_right, ar, al, au, ad, following):
+    lows, highs = radial_ends(even, odd, 5)
     lane = iota((ROWS, CE), 1)
     for i, j in enumerate((0, 2)):
         layers = [lows[3 + i]] + [m[j, r] for r in range(CR)] + [highs[3 + i]]
@@ -265,36 +273,44 @@
             following[k, r] = 2.0 * u[k, r] - v[k, r] + c[r] * total
 
 
+def thirds(x):
+    high = x.astype(jnp.bfloat16).astype(F32)
+    rest = x - high
+    middle = rest.astype(jnp.bfloat16).astype(F32)
+    return high, middle, rest - middle
+
+
 def gather_sources(steps, got, weights, picks):
     turned = jnp.transpose(jnp.concatenate([got[:, 0, :128], got[:, 0, 128:]], axis=0))
+    parts = thirds(turned)
     cell_rows, cell_lanes = iota((CR * ROWS, 128), 0), iota((CE, 128), 0)
     for j in range(SLOTS):
-        span = slice(128 * j, 128 * j + 128)
         place = turned[96 + j : 97 + j].astype(I32)
         around = turned[104 + j : 105 + j].astype(I32)
-        picks[:, span] = jnp.where(cell_lanes == around, 1.0, 0.0)
+        pick = jnp.where(cell_lanes == around, 1.0, 0.0)
         here = cell_rows == place
-        for i, t in enumerate(steps):
-            for k in range(3):
-                line = (k * STEPS + t) * 8 + j
-                at = (i * 3 + k) * CR * ROWS
-                weights[at : at + CR * ROWS, span] = jnp.where(here, turned[line : line + 1], 0.0)
+        for p in range(3):
+            span = slice((p * SLOTS + j) * 128, (p * SLOTS + j + 1) * 128)
+            picks[:, span] = pick
+            for i, t in enumerate(steps):
+                for k in range(3):
+                    line = (k * STEPS + t) * 8 + j
+                    at = (i * 3 + k) * CR * ROWS
+                    weights[at : at + CR * ROWS, span] = jnp.where(
+                        here, parts[p][line : line + 1], 0.0
+                    )
     return lax.dot_general(
-        weights[...],
-        picks[...],
-        (((1,), (1,)), ((), ())),
-        precision=lax.Precision.HIGHEST,
-        preferred_element_type=F32,
-    )
-
-
-def first_kernel(got, free, c, first, down, up, left, right, weights, picks):
+        weights[...], picks[...], (((1,), (1,)), ((), ())), preferred_element_type=F32
+    )
+
+
+def first_kernel(got, free, c, first, even, odd, left, right, weights, picks):
     summed = gather_sources((0,), got, weights, picks)
     for k in range(3):
         for r in range(CR):
             at = (k * CR + r) * ROWS
             first[k, r] = free[k, r] + summed[at : at + ROWS] * c[r]
-    put_faces(first, down, up, left, right)
+    put_faces(first, even, odd, left, right)
 
 
 def sources_kernel(got, c, sources, weights, picks):
@@ -306,8 +322,8 @@
                 sources[t, k, r] = summed[at : at + ROWS] * c[r]
 
 
-def step_kernel(t, u, v, c, sources, low, high, at_left, at_right, ar, al, au, ad, *outs):
-    lows, highs = radial_ends(low, high, 3)
+def step_kernel(t, u, v, c, sources, even, odd, at_left, at_right, ar, al, au, ad, *outs):
+    lows, highs = radial_ends(even, odd, 3)
     following = outs[0]
     last = t == STEPS - 1
     for k in range(3):
@@ -344,12 +360,17 @@
     return lax.ppermute(block, axis, [(i, (i + by) % count) for i in range(count)])
 
 
-def swap_faces(down, up, left, right):
-    low = shifted(up, "rad", 1)
-    high = shifted(down, "rad", -1)
+def swapped(block, axis, odd):
+    count = lax.axis_size(axis)
+    pairs = [(i, (i + (1 if (i + odd) % 2 == 0 else -1)) % count) for i in range(count)]
+    return lax.ppermute(block, axis, pairs)
+
+
+def swap_faces(even, odd, left, right):
+    even, odd = swapped(even, "rad", 0), swapped(odd, "rad", 1)
     at_left = shifted(right, "span", 1)
     at_right = shifted(left, "span", -1)
-    return low, high, at_left, at_right
+    return even, odd, at_left, at_right
 
 
 def on_device(current, previous, moduli, density, traces, receivers, owners, offsets):
@@ -395,18 +416,18 @@
         [(2, CR + 1, ROWS, CE), wide, wide, wide, wide],
         (u, v, m, c, *swap_faces(*ends)),
     )
-    cells = CR * ROWS
+    cells, lanes = CR * ROWS, 3 * SLOTS * 128
     first, *ends = call(
         first_kernel,
         [wide] + faces,
         (got, free, c),
-        scratch=[(3 * cells, 128 * SLOTS), (CE, 128 * SLOTS)],
+        scratch=[(3 * cells, lanes), (CE, lanes)],
     )
     (sources,) = call(
         sources_kernel,
         [(STEPS - 1,) + wide],
         (got, c),
-        scratch=[(3 * (STEPS - 1) * cells, 128 * SLOTS), (CE, 128 * SLOTS)],
+        scratch=[(3 * (STEPS - 1) * cells, lanes), (CE, lanes)],
         us=3.0,
     )
     v, u = u, first

time: 60.9 us -> 57.2 us (0.939)
  starting transfers between devices: 37.6 us -> 34.9 us
  Pallas kernels: 10.8 us -> 9.27 us
    ppermute x18 -> x10, starting transfers between devices: 25.5 us -> 13.1 us  [shifted(): lax.ppermute(block, axis, [(i, (i + by) % count) for i in range(count)])]
    ppermute x0 -> x8, starting transfers between devices: none -> 9.68 us  [swapped(): return lax.ppermute(block, axis, pairs)]
    ppermute x18 -> x10, waiting for transfers between devices: 9.96 us -> 11.5 us  [shifted(): lax.ppermute(block, axis, [(i, (i + by) % count) for i in range(count)])]
    pallas_call x9, Pallas kernels: 10.8 us -> 9.27 us  [call(): pl.pallas_call(kernel, out_shape=[jax.ShapeDtypeStruct(shape, F32) for sh...]
    all_to_all x1, waiting for transfers between devices: 1.58 us -> 0.53 us  [on_device(): got = lax.all_to_all(packed, ('lat', 'rad'), 0, 0, tiled=True)]
  transfers between devices with their start and end apart: 19 -> 19, of which waited for: 8 -> 8; matrix products, arithmetic and copies ran while one was open for 0% -> 0% of each run, Pallas kernels for 10% -> 9%
where the time goes in v4:
time: 57.2 us; the launch traced here: 57 us
  starting transfers between devices  34.9 us (61%)
  waiting for transfers between devices  12 us (21%)
  Pallas kernels  9.27 us (16%)
  between operations  0.76 us (1%)
    ppermute x10, starting transfers between devices, shifted(): lax.ppermute(block, axis, [(i, (i + by) % count) for i in range(count)])  13.1 us
    all_to_all x1, starting transfers between devices, on_device(): got = lax.all_to_all(packed, ('lat', 'rad'), 0, 0, tiled=True)  12.1 us
    ppermute x10, waiting for transfers between devices, shifted(): lax.ppermute(block, axis, [(i, (i + by) % count) for i in range(count)])  11.5 us
    ppermute x8, starting transfers between devices, swapped(): return lax.ppermute(block, axis, pairs)  9.68 us
    pallas_call x9, Pallas kernels, call(): pl.pallas_call(kernel, out_shape=[jax.ShapeDtypeStruct(shape, F32) for sh...  9.27 us
  transfers between devices with their start and end apart: 19, of which 8 were waited for; matrix products, arithmetic and copies ran while one was open for 0% of the time, Pallas kernels for 9%

profile of v4, /device:TPU:1, one launch (start us, length us, event | category | flops | bytes accessed | tf_op | source)
XLA Modules:
  0.0 57.0 jit_solution(14365748352697435458)
XLA Ops:
  0.6 1.6 %shard_map.96 = f32[11,2,8,128]{3,2,1,0:T(8,128)} custom-call(f32[3,4,16,128]{3,2,1,0:T(8,128)} %cur.5, f32[3,4,16,128]{3,2,1,0:T(8,128)} %prv.5, f32[4,4,16,128]{3,2,1,0:T(8,128)} %mod.5, f32[1,4,16,128]{3,2,1,0:T(8,128)} %bitcast.5), custom_call_target="tpu_custom_call" | custom-call | bytes 3000000 | tf_op jit(solution)/shard_map/pallas_call | solution.py:345
  2.2 3.8 %collective-permute-start = (f32[11,2,8,128]{3,2,1,0:T(8,128)}, f32[11,2,8,128]{3,2,1,0:T(8,128)S(1)}, u32[]{:S(2)}, u32[]{:S(2)}) collective-permute-start(f32[11,2,8,128]{3,2,1,0:T(8,128)} %shard_map.96), channel_id=1, source_target_pairs={{0,8},{8,16},{16,24},{24,32},{32,40},{40,48},{48,56},{56,0},{1,9},... | collective-permute-start | bytes 270344 | tf_op jit(solution)/shard_map/ppermute | solution.py:360
  6.1 2.8 %shard_map.95 = (f32[64,1,256]{2,1,0:T(1,128)}, f32[11,2,8,128]{3,2,1,0:T(8,128)}) custom-call(s32[1,128]{1,0:T(1,128)} %bitcast.8, s32[1,128]{1,0:T(1,128)} %bitcast.9, s32[1,128]{1,0:T(1,128)} %bitcast.10, f32[3,128,512]{2,1,0:T(8,128)} %bitcast.7, f32[3,4,16,128]{3,2,1,0:T(8,128)} %cur.5, f32[3,4,16,128]{3,2,1,0:T(8,128)} %prv.5, f32[4,4,16,128]{3,2,1,0:T(8,128)} %mod.5, ...), custom_call_target="tpu_custom_call" | custom-call | bytes 6000000 | tf_op jit(solution)/shard_map/pallas_call | solution.py:345
  8.9 2.3 %collective-permute-start.1 = (f32[11,2,8,128]{3,2,1,0:T(8,128)}, f32[11,2,8,128]{3,2,1,0:T(8,128)S(1)}, u32[]{:S(2)}, u32[]{:S(2)}) collective-permute-start(f32[11,2,8,128]{3,2,1,0:T(8,128)} %get-tuple-element.33), channel_id=1, source_target_pairs={{0,56},{8,0},{16,8},{24,16},{32,24},{40,32},{48,40},{56,48},{1,57}... | collective-permute-start | bytes 270344 | tf_op jit(solution)/shard_map/ppermute | solution.py:360
  11.2 12.1 %all-to-all-start = ((f32[64,1,256]{2,1,0:T(1,128)}), f32[64,1,256]{2,1,0:T(1,128)S(1)}, u32[]{:S(2)}, u32[]{:S(2)}) async-start(f32[64,1,256]{2,1,0:T(1,128)} %get-tuple-element.32), calls=%async_computation | async-start | bytes 131072 | tf_op jit(solution)/shard_map/all_to_all | solution.py:406
  23.7 1.1 %collective-permute-start.2 = (f32[5,24,128]{2,1,0:T(8,128)S(1)}, f32[5,24,128]{2,1,0:T(8,128)S(1)}, u32[]{:S(2)}, u32[]{:S(2)}) collective-permute-start(f32[5,24,128]{2,1,0:T(8,128)S(1)} %get-tuple-element.38), channel_id=1, source_target_pairs={{0,1},{1,0},{2,3},{3,2},{4,5},{5,4},{6,7},{7,6},{8,9},{9,8},{10,11... | collective-permute-start | bytes 184328 | tf_op jit(solution)/shard_map/ppermute | solution.py:366
  24.8 2.4 %collective-permute-start.3 = (f32[5,24,128]{2,1,0:T(8,128)S(1)}, f32[5,24,128]{2,1,0:T(8,128)S(1)}, u32[]{:S(2)}, u32[]{:S(2)}) collective-permute-start(f32[5,24,128]{2,1,0:T(8,128)S(1)} %get-tuple-element.39), channel_id=1, source_target_pairs={{0,7},{1,2},{2,1},{3,4},{4,3},{5,6},{6,5},{7,0},{8,15},{9,10},{10,... | collective-permute-start | bytes 184328 | tf_op jit(solution)/shard_map/ppermute | solution.py:366
  27.2 2.6 %collective-permute-start.4 = (f32[8,128]{1,0:T(8,128)S(1)}, f32[8,128]{1,0:T(8,128)S(1)}, u32[]{:S(2)}, u32[]{:S(2)}) collective-permute-start(f32[8,128]{1,0:T(8,128)S(1)} %get-tuple-element.40), channel_id=1, source_target_pairs={{0,64},{64,128},{128,192},{192,0},{1,65},{65,129},{129,193},{193,1... | collective-permute-start | bytes 12296 | tf_op jit(solution)/shard_map/ppermute | solution.py:360
  29.8 0.8 %collective-permute-done.4.at_left = f32[8,128]{1,0:T(8,128)S(1)} collective-permute-done((f32[8,128]{1,0:T(8,128)S(1)}, f32[8,128]{1,0:T(8,128)S(1)}, u32[]{:S(2)}, u32[]{:S(2)}) %collective-permute-start.4) | collective-permute-done | bytes 4128 | tf_op jit(solution)/shard_map/ppermute | solution.py:360
  30.5 2.6 %collective-permute-done.5.at_right = f32[8,128]{1,0:T(8,128)S(1)} collective-permute-done((f32[8,128]{1,0:T(8,128)S(1)}, f32[8,128]{1,0:T(8,128)S(1)}, u32[]{:S(2)}, u32[]{:S(2)}) %collective-permute-start.5) | collective-permute-done | bytes 4128 | tf_op jit(solution)/shard_map/ppermute | solution.py:360
  34.3 0.7 %shard_map.99 = (f32[3,4,24,128]{3,2,1,0:T(8,128)S(1)}, f32[3,24,128]{2,1,0:T(8,128)S(1)}, f32[3,24,128]{2,1,0:T(8,128)S(1)}, f32[8,128]{1,0:T(8,128)S(1)}, f32[8,128]{1,0:T(8,128)S(1)}) custom-call(f32[64,1,256]{2,1,0:T(1,128)S(1)} %all-to-all-done.got, f32[3,4,24,128]{3,2,1,0:T(8,128)S(1)} %get-tuple-element.42.free, ...), custom_call_target="tpu_custom_call" | custom-call | bytes 3000000 | tf_op jit(solution)/shard_map/pallas_call | solution.py:345
  35.6 1.4 %collective-permute-start.7 = (f32[3,24,128]{2,1,0:T(8,128)S(1)}, f32[3,24,128]{2,1,0:T(8,128)S(1)}, u32[]{:S(2)}, u32[]{:S(2)}) collective-permute-start(f32[3,24,128]{2,1,0:T(8,128)S(1)} %get-tuple-element.45), channel_id=1, source_target_pairs={{0,7},{1,2},{2,1},{3,4},{4,3},{5,6},{6,5},{7,0},{8,15},{9,10},{10,... | collective-permute-start | bytes 110600 | tf_op jit(solution)/shard_map/ppermute | solution.py:366
  37.0 2.7 %collective-permute-start.8 = (f32[8,128]{1,0:T(8,128)S(1)}, f32[8,128]{1,0:T(8,128)S(1)}, u32[]{:S(2)}, u32[]{:S(2)}) collective-permute-start(f32[8,128]{1,0:T(8,128)S(1)} %get-tuple-element.46), channel_id=1, source_target_pairs={{0,64},{64,128},{128,192},{192,0},{1,65},{65,129},{129,193},{193,1... | collective-permute-start | bytes 12296 | tf_op jit(solution)/shard_map/ppermute | solution.py:360
  39.7 1.3 %shard_map.100.refs_3_ = f32[3,3,4,24,128]{4,3,2,1,0:T(8,128)S(1)} custom-call(f32[64,1,256]{2,1,0:T(1,128)S(1)} %all-to-all-done.got, f32[4,24,128]{2,1,0:T(8,128)S(1)} %get-tuple-element.37.c.refs_2_), custom_call_target="tpu_custom_call" | custom-call | bytes 9000000 | tf_op jit(solution)/shard_map/pallas_call | solution.py:345
  41.0 2.0 %collective-permute-done.9.refs_7_ = f32[8,128]{1,0:T(8,128)S(1)} collective-permute-done((f32[8,128]{1,0:T(8,128)S(1)}, f32[8,128]{1,0:T(8,128)S(1)}, u32[]{:S(2)}, u32[]{:S(2)}) %collective-permute-start.9) | collective-permute-done | bytes 4128 | tf_op jit(solution)/shard_map/ppermute | solution.py:360
  43.9 2.0 %collective-permute-start.11 = (f32[3,24,128]{2,1,0:T(8,128)S(1)}, f32[3,24,128]{2,1,0:T(8,128)S(1)}, u32[]{:S(2)}, u32[]{:S(2)}) collective-permute-start(f32[3,24,128]{2,1,0:T(8,128)S(1)} %get-tuple-element.54), channel_id=1, source_target_pairs={{0,7},{1,2},{2,1},{3,4},{4,3},{5,6},{6,5},{7,0},{8,15},{9,10},{10,... | collective-permute-start | bytes 110600 | tf_op jit(solution)/shard_map/ppermute | solution.py:366
  46.4 0.7 %collective-permute-done.12.refs_6_ = f32[8,128]{1,0:T(8,128)S(1)} collective-permute-done((f32[8,128]{1,0:T(8,128)S(1)}, f32[8,128]{1,0:T(8,128)S(1)}, u32[]{:S(2)}, u32[]{:S(2)}) %collective-permute-start.12) | collective-permute-done | bytes 4128 | tf_op jit(solution)/shard_map/ppermute | solution.py:360
  47.1 2.5 %collective-permute-done.13.refs_7_ = f32[8,128]{1,0:T(8,128)S(1)} collective-permute-done((f32[8,128]{1,0:T(8,128)S(1)}, f32[8,128]{1,0:T(8,128)S(1)}, u32[]{:S(2)}, u32[]{:S(2)}) %collective-permute-start.13) | collective-permute-done | bytes 4128 | tf_op jit(solution)/shard_map/ppermute | solution.py:360
  50.1 0.9 %collective-permute-start.14 = (f32[3,24,128]{2,1,0:T(8,128)S(1)}, f32[3,24,128]{2,1,0:T(8,128)S(1)}, u32[]{:S(2)}, u32[]{:S(2)}) collective-permute-start(f32[3,24,128]{2,1,0:T(8,128)S(1)} %get-tuple-element.58), channel_id=1, source_target_pairs={{0,1},{1,0},{2,3},{3,2},{4,5},{5,4},{6,7},{7,6},{8,9},{9,8},{10,11... | collective-permute-start | bytes 110600 | tf_op jit(solution)/shard_map/ppermute | solution.py:366
  51.0 0.9 %collective-permute-start.15 = (f32[3,24,128]{2,1,0:T(8,128)S(1)}, f32[3,24,128]{2,1,0:T(8,128)S(1)}, u32[]{:S(2)}, u32[]{:S(2)}) collective-permute-start(f32[3,24,128]{2,1,0:T(8,128)S(1)} %get-tuple-element.59), channel_id=1, source_target_pairs={{0,7},{1,2},{2,1},{3,4},{4,3},{5,6},{6,5},{7,0},{8,15},{9,10},{10,... | collective-permute-start | bytes 110600 | tf_op jit(solution)/shard_map/ppermute | solution.py:366
  51.9 1.1 %collective-permute-start.16 = (f32[8,128]{1,0:T(8,128)S(1)}, f32[8,128]{1,0:T(8,128)S(1)}, u32[]{:S(2)}, u32[]{:S(2)}) collective-permute-start(f32[8,128]{1,0:T(8,128)S(1)} %get-tuple-element.60), channel_id=1, source_target_pairs={{0,64},{64,128},{128,192},{192,0},{1,65},{65,129},{129,193},{193,1... | collective-permute-start | bytes 12296 | tf_op jit(solution)/shard_map/ppermute | solution.py:360
  53.0 0.8 %collective-permute-done.16.refs_6_ = f32[8,128]{1,0:T(8,128)S(1)} collective-permute-done((f32[8,128]{1,0:T(8,128)S(1)}, f32[8,128]{1,0:T(8,128)S(1)}, u32[]{:S(2)}, u32[]{:S(2)}) %collective-permute-start.16) | collective-permute-done | bytes 4128 | tf_op jit(solution)/shard_map/ppermute | solution.py:360
  53.8 2.3 %collective-permute-done.17.refs_7_ = f32[8,128]{1,0:T(8,128)S(1)} collective-permute-done((f32[8,128]{1,0:T(8,128)S(1)}, f32[8,128]{1,0:T(8,128)S(1)}, u32[]{:S(2)}, u32[]{:S(2)}) %collective-permute-start.17) | collective-permute-done | bytes 4128 | tf_op jit(solution)/shard_map/ppermute | solution.py:360
  56.1 0.9 %shard_map.103 = (f32[3,4,16,128]{3,2,1,0:T(8,128)}, f32[3,4,16,128]{3,2,1,0:T(8,128)}) custom-call(f32[3,4,24,128]{3,2,1,0:T(8,128)S(1)} %get-tuple-element.57.refs_0_, f32[3,4,24,128]{3,2,1,0:T(8,128)S(1)} %get-tuple-element.52.refs_0_.refs_1_, f32[4,24,128]{2,1,0:T(8,128)S(1)} %get-tuple-element.37.c.refs_2_, ...), custom_call_target="tpu_custom_call" | custom-call | bytes 3000000 | tf_op jit(solution)/shard_map/pallas_call | solution.py:345
  (31 shorter events, 3.9 us)
Async XLA Ops:
  2.2 21.1 %collective-permute-start = (f32[11,2,8,128]{3,2,1,0:T(8,128)}, f32[11,2,8,128]{3,2,1,0:T(8,128)S(1)}, u32[]{:S(2)}, u32[]{:S(2)}) collective-permute-start(f32[11,2,8,128]{3,2,1,0:T(8,128)} %shard_map.96), channel_id=1, source_target_pairs={{0,8},{8,16},{16,24},{24,32},{32,40},{40,48},{48,56},{56,0},{1,9},... | collective-permute-start | bytes 270344 | tf_op jit(solution)/shard_map/ppermute | solution.py:360
  6.0 17.3 %copy-start.1 = (f32[3,4,16,128]{3,2,1,0:T(8,128)S(1)}, f32[3,4,16,128]{3,2,1,0:T(8,128)}, u32[]{:S(2)}) copy-start(f32[3,4,16,128]{3,2,1,0:T(8,128)} %cur.5) | copy-start | bytes 294916
  6.0 17.3 %copy-start.2 = (f32[3,4,16,128]{3,2,1,0:T(8,128)S(1)}, f32[3,4,16,128]{3,2,1,0:T(8,128)}, u32[]{:S(2)}) copy-start(f32[3,4,16,128]{3,2,1,0:T(8,128)} %prv.5) | copy-start | bytes 294916
  6.1 17.3 %copy-start.3 = (f32[4,16,128]{2,1,0:T(8,128)S(1)}, f32[4,16,128]{2,1,0:T(8,128)}, u32[]{:S(2)}) copy-start(f32[4,16,128]{2,1,0:T(8,128)} %den.1) | copy-start | bytes 98308
  8.9 14.5 %copy-start = (f32[4,4,16,128]{3,2,1,0:T(8,128)S(1)}, f32[4,4,16,128]{3,2,1,0:T(8,128)}, u32[]{:S(2)}) copy-start(f32[4,4,16,128]{3,2,1,0:T(8,128)} %mod.5) | copy-start | bytes 393220
  8.9 14.4 %collective-permute-start.1 = (f32[11,2,8,128]{3,2,1,0:T(8,128)}, f32[11,2,8,128]{3,2,1,0:T(8,128)S(1)}, u32[]{:S(2)}, u32[]{:S(2)}) collective-permute-start(f32[11,2,8,128]{3,2,1,0:T(8,128)} %get-tuple-element.33), channel_id=1, source_target_pairs={{0,56},{8,0},{16,8},{24,16},{32,24},{40,32},{48,40},{56,48},{1,57}... | collective-permute-start | bytes 270344 | tf_op jit(solution)/shard_map/ppermute | solution.py:360
  11.2 23.1 %all-to-all-start = ((f32[64,1,256]{2,1,0:T(1,128)}), f32[64,1,256]{2,1,0:T(1,128)S(1)}, u32[]{:S(2)}, u32[]{:S(2)}) async-start(f32[64,1,256]{2,1,0:T(1,128)} %get-tuple-element.32), calls=%async_computation | async-start | bytes 131072 | tf_op jit(solution)/shard_map/all_to_all | solution.py:406
  23.7 9.5 %collective-permute-start.2 = (f32[5,24,128]{2,1,0:T(8,128)S(1)}, f32[5,24,128]{2,1,0:T(8,128)S(1)}, u32[]{:S(2)}, u32[]{:S(2)}) collective-permute-start(f32[5,24,128]{2,1,0:T(8,128)S(1)} %get-tuple-element.38), channel_id=1, source_target_pairs={{0,1},{1,0},{2,3},{3,2},{4,5},{5,4},{6,7},{7,6},{8,9},{9,8},{10,11... | collective-permute-start | bytes 184328 | tf_op jit(solution)/shard_map/ppermute | solution.py:366
  24.8 8.4 %collective-permute-start.3 = (f32[5,24,128]{2,1,0:T(8,128)S(1)}, f32[5,24,128]{2,1,0:T(8,128)S(1)}, u32[]{:S(2)}, u32[]{:S(2)}) collective-permute-start(f32[5,24,128]{2,1,0:T(8,128)S(1)} %get-tuple-element.39), channel_id=1, source_target_pairs={{0,7},{1,2},{2,1},{3,4},{4,3},{5,6},{6,5},{7,0},{8,15},{9,10},{10,... | collective-permute-start | bytes 184328 | tf_op jit(solution)/shard_map/ppermute | solution.py:366
  27.2 3.4 %collective-permute-start.4 = (f32[8,128]{1,0:T(8,128)S(1)}, f32[8,128]{1,0:T(8,128)S(1)}, u32[]{:S(2)}, u32[]{:S(2)}) collective-permute-start(f32[8,128]{1,0:T(8,128)S(1)} %get-tuple-element.40), channel_id=1, source_target_pairs={{0,64},{64,128},{128,192},{192,0},{1,65},{65,129},{129,193},{193,1... | collective-permute-start | bytes 12296 | tf_op jit(solution)/shard_map/ppermute | solution.py:360
  29.8 3.3 %collective-permute-start.5 = (f32[8,128]{1,0:T(8,128)S(1)}, f32[8,128]{1,0:T(8,128)S(1)}, u32[]{:S(2)}, u32[]{:S(2)}) collective-permute-start(f32[8,128]{1,0:T(8,128)S(1)} %get-tuple-element.41), channel_id=1, source_target_pairs={{0,192},{64,0},{128,64},{192,128},{1,193},{65,1},{129,65},{193,129... | collective-permute-start | bytes 12296 | tf_op jit(solution)/shard_map/ppermute | solution.py:360
  35.0 8.0 %collective-permute-start.6 = (f32[3,24,128]{2,1,0:T(8,128)S(1)}, f32[3,24,128]{2,1,0:T(8,128)S(1)}, u32[]{:S(2)}, u32[]{:S(2)}) collective-permute-start(f32[3,24,128]{2,1,0:T(8,128)S(1)} %get-tuple-element.44), channel_id=1, source_target_pairs={{0,1},{1,0},{2,3},{3,2},{4,5},{5,4},{6,7},{7,6},{8,9},{9,8},{10,11... | collective-permute-start | bytes 110600 | tf_op jit(solution)/shard_map/ppermute | solution.py:366
  35.6 7.4 %collective-permute-start.7 = (f32[3,24,128]{2,1,0:T(8,128)S(1)}, f32[3,24,128]{2,1,0:T(8,128)S(1)}, u32[]{:S(2)}, u32[]{:S(2)}) collective-permute-start(f32[3,24,128]{2,1,0:T(8,128)S(1)} %get-tuple-element.45), channel_id=1, source_target_pairs={{0,7},{1,2},{2,1},{3,4},{4,3},{5,6},{6,5},{7,0},{8,15},{9,10},{10,... | collective-permute-start | bytes 110600 | tf_op jit(solution)/shard_map/ppermute | solution.py:366
  37.0 4.0 %collective-permute-start.8 = (f32[8,128]{1,0:T(8,128)S(1)}, f32[8,128]{1,0:T(8,128)S(1)}, u32[]{:S(2)}, u32[]{:S(2)}) collective-permute-start(f32[8,128]{1,0:T(8,128)S(1)} %get-tuple-element.46), channel_id=1, source_target_pairs={{0,64},{64,128},{128,192},{192,0},{1,65},{65,129},{129,193},{193,1... | collective-permute-start | bytes 12296 | tf_op jit(solution)/shard_map/ppermute | solution.py:360
  39.7 3.3 %collective-permute-start.9 = (f32[8,128]{1,0:T(8,128)S(1)}, f32[8,128]{1,0:T(8,128)S(1)}, u32[]{:S(2)}, u32[]{:S(2)}) collective-permute-start(f32[8,128]{1,0:T(8,128)S(1)} %get-tuple-element.47), channel_id=1, source_target_pairs={{0,192},{64,0},{128,64},{192,128},{1,193},{65,1},{129,65},{193,129... | collective-permute-start | bytes 12296 | tf_op jit(solution)/shard_map/ppermute | solution.py:360
  43.5 6.1 %collective-permute-start.10 = (f32[3,24,128]{2,1,0:T(8,128)S(1)}, f32[3,24,128]{2,1,0:T(8,128)S(1)}, u32[]{:S(2)}, u32[]{:S(2)}) collective-permute-start(f32[3,24,128]{2,1,0:T(8,128)S(1)} %get-tuple-element.53), channel_id=1, source_target_pairs={{0,1},{1,0},{2,3},{3,2},{4,5},{5,4},{6,7},{7,6},{8,9},{9,8},{10,11... | collective-permute-start | bytes 110600 | tf_op jit(solution)/shard_map/ppermute | solution.py:366
  43.9 5.7 %collective-permute-start.11 = (f32[3,24,128]{2,1,0:T(8,128)S(1)}, f32[3,24,128]{2,1,0:T(8,128)S(1)}, u32[]{:S(2)}, u32[]{:S(2)}) collective-permute-start(f32[3,24,128]{2,1,0:T(8,128)S(1)} %get-tuple-element.54), channel_id=1, source_target_pairs={{0,7},{1,2},{2,1},{3,4},{4,3},{5,6},{6,5},{7,0},{8,15},{9,10},{10,... | collective-permute-start | bytes 110600 | tf_op jit(solution)/shard_map/ppermute | solution.py:366
  45.9 1.2 %collective-permute-start.12 = (f32[8,128]{1,0:T(8,128)S(1)}, f32[8,128]{1,0:T(8,128)S(1)}, u32[]{:S(2)}, u32[]{:S(2)}) collective-permute-start(f32[8,128]{1,0:T(8,128)S(1)} %get-tuple-element.55), channel_id=1, source_target_pairs={{0,64},{64,128},{128,192},{192,0},{1,65},{65,129},{129,193},{193,1... | collective-permute-start | bytes 12296 | tf_op jit(solution)/shard_map/ppermute | solution.py:360
  46.3 3.3 %collective-permute-start.13 = (f32[8,128]{1,0:T(8,128)S(1)}, f32[8,128]{1,0:T(8,128)S(1)}, u32[]{:S(2)}, u32[]{:S(2)}) collective-permute-start(f32[8,128]{1,0:T(8,128)S(1)} %get-tuple-element.56), channel_id=1, source_target_pairs={{0,192},{64,0},{128,64},{192,128},{1,193},{65,1},{129,65},{193,129... | collective-permute-start | bytes 12296 | tf_op jit(solution)/shard_map/ppermute | solution.py:360
  50.1 6.0 %collective-permute-start.14 = (f32[3,24,128]{2,1,0:T(8,128)S(1)}, f32[3,24,128]{2,1,0:T(8,128)S(1)}, u32[]{:S(2)}, u32[]{:S(2)}) collective-permute-start(f32[3,24,128]{2,1,0:T(8,128)S(1)} %get-tuple-element.58), channel_id=1, source_target_pairs={{0,1},{1,0},{2,3},{3,2},{4,5},{5,4},{6,7},{7,6},{8,9},{9,8},{10,11... | collective-permute-start | bytes 110600 | tf_op jit(solution)/shard_map/ppermute | solution.py:366
  51.0 5.1 %collective-permute-start.15 = (f32[3,24,128]{2,1,0:T(8,128)S(1)}, f32[3,24,128]{2,1,0:T(8,128)S(1)}, u32[]{:S(2)}, u32[]{:S(2)}) collective-permute-start(f32[3,24,128]{2,1,0:T(8,128)S(1)} %get-tuple-element.59), channel_id=1, source_target_pairs={{0,7},{1,2},{2,1},{3,4},{4,3},{5,6},{6,5},{7,0},{8,15},{9,10},{10,... | collective-permute-start | bytes 110600 | tf_op jit(solution)/shard_map/ppermute | solution.py:366
  51.9 1.9 %collective-permute-start.16 = (f32[8,128]{1,0:T(8,128)S(1)}, f32[8,128]{1,0:T(8,128)S(1)}, u32[]{:S(2)}, u32[]{:S(2)}) collective-permute-start(f32[8,128]{1,0:T(8,128)S(1)} %get-tuple-element.60), channel_id=1, source_target_pairs={{0,64},{64,128},{128,192},{192,0},{1,65},{65,129},{129,193},{193,1... | collective-permute-start | bytes 12296 | tf_op jit(solution)/shard_map/ppermute | solution.py:360
  53.0 3.0 %collective-permute-start.17 = (f32[8,128]{1,0:T(8,128)S(1)}, f32[8,128]{1,0:T(8,128)S(1)}, u32[]{:S(2)}, u32[]{:S(2)}) collective-permute-start(f32[8,128]{1,0:T(8,128)S(1)} %get-tuple-element.61), channel_id=1, source_target_pairs={{0,192},{64,0},{128,64},{192,128},{1,193},{65,1},{129,65},{193,129... | collective-permute-start | bytes 12296 | tf_op jit(solution)/shard_map/ppermute | solution.py:360

commit v5 on v4

--- a/solution.py
+++ b/solution.py
@@ -60,12 +60,12 @@
             ref[first_row + i : first_row + i + 1, :] = row
 
 
-def rad_is_even():
-    return lax.axis_index("rad") % 2 == 0
+def is_even(axis):
+    return lax.axis_index(axis) % 2 == 0
 
 
 def put_layers(ref, ks, even_ref, odd_ref, first=0):
-    top = jnp.where(rad_is_even(), CR - 1, 0)
+    top = jnp.where(is_even("rad"), CR - 1, 0)
     rows = even_ref.shape[1]
     for i, k in enumerate(ks):
         even_ref[first + i] = ref[k, top, :rows, :]
@@ -79,8 +79,9 @@
     put_columns(tiles_of(u_ref, 3), left_ref, right_ref, 0)
 
 
-def edge_rows(start, fields, out, room, sems):
+def edge_rows(upper, fields, out, room, sems):
     first, copies = 0, []
+    start = pl.multiple_of(jnp.where(upper, CL - 8, 0), 8)
     for i, ref in enumerate(fields):
         count = ref.shape[0]
         copies.append(
@@ -95,21 +96,22 @@
     def finish():
         for copy in copies:
             copy.wait()
-        inner = slice(0, HALO) if start == 0 else slice(8 - HALO, 8)
         for f in range(first):
             for r in range(CR):
                 spot = slice(HALO * (r % 2), HALO * (r % 2) + HALO)
-                out[f, r // 2, spot, :] = room[f, r, inner, :]
+                out[f, r // 2, spot, :] = jnp.where(
+                    upper, room[f, r, 8 - HALO : 8, :], room[f, r, 0:HALO, :]
+                )
 
     return finish
 
 
-def high_kernel(cur, prv, mod, den, high, room, sems):
-    edge_rows(CL - 8, (cur, prv, mod, den), high, room, sems)()
+def even_edge_kernel(cur, prv, mod, den, edge, room, sems):
+    edge_rows(is_even("lat"), (cur, prv, mod, den), edge, room, sems)()
 
 
 def pack_kernel(
-    offsets_in, receivers_in, owners_in, traces_in, cur, prv, mod, den, out, low,
+    offsets_in, receivers_in, owners_in, traces_in, cur, prv, mod, den, out, edge,
     room, sems, traces, words_in, trace_sem, word_sems,
 ):
     copy = pltpu.make_async_copy(traces_in, traces, trace_sem)
@@ -120,7 +122,7 @@
     ]
     for one in small:
         one.start()
-    finish_low = edge_rows(0, (cur, prv, mod, den), low, room, sems)
+    finish_edge = edge_rows(~is_even("lat"), (cur, prv, mod, den), edge, room, sems)
     for one in small:
         one.wait()
     offset_row, q, owner_row = words_in[0:1], words_in[1:2], words_in[2:3]
@@ -152,7 +154,7 @@
         lefts.append(jnp.where(wide_sub == place, 1.0, 0.0))
         lines += [j.astype(F32), (r * ROWS + row).astype(F32)]
     sheet = jnp.transpose(jnp.concatenate(lines + [jnp.zeros((1, 128), F32)], axis=0))
-    finish_low()
+    finish_edge()
 
     inside = offsets % 128
     tile = offsets // 128 + jnp.where(wide_lane < inside, 1, 0)
@@ -186,19 +188,21 @@
 
 
 def widen_kernel(
-    cur, prv, mod, den, from_low, from_high, u, v, m, c, even, odd, left, right
+    cur, prv, mod, den, by_even, by_odd, u, v, m, c, even, odd, left, right
 ):
     lat = lax.axis_index("lat")
     has_low, has_high = lat > 0, lat < lax.axis_size("lat") - 1
+    even_lat = is_even("lat")
+
+    def received(f, r):
+        spot = slice(HALO * (r % 2), HALO * (r % 2) + HALO)
+        one, other = by_even[f, r // 2, spot, :], by_odd[f, r // 2, spot, :]
+        return jnp.where(even_lat, one, other), jnp.where(even_lat, other, one)
 
     def ghosts(f, r):
-        spot = slice(HALO * (r % 2), HALO * (r % 2) + HALO)
+        high, low = received(f, r)
         return jnp.concatenate(
-            [
-                jnp.where(has_high, from_high[f, r // 2, spot, :], 0.0),
-                jnp.where(has_low, from_low[f, r // 2, spot, :], 0.0),
-            ],
-            axis=0,
+            [jnp.where(has_high, high, 0.0), jnp.where(has_low, low, 0.0)], axis=0
         )
 
     for r in range(CR):
@@ -211,10 +215,7 @@
             m[j, r, 0:CL, :] = mod[j, r]
             m[j, r, CL:ROWS, :] = ghosts(6 + j, r)
         c[r, 0:CL, :] = STEP_SQUARE / den[r]
-        spot = slice(HALO * (r % 2), HALO * (r % 2) + HALO)
-        outer = STEP_SQUARE / jnp.concatenate(
-            [from_high[10, r // 2, spot, :], from_low[10, r // 2, spot, :]], axis=0
-        )
+        outer = STEP_SQUARE / jnp.concatenate(received(10, r), axis=0)
         present = jnp.where(iota((8, 128), 0) < HALO, has_high.astype(I32), has_low.astype(I32))
         c[r, CL:ROWS, :] = jnp.where(present > 0, outer, 0.0)
     put_layers(u, range(3), even, odd)
@@ -240,11 +241,11 @@
 
 
 def radial_ends(even, odd, count):
-    rad, is_even = lax.axis_index("rad"), rad_is_even()
+    rad, even_rad = lax.axis_index("rad"), is_even("rad")
     lows, highs = [], []
     for k in range(count):
-        low = jnp.where(is_even, odd[k], even[k])
-        high = jnp.where(is_even, even[k], odd[k])
+        low = jnp.where(even_rad, odd[k], even[k])
+        high = jnp.where(even_rad, even[k], odd[k])
         lows.append(jnp.where(rad > 0, low, 0.0))
         highs.append(jnp.where(rad < lax.axis_size("rad") - 1, high, 0.0))
     return lows, highs
@@ -322,31 +323,46 @@
                 sources[t, k, r] = summed[at : at + ROWS] * c[r]
 
 
-def step_kernel(t, u, v, c, sources, even, odd, at_left, at_right, ar, al, au, ad, *outs):
+def step_kernel(
+    t, u, v, c, sources, even, odd, at_left, at_right, ar, al, au, ad, following, *faces
+):
     lows, highs = radial_ends(even, odd, 3)
-    following = outs[0]
-    last = t == STEPS - 1
     for k in range(3):
         for r in range(CR):
             total = force(k, r, u, lows, highs, at_left, at_right, ar, al, au, ad)
-            value = 2.0 * u[k, r] - v[k, r] + c[r] * total + sources[t - 1, k, r]
-            if last:
-                following[k, r] = value[:CL]
-                outs[1][k, r] = u[k, r, 0:CL, :]
-            else:
-                following[k, r] = value
-    if not last:
-        put_faces(following, *outs[1:])
-
-
-def call(kernel, outs, args, scratch=(), hbm=0, us=1.0):
+            following[k, r] = 2.0 * u[k, r] - v[k, r] + c[r] * total + sources[t - 1, k, r]
+    put_faces(following, *faces)
+
+
+def last_kernel(
+    u, v, c, sources, even, odd, at_left, at_right, ar, al, au, ad, final, before_final,
+    made, sems,
+):
+    copies = [pltpu.make_async_copy(u.at[:, :, pl.ds(0, CL), :], before_final, sems.at[3])]
+    copies[0].start()
+    lows, highs = radial_ends(even, odd, 3)
+    rest = jnp.zeros((ROWS - CL, CE), F32)
+    lows = [jnp.concatenate([x, rest], axis=0) for x in lows]
+    highs = [jnp.concatenate([x, rest], axis=0) for x in highs]
+    for k in range(3):
+        for r in range(CR):
+            total = force(k, r, u, lows, highs, at_left, at_right, ar, al, au, ad)
+            value = 2.0 * u[k, r] - v[k, r] + c[r] * total + sources[STEPS - 2, k, r]
+            made[k, r] = value[:CL]
+        copies.append(pltpu.make_async_copy(made.at[k], final.at[k], sems.at[k]))
+        copies[-1].start()
+    for copy in copies:
+        copy.wait()
+
+
+def call(kernel, outs, args, scratch=(), hbm=0, us=1.0, out_space=pltpu.VMEM):
     vmem = pl.BlockSpec(memory_space=pltpu.VMEM)
     specs = [pl.BlockSpec(memory_space=pltpu.HBM)] * hbm + [vmem] * (len(args) - hbm)
     return pl.pallas_call(
         kernel,
         out_shape=[jax.ShapeDtypeStruct(shape, F32) for shape in outs],
         in_specs=specs,
-        out_specs=[vmem] * len(outs),
+        out_specs=[pl.BlockSpec(memory_space=out_space)] * len(outs),
         scratch_shapes=[pltpu.VMEM(s, F32) if isinstance(s, tuple) else s for s in scratch],
         cost_estimate=pl.CostEstimate(
             flops=0, bytes_accessed=int(us * 3_000_000), transcendentals=0
@@ -367,7 +383,7 @@
 
 
 def swap_faces(even, odd, left, right):
-    even, odd = swapped(even, "rad", 0), swapped(odd, "rad", 1)
+    odd, even = swapped(odd, "rad", 1), swapped(even, "rad", 0)
     at_left = shifted(right, "span", 1)
     at_right = shifted(left, "span", -1)
     return even, odd, at_left, at_right
@@ -380,9 +396,9 @@
 
     fields = (current, previous, moduli, density.reshape((1,) + density.shape))
     rooms = [(11, CR, 8, CE), pltpu.SemaphoreType.DMA((4,))]
-    (high_rows,) = call(high_kernel, [edge], fields, scratch=rooms, hbm=4)
-    from_low = shifted(high_rows, "lat", 1)
-    packed, low_rows = call(
+    (even_rows,) = call(even_edge_kernel, [edge], fields, scratch=rooms, hbm=4)
+    by_even = swapped(even_rows, "lat", 0)
+    packed, odd_rows = call(
         pack_kernel,
         [(64, 1, 256), edge],
         (
@@ -402,14 +418,14 @@
         hbm=8,
         us=2.0,
     )
-    from_high = shifted(low_rows, "lat", -1)
+    by_odd = swapped(odd_rows, "lat", 1)
     got = lax.all_to_all(packed, ("lat", "rad"), 0, 0, tiled=True)
 
     u, v, m, c, *ends = call(
         widen_kernel,
         [wide, wide, (4, CR, ROWS, CE), (CR, ROWS, CE)]
         + [(5, ROWS, CE), (5, ROWS, CE), (8, CE), (8, CE)],
-        (current, previous, moduli, density, from_low, from_high),
+        (current, previous, moduli, density, by_even, by_odd),
     )
     *coefficients, free = call(
         prepare_kernel,
@@ -431,16 +447,26 @@
         us=3.0,
     )
     v, u = u, first
-    for t in range(1, STEPS):
-        args = (u, v, c, sources, *swap_faces(*ends), *coefficients)
+    for t in range(1, STEPS - 1):
 
         def kernel(*refs, t=t):
             step_kernel(t, *refs)
 
-        if t == STEPS - 1:
-            return tuple(call(kernel, [(3, CR, CL, CE)] * 2, args))
-        following, *ends = call(kernel, [wide] + faces, args)
-        v, u = u, following
+        if t == STEPS - 2:
+            faces = [(3, CL, CE)] * 2 + faces[2:]
+        following, *next_ends = call(
+            kernel, [wide] + faces, (u, v, c, sources, *swap_faces(*ends), *coefficients)
+        )
+        v, u, ends = u, following, next_ends
+    return tuple(
+        call(
+            last_kernel,
+            [(3, CR, CL, CE)] * 2,
+            (u, v, c, sources, *swap_faces(*ends), *coefficients),
+            scratch=[(3, CR, CL, CE), pltpu.SemaphoreType.DMA((4,))],
+            out_space=pltpu.HBM,
+        )
+    )
 
 
 def solution(mesh):

time: 57.2 us -> 57.8 us (1.010)
    ppermute x10 -> x8, starting transfers between devices: 13.1 us -> 6.97 us  [shifted(): lax.ppermute(block, axis, [(i, (i + by) % count) for i in range(count)])]
    ppermute x8 -> x10, starting transfers between devices: 9.68 us -> 15.7 us  [swapped(): return lax.ppermute(block, axis, pairs)]
    all_to_all x1, starting transfers between devices: 12.1 us -> 12.7 us  [on_device(): got = lax.all_to_all(packed, ('lat', 'rad'), 0, 0, tiled=True)]
    ppermute x10 -> x8, waiting for transfers between devices: 11.5 us -> 11.5 us  [shifted(): lax.ppermute(block, axis, [(i, (i + by) % count) for i in range(count)])]
where the time goes in v5:
time: 57.8 us; the launch traced here: 57.6 us
  starting transfers between devices  35.4 us (61%)
  waiting for transfers between devices  12.1 us (21%)
  Pallas kernels  9.2 us (16%)
  between operations  0.92 us (2%)
    ppermute x10, starting transfers between devices, swapped(): return lax.ppermute(block, axis, pairs)  15.7 us
    all_to_all x1, starting transfers between devices, on_device(): got = lax.all_to_all(packed, ('lat', 'rad'), 0, 0, tiled=True)  12.7 us
    ppermute x8, waiting for transfers between devices, shifted(): lax.ppermute(block, axis, [(i, (i + by) % count) for i in range(count)])  11.5 us
    pallas_call x9, Pallas kernels, call(): pl.pallas_call(kernel, out_shape=[jax.ShapeDtypeStruct(shape, F32) for sh...  9.2 us
    ppermute x8, starting transfers between devices, shifted(): lax.ppermute(block, axis, [(i, (i + by) % count) for i in range(count)])  6.97 us
  transfers between devices with their start and end apart: 19, of which 8 were waited for; matrix products, arithmetic and copies ran while one was open for 0% of the time, Pallas kernels for 9%

profile of v5, /device:TPU:1, one launch (start us, length us, event | category | flops | bytes accessed | tf_op | source)
XLA Modules:
  0.0 57.6 jit_solution(2471328438043547068)
XLA Ops:
  0.6 1.6 %shard_map.96 = f32[11,2,8,128]{3,2,1,0:T(8,128)} custom-call(f32[3,4,16,128]{3,2,1,0:T(8,128)} %cur.5, f32[3,4,16,128]{3,2,1,0:T(8,128)} %prv.5, f32[4,4,16,128]{3,2,1,0:T(8,128)} %mod.5, f32[1,4,16,128]{3,2,1,0:T(8,128)} %bitcast.5), custom_call_target="tpu_custom_call" | custom-call | bytes 3000000 | tf_op jit(solution)/shard_map/pallas_call | solution.py:361
  2.2 3.8 %collective-permute-start = (f32[11,2,8,128]{3,2,1,0:T(8,128)}, f32[11,2,8,128]{3,2,1,0:T(8,128)S(1)}, u32[]{:S(2)}, u32[]{:S(2)}) collective-permute-start(f32[11,2,8,128]{3,2,1,0:T(8,128)} %shard_map.96), channel_id=1, source_target_pairs={{0,8},{8,0},{16,24},{24,16},{32,40},{40,32},{48,56},{56,48},{1,9},... | collective-permute-start | bytes 270344 | tf_op jit(solution)/shard_map/ppermute | solution.py:382
  6.1 2.7 %shard_map.95 = (f32[64,1,256]{2,1,0:T(1,128)}, f32[11,2,8,128]{3,2,1,0:T(8,128)}) custom-call(s32[1,128]{1,0:T(1,128)} %bitcast.8, s32[1,128]{1,0:T(1,128)} %bitcast.9, s32[1,128]{1,0:T(1,128)} %bitcast.10, f32[3,128,512]{2,1,0:T(8,128)} %bitcast.7, f32[3,4,16,128]{3,2,1,0:T(8,128)} %cur.5, f32[3,4,16,128]{3,2,1,0:T(8,128)} %prv.5, f32[4,4,16,128]{3,2,1,0:T(8,128)} %mod.5, ...), custom_call_target="tpu_custom_call" | custom-call | bytes 6000000 | tf_op jit(solution)/shard_map/pallas_call | solution.py:361
  8.8 2.3 %collective-permute-start.1 = (f32[11,2,8,128]{3,2,1,0:T(8,128)}, f32[11,2,8,128]{3,2,1,0:T(8,128)S(1)}, u32[]{:S(2)}, u32[]{:S(2)}) collective-permute-start(f32[11,2,8,128]{3,2,1,0:T(8,128)} %get-tuple-element.33), channel_id=1, source_target_pairs={{0,56},{8,16},{16,8},{24,32},{32,24},{40,48},{48,40},{56,0},{1,57}... | collective-permute-start | bytes 270344 | tf_op jit(solution)/shard_map/ppermute | solution.py:382
  11.2 12.7 %all-to-all-start = ((f32[64,1,256]{2,1,0:T(1,128)}), f32[64,1,256]{2,1,0:T(1,128)S(1)}, u32[]{:S(2)}, u32[]{:S(2)}) async-start(f32[64,1,256]{2,1,0:T(1,128)} %get-tuple-element.32), calls=%async_computation | async-start | bytes 131072 | tf_op jit(solution)/shard_map/all_to_all | solution.py:422
  24.2 1.1 %collective-permute-start.2 = (f32[5,24,128]{2,1,0:T(8,128)S(1)}, f32[5,24,128]{2,1,0:T(8,128)S(1)}, u32[]{:S(2)}, u32[]{:S(2)}) collective-permute-start(f32[5,24,128]{2,1,0:T(8,128)S(1)} %get-tuple-element.38), channel_id=1, source_target_pairs={{0,1},{1,0},{2,3},{3,2},{4,5},{5,4},{6,7},{7,6},{8,9},{9,8},{10,11... | collective-permute-start | bytes 184328 | tf_op jit(solution)/shard_map/ppermute | solution.py:382
  25.3 2.4 %collective-permute-start.3 = (f32[5,24,128]{2,1,0:T(8,128)S(1)}, f32[5,24,128]{2,1,0:T(8,128)S(1)}, u32[]{:S(2)}, u32[]{:S(2)}) collective-permute-start(f32[5,24,128]{2,1,0:T(8,128)S(1)} %get-tuple-element.39), channel_id=1, source_target_pairs={{0,7},{1,2},{2,1},{3,4},{4,3},{5,6},{6,5},{7,0},{8,15},{9,10},{10,... | collective-permute-start | bytes 184328 | tf_op jit(solution)/shard_map/ppermute | solution.py:382
  27.7 2.6 %collective-permute-start.4 = (f32[8,128]{1,0:T(8,128)S(1)}, f32[8,128]{1,0:T(8,128)S(1)}, u32[]{:S(2)}, u32[]{:S(2)}) collective-permute-start(f32[8,128]{1,0:T(8,128)S(1)} %get-tuple-element.40), channel_id=1, source_target_pairs={{0,64},{64,128},{128,192},{192,0},{1,65},{65,129},{129,193},{193,1... | collective-permute-start | bytes 12296 | tf_op jit(solution)/shard_map/ppermute | solution.py:376
  30.4 0.8 %collective-permute-done.4.at_left = f32[8,128]{1,0:T(8,128)S(1)} collective-permute-done((f32[8,128]{1,0:T(8,128)S(1)}, f32[8,128]{1,0:T(8,128)S(1)}, u32[]{:S(2)}, u32[]{:S(2)}) %collective-permute-start.4) | collective-permute-done | bytes 4128 | tf_op jit(solution)/shard_map/ppermute | solution.py:376
  31.1 2.6 %collective-permute-done.5.at_right = f32[8,128]{1,0:T(8,128)S(1)} collective-permute-done((f32[8,128]{1,0:T(8,128)S(1)}, f32[8,128]{1,0:T(8,128)S(1)}, u32[]{:S(2)}, u32[]{:S(2)}) %collective-permute-start.5) | collective-permute-done | bytes 4128 | tf_op jit(solution)/shard_map/ppermute | solution.py:376
  34.9 0.7 %shard_map.99 = (f32[3,4,24,128]{3,2,1,0:T(8,128)S(1)}, f32[3,24,128]{2,1,0:T(8,128)S(1)}, f32[3,24,128]{2,1,0:T(8,128)S(1)}, f32[8,128]{1,0:T(8,128)S(1)}, f32[8,128]{1,0:T(8,128)S(1)}) custom-call(f32[64,1,256]{2,1,0:T(1,128)S(1)} %all-to-all-done.got, f32[3,4,24,128]{3,2,1,0:T(8,128)S(1)} %get-tuple-element.42.free, ...), custom_call_target="tpu_custom_call" | custom-call | bytes 3000000 | tf_op jit(solution)/shard_map/pallas_call | solution.py:361
  36.2 1.4 %collective-permute-start.7 = (f32[3,24,128]{2,1,0:T(8,128)S(1)}, f32[3,24,128]{2,1,0:T(8,128)S(1)}, u32[]{:S(2)}, u32[]{:S(2)}) collective-permute-start(f32[3,24,128]{2,1,0:T(8,128)S(1)} %get-tuple-element.45), channel_id=1, source_target_pairs={{0,7},{1,2},{2,1},{3,4},{4,3},{5,6},{6,5},{7,0},{8,15},{9,10},{10,... | collective-permute-start | bytes 110600 | tf_op jit(solution)/shard_map/ppermute | solution.py:382
  37.5 2.7 %collective-permute-start.8 = (f32[8,128]{1,0:T(8,128)S(1)}, f32[8,128]{1,0:T(8,128)S(1)}, u32[]{:S(2)}, u32[]{:S(2)}) collective-permute-start(f32[8,128]{1,0:T(8,128)S(1)} %get-tuple-element.46), channel_id=1, source_target_pairs={{0,64},{64,128},{128,192},{192,0},{1,65},{65,129},{129,193},{193,1... | collective-permute-start | bytes 12296 | tf_op jit(solution)/shard_map/ppermute | solution.py:376
  40.3 1.3 %shard_map.100.refs_3_.sources = f32[3,3,4,24,128]{4,3,2,1,0:T(8,128)S(1)} custom-call(f32[64,1,256]{2,1,0:T(1,128)S(1)} %all-to-all-done.got, f32[4,24,128]{2,1,0:T(8,128)S(1)} %get-tuple-element.37.c.refs_2_), custom_call_target="tpu_custom_call" | custom-call | bytes 9000000 | tf_op jit(solution)/shard_map/pallas_call | solution.py:361
  41.6 2.0 %collective-permute-done.9.refs_7_ = f32[8,128]{1,0:T(8,128)S(1)} collective-permute-done((f32[8,128]{1,0:T(8,128)S(1)}, f32[8,128]{1,0:T(8,128)S(1)}, u32[]{:S(2)}, u32[]{:S(2)}) %collective-permute-start.9) | collective-permute-done | bytes 4128 | tf_op jit(solution)/shard_map/ppermute | solution.py:376
  44.3 2.2 %collective-permute-start.11 = (f32[3,24,128]{2,1,0:T(8,128)S(1)}, f32[3,24,128]{2,1,0:T(8,128)S(1)}, u32[]{:S(2)}, u32[]{:S(2)}) collective-permute-start(f32[3,24,128]{2,1,0:T(8,128)S(1)} %get-tuple-element.54), channel_id=1, source_target_pairs={{0,7},{1,2},{2,1},{3,4},{4,3},{5,6},{6,5},{7,0},{8,15},{9,10},{10,... | collective-permute-start | bytes 110600 | tf_op jit(solution)/shard_map/ppermute | solution.py:382
  47.1 0.7 %collective-permute-done.12.refs_6_ = f32[8,128]{1,0:T(8,128)S(1)} collective-permute-done((f32[8,128]{1,0:T(8,128)S(1)}, f32[8,128]{1,0:T(8,128)S(1)}, u32[]{:S(2)}, u32[]{:S(2)}) %collective-permute-start.12) | collective-permute-done | bytes 4128 | tf_op jit(solution)/shard_map/ppermute | solution.py:376
  47.7 2.5 %collective-permute-done.13.refs_7_ = f32[8,128]{1,0:T(8,128)S(1)} collective-permute-done((f32[8,128]{1,0:T(8,128)S(1)}, f32[8,128]{1,0:T(8,128)S(1)}, u32[]{:S(2)}, u32[]{:S(2)}) %collective-permute-start.13) | collective-permute-done | bytes 4128 | tf_op jit(solution)/shard_map/ppermute | solution.py:376
  50.7 0.7 %collective-permute-start.14 = (f32[3,16,128]{2,1,0:T(8,128)S(1)}, f32[3,16,128]{2,1,0:T(8,128)S(1)}, u32[]{:S(2)}, u32[]{:S(2)}) collective-permute-start(f32[3,16,128]{2,1,0:T(8,128)S(1)} %get-tuple-element.58), channel_id=1, source_target_pairs={{0,1},{1,0},{2,3},{3,2},{4,5},{5,4},{6,7},{7,6},{8,9},{9,8},{10,11... | collective-permute-start | bytes 73736 | tf_op jit(solution)/shard_map/ppermute | solution.py:382
  51.4 1.0 %collective-permute-start.15 = (f32[3,16,128]{2,1,0:T(8,128)S(1)}, f32[3,16,128]{2,1,0:T(8,128)S(1)}, u32[]{:S(2)}, u32[]{:S(2)}) collective-permute-start(f32[3,16,128]{2,1,0:T(8,128)S(1)} %get-tuple-element.59), channel_id=1, source_target_pairs={{0,7},{1,2},{2,1},{3,4},{4,3},{5,6},{6,5},{7,0},{8,15},{9,10},{10,... | collective-permute-start | bytes 73736 | tf_op jit(solution)/shard_map/ppermute | solution.py:382
  52.4 1.1 %collective-permute-start.16 = (f32[8,128]{1,0:T(8,128)S(1)}, f32[8,128]{1,0:T(8,128)S(1)}, u32[]{:S(2)}, u32[]{:S(2)}) collective-permute-start(f32[8,128]{1,0:T(8,128)S(1)} %get-tuple-element.60), channel_id=1, source_target_pairs={{0,64},{64,128},{128,192},{192,0},{1,65},{65,129},{129,193},{193,1... | collective-permute-start | bytes 12296 | tf_op jit(solution)/shard_map/ppermute | solution.py:376
  53.5 0.8 %collective-permute-done.16.at_left = f32[8,128]{1,0:T(8,128)S(1)} collective-permute-done((f32[8,128]{1,0:T(8,128)S(1)}, f32[8,128]{1,0:T(8,128)S(1)}, u32[]{:S(2)}, u32[]{:S(2)}) %collective-permute-start.16) | collective-permute-done | bytes 4128 | tf_op jit(solution)/shard_map/ppermute | solution.py:376
  54.2 2.3 %collective-permute-done.17.at_right = f32[8,128]{1,0:T(8,128)S(1)} collective-permute-done((f32[8,128]{1,0:T(8,128)S(1)}, f32[8,128]{1,0:T(8,128)S(1)}, u32[]{:S(2)}, u32[]{:S(2)}) %collective-permute-start.17) | collective-permute-done | bytes 4128 | tf_op jit(solution)/shard_map/ppermute | solution.py:376
  56.5 0.9 %shard_map.103 = (f32[3,4,16,128]{3,2,1,0:T(8,128)}, f32[3,4,16,128]{3,2,1,0:T(8,128)}) custom-call(f32[3,4,24,128]{3,2,1,0:T(8,128)S(1)} %get-tuple-element.57.u, f32[3,4,24,128]{3,2,1,0:T(8,128)S(1)} %get-tuple-element.52.refs_0_.v, f32[4,24,128]{2,1,0:T(8,128)S(1)} %get-tuple-element.37.c.refs_2_, f32[3,3,4,24,128]{4,3,2,1,0:T(8,128)S(1)} %shard_map.100.refs_3_.sources, ...), custom_call_target="tpu_custom_call" | custom-call | bytes 3000000 | tf_op jit(solution)/shard_map/pallas_call | solution.py:361
  (31 shorter events, 3.7 us)
Async XLA Ops:
  2.2 21.7 %collective-permute-start = (f32[11,2,8,128]{3,2,1,0:T(8,128)}, f32[11,2,8,128]{3,2,1,0:T(8,128)S(1)}, u32[]{:S(2)}, u32[]{:S(2)}) collective-permute-start(f32[11,2,8,128]{3,2,1,0:T(8,128)} %shard_map.96), channel_id=1, source_target_pairs={{0,8},{8,0},{16,24},{24,16},{32,40},{40,32},{48,56},{56,48},{1,9},... | collective-permute-start | bytes 270344 | tf_op jit(solution)/shard_map/ppermute | solution.py:382
  6.1 17.9 %copy-start.1 = (f32[3,4,16,128]{3,2,1,0:T(8,128)S(1)}, f32[3,4,16,128]{3,2,1,0:T(8,128)}, u32[]{:S(2)}) copy-start(f32[3,4,16,128]{3,2,1,0:T(8,128)} %cur.5) | copy-start | bytes 294916
  6.1 17.9 %copy-start.2 = (f32[3,4,16,128]{3,2,1,0:T(8,128)S(1)}, f32[3,4,16,128]{3,2,1,0:T(8,128)}, u32[]{:S(2)}) copy-start(f32[3,4,16,128]{3,2,1,0:T(8,128)} %prv.5) | copy-start | bytes 294916
  6.1 17.9 %copy-start.3 = (f32[4,16,128]{2,1,0:T(8,128)S(1)}, f32[4,16,128]{2,1,0:T(8,128)}, u32[]{:S(2)}) copy-start(f32[4,16,128]{2,1,0:T(8,128)} %den.1) | copy-start | bytes 98308
  8.8 15.1 %copy-start = (f32[4,4,16,128]{3,2,1,0:T(8,128)S(1)}, f32[4,4,16,128]{3,2,1,0:T(8,128)}, u32[]{:S(2)}) copy-start(f32[4,4,16,128]{3,2,1,0:T(8,128)} %mod.5) | copy-start | bytes 393220
  8.8 15.1 %collective-permute-start.1 = (f32[11,2,8,128]{3,2,1,0:T(8,128)}, f32[11,2,8,128]{3,2,1,0:T(8,128)S(1)}, u32[]{:S(2)}, u32[]{:S(2)}) collective-permute-start(f32[11,2,8,128]{3,2,1,0:T(8,128)} %get-tuple-element.33), channel_id=1, source_target_pairs={{0,56},{8,16},{16,8},{24,32},{32,24},{40,48},{48,40},{56,0},{1,57}... | collective-permute-start | bytes 270344 | tf_op jit(solution)/shard_map/ppermute | solution.py:382
  11.2 23.7 %all-to-all-start = ((f32[64,1,256]{2,1,0:T(1,128)}), f32[64,1,256]{2,1,0:T(1,128)S(1)}, u32[]{:S(2)}, u32[]{:S(2)}) async-start(f32[64,1,256]{2,1,0:T(1,128)} %get-tuple-element.32), calls=%async_computation | async-start | bytes 131072 | tf_op jit(solution)/shard_map/all_to_all | solution.py:422
  24.2 9.5 %collective-permute-start.2 = (f32[5,24,128]{2,1,0:T(8,128)S(1)}, f32[5,24,128]{2,1,0:T(8,128)S(1)}, u32[]{:S(2)}, u32[]{:S(2)}) collective-permute-start(f32[5,24,128]{2,1,0:T(8,128)S(1)} %get-tuple-element.38), channel_id=1, source_target_pairs={{0,1},{1,0},{2,3},{3,2},{4,5},{5,4},{6,7},{7,6},{8,9},{9,8},{10,11... | collective-permute-start | bytes 184328 | tf_op jit(solution)/shard_map/ppermute | solution.py:382
  25.3 8.4 %collective-permute-start.3 = (f32[5,24,128]{2,1,0:T(8,128)S(1)}, f32[5,24,128]{2,1,0:T(8,128)S(1)}, u32[]{:S(2)}, u32[]{:S(2)}) collective-permute-start(f32[5,24,128]{2,1,0:T(8,128)S(1)} %get-tuple-element.39), channel_id=1, source_target_pairs={{0,7},{1,2},{2,1},{3,4},{4,3},{5,6},{6,5},{7,0},{8,15},{9,10},{10,... | collective-permute-start | bytes 184328 | tf_op jit(solution)/shard_map/ppermute | solution.py:382
  27.7 3.4 %collective-permute-start.4 = (f32[8,128]{1,0:T(8,128)S(1)}, f32[8,128]{1,0:T(8,128)S(1)}, u32[]{:S(2)}, u32[]{:S(2)}) collective-permute-start(f32[8,128]{1,0:T(8,128)S(1)} %get-tuple-element.40), channel_id=1, source_target_pairs={{0,64},{64,128},{128,192},{192,0},{1,65},{65,129},{129,193},{193,1... | collective-permute-start | bytes 12296 | tf_op jit(solution)/shard_map/ppermute | solution.py:376
  30.4 3.3 %collective-permute-start.5 = (f32[8,128]{1,0:T(8,128)S(1)}, f32[8,128]{1,0:T(8,128)S(1)}, u32[]{:S(2)}, u32[]{:S(2)}) collective-permute-start(f32[8,128]{1,0:T(8,128)S(1)} %get-tuple-element.41), channel_id=1, source_target_pairs={{0,192},{64,0},{128,64},{192,128},{1,193},{65,1},{129,65},{193,129... | collective-permute-start | bytes 12296 | tf_op jit(solution)/shard_map/ppermute | solution.py:376
  35.6 8.0 %collective-permute-start.6 = (f32[3,24,128]{2,1,0:T(8,128)S(1)}, f32[3,24,128]{2,1,0:T(8,128)S(1)}, u32[]{:S(2)}, u32[]{:S(2)}) collective-permute-start(f32[3,24,128]{2,1,0:T(8,128)S(1)} %get-tuple-element.44), channel_id=1, source_target_pairs={{0,1},{1,0},{2,3},{3,2},{4,5},{5,4},{6,7},{7,6},{8,9},{9,8},{10,11... | collective-permute-start | bytes 110600 | tf_op jit(solution)/shard_map/ppermute | solution.py:382
  36.2 7.4 %collective-permute-start.7 = (f32[3,24,128]{2,1,0:T(8,128)S(1)}, f32[3,24,128]{2,1,0:T(8,128)S(1)}, u32[]{:S(2)}, u32[]{:S(2)}) collective-permute-start(f32[3,24,128]{2,1,0:T(8,128)S(1)} %get-tuple-element.45), channel_id=1, source_target_pairs={{0,7},{1,2},{2,1},{3,4},{4,3},{5,6},{6,5},{7,0},{8,15},{9,10},{10,... | collective-permute-start | bytes 110600 | tf_op jit(solution)/shard_map/ppermute | solution.py:382
  37.5 4.1 %collective-permute-start.8 = (f32[8,128]{1,0:T(8,128)S(1)}, f32[8,128]{1,0:T(8,128)S(1)}, u32[]{:S(2)}, u32[]{:S(2)}) collective-permute-start(f32[8,128]{1,0:T(8,128)S(1)} %get-tuple-element.46), channel_id=1, source_target_pairs={{0,64},{64,128},{128,192},{192,0},{1,65},{65,129},{129,193},{193,1... | collective-permute-start | bytes 12296 | tf_op jit(solution)/shard_map/ppermute | solution.py:376
  40.3 3.3 %collective-permute-start.9 = (f32[8,128]{1,0:T(8,128)S(1)}, f32[8,128]{1,0:T(8,128)S(1)}, u32[]{:S(2)}, u32[]{:S(2)}) collective-permute-start(f32[8,128]{1,0:T(8,128)S(1)} %get-tuple-element.47), channel_id=1, source_target_pairs={{0,192},{64,0},{128,64},{192,128},{1,193},{65,1},{129,65},{193,129... | collective-permute-start | bytes 12296 | tf_op jit(solution)/shard_map/ppermute | solution.py:376
  44.1 6.1 %collective-permute-start.10 = (f32[3,24,128]{2,1,0:T(8,128)S(1)}, f32[3,24,128]{2,1,0:T(8,128)S(1)}, u32[]{:S(2)}, u32[]{:S(2)}) collective-permute-start(f32[3,24,128]{2,1,0:T(8,128)S(1)} %get-tuple-element.53), channel_id=1, source_target_pairs={{0,1},{1,0},{2,3},{3,2},{4,5},{5,4},{6,7},{7,6},{8,9},{9,8},{10,11... | collective-permute-start | bytes 110600 | tf_op jit(solution)/shard_map/ppermute | solution.py:382
  44.3 5.9 %collective-permute-start.11 = (f32[3,24,128]{2,1,0:T(8,128)S(1)}, f32[3,24,128]{2,1,0:T(8,128)S(1)}, u32[]{:S(2)}, u32[]{:S(2)}) collective-permute-start(f32[3,24,128]{2,1,0:T(8,128)S(1)} %get-tuple-element.54), channel_id=1, source_target_pairs={{0,7},{1,2},{2,1},{3,4},{4,3},{5,6},{6,5},{7,0},{8,15},{9,10},{10,... | collective-permute-start | bytes 110600 | tf_op jit(solution)/shard_map/ppermute | solution.py:382
  46.5 1.2 %collective-permute-start.12 = (f32[8,128]{1,0:T(8,128)S(1)}, f32[8,128]{1,0:T(8,128)S(1)}, u32[]{:S(2)}, u32[]{:S(2)}) collective-permute-start(f32[8,128]{1,0:T(8,128)S(1)} %get-tuple-element.55), channel_id=1, source_target_pairs={{0,64},{64,128},{128,192},{192,0},{1,65},{65,129},{129,193},{193,1... | collective-permute-start | bytes 12296 | tf_op jit(solution)/shard_map/ppermute | solution.py:376
  46.9 3.3 %collective-permute-start.13 = (f32[8,128]{1,0:T(8,128)S(1)}, f32[8,128]{1,0:T(8,128)S(1)}, u32[]{:S(2)}, u32[]{:S(2)}) collective-permute-start(f32[8,128]{1,0:T(8,128)S(1)} %get-tuple-element.56), channel_id=1, source_target_pairs={{0,192},{64,0},{128,64},{192,128},{1,193},{65,1},{129,65},{193,129... | collective-permute-start | bytes 12296 | tf_op jit(solution)/shard_map/ppermute | solution.py:376
  50.7 5.8 %collective-permute-start.14 = (f32[3,16,128]{2,1,0:T(8,128)S(1)}, f32[3,16,128]{2,1,0:T(8,128)S(1)}, u32[]{:S(2)}, u32[]{:S(2)}) collective-permute-start(f32[3,16,128]{2,1,0:T(8,128)S(1)} %get-tuple-element.58), channel_id=1, source_target_pairs={{0,1},{1,0},{2,3},{3,2},{4,5},{5,4},{6,7},{7,6},{8,9},{9,8},{10,11... | collective-permute-start | bytes 73736 | tf_op jit(solution)/shard_map/ppermute | solution.py:382
  51.4 5.1 %collective-permute-start.15 = (f32[3,16,128]{2,1,0:T(8,128)S(1)}, f32[3,16,128]{2,1,0:T(8,128)S(1)}, u32[]{:S(2)}, u32[]{:S(2)}) collective-permute-start(f32[3,16,128]{2,1,0:T(8,128)S(1)} %get-tuple-element.59), channel_id=1, source_target_pairs={{0,7},{1,2},{2,1},{3,4},{4,3},{5,6},{6,5},{7,0},{8,15},{9,10},{10,... | collective-permute-start | bytes 73736 | tf_op jit(solution)/shard_map/ppermute | solution.py:382
  52.4 1.8 %collective-permute-start.16 = (f32[8,128]{1,0:T(8,128)S(1)}, f32[8,128]{1,0:T(8,128)S(1)}, u32[]{:S(2)}, u32[]{:S(2)}) collective-permute-start(f32[8,128]{1,0:T(8,128)S(1)} %get-tuple-element.60), channel_id=1, source_target_pairs={{0,64},{64,128},{128,192},{192,0},{1,65},{65,129},{129,193},{193,1... | collective-permute-start | bytes 12296 | tf_op jit(solution)/shard_map/ppermute | solution.py:376
  53.5 3.0 %collective-permute-start.17 = (f32[8,128]{1,0:T(8,128)S(1)}, f32[8,128]{1,0:T(8,128)S(1)}, u32[]{:S(2)}, u32[]{:S(2)}) collective-permute-start(f32[8,128]{1,0:T(8,128)S(1)} %get-tuple-element.61), channel_id=1, source_target_pairs={{0,192},{64,0},{128,64},{192,128},{1,193},{65,1},{129,65},{193,129... | collective-permute-start | bytes 12296 | tf_op jit(solution)/shard_map/ppermute | solution.py:376

commit v6 on v4

--- a/solution.py
+++ b/solution.py
@@ -36,7 +36,7 @@
 
 def unfold(ref, first_row, tile):
     row = first_row + tile // 16
-    spread = jnp.broadcast_to(ref[row : row + 1, :], (8, 128))
+    spread = jnp.broadcast_to(ref[pl.ds(row, 1), :], (8, 128))
     return jnp.take_along_axis(spread, (tile % 16) * 8 + iota((8, 128), 0), axis=1)
 
 
@@ -64,16 +64,16 @@
     return lax.axis_index("rad") % 2 == 0
 
 
-def put_layers(ref, ks, even_ref, odd_ref, first=0):
+def end_layers():
     top = jnp.where(rad_is_even(), CR - 1, 0)
-    rows = even_ref.shape[1]
-    for i, k in enumerate(ks):
-        even_ref[first + i] = ref[k, top, :rows, :]
-        odd_ref[first + i] = ref[k, CR - 1 - top, :rows, :]
-
-
-def put_faces(u_ref, even_ref, odd_ref, left_ref, right_ref):
-    put_layers(u_ref, range(3), even_ref, odd_ref)
+    return top, CR - 1 - top
+
+
+def put_rest(u_ref, odd_ref, left_ref, right_ref):
+    _, bottom = end_layers()
+    rows = odd_ref.shape[1]
+    for k in range(3):
+        odd_ref[k] = u_ref[k, bottom, :rows, :]
     left_ref[...] = jnp.zeros_like(left_ref)
     right_ref[...] = jnp.zeros_like(right_ref)
     put_columns(tiles_of(u_ref, 3), left_ref, right_ref, 0)
@@ -217,26 +217,32 @@
         )
         present = jnp.where(iota((8, 128), 0) < HALO, has_high.astype(I32), has_low.astype(I32))
         c[r, CL:ROWS, :] = jnp.where(present > 0, outer, 0.0)
-    put_layers(u, range(3), even, odd)
-    put_layers(m, (0, 2), even, odd, 3)
+    top, bottom = end_layers()
+    for i, (field, k) in enumerate(((u, 0), (u, 1), (u, 2), (m, 0), (m, 2))):
+        even[i] = field[k, top]
+        odd[i] = field[k, bottom]
     left[...] = jnp.zeros_like(left)
     right[...] = jnp.zeros_like(right)
     put_columns(tiles_of(u, 3), left, right, 0)
     put_columns(tiles_of(m, 3, 1), left, right, 3)
 
 
-def force(k, r, u, low, high, at_left, at_right, ar, al, au, ad):
-    jr, jl, je = TABLE[k]
-    here = u[k, r]
-    below = u[k, r - 1] if r > 0 else low[k]
-    above = u[k, r + 1] if r < CR - 1 else high[k]
-    total = ar[jr // 2, r + 1] * (above - here) - ar[jr // 2, r] * (here - below)
+def level(k, r, here, at_left, at_right, al, au, ad):
+    _, jl, je = TABLE[k]
     flux = al[jl - 1, r] * (pltpu.roll(here, ROWS - 1, 0) - here)
-    total = total + (flux - pltpu.roll(flux, 1, 0))
+    total = flux - pltpu.roll(flux, 1, 0)
     lane = iota((ROWS, CE), 1)
     after = jnp.where(lane == CE - 1, column(at_right, 0, k, r), pltpu.roll(here, CE - 1, 1))
     before = jnp.where(lane == 0, column(at_left, 0, k, r), pltpu.roll(here, 1, 1))
     return total + (au[je - 1, r] * (after - here) + ad[je - 1, r] * (before - here))
+
+
+def force(k, r, u, low, high, at_left, at_right, ar, al, au, ad):
+    i, here = TABLE[k][0] // 2, u[k, r]
+    below = u[k, r - 1] if r > 0 else low[k]
+    above = u[k, r + 1] if r < CR - 1 else high[k]
+    total = ar[i, r + 1] * (above - here) - ar[i, r] * (here - below)
+    return total + level(k, r, here, at_left, at_right, al, au, ad)
 
 
 def radial_ends(even, odd, count):
@@ -280,10 +286,11 @@
     return high, middle, rest - middle
 
 
-def gather_sources(steps, got, weights, picks):
+def gather_sources(steps, got, weights, picks, layer=0, layers=CR):
     turned = jnp.transpose(jnp.concatenate([got[:, 0, :128], got[:, 0, 128:]], axis=0))
     parts = thirds(turned)
-    cell_rows, cell_lanes = iota((CR * ROWS, 128), 0), iota((CE, 128), 0)
+    cells = layers * ROWS
+    cell_rows, cell_lanes = iota((cells, 128), 0) + layer * ROWS, iota((CE, 128), 0)
     for j in range(SLOTS):
         place = turned[96 + j : 97 + j].astype(I32)
         around = turned[104 + j : 105 + j].astype(I32)
@@ -295,8 +302,8 @@
             for i, t in enumerate(steps):
                 for k in range(3):
                     line = (k * STEPS + t) * 8 + j
-                    at = (i * 3 + k) * CR * ROWS
-                    weights[at : at + CR * ROWS, span] = jnp.where(
+                    at = (i * 3 + k) * cells
+                    weights[at : at + cells, span] = jnp.where(
                         here, parts[p][line : line + 1], 0.0
                     )
     return lax.dot_general(
@@ -304,13 +311,20 @@
     )
 
 
-def first_kernel(got, free, c, first, even, odd, left, right, weights, picks):
+def first_lead_kernel(got, free, c, even, weights, picks):
+    top, _ = end_layers()
+    summed = gather_sources((0,), got, weights, picks, top, 1)
+    for k in range(3):
+        even[k] = free[k, top] + summed[k * ROWS : (k + 1) * ROWS] * c[top]
+
+
+def first_kernel(got, free, c, first, odd, left, right, weights, picks):
     summed = gather_sources((0,), got, weights, picks)
     for k in range(3):
         for r in range(CR):
             at = (k * CR + r) * ROWS
             first[k, r] = free[k, r] + summed[at : at + ROWS] * c[r]
-    put_faces(first, even, odd, left, right)
+    put_rest(first, odd, left, right)
 
 
 def sources_kernel(got, c, sources, weights, picks):
@@ -322,21 +336,43 @@
                 sources[t, k, r] = summed[at : at + ROWS] * c[r]
 
 
-def step_kernel(t, u, v, c, sources, even, odd, at_left, at_right, ar, al, au, ad, *outs):
+def lead_kernel(t, u, v, c, sources, even, at_left, at_right, ar, al, au, ad, out):
+    top, _ = end_layers()
+    upwards = rad_is_even()
+    inner = jnp.where(upwards, CR - 2, 1)
+    outer_face, inner_face = jnp.where(upwards, CR, 0), jnp.where(upwards, CR - 1, 1)
+    for k in range(3):
+        i, here = TABLE[k][0] // 2, u[k, top]
+        total = ar[i, outer_face] * (even[k] - here) + ar[i, inner_face] * (u[k, inner] - here)
+        total = total + level(k, top, here, at_left, at_right, al, au, ad)
+        value = 2.0 * here - v[k, top] + c[top] * total + sources[t - 1, k, top]
+        out[k] = value[: out.shape[1]]
+
+
+def step_kernel(
+    t, u, v, c, sources, even, odd, at_left, at_right, ar, al, au, ad, following, *rest
+):
     lows, highs = radial_ends(even, odd, 3)
-    following = outs[0]
-    last = t == STEPS - 1
     for k in range(3):
         for r in range(CR):
             total = force(k, r, u, lows, highs, at_left, at_right, ar, al, au, ad)
-            value = 2.0 * u[k, r] - v[k, r] + c[r] * total + sources[t - 1, k, r]
-            if last:
-                following[k, r] = value[:CL]
-                outs[1][k, r] = u[k, r, 0:CL, :]
-            else:
-                following[k, r] = value
-    if not last:
-        put_faces(following, *outs[1:])
+            following[k, r] = 2.0 * u[k, r] - v[k, r] + c[r] * total + sources[t - 1, k, r]
+    put_rest(following, *rest)
+
+
+def last_kernel(
+    u, v, c, sources, even, odd, at_left, at_right, ar, al, au, ad, final, before_final
+):
+    lows, highs = radial_ends(even, odd, 3)
+    beside = jnp.zeros((ROWS - CL, CE), F32)
+    lows = [jnp.concatenate([x, beside], axis=0) for x in lows]
+    highs = [jnp.concatenate([x, beside], axis=0) for x in highs]
+    for k in range(3):
+        for r in range(CR):
+            total = force(k, r, u, lows, highs, at_left, at_right, ar, al, au, ad)
+            value = 2.0 * u[k, r] - v[k, r] + c[r] * total + sources[STEPS - 2, k, r]
+            final[k, r] = value[:CL]
+            before_final[k, r] = u[k, r, 0:CL, :]
 
 
 def call(kernel, outs, args, scratch=(), hbm=0, us=1.0):
@@ -366,17 +402,14 @@
     return lax.ppermute(block, axis, pairs)
 
 
-def swap_faces(even, odd, left, right):
-    even, odd = swapped(even, "rad", 0), swapped(odd, "rad", 1)
-    at_left = shifted(right, "span", 1)
-    at_right = shifted(left, "span", -1)
-    return even, odd, at_left, at_right
+def swap_columns(left, right):
+    return shifted(right, "span", 1), shifted(left, "span", -1)
 
 
 def on_device(current, previous, moduli, density, traces, receivers, owners, offsets):
     wide = (3, CR, ROWS, CE)
     edge = (11, 2, 8, CE)
-    faces = [(3, ROWS, CE), (3, ROWS, CE), (8, CE), (8, CE)]
+    layer, columns = (3, ROWS, CE), [(8, CE), (8, CE)]
 
     fields = (current, previous, moduli, density.reshape((1,) + density.shape))
     rooms = [(11, CR, 8, CE), pltpu.SemaphoreType.DMA((4,))]
@@ -405,7 +438,7 @@
     from_high = shifted(low_rows, "lat", -1)
     got = lax.all_to_all(packed, ("lat", "rad"), 0, 0, tiled=True)
 
-    u, v, m, c, *ends = call(
+    u, v, m, c, even, odd, *ends = call(
         widen_kernel,
         [wide, wide, (4, CR, ROWS, CE), (CR, ROWS, CE)]
         + [(5, ROWS, CE), (5, ROWS, CE), (8, CE), (8, CE)],
@@ -414,12 +447,19 @@
     *coefficients, free = call(
         prepare_kernel,
         [(2, CR + 1, ROWS, CE), wide, wide, wide, wide],
-        (u, v, m, c, *swap_faces(*ends)),
+        (u, v, m, c, swapped(even, "rad", 0), swapped(odd, "rad", 1), *swap_columns(*ends)),
     )
     cells, lanes = CR * ROWS, 3 * SLOTS * 128
-    first, *ends = call(
+    (even,) = call(
+        first_lead_kernel,
+        [layer],
+        (got, free, c),
+        scratch=[(3 * ROWS, lanes), (CE, lanes)],
+    )
+    even = swapped(even, "rad", 0)
+    first, odd, *ends = call(
         first_kernel,
-        [wide] + faces,
+        [wide, layer] + columns,
         (got, free, c),
         scratch=[(3 * cells, lanes), (CE, lanes)],
     )
@@ -432,15 +472,25 @@
     )
     v, u = u, first
     for t in range(1, STEPS):
-        args = (u, v, c, sources, *swap_faces(*ends), *coefficients)
-
-        def kernel(*refs, t=t):
+        odd = swapped(odd, "rad", 1)
+        at_left, at_right = swap_columns(*ends)
+        before = (u, v, c, sources, even)
+        after = (at_left, at_right, *coefficients)
+        if t == STEPS - 1:
+            return tuple(call(last_kernel, [(3, CR, CL, CE)] * 2, before + (odd,) + after))
+        if t == STEPS - 2:
+            layer = (3, CL, CE)
+
+        def lead(*refs, t=t):
+            lead_kernel(t, *refs)
+
+        def step(*refs, t=t):
             step_kernel(t, *refs)
 
-        if t == STEPS - 1:
-            return tuple(call(kernel, [(3, CR, CL, CE)] * 2, args))
-        following, *ends = call(kernel, [wide] + faces, args)
-        v, u = u, following
+        (next_even,) = call(lead, [layer], before + after)
+        next_even = swapped(next_even, "rad", 0)
+        following, odd, *ends = call(step, [wide, layer] + columns, before + (odd,) + after)
+        v, u, even = u, following, next_even
 
 
 def solution(mesh):

time: 57.2 us -> 57.6 us (level)
  Pallas kernels: 9.27 us -> 9.94 us
    pallas_call x9 -> x12, Pallas kernels: 9.27 us -> 9.94 us  [call(): pl.pallas_call(kernel, out_shape=[jax.ShapeDtypeStruct(shape, F32) for sh...]
  transfers between devices with their start and end apart: 19 -> 19, of which waited for: 8 -> 8; matrix products, arithmetic and copies ran while one was open for 0% -> 0% of each run, Pallas kernels for 9% -> 12%
where the time goes in v6:
time: 57.6 us; the launch traced here: 57.4 us
  starting transfers between devices  34.9 us (61%)
  waiting for transfers between devices  11.8 us (20%)
  Pallas kernels  9.94 us (17%)
  between operations  0.79 us (1%)
    ppermute x10, starting transfers between devices, shifted(): lax.ppermute(block, axis, [(i, (i + by) % count) for i in range(count)])  12.6 us
    all_to_all x1, starting transfers between devices, on_device(): got = lax.all_to_all(packed, ('lat', 'rad'), 0, 0, tiled=True)  12.1 us
    ppermute x10, waiting for transfers between devices, shifted(): lax.ppermute(block, axis, [(i, (i + by) % count) for i in range(count)])  11.2 us
    ppermute x8, starting transfers between devices, swapped(): return lax.ppermute(block, axis, pairs)  10.2 us
    pallas_call x12, Pallas kernels, call(): pl.pallas_call(kernel, out_shape=[jax.ShapeDtypeStruct(shape, F32) for sh...  9.94 us
  transfers between devices with their start and end apart: 19, of which 8 were waited for; matrix products, arithmetic and copies ran while one was open for 0% of the time, Pallas kernels for 12%

profile of v6, /device:TPU:1, one launch (start us, length us, event | category | flops | bytes accessed | tf_op | source)
XLA Modules:
  0.0 57.4 jit_solution(14635707434830268351)
XLA Ops:
  0.6 1.6 %shard_map.96 = f32[11,2,8,128]{3,2,1,0:T(8,128)} custom-call(f32[3,4,16,128]{3,2,1,0:T(8,128)} %cur.5, f32[3,4,16,128]{3,2,1,0:T(8,128)} %prv.5, f32[4,4,16,128]{3,2,1,0:T(8,128)} %mod.5, f32[1,4,16,128]{3,2,1,0:T(8,128)} %bitcast.5), custom_call_target="tpu_custom_call" | custom-call | bytes 3000000 | tf_op jit(solution)/shard_map/pallas_call | solution.py:381
  2.2 3.8 %collective-permute-start = (f32[11,2,8,128]{3,2,1,0:T(8,128)}, f32[11,2,8,128]{3,2,1,0:T(8,128)S(1)}, u32[]{:S(2)}, u32[]{:S(2)}) collective-permute-start(f32[11,2,8,128]{3,2,1,0:T(8,128)} %shard_map.96), channel_id=1, source_target_pairs={{0,8},{8,16},{16,24},{24,32},{32,40},{40,48},{48,56},{56,0},{1,9},... | collective-permute-start | bytes 270344 | tf_op jit(solution)/shard_map/ppermute | solution.py:396
  6.1 2.8 %shard_map.95 = (f32[64,1,256]{2,1,0:T(1,128)}, f32[11,2,8,128]{3,2,1,0:T(8,128)}) custom-call(s32[1,128]{1,0:T(1,128)} %bitcast.8, s32[1,128]{1,0:T(1,128)} %bitcast.9, s32[1,128]{1,0:T(1,128)} %bitcast.10, f32[3,128,512]{2,1,0:T(8,128)} %bitcast.7, f32[3,4,16,128]{3,2,1,0:T(8,128)} %cur.5, f32[3,4,16,128]{3,2,1,0:T(8,128)} %prv.5, f32[4,4,16,128]{3,2,1,0:T(8,128)} %mod.5, ...), custom_call_target="tpu_custom_call" | custom-call | bytes 6000000 | tf_op jit(solution)/shard_map/pallas_call | solution.py:381
  8.9 2.3 %collective-permute-start.1 = (f32[11,2,8,128]{3,2,1,0:T(8,128)}, f32[11,2,8,128]{3,2,1,0:T(8,128)S(1)}, u32[]{:S(2)}, u32[]{:S(2)}) collective-permute-start(f32[11,2,8,128]{3,2,1,0:T(8,128)} %get-tuple-element.30), channel_id=1, source_target_pairs={{0,56},{8,0},{16,8},{24,16},{32,24},{40,32},{48,40},{56,48},{1,57}... | collective-permute-start | bytes 270344 | tf_op jit(solution)/shard_map/ppermute | solution.py:396
  11.2 12.1 %all-to-all-start = ((f32[64,1,256]{2,1,0:T(1,128)}), f32[64,1,256]{2,1,0:T(1,128)S(1)}, u32[]{:S(2)}, u32[]{:S(2)}) async-start(f32[64,1,256]{2,1,0:T(1,128)} %get-tuple-element.29), calls=%async_computation | async-start | bytes 131072 | tf_op jit(solution)/shard_map/all_to_all | solution.py:439
  23.7 1.1 %collective-permute-start.2 = (f32[5,24,128]{2,1,0:T(8,128)S(1)}, f32[5,24,128]{2,1,0:T(8,128)S(1)}, u32[]{:S(2)}, u32[]{:S(2)}) collective-permute-start(f32[5,24,128]{2,1,0:T(8,128)S(1)} %get-tuple-element.35), channel_id=1, source_target_pairs={{0,1},{1,0},{2,3},{3,2},{4,5},{5,4},{6,7},{7,6},{8,9},{9,8},{10,11... | collective-permute-start | bytes 184328 | tf_op jit(solution)/shard_map/ppermute | solution.py:402
  24.8 2.4 %collective-permute-start.3 = (f32[5,24,128]{2,1,0:T(8,128)S(1)}, f32[5,24,128]{2,1,0:T(8,128)S(1)}, u32[]{:S(2)}, u32[]{:S(2)}) collective-permute-start(f32[5,24,128]{2,1,0:T(8,128)S(1)} %get-tuple-element.36), channel_id=1, source_target_pairs={{0,7},{1,2},{2,1},{3,4},{4,3},{5,6},{6,5},{7,0},{8,15},{9,10},{10,... | collective-permute-start | bytes 184328 | tf_op jit(solution)/shard_map/ppermute | solution.py:402
  27.2 2.6 %collective-permute-start.4 = (f32[8,128]{1,0:T(8,128)S(1)}, f32[8,128]{1,0:T(8,128)S(1)}, u32[]{:S(2)}, u32[]{:S(2)}) collective-permute-start(f32[8,128]{1,0:T(8,128)S(1)} %get-tuple-element.37), channel_id=1, source_target_pairs={{0,64},{64,128},{128,192},{192,0},{1,65},{65,129},{129,193},{193,1... | collective-permute-start | bytes 12296 | tf_op jit(solution)/shard_map/ppermute | solution.py:396
  29.8 0.8 %collective-permute-done.4.at_left = f32[8,128]{1,0:T(8,128)S(1)} collective-permute-done((f32[8,128]{1,0:T(8,128)S(1)}, f32[8,128]{1,0:T(8,128)S(1)}, u32[]{:S(2)}, u32[]{:S(2)}) %collective-permute-start.4) | collective-permute-done | bytes 4128 | tf_op jit(solution)/shard_map/ppermute | solution.py:396
  30.5 2.6 %collective-permute-done.5.at_right = f32[8,128]{1,0:T(8,128)S(1)} collective-permute-done((f32[8,128]{1,0:T(8,128)S(1)}, f32[8,128]{1,0:T(8,128)S(1)}, u32[]{:S(2)}, u32[]{:S(2)}) %collective-permute-start.5) | collective-permute-done | bytes 4128 | tf_op jit(solution)/shard_map/ppermute | solution.py:396
  33.1 0.6 %shard_map.98 = (f32[2,5,24,128]{3,2,1,0:T(8,128)S(1)}, f32[3,4,24,128]{3,2,1,0:T(8,128)S(1)}, f32[3,4,24,128]{3,2,1,0:T(8,128)S(1)}, f32[3,4,24,128]{3,2,1,0:T(8,128)S(1)}, f32[3,4,24,128]{3,2,1,0:T(8,128)S(1)}) custom-call(f32[3,4,24,128]{3,2,1,0:T(8,128)S(1)} %get-tuple-element.31.u.refs_1_, f32[3,4,24,128]{3,2,1,0:T(8,128)S(1)} %get-tuple-element.32.v, ...), custom_call_target="tpu_custom_call" | custom-call | bytes 3000000 | tf_op jit(solution)/shard_map/pallas_call | solution.py:381
  35.3 0.7 %shard_map.99 = (f32[3,4,24,128]{3,2,1,0:T(8,128)S(1)}, f32[3,24,128]{2,1,0:T(8,128)S(1)}, f32[8,128]{1,0:T(8,128)S(1)}, f32[8,128]{1,0:T(8,128)S(1)}) custom-call(f32[64,1,256]{2,1,0:T(1,128)S(1)} %all-to-all-done.got, f32[3,4,24,128]{3,2,1,0:T(8,128)S(1)} %get-tuple-element.39.free, f32[4,24,128]{2,1,0:T(8,128)S(1)} %get-tuple-element.34.c.refs_2_), custom_call_target="tpu_custom_call" | custom-call | bytes 3000000 | tf_op jit(solution)/shard_map/pallas_call | solution.py:381
  36.0 1.5 %collective-permute-start.7 = (f32[3,24,128]{2,1,0:T(8,128)S(1)}, f32[3,24,128]{2,1,0:T(8,128)S(1)}, u32[]{:S(2)}, u32[]{:S(2)}) collective-permute-start(f32[3,24,128]{2,1,0:T(8,128)S(1)} %get-tuple-element.41), channel_id=1, source_target_pairs={{0,7},{1,2},{2,1},{3,4},{4,3},{5,6},{6,5},{7,0},{8,15},{9,10},{10,... | collective-permute-start | bytes 110600 | tf_op jit(solution)/shard_map/ppermute | solution.py:402
  37.5 2.7 %collective-permute-start.8 = (f32[8,128]{1,0:T(8,128)S(1)}, f32[8,128]{1,0:T(8,128)S(1)}, u32[]{:S(2)}, u32[]{:S(2)}) collective-permute-start(f32[8,128]{1,0:T(8,128)S(1)} %get-tuple-element.42), channel_id=1, source_target_pairs={{0,64},{64,128},{128,192},{192,0},{1,65},{65,129},{129,193},{193,1... | collective-permute-start | bytes 12296 | tf_op jit(solution)/shard_map/ppermute | solution.py:396
  40.2 1.3 %shard_map.100.refs_3_.sources = f32[3,3,4,24,128]{4,3,2,1,0:T(8,128)S(1)} custom-call(f32[64,1,256]{2,1,0:T(1,128)S(1)} %all-to-all-done.got, f32[4,24,128]{2,1,0:T(8,128)S(1)} %get-tuple-element.34.c.refs_2_), custom_call_target="tpu_custom_call" | custom-call | bytes 9000000 | tf_op jit(solution)/shard_map/pallas_call | solution.py:381
  41.6 2.0 %collective-permute-done.9.refs_7_.refs_6_ = f32[8,128]{1,0:T(8,128)S(1)} collective-permute-done((f32[8,128]{1,0:T(8,128)S(1)}, f32[8,128]{1,0:T(8,128)S(1)}, u32[]{:S(2)}, u32[]{:S(2)}) %collective-permute-start.9) | collective-permute-done | bytes 4128 | tf_op jit(solution)/shard_map/ppermute | solution.py:396
  44.6 2.1 %collective-permute-start.11 = (f32[3,24,128]{2,1,0:T(8,128)S(1)}, f32[3,24,128]{2,1,0:T(8,128)S(1)}, u32[]{:S(2)}, u32[]{:S(2)}) collective-permute-start(f32[3,24,128]{2,1,0:T(8,128)S(1)} %get-tuple-element.49), channel_id=1, source_target_pairs={{0,7},{1,2},{2,1},{3,4},{4,3},{5,6},{6,5},{7,0},{8,15},{9,10},{10,... | collective-permute-start | bytes 110600 | tf_op jit(solution)/shard_map/ppermute | solution.py:402
  47.1 0.7 %collective-permute-done.12.refs_6_.refs_5_ = f32[8,128]{1,0:T(8,128)S(1)} collective-permute-done((f32[8,128]{1,0:T(8,128)S(1)}, f32[8,128]{1,0:T(8,128)S(1)}, u32[]{:S(2)}, u32[]{:S(2)}) %collective-permute-start.12) | collective-permute-done | bytes 4128 | tf_op jit(solution)/shard_map/ppermute | solution.py:396
  47.8 2.2 %collective-permute-done.13.refs_7_.refs_6_ = f32[8,128]{1,0:T(8,128)S(1)} collective-permute-done((f32[8,128]{1,0:T(8,128)S(1)}, f32[8,128]{1,0:T(8,128)S(1)}, u32[]{:S(2)}, u32[]{:S(2)}) %collective-permute-start.13) | collective-permute-done | bytes 4128 | tf_op jit(solution)/shard_map/ppermute | solution.py:396
  50.7 2.1 %collective-permute-start.15 = (f32[3,16,128]{2,1,0:T(8,128)S(1)}, f32[3,16,128]{2,1,0:T(8,128)S(1)}, u32[]{:S(2)}, u32[]{:S(2)}) collective-permute-start(f32[3,16,128]{2,1,0:T(8,128)S(1)} %get-tuple-element.53), channel_id=1, source_target_pairs={{0,7},{1,2},{2,1},{3,4},{4,3},{5,6},{6,5},{7,0},{8,15},{9,10},{10,... | collective-permute-start | bytes 73736 | tf_op jit(solution)/shard_map/ppermute | solution.py:402
  52.9 0.6 %collective-permute-start.16 = (f32[8,128]{1,0:T(8,128)S(1)}, f32[8,128]{1,0:T(8,128)S(1)}, u32[]{:S(2)}, u32[]{:S(2)}) collective-permute-start(f32[8,128]{1,0:T(8,128)S(1)} %get-tuple-element.54), channel_id=1, source_target_pairs={{0,64},{64,128},{128,192},{192,0},{1,65},{65,129},{129,193},{193,1... | collective-permute-start | bytes 12296 | tf_op jit(solution)/shard_map/ppermute | solution.py:396
  53.5 0.8 %collective-permute-done.16.at_left = f32[8,128]{1,0:T(8,128)S(1)} collective-permute-done((f32[8,128]{1,0:T(8,128)S(1)}, f32[8,128]{1,0:T(8,128)S(1)}, u32[]{:S(2)}, u32[]{:S(2)}) %collective-permute-start.16) | collective-permute-done | bytes 4128 | tf_op jit(solution)/shard_map/ppermute | solution.py:396
  54.2 2.3 %collective-permute-done.17.at_right = f32[8,128]{1,0:T(8,128)S(1)} collective-permute-done((f32[8,128]{1,0:T(8,128)S(1)}, f32[8,128]{1,0:T(8,128)S(1)}, u32[]{:S(2)}, u32[]{:S(2)}) %collective-permute-start.17) | collective-permute-done | bytes 4128 | tf_op jit(solution)/shard_map/ppermute | solution.py:396
  56.5 0.9 %shard_map.106 = (f32[3,4,16,128]{3,2,1,0:T(8,128)}, f32[3,4,16,128]{3,2,1,0:T(8,128)}) custom-call(f32[3,4,24,128]{3,2,1,0:T(8,128)S(1)} %get-tuple-element.52.u, f32[3,4,24,128]{3,2,1,0:T(8,128)S(1)} %get-tuple-element.48.refs_0_.v, f32[4,24,128]{2,1,0:T(8,128)S(1)} %get-tuple-element.34.c.refs_2_, f32[3,3,4,24,128]{4,3,2,1,0:T(8,128)S(1)} %shard_map.100.refs_3_.sources, ...), custom_call_target="tpu_custom_call" | custom-call | bytes 3000000 | tf_op jit(solution)/shard_map/pallas_call | solution.py:381
  (34 shorter events, 4.1 us)
Async XLA Ops:
  2.2 21.1 %collective-permute-start = (f32[11,2,8,128]{3,2,1,0:T(8,128)}, f32[11,2,8,128]{3,2,1,0:T(8,128)S(1)}, u32[]{:S(2)}, u32[]{:S(2)}) collective-permute-start(f32[11,2,8,128]{3,2,1,0:T(8,128)} %shard_map.96), channel_id=1, source_target_pairs={{0,8},{8,16},{16,24},{24,32},{32,40},{40,48},{48,56},{56,0},{1,9},... | collective-permute-start | bytes 270344 | tf_op jit(solution)/shard_map/ppermute | solution.py:396
  6.0 17.3 %copy-start.1 = (f32[3,4,16,128]{3,2,1,0:T(8,128)S(1)}, f32[3,4,16,128]{3,2,1,0:T(8,128)}, u32[]{:S(2)}) copy-start(f32[3,4,16,128]{3,2,1,0:T(8,128)} %cur.5) | copy-start | bytes 294916
  6.0 17.3 %copy-start.2 = (f32[3,4,16,128]{3,2,1,0:T(8,128)S(1)}, f32[3,4,16,128]{3,2,1,0:T(8,128)}, u32[]{:S(2)}) copy-start(f32[3,4,16,128]{3,2,1,0:T(8,128)} %prv.5) | copy-start | bytes 294916
  6.1 17.3 %copy-start.3 = (f32[4,16,128]{2,1,0:T(8,128)S(1)}, f32[4,16,128]{2,1,0:T(8,128)}, u32[]{:S(2)}) copy-start(f32[4,16,128]{2,1,0:T(8,128)} %den.1) | copy-start | bytes 98308
  8.9 14.5 %copy-start = (f32[4,4,16,128]{3,2,1,0:T(8,128)S(1)}, f32[4,4,16,128]{3,2,1,0:T(8,128)}, u32[]{:S(2)}) copy-start(f32[4,4,16,128]{3,2,1,0:T(8,128)} %mod.5) | copy-start | bytes 393220
  8.9 14.4 %collective-permute-start.1 = (f32[11,2,8,128]{3,2,1,0:T(8,128)}, f32[11,2,8,128]{3,2,1,0:T(8,128)S(1)}, u32[]{:S(2)}, u32[]{:S(2)}) collective-permute-start(f32[11,2,8,128]{3,2,1,0:T(8,128)} %get-tuple-element.30), channel_id=1, source_target_pairs={{0,56},{8,0},{16,8},{24,16},{32,24},{40,32},{48,40},{56,48},{1,57}... | collective-permute-start | bytes 270344 | tf_op jit(solution)/shard_map/ppermute | solution.py:396
  11.2 23.1 %all-to-all-start = ((f32[64,1,256]{2,1,0:T(1,128)}), f32[64,1,256]{2,1,0:T(1,128)S(1)}, u32[]{:S(2)}, u32[]{:S(2)}) async-start(f32[64,1,256]{2,1,0:T(1,128)} %get-tuple-element.29), calls=%async_computation | async-start | bytes 131072 | tf_op jit(solution)/shard_map/all_to_all | solution.py:439
  23.7 9.5 %collective-permute-start.2 = (f32[5,24,128]{2,1,0:T(8,128)S(1)}, f32[5,24,128]{2,1,0:T(8,128)S(1)}, u32[]{:S(2)}, u32[]{:S(2)}) collective-permute-start(f32[5,24,128]{2,1,0:T(8,128)S(1)} %get-tuple-element.35), channel_id=1, source_target_pairs={{0,1},{1,0},{2,3},{3,2},{4,5},{5,4},{6,7},{7,6},{8,9},{9,8},{10,11... | collective-permute-start | bytes 184328 | tf_op jit(solution)/shard_map/ppermute | solution.py:402
  24.8 8.4 %collective-permute-start.3 = (f32[5,24,128]{2,1,0:T(8,128)S(1)}, f32[5,24,128]{2,1,0:T(8,128)S(1)}, u32[]{:S(2)}, u32[]{:S(2)}) collective-permute-start(f32[5,24,128]{2,1,0:T(8,128)S(1)} %get-tuple-element.36), channel_id=1, source_target_pairs={{0,7},{1,2},{2,1},{3,4},{4,3},{5,6},{6,5},{7,0},{8,15},{9,10},{10,... | collective-permute-start | bytes 184328 | tf_op jit(solution)/shard_map/ppermute | solution.py:402
  27.2 3.4 %collective-permute-start.4 = (f32[8,128]{1,0:T(8,128)S(1)}, f32[8,128]{1,0:T(8,128)S(1)}, u32[]{:S(2)}, u32[]{:S(2)}) collective-permute-start(f32[8,128]{1,0:T(8,128)S(1)} %get-tuple-element.37), channel_id=1, source_target_pairs={{0,64},{64,128},{128,192},{192,0},{1,65},{65,129},{129,193},{193,1... | collective-permute-start | bytes 12296 | tf_op jit(solution)/shard_map/ppermute | solution.py:396
  29.8 3.3 %collective-permute-start.5 = (f32[8,128]{1,0:T(8,128)S(1)}, f32[8,128]{1,0:T(8,128)S(1)}, u32[]{:S(2)}, u32[]{:S(2)}) collective-permute-start(f32[8,128]{1,0:T(8,128)S(1)} %get-tuple-element.38), channel_id=1, source_target_pairs={{0,192},{64,0},{128,64},{192,128},{1,193},{65,1},{129,65},{193,129... | collective-permute-start | bytes 12296 | tf_op jit(solution)/shard_map/ppermute | solution.py:396
  34.7 8.8 %collective-permute-start.6 = (f32[3,24,128]{2,1,0:T(8,128)S(1)}, f32[3,24,128]{2,1,0:T(8,128)S(1)}, u32[]{:S(2)}, u32[]{:S(2)}) collective-permute-start(f32[3,24,128]{2,1,0:T(8,128)S(1)} %shard_map.101), channel_id=1, source_target_pairs={{0,1},{1,0},{2,3},{3,2},{4,5},{5,4},{6,7},{7,6},{8,9},{9,8},{10,11... | collective-permute-start | bytes 110600 | tf_op jit(solution)/shard_map/ppermute | solution.py:402
  36.0 8.1 %collective-permute-start.7 = (f32[3,24,128]{2,1,0:T(8,128)S(1)}, f32[3,24,128]{2,1,0:T(8,128)S(1)}, u32[]{:S(2)}, u32[]{:S(2)}) collective-permute-start(f32[3,24,128]{2,1,0:T(8,128)S(1)} %get-tuple-element.41), channel_id=1, source_target_pairs={{0,7},{1,2},{2,1},{3,4},{4,3},{5,6},{6,5},{7,0},{8,15},{9,10},{10,... | collective-permute-start | bytes 110600 | tf_op jit(solution)/shard_map/ppermute | solution.py:402
  37.5 4.1 %collective-permute-start.8 = (f32[8,128]{1,0:T(8,128)S(1)}, f32[8,128]{1,0:T(8,128)S(1)}, u32[]{:S(2)}, u32[]{:S(2)}) collective-permute-start(f32[8,128]{1,0:T(8,128)S(1)} %get-tuple-element.42), channel_id=1, source_target_pairs={{0,64},{64,128},{128,192},{192,0},{1,65},{65,129},{129,193},{193,1... | collective-permute-start | bytes 12296 | tf_op jit(solution)/shard_map/ppermute | solution.py:396
  40.2 3.3 %collective-permute-start.9 = (f32[8,128]{1,0:T(8,128)S(1)}, f32[8,128]{1,0:T(8,128)S(1)}, u32[]{:S(2)}, u32[]{:S(2)}) collective-permute-start(f32[8,128]{1,0:T(8,128)S(1)} %get-tuple-element.43), channel_id=1, source_target_pairs={{0,192},{64,0},{128,64},{192,128},{1,193},{65,1},{129,65},{193,129... | collective-permute-start | bytes 12296 | tf_op jit(solution)/shard_map/ppermute | solution.py:396
  43.7 6.3 %collective-permute-start.10 = (f32[3,24,128]{2,1,0:T(8,128)S(1)}, f32[3,24,128]{2,1,0:T(8,128)S(1)}, u32[]{:S(2)}, u32[]{:S(2)}) collective-permute-start(f32[3,24,128]{2,1,0:T(8,128)S(1)} %shard_map.103), channel_id=1, source_target_pairs={{0,1},{1,0},{2,3},{3,2},{4,5},{5,4},{6,7},{7,6},{8,9},{9,8},{10,11... | collective-permute-start | bytes 110600 | tf_op jit(solution)/shard_map/ppermute | solution.py:402
  44.6 5.7 %collective-permute-start.11 = (f32[3,24,128]{2,1,0:T(8,128)S(1)}, f32[3,24,128]{2,1,0:T(8,128)S(1)}, u32[]{:S(2)}, u32[]{:S(2)}) collective-permute-start(f32[3,24,128]{2,1,0:T(8,128)S(1)} %get-tuple-element.49), channel_id=1, source_target_pairs={{0,7},{1,2},{2,1},{3,4},{4,3},{5,6},{6,5},{7,0},{8,15},{9,10},{10,... | collective-permute-start | bytes 110600 | tf_op jit(solution)/shard_map/ppermute | solution.py:402
  46.6 1.2 %collective-permute-start.12 = (f32[8,128]{1,0:T(8,128)S(1)}, f32[8,128]{1,0:T(8,128)S(1)}, u32[]{:S(2)}, u32[]{:S(2)}) collective-permute-start(f32[8,128]{1,0:T(8,128)S(1)} %get-tuple-element.50), channel_id=1, source_target_pairs={{0,64},{64,128},{128,192},{192,0},{1,65},{65,129},{129,193},{193,1... | collective-permute-start | bytes 12296 | tf_op jit(solution)/shard_map/ppermute | solution.py:396
  47.0 3.0 %collective-permute-start.13 = (f32[8,128]{1,0:T(8,128)S(1)}, f32[8,128]{1,0:T(8,128)S(1)}, u32[]{:S(2)}, u32[]{:S(2)}) collective-permute-start(f32[8,128]{1,0:T(8,128)S(1)} %get-tuple-element.51), channel_id=1, source_target_pairs={{0,192},{64,0},{128,64},{192,128},{1,193},{65,1},{129,65},{193,129... | collective-permute-start | bytes 12296 | tf_op jit(solution)/shard_map/ppermute | solution.py:396
  50.1 6.4 %collective-permute-start.14 = (f32[3,16,128]{2,1,0:T(8,128)S(1)}, f32[3,16,128]{2,1,0:T(8,128)S(1)}, u32[]{:S(2)}, u32[]{:S(2)}) collective-permute-start(f32[3,16,128]{2,1,0:T(8,128)S(1)} %shard_map.105), channel_id=1, source_target_pairs={{0,1},{1,0},{2,3},{3,2},{4,5},{5,4},{6,7},{7,6},{8,9},{9,8},{10,11... | collective-permute-start | bytes 73736 | tf_op jit(solution)/shard_map/ppermute | solution.py:402
  50.7 5.8 %collective-permute-start.15 = (f32[3,16,128]{2,1,0:T(8,128)S(1)}, f32[3,16,128]{2,1,0:T(8,128)S(1)}, u32[]{:S(2)}, u32[]{:S(2)}) collective-permute-start(f32[3,16,128]{2,1,0:T(8,128)S(1)} %get-tuple-element.53), channel_id=1, source_target_pairs={{0,7},{1,2},{2,1},{3,4},{4,3},{5,6},{6,5},{7,0},{8,15},{9,10},{10,... | collective-permute-start | bytes 73736 | tf_op jit(solution)/shard_map/ppermute | solution.py:402
  52.9 1.4 %collective-permute-start.16 = (f32[8,128]{1,0:T(8,128)S(1)}, f32[8,128]{1,0:T(8,128)S(1)}, u32[]{:S(2)}, u32[]{:S(2)}) collective-permute-start(f32[8,128]{1,0:T(8,128)S(1)} %get-tuple-element.54), channel_id=1, source_target_pairs={{0,64},{64,128},{128,192},{192,0},{1,65},{65,129},{129,193},{193,1... | collective-permute-start | bytes 12296 | tf_op jit(solution)/shard_map/ppermute | solution.py:396
  53.5 3.0 %collective-permute-start.17 = (f32[8,128]{1,0:T(8,128)S(1)}, f32[8,128]{1,0:T(8,128)S(1)}, u32[]{:S(2)}, u32[]{:S(2)}) collective-permute-start(f32[8,128]{1,0:T(8,128)S(1)} %get-tuple-element.55), channel_id=1, source_target_pairs={{0,192},{64,0},{128,64},{192,128},{1,193},{65,1},{129,65},{193,129... | collective-permute-start | bytes 12296 | tf_op jit(solution)/shard_map/ppermute | solution.py:396

commit v7 on v6

--- a/solution.py
+++ b/solution.py
@@ -65,15 +65,22 @@
 
 
 def end_layers():
-    top = jnp.where(rad_is_even(), CR - 1, 0)
-    return top, CR - 1 - top
-
-
-def put_rest(u_ref, odd_ref, left_ref, right_ref):
-    _, bottom = end_layers()
-    rows = odd_ref.shape[1]
-    for k in range(3):
-        odd_ref[k] = u_ref[k, bottom, :rows, :]
+    lead = jnp.where(rad_is_even(), 0, CR - 1)
+    return lead, CR - 1 - lead
+
+
+def keep_lead(u_ref, made):
+    lead, _ = end_layers()
+    rows = made.shape[1]
+    for k in range(3):
+        u_ref[k, lead, :rows, :] = made[k]
+
+
+def put_rest(u_ref, even_ref, left_ref, right_ref):
+    _, rest = end_layers()
+    rows = even_ref.shape[1]
+    for k in range(3):
+        even_ref[k] = u_ref[k, rest, :rows, :]
     left_ref[...] = jnp.zeros_like(left_ref)
     right_ref[...] = jnp.zeros_like(right_ref)
     put_columns(tiles_of(u_ref, 3), left_ref, right_ref, 0)
@@ -217,10 +224,10 @@
         )
         present = jnp.where(iota((8, 128), 0) < HALO, has_high.astype(I32), has_low.astype(I32))
         c[r, CL:ROWS, :] = jnp.where(present > 0, outer, 0.0)
-    top, bottom = end_layers()
+    lead, rest = end_layers()
     for i, (field, k) in enumerate(((u, 0), (u, 1), (u, 2), (m, 0), (m, 2))):
-        even[i] = field[k, top]
-        odd[i] = field[k, bottom]
+        even[i] = field[k, rest]
+        odd[i] = field[k, lead]
     left[...] = jnp.zeros_like(left)
     right[...] = jnp.zeros_like(right)
     put_columns(tiles_of(u, 3), left, right, 0)
@@ -311,20 +318,21 @@
     )
 
 
-def first_lead_kernel(got, free, c, even, weights, picks):
-    top, _ = end_layers()
-    summed = gather_sources((0,), got, weights, picks, top, 1)
-    for k in range(3):
-        even[k] = free[k, top] + summed[k * ROWS : (k + 1) * ROWS] * c[top]
-
-
-def first_kernel(got, free, c, first, odd, left, right, weights, picks):
+def first_lead_kernel(got, free, c, odd, weights, picks):
+    lead, _ = end_layers()
+    summed = gather_sources((0,), got, weights, picks, lead, 1)
+    for k in range(3):
+        odd[k] = free[k, lead] + summed[k * ROWS : (k + 1) * ROWS] * c[lead]
+
+
+def first_kernel(got, free, c, made, first, even, left, right, weights, picks):
     summed = gather_sources((0,), got, weights, picks)
     for k in range(3):
         for r in range(CR):
             at = (k * CR + r) * ROWS
             first[k, r] = free[k, r] + summed[at : at + ROWS] * c[r]
-    put_rest(first, odd, left, right)
+    keep_lead(first, made)
+    put_rest(first, even, left, right)
 
 
 def sources_kernel(got, c, sources, weights, picks):
@@ -336,27 +344,30 @@
                 sources[t, k, r] = summed[at : at + ROWS] * c[r]
 
 
-def lead_kernel(t, u, v, c, sources, even, at_left, at_right, ar, al, au, ad, out):
-    top, _ = end_layers()
-    upwards = rad_is_even()
-    inner = jnp.where(upwards, CR - 2, 1)
-    outer_face, inner_face = jnp.where(upwards, CR, 0), jnp.where(upwards, CR - 1, 1)
-    for k in range(3):
-        i, here = TABLE[k][0] // 2, u[k, top]
-        total = ar[i, outer_face] * (even[k] - here) + ar[i, inner_face] * (u[k, inner] - here)
-        total = total + level(k, top, here, at_left, at_right, al, au, ad)
-        value = 2.0 * here - v[k, top] + c[top] * total + sources[t - 1, k, top]
+def lead_kernel(t, u, v, c, sources, odd, at_left, at_right, ar, al, au, ad, out):
+    lead, _ = end_layers()
+    rad, downwards = lax.axis_index("rad"), rad_is_even()
+    joined = jnp.where(downwards, rad > 0, rad < lax.axis_size("rad") - 1)
+    inner = jnp.where(downwards, 1, CR - 2)
+    outer_face, inner_face = jnp.where(downwards, 0, CR), jnp.where(downwards, 1, CR - 1)
+    for k in range(3):
+        i, here = TABLE[k][0] // 2, u[k, lead]
+        outer = jnp.where(joined, odd[k], 0.0)
+        total = ar[i, outer_face] * (outer - here) + ar[i, inner_face] * (u[k, inner] - here)
+        total = total + level(k, lead, here, at_left, at_right, al, au, ad)
+        value = 2.0 * here - v[k, lead] + c[lead] * total + sources[t - 1, k, lead]
         out[k] = value[: out.shape[1]]
 
 
 def step_kernel(
-    t, u, v, c, sources, even, odd, at_left, at_right, ar, al, au, ad, following, *rest
+    t, u, v, c, sources, even, odd, at_left, at_right, ar, al, au, ad, made, following, *rest
 ):
     lows, highs = radial_ends(even, odd, 3)
     for k in range(3):
         for r in range(CR):
             total = force(k, r, u, lows, highs, at_left, at_right, ar, al, au, ad)
             following[k, r] = 2.0 * u[k, r] - v[k, r] + c[r] * total + sources[t - 1, k, r]
+    keep_lead(following, made)
     put_rest(following, *rest)
 
 
@@ -450,17 +461,17 @@
         (u, v, m, c, swapped(even, "rad", 0), swapped(odd, "rad", 1), *swap_columns(*ends)),
     )
     cells, lanes = CR * ROWS, 3 * SLOTS * 128
-    (even,) = call(
+    (made,) = call(
         first_lead_kernel,
         [layer],
         (got, free, c),
         scratch=[(3 * ROWS, lanes), (CE, lanes)],
     )
-    even = swapped(even, "rad", 0)
-    first, odd, *ends = call(
+    odd = swapped(made, "rad", 1)
+    first, even, *ends = call(
         first_kernel,
         [wide, layer] + columns,
-        (got, free, c),
+        (got, free, c, made),
         scratch=[(3 * cells, lanes), (CE, lanes)],
     )
     (sources,) = call(
@@ -472,12 +483,12 @@
     )
     v, u = u, first
     for t in range(1, STEPS):
-        odd = swapped(odd, "rad", 1)
+        even = swapped(even, "rad", 0)
         at_left, at_right = swap_columns(*ends)
-        before = (u, v, c, sources, even)
+        before = (u, v, c, sources)
         after = (at_left, at_right, *coefficients)
         if t == STEPS - 1:
-            return tuple(call(last_kernel, [(3, CR, CL, CE)] * 2, before + (odd,) + after))
+            return tuple(call(last_kernel, [(3, CR, CL, CE)] * 2, before + (even, odd) + after))
         if t == STEPS - 2:
             layer = (3, CL, CE)
 
@@ -487,10 +498,12 @@
         def step(*refs, t=t):
             step_kernel(t, *refs)
 
-        (next_even,) = call(lead, [layer], before + after)
-        next_even = swapped(next_even, "rad", 0)
-        following, odd, *ends = call(step, [wide, layer] + columns, before + (odd,) + after)
-        v, u, even = u, following, next_even
+        (made,) = call(lead, [layer], before + (odd,) + after)
+        next_odd = swapped(made, "rad", 1)
+        following, even, *ends = call(
+            step, [wide, layer] + columns, before + (even, odd) + after + (made,)
+        )
+        v, u, odd = u, following, next_odd
 
 
 def solution(mesh):

time: 57.6 us -> 57.6 us (level)
    ppermute x10, starting transfers between devices: 12.6 us -> 13.5 us  [shifted(): lax.ppermute(block, axis, [(i, (i + by) % count) for i in range(count)])]
    ppermute x8, starting transfers between devices: 10.2 us -> 9.48 us  [swapped(): return lax.ppermute(block, axis, pairs)]
  transfers between devices with their start and end apart: 19 -> 19, of which waited for: 8 -> 8; matrix products, arithmetic and copies ran while one was open for 0% -> 0% of each run, Pallas kernels for 12% -> 11%
where the time goes in v7:
time: 57.6 us; the launch traced here: 57.4 us
  starting transfers between devices  35.1 us (61%)
  waiting for transfers between devices  11.5 us (20%)
  Pallas kernels  10 us (17%)
  between operations  0.8 us (1%)
    ppermute x10, starting transfers between devices, shifted(): lax.ppermute(block, axis, [(i, (i + by) % count) for i in range(count)])  13.5 us
    all_to_all x1, starting transfers between devices, on_device(): got = lax.all_to_all(packed, ('lat', 'rad'), 0, 0, tiled=True)  12.1 us
    ppermute x10, waiting for transfers between devices, shifted(): lax.ppermute(block, axis, [(i, (i + by) % count) for i in range(count)])  10.9 us
    pallas_call x12, Pallas kernels, call(): pl.pallas_call(kernel, out_shape=[jax.ShapeDtypeStruct(shape, F32) for sh...  10 us
    ppermute x8, starting transfers between devices, swapped(): return lax.ppermute(block, axis, pairs)  9.48 us
  transfers between devices with their start and end apart: 19, of which 8 were waited for; matrix products, arithmetic and copies ran while one was open for 0% of the time, Pallas kernels for 11%

profile of v7, /device:TPU:1, one launch (start us, length us, event | category | flops | bytes accessed | tf_op | source)
XLA Modules:
  0.0 57.4 jit_solution(12055244029542289308)
XLA Ops:
  0.6 1.6 %shard_map.96 = f32[11,2,8,128]{3,2,1,0:T(8,128)} custom-call(f32[3,4,16,128]{3,2,1,0:T(8,128)} %cur.5, f32[3,4,16,128]{3,2,1,0:T(8,128)} %prv.5, f32[4,4,16,128]{3,2,1,0:T(8,128)} %mod.5, f32[1,4,16,128]{3,2,1,0:T(8,128)} %bitcast.5), custom_call_target="tpu_custom_call" | custom-call | bytes 3000000 | tf_op jit(solution)/shard_map/pallas_call | solution.py:392
  2.2 3.8 %collective-permute-start = (f32[11,2,8,128]{3,2,1,0:T(8,128)}, f32[11,2,8,128]{3,2,1,0:T(8,128)S(1)}, u32[]{:S(2)}, u32[]{:S(2)}) collective-permute-start(f32[11,2,8,128]{3,2,1,0:T(8,128)} %shard_map.96), channel_id=1, source_target_pairs={{0,8},{8,16},{16,24},{24,32},{32,40},{40,48},{48,56},{56,0},{1,9},... | collective-permute-start | bytes 270344 | tf_op jit(solution)/shard_map/ppermute | solution.py:407
  6.1 2.8 %shard_map.95 = (f32[64,1,256]{2,1,0:T(1,128)}, f32[11,2,8,128]{3,2,1,0:T(8,128)}) custom-call(s32[1,128]{1,0:T(1,128)} %bitcast.8, s32[1,128]{1,0:T(1,128)} %bitcast.9, s32[1,128]{1,0:T(1,128)} %bitcast.10, f32[3,128,512]{2,1,0:T(8,128)} %bitcast.7, f32[3,4,16,128]{3,2,1,0:T(8,128)} %cur.5, f32[3,4,16,128]{3,2,1,0:T(8,128)} %prv.5, f32[4,4,16,128]{3,2,1,0:T(8,128)} %mod.5, ...), custom_call_target="tpu_custom_call" | custom-call | bytes 6000000 | tf_op jit(solution)/shard_map/pallas_call | solution.py:392
  8.9 2.3 %collective-permute-start.1 = (f32[11,2,8,128]{3,2,1,0:T(8,128)}, f32[11,2,8,128]{3,2,1,0:T(8,128)S(1)}, u32[]{:S(2)}, u32[]{:S(2)}) collective-permute-start(f32[11,2,8,128]{3,2,1,0:T(8,128)} %get-tuple-element.30), channel_id=1, source_target_pairs={{0,56},{8,0},{16,8},{24,16},{32,24},{40,32},{48,40},{56,48},{1,57}... | collective-permute-start | bytes 270344 | tf_op jit(solution)/shard_map/ppermute | solution.py:407
  11.2 12.1 %all-to-all-start = ((f32[64,1,256]{2,1,0:T(1,128)}), f32[64,1,256]{2,1,0:T(1,128)S(1)}, u32[]{:S(2)}, u32[]{:S(2)}) async-start(f32[64,1,256]{2,1,0:T(1,128)} %get-tuple-element.29), calls=%async_computation | async-start | bytes 131072 | tf_op jit(solution)/shard_map/all_to_all | solution.py:450
  23.7 1.1 %collective-permute-start.2 = (f32[5,24,128]{2,1,0:T(8,128)S(1)}, f32[5,24,128]{2,1,0:T(8,128)S(1)}, u32[]{:S(2)}, u32[]{:S(2)}) collective-permute-start(f32[5,24,128]{2,1,0:T(8,128)S(1)} %get-tuple-element.35), channel_id=1, source_target_pairs={{0,1},{1,0},{2,3},{3,2},{4,5},{5,4},{6,7},{7,6},{8,9},{9,8},{10,11... | collective-permute-start | bytes 184328 | tf_op jit(solution)/shard_map/ppermute | solution.py:413
  24.8 2.4 %collective-permute-start.3 = (f32[5,24,128]{2,1,0:T(8,128)S(1)}, f32[5,24,128]{2,1,0:T(8,128)S(1)}, u32[]{:S(2)}, u32[]{:S(2)}) collective-permute-start(f32[5,24,128]{2,1,0:T(8,128)S(1)} %get-tuple-element.36), channel_id=1, source_target_pairs={{0,7},{1,2},{2,1},{3,4},{4,3},{5,6},{6,5},{7,0},{8,15},{9,10},{10,... | collective-permute-start | bytes 184328 | tf_op jit(solution)/shard_map/ppermute | solution.py:413
  27.2 2.6 %collective-permute-start.4 = (f32[8,128]{1,0:T(8,128)S(1)}, f32[8,128]{1,0:T(8,128)S(1)}, u32[]{:S(2)}, u32[]{:S(2)}) collective-permute-start(f32[8,128]{1,0:T(8,128)S(1)} %get-tuple-element.37), channel_id=1, source_target_pairs={{0,64},{64,128},{128,192},{192,0},{1,65},{65,129},{129,193},{193,1... | collective-permute-start | bytes 12296 | tf_op jit(solution)/shard_map/ppermute | solution.py:407
  29.8 0.8 %collective-permute-done.4.at_left = f32[8,128]{1,0:T(8,128)S(1)} collective-permute-done((f32[8,128]{1,0:T(8,128)S(1)}, f32[8,128]{1,0:T(8,128)S(1)}, u32[]{:S(2)}, u32[]{:S(2)}) %collective-permute-start.4) | collective-permute-done | bytes 4128 | tf_op jit(solution)/shard_map/ppermute | solution.py:407
  30.5 2.6 %collective-permute-done.5.at_right = f32[8,128]{1,0:T(8,128)S(1)} collective-permute-done((f32[8,128]{1,0:T(8,128)S(1)}, f32[8,128]{1,0:T(8,128)S(1)}, u32[]{:S(2)}, u32[]{:S(2)}) %collective-permute-start.5) | collective-permute-done | bytes 4128 | tf_op jit(solution)/shard_map/ppermute | solution.py:407
  33.1 0.6 %shard_map.98 = (f32[2,5,24,128]{3,2,1,0:T(8,128)S(1)}, f32[3,4,24,128]{3,2,1,0:T(8,128)S(1)}, f32[3,4,24,128]{3,2,1,0:T(8,128)S(1)}, f32[3,4,24,128]{3,2,1,0:T(8,128)S(1)}, f32[3,4,24,128]{3,2,1,0:T(8,128)S(1)}) custom-call(f32[3,4,24,128]{3,2,1,0:T(8,128)S(1)} %get-tuple-element.31.u.refs_1_, f32[3,4,24,128]{3,2,1,0:T(8,128)S(1)} %get-tuple-element.32.v, ...), custom_call_target="tpu_custom_call" | custom-call | bytes 3000000 | tf_op jit(solution)/shard_map/pallas_call | solution.py:392
  34.7 0.8 %collective-permute-start.7 = (f32[3,24,128]{2,1,0:T(8,128)S(1)}, f32[3,24,128]{2,1,0:T(8,128)S(1)}, u32[]{:S(2)}, u32[]{:S(2)}) collective-permute-start(f32[3,24,128]{2,1,0:T(8,128)S(1)} %shard_map.99.made), channel_id=1, source_target_pairs={{0,7},{1,2},{2,1},{3,4},{4,3},{5,6},{6,5},{7,0},{8,15},{9,10},{10,... | collective-permute-start | bytes 110600 | tf_op jit(solution)/shard_map/ppermute | solution.py:413
  35.5 0.7 %shard_map.100 = (f32[3,4,24,128]{3,2,1,0:T(8,128)S(1)}, f32[3,24,128]{2,1,0:T(8,128)S(1)}, f32[8,128]{1,0:T(8,128)S(1)}, f32[8,128]{1,0:T(8,128)S(1)}) custom-call(f32[64,1,256]{2,1,0:T(1,128)S(1)} %all-to-all-done.got, f32[3,4,24,128]{3,2,1,0:T(8,128)S(1)} %get-tuple-element.39.free, f32[4,24,128]{2,1,0:T(8,128)S(1)} %get-tuple-element.34.c.refs_2_, ...), custom_call_target="tpu_custom_call" | custom-call | bytes 3000000 | tf_op jit(solution)/shard_map/pallas_call | solution.py:392
  36.7 3.5 %collective-permute-start.8 = (f32[8,128]{1,0:T(8,128)S(1)}, f32[8,128]{1,0:T(8,128)S(1)}, u32[]{:S(2)}, u32[]{:S(2)}) collective-permute-start(f32[8,128]{1,0:T(8,128)S(1)} %get-tuple-element.42), channel_id=1, source_target_pairs={{0,64},{64,128},{128,192},{192,0},{1,65},{65,129},{129,193},{193,1... | collective-permute-start | bytes 12296 | tf_op jit(solution)/shard_map/ppermute | solution.py:407
  40.3 1.3 %shard_map.101.refs_3_.sources = f32[3,3,4,24,128]{4,3,2,1,0:T(8,128)S(1)} custom-call(f32[64,1,256]{2,1,0:T(1,128)S(1)} %all-to-all-done.got, f32[4,24,128]{2,1,0:T(8,128)S(1)} %get-tuple-element.34.c.refs_2_), custom_call_target="tpu_custom_call" | custom-call | bytes 9000000 | tf_op jit(solution)/shard_map/pallas_call | solution.py:392
  41.6 1.7 %collective-permute-done.9.refs_6_.refs_7_ = f32[8,128]{1,0:T(8,128)S(1)} collective-permute-done((f32[8,128]{1,0:T(8,128)S(1)}, f32[8,128]{1,0:T(8,128)S(1)}, u32[]{:S(2)}, u32[]{:S(2)}) %collective-permute-start.9) | collective-permute-done | bytes 4128 | tf_op jit(solution)/shard_map/ppermute | solution.py:407
  43.4 1.9 %collective-permute-start.11 = (f32[3,24,128]{2,1,0:T(8,128)S(1)}, f32[3,24,128]{2,1,0:T(8,128)S(1)}, u32[]{:S(2)}, u32[]{:S(2)}) collective-permute-start(f32[3,24,128]{2,1,0:T(8,128)S(1)} %shard_map.102.refs_12_), channel_id=1, source_target_pairs={{0,7},{1,2},{2,1},{3,4},{4,3},{5,6},{6,5},{7,0},{8,15},{9,10},{10,... | collective-permute-start | bytes 110600 | tf_op jit(solution)/shard_map/ppermute | solution.py:413
  46.5 0.7 %collective-permute-done.12.refs_5_.refs_6_ = f32[8,128]{1,0:T(8,128)S(1)} collective-permute-done((f32[8,128]{1,0:T(8,128)S(1)}, f32[8,128]{1,0:T(8,128)S(1)}, u32[]{:S(2)}, u32[]{:S(2)}) %collective-permute-start.12) | collective-permute-done | bytes 4128 | tf_op jit(solution)/shard_map/ppermute | solution.py:407
  47.2 2.2 %collective-permute-done.13.refs_6_.refs_7_ = f32[8,128]{1,0:T(8,128)S(1)} collective-permute-done((f32[8,128]{1,0:T(8,128)S(1)}, f32[8,128]{1,0:T(8,128)S(1)}, u32[]{:S(2)}, u32[]{:S(2)}) %collective-permute-start.13) | collective-permute-done | bytes 4128 | tf_op jit(solution)/shard_map/ppermute | solution.py:407
  50.1 1.6 %collective-permute-start.14 = (f32[3,16,128]{2,1,0:T(8,128)S(1)}, f32[3,16,128]{2,1,0:T(8,128)S(1)}, u32[]{:S(2)}, u32[]{:S(2)}) collective-permute-start(f32[3,16,128]{2,1,0:T(8,128)S(1)} %get-tuple-element.53), channel_id=1, source_target_pairs={{0,1},{1,0},{2,3},{3,2},{4,5},{5,4},{6,7},{7,6},{8,9},{9,8},{10,11... | collective-permute-start | bytes 73736 | tf_op jit(solution)/shard_map/ppermute | solution.py:413
  51.6 1.2 %collective-permute-start.15 = (f32[3,16,128]{2,1,0:T(8,128)S(1)}, f32[3,16,128]{2,1,0:T(8,128)S(1)}, u32[]{:S(2)}, u32[]{:S(2)}) collective-permute-start(f32[3,16,128]{2,1,0:T(8,128)S(1)} %shard_map.104.refs_12_), channel_id=1, source_target_pairs={{0,7},{1,2},{2,1},{3,4},{4,3},{5,6},{6,5},{7,0},{8,15},{9,10},{10,... | collective-permute-start | bytes 73736 | tf_op jit(solution)/shard_map/ppermute | solution.py:413
  53.5 0.8 %collective-permute-done.16.at_left = f32[8,128]{1,0:T(8,128)S(1)} collective-permute-done((f32[8,128]{1,0:T(8,128)S(1)}, f32[8,128]{1,0:T(8,128)S(1)}, u32[]{:S(2)}, u32[]{:S(2)}) %collective-permute-start.16) | collective-permute-done | bytes 4128 | tf_op jit(solution)/shard_map/ppermute | solution.py:407
  54.2 2.3 %collective-permute-done.17.at_right = f32[8,128]{1,0:T(8,128)S(1)} collective-permute-done((f32[8,128]{1,0:T(8,128)S(1)}, f32[8,128]{1,0:T(8,128)S(1)}, u32[]{:S(2)}, u32[]{:S(2)}) %collective-permute-start.17) | collective-permute-done | bytes 4128 | tf_op jit(solution)/shard_map/ppermute | solution.py:407
  56.5 0.9 %shard_map.106 = (f32[3,4,16,128]{3,2,1,0:T(8,128)}, f32[3,4,16,128]{3,2,1,0:T(8,128)}) custom-call(f32[3,4,24,128]{3,2,1,0:T(8,128)S(1)} %get-tuple-element.52.u, f32[3,4,24,128]{3,2,1,0:T(8,128)S(1)} %get-tuple-element.48.refs_0_.v, f32[4,24,128]{2,1,0:T(8,128)S(1)} %get-tuple-element.34.c.refs_2_, f32[3,3,4,24,128]{4,3,2,1,0:T(8,128)S(1)} %shard_map.101.refs_3_.sources, ...), custom_call_target="tpu_custom_call" | custom-call | bytes 3000000 | tf_op jit(solution)/shard_map/pallas_call | solution.py:392
  (34 shorter events, 4.3 us)
Async XLA Ops:
  2.2 21.1 %collective-permute-start = (f32[11,2,8,128]{3,2,1,0:T(8,128)}, f32[11,2,8,128]{3,2,1,0:T(8,128)S(1)}, u32[]{:S(2)}, u32[]{:S(2)}) collective-permute-start(f32[11,2,8,128]{3,2,1,0:T(8,128)} %shard_map.96), channel_id=1, source_target_pairs={{0,8},{8,16},{16,24},{24,32},{32,40},{40,48},{48,56},{56,0},{1,9},... | collective-permute-start | bytes 270344 | tf_op jit(solution)/shard_map/ppermute | solution.py:407
  6.0 17.3 %copy-start.1 = (f32[3,4,16,128]{3,2,1,0:T(8,128)S(1)}, f32[3,4,16,128]{3,2,1,0:T(8,128)}, u32[]{:S(2)}) copy-start(f32[3,4,16,128]{3,2,1,0:T(8,128)} %cur.5) | copy-start | bytes 294916
  6.0 17.3 %copy-start.2 = (f32[3,4,16,128]{3,2,1,0:T(8,128)S(1)}, f32[3,4,16,128]{3,2,1,0:T(8,128)}, u32[]{:S(2)}) copy-start(f32[3,4,16,128]{3,2,1,0:T(8,128)} %prv.5) | copy-start | bytes 294916
  6.1 17.3 %copy-start.3 = (f32[4,16,128]{2,1,0:T(8,128)S(1)}, f32[4,16,128]{2,1,0:T(8,128)}, u32[]{:S(2)}) copy-start(f32[4,16,128]{2,1,0:T(8,128)} %den.1) | copy-start | bytes 98308
  8.9 14.5 %copy-start = (f32[4,4,16,128]{3,2,1,0:T(8,128)S(1)}, f32[4,4,16,128]{3,2,1,0:T(8,128)}, u32[]{:S(2)}) copy-start(f32[4,4,16,128]{3,2,1,0:T(8,128)} %mod.5) | copy-start | bytes 393220
  8.9 14.4 %collective-permute-start.1 = (f32[11,2,8,128]{3,2,1,0:T(8,128)}, f32[11,2,8,128]{3,2,1,0:T(8,128)S(1)}, u32[]{:S(2)}, u32[]{:S(2)}) collective-permute-start(f32[11,2,8,128]{3,2,1,0:T(8,128)} %get-tuple-element.30), channel_id=1, source_target_pairs={{0,56},{8,0},{16,8},{24,16},{32,24},{40,32},{48,40},{56,48},{1,57}... | collective-permute-start | bytes 270344 | tf_op jit(solution)/shard_map/ppermute | solution.py:407
  11.2 23.1 %all-to-all-start = ((f32[64,1,256]{2,1,0:T(1,128)}), f32[64,1,256]{2,1,0:T(1,128)S(1)}, u32[]{:S(2)}, u32[]{:S(2)}) async-start(f32[64,1,256]{2,1,0:T(1,128)} %get-tuple-element.29), calls=%async_computation | async-start | bytes 131072 | tf_op jit(solution)/shard_map/all_to_all | solution.py:450
  23.7 9.5 %collective-permute-start.2 = (f32[5,24,128]{2,1,0:T(8,128)S(1)}, f32[5,24,128]{2,1,0:T(8,128)S(1)}, u32[]{:S(2)}, u32[]{:S(2)}) collective-permute-start(f32[5,24,128]{2,1,0:T(8,128)S(1)} %get-tuple-element.35), channel_id=1, source_target_pairs={{0,1},{1,0},{2,3},{3,2},{4,5},{5,4},{6,7},{7,6},{8,9},{9,8},{10,11... | collective-permute-start | bytes 184328 | tf_op jit(solution)/shard_map/ppermute | solution.py:413
  24.8 8.4 %collective-permute-start.3 = (f32[5,24,128]{2,1,0:T(8,128)S(1)}, f32[5,24,128]{2,1,0:T(8,128)S(1)}, u32[]{:S(2)}, u32[]{:S(2)}) collective-permute-start(f32[5,24,128]{2,1,0:T(8,128)S(1)} %get-tuple-element.36), channel_id=1, source_target_pairs={{0,7},{1,2},{2,1},{3,4},{4,3},{5,6},{6,5},{7,0},{8,15},{9,10},{10,... | collective-permute-start | bytes 184328 | tf_op jit(solution)/shard_map/ppermute | solution.py:413
  27.2 3.4 %collective-permute-start.4 = (f32[8,128]{1,0:T(8,128)S(1)}, f32[8,128]{1,0:T(8,128)S(1)}, u32[]{:S(2)}, u32[]{:S(2)}) collective-permute-start(f32[8,128]{1,0:T(8,128)S(1)} %get-tuple-element.37), channel_id=1, source_target_pairs={{0,64},{64,128},{128,192},{192,0},{1,65},{65,129},{129,193},{193,1... | collective-permute-start | bytes 12296 | tf_op jit(solution)/shard_map/ppermute | solution.py:407
  29.8 3.3 %collective-permute-start.5 = (f32[8,128]{1,0:T(8,128)S(1)}, f32[8,128]{1,0:T(8,128)S(1)}, u32[]{:S(2)}, u32[]{:S(2)}) collective-permute-start(f32[8,128]{1,0:T(8,128)S(1)} %get-tuple-element.38), channel_id=1, source_target_pairs={{0,192},{64,0},{128,64},{192,128},{1,193},{65,1},{129,65},{193,129... | collective-permute-start | bytes 12296 | tf_op jit(solution)/shard_map/ppermute | solution.py:407
  34.7 8.5 %collective-permute-start.7 = (f32[3,24,128]{2,1,0:T(8,128)S(1)}, f32[3,24,128]{2,1,0:T(8,128)S(1)}, u32[]{:S(2)}, u32[]{:S(2)}) collective-permute-start(f32[3,24,128]{2,1,0:T(8,128)S(1)} %shard_map.99.made), channel_id=1, source_target_pairs={{0,7},{1,2},{2,1},{3,4},{4,3},{5,6},{6,5},{7,0},{8,15},{9,10},{10,... | collective-permute-start | bytes 110600 | tf_op jit(solution)/shard_map/ppermute | solution.py:413
  36.3 9.0 %collective-permute-start.6 = (f32[3,24,128]{2,1,0:T(8,128)S(1)}, f32[3,24,128]{2,1,0:T(8,128)S(1)}, u32[]{:S(2)}, u32[]{:S(2)}) collective-permute-start(f32[3,24,128]{2,1,0:T(8,128)S(1)} %get-tuple-element.41), channel_id=1, source_target_pairs={{0,1},{1,0},{2,3},{3,2},{4,5},{5,4},{6,7},{7,6},{8,9},{9,8},{10,11... | collective-permute-start | bytes 110600 | tf_op jit(solution)/shard_map/ppermute | solution.py:413
  36.7 4.9 %collective-permute-start.8 = (f32[8,128]{1,0:T(8,128)S(1)}, f32[8,128]{1,0:T(8,128)S(1)}, u32[]{:S(2)}, u32[]{:S(2)}) collective-permute-start(f32[8,128]{1,0:T(8,128)S(1)} %get-tuple-element.42), channel_id=1, source_target_pairs={{0,64},{64,128},{128,192},{192,0},{1,65},{65,129},{129,193},{193,1... | collective-permute-start | bytes 12296 | tf_op jit(solution)/shard_map/ppermute | solution.py:407
  40.3 3.0 %collective-permute-start.9 = (f32[8,128]{1,0:T(8,128)S(1)}, f32[8,128]{1,0:T(8,128)S(1)}, u32[]{:S(2)}, u32[]{:S(2)}) collective-permute-start(f32[8,128]{1,0:T(8,128)S(1)} %get-tuple-element.43), channel_id=1, source_target_pairs={{0,192},{64,0},{128,64},{192,128},{1,193},{65,1},{129,65},{193,129... | collective-permute-start | bytes 12296 | tf_op jit(solution)/shard_map/ppermute | solution.py:407
  43.4 6.0 %collective-permute-start.11 = (f32[3,24,128]{2,1,0:T(8,128)S(1)}, f32[3,24,128]{2,1,0:T(8,128)S(1)}, u32[]{:S(2)}, u32[]{:S(2)}) collective-permute-start(f32[3,24,128]{2,1,0:T(8,128)S(1)} %shard_map.102.refs_12_), channel_id=1, source_target_pairs={{0,7},{1,2},{2,1},{3,4},{4,3},{5,6},{6,5},{7,0},{8,15},{9,10},{10,... | collective-permute-start | bytes 110600 | tf_op jit(solution)/shard_map/ppermute | solution.py:413
  45.8 3.7 %collective-permute-start.10 = (f32[3,24,128]{2,1,0:T(8,128)S(1)}, f32[3,24,128]{2,1,0:T(8,128)S(1)}, u32[]{:S(2)}, u32[]{:S(2)}) collective-permute-start(f32[3,24,128]{2,1,0:T(8,128)S(1)} %get-tuple-element.49), channel_id=1, source_target_pairs={{0,1},{1,0},{2,3},{3,2},{4,5},{5,4},{6,7},{7,6},{8,9},{9,8},{10,11... | collective-permute-start | bytes 110600 | tf_op jit(solution)/shard_map/ppermute | solution.py:413
  45.9 1.2 %collective-permute-start.12 = (f32[8,128]{1,0:T(8,128)S(1)}, f32[8,128]{1,0:T(8,128)S(1)}, u32[]{:S(2)}, u32[]{:S(2)}) collective-permute-start(f32[8,128]{1,0:T(8,128)S(1)} %get-tuple-element.50), channel_id=1, source_target_pairs={{0,64},{64,128},{128,192},{192,0},{1,65},{65,129},{129,193},{193,1... | collective-permute-start | bytes 12296 | tf_op jit(solution)/shard_map/ppermute | solution.py:407
  46.2 3.2 %collective-permute-start.13 = (f32[8,128]{1,0:T(8,128)S(1)}, f32[8,128]{1,0:T(8,128)S(1)}, u32[]{:S(2)}, u32[]{:S(2)}) collective-permute-start(f32[8,128]{1,0:T(8,128)S(1)} %get-tuple-element.51), channel_id=1, source_target_pairs={{0,192},{64,0},{128,64},{192,128},{1,193},{65,1},{129,65},{193,129... | collective-permute-start | bytes 12296 | tf_op jit(solution)/shard_map/ppermute | solution.py:407
  50.1 6.5 %collective-permute-start.14 = (f32[3,16,128]{2,1,0:T(8,128)S(1)}, f32[3,16,128]{2,1,0:T(8,128)S(1)}, u32[]{:S(2)}, u32[]{:S(2)}) collective-permute-start(f32[3,16,128]{2,1,0:T(8,128)S(1)} %get-tuple-element.53), channel_id=1, source_target_pairs={{0,1},{1,0},{2,3},{3,2},{4,5},{5,4},{6,7},{7,6},{8,9},{9,8},{10,11... | collective-permute-start | bytes 73736 | tf_op jit(solution)/shard_map/ppermute | solution.py:413
  51.6 4.9 %collective-permute-start.15 = (f32[3,16,128]{2,1,0:T(8,128)S(1)}, f32[3,16,128]{2,1,0:T(8,128)S(1)}, u32[]{:S(2)}, u32[]{:S(2)}) collective-permute-start(f32[3,16,128]{2,1,0:T(8,128)S(1)} %shard_map.104.refs_12_), channel_id=1, source_target_pairs={{0,7},{1,2},{2,1},{3,4},{4,3},{5,6},{6,5},{7,0},{8,15},{9,10},{10,... | collective-permute-start | bytes 73736 | tf_op jit(solution)/shard_map/ppermute | solution.py:413
  52.9 1.4 %collective-permute-start.16 = (f32[8,128]{1,0:T(8,128)S(1)}, f32[8,128]{1,0:T(8,128)S(1)}, u32[]{:S(2)}, u32[]{:S(2)}) collective-permute-start(f32[8,128]{1,0:T(8,128)S(1)} %get-tuple-element.54), channel_id=1, source_target_pairs={{0,64},{64,128},{128,192},{192,0},{1,65},{65,129},{129,193},{193,1... | collective-permute-start | bytes 12296 | tf_op jit(solution)/shard_map/ppermute | solution.py:407
  53.5 3.0 %collective-permute-start.17 = (f32[8,128]{1,0:T(8,128)S(1)}, f32[8,128]{1,0:T(8,128)S(1)}, u32[]{:S(2)}, u32[]{:S(2)}) collective-permute-start(f32[8,128]{1,0:T(8,128)S(1)} %get-tuple-element.55), channel_id=1, source_target_pairs={{0,192},{64,0},{128,64},{192,128},{1,193},{65,1},{129,65},{193,129... | collective-permute-start | bytes 12296 | tf_op jit(solution)/shard_map/ppermute | solution.py:407

commit v8 on v7

--- a/solution.py
+++ b/solution.py
@@ -71,16 +71,14 @@
 
 def keep_lead(u_ref, made):
     lead, _ = end_layers()
-    rows = made.shape[1]
-    for k in range(3):
-        u_ref[k, lead, :rows, :] = made[k]
+    for k in range(3):
+        u_ref[k, lead] = made[k]
 
 
 def put_rest(u_ref, even_ref, left_ref, right_ref):
     _, rest = end_layers()
-    rows = even_ref.shape[1]
-    for k in range(3):
-        even_ref[k] = u_ref[k, rest, :rows, :]
+    for k in range(3):
+        even_ref[k] = u_ref[k, rest]
     left_ref[...] = jnp.zeros_like(left_ref)
     right_ref[...] = jnp.zeros_like(right_ref)
     put_columns(tiles_of(u_ref, 3), left_ref, right_ref, 0)
@@ -318,20 +316,15 @@
     )
 
 
-def first_lead_kernel(got, free, c, odd, weights, picks):
-    lead, _ = end_layers()
-    summed = gather_sources((0,), got, weights, picks, lead, 1)
-    for k in range(3):
-        odd[k] = free[k, lead] + summed[k * ROWS : (k + 1) * ROWS] * c[lead]
-
-
-def first_kernel(got, free, c, made, first, even, left, right, weights, picks):
+def first_kernel(got, free, c, first, even, odd, left, right, weights, picks):
     summed = gather_sources((0,), got, weights, picks)
     for k in range(3):
         for r in range(CR):
             at = (k * CR + r) * ROWS
             first[k, r] = free[k, r] + summed[at : at + ROWS] * c[r]
-    keep_lead(first, made)
+    lead, _ = end_layers()
+    for k in range(3):
+        odd[k] = first[k, lead]
     put_rest(first, even, left, right)
 
 
@@ -355,8 +348,7 @@
         outer = jnp.where(joined, odd[k], 0.0)
         total = ar[i, outer_face] * (outer - here) + ar[i, inner_face] * (u[k, inner] - here)
         total = total + level(k, lead, here, at_left, at_right, al, au, ad)
-        value = 2.0 * here - v[k, lead] + c[lead] * total + sources[t - 1, k, lead]
-        out[k] = value[: out.shape[1]]
+        out[k] = 2.0 * here - v[k, lead] + c[lead] * total + sources[t - 1, k, lead]
 
 
 def step_kernel(
@@ -372,18 +364,18 @@
 
 
 def last_kernel(
-    u, v, c, sources, even, odd, at_left, at_right, ar, al, au, ad, final, before_final
+    u, v, c, sources, even, odd, at_left, at_right, ar, al, au, ad, made, final, before_final
 ):
     lows, highs = radial_ends(even, odd, 3)
-    beside = jnp.zeros((ROWS - CL, CE), F32)
-    lows = [jnp.concatenate([x, beside], axis=0) for x in lows]
-    highs = [jnp.concatenate([x, beside], axis=0) for x in highs]
     for k in range(3):
         for r in range(CR):
             total = force(k, r, u, lows, highs, at_left, at_right, ar, al, au, ad)
             value = 2.0 * u[k, r] - v[k, r] + c[r] * total + sources[STEPS - 2, k, r]
             final[k, r] = value[:CL]
             before_final[k, r] = u[k, r, 0:CL, :]
+    lead, _ = end_layers()
+    for k in range(3):
+        final[k, lead] = made[k, 0:CL, :]
 
 
 def call(kernel, outs, args, scratch=(), hbm=0, us=1.0):
@@ -461,17 +453,10 @@
         (u, v, m, c, swapped(even, "rad", 0), swapped(odd, "rad", 1), *swap_columns(*ends)),
     )
     cells, lanes = CR * ROWS, 3 * SLOTS * 128
-    (made,) = call(
-        first_lead_kernel,
-        [layer],
+    first, even, odd, *ends = call(
+        first_kernel,
+        [wide, layer, layer] + columns,
         (got, free, c),
-        scratch=[(3 * ROWS, lanes), (CE, lanes)],
-    )
-    odd = swapped(made, "rad", 1)
-    first, even, *ends = call(
-        first_kernel,
-        [wide, layer] + columns,
-        (got, free, c, made),
         scratch=[(3 * cells, lanes), (CE, lanes)],
     )
     (sources,) = call(
@@ -481,16 +466,13 @@
         scratch=[(3 * (STEPS - 1) * cells, lanes), (CE, lanes)],
         us=3.0,
     )
+    odd = swapped(odd, "rad", 1)
     v, u = u, first
     for t in range(1, STEPS):
         even = swapped(even, "rad", 0)
         at_left, at_right = swap_columns(*ends)
         before = (u, v, c, sources)
         after = (at_left, at_right, *coefficients)
-        if t == STEPS - 1:
-            return tuple(call(last_kernel, [(3, CR, CL, CE)] * 2, before + (even, odd) + after))
-        if t == STEPS - 2:
-            layer = (3, CL, CE)
 
         def lead(*refs, t=t):
             lead_kernel(t, *refs)
@@ -499,6 +481,9 @@
             step_kernel(t, *refs)
 
         (made,) = call(lead, [layer], before + (odd,) + after)
+        if t == STEPS - 1:
+            args = before + (even, odd) + after + (made,)
+            return tuple(call(last_kernel, [(3, CR, CL, CE)] * 2, args))
         next_odd = swapped(made, "rad", 1)
         following, even, *ends = call(
             step, [wide, layer] + columns, before + (even, odd) + after + (made,)

time: 57.6 us -> 56.2 us (0.976)
  starting transfers between devices: 35.1 us -> 34 us
    ppermute x8, starting transfers between devices: 9.48 us -> 8.42 us  [swapped(): return lax.ppermute(block, axis, pairs)]
  transfers between devices with their start and end apart: 19 -> 19, of which waited for: 8 -> 8; matrix products, arithmetic and copies ran while one was open for 0% -> 0% of each run, Pallas kernels for 11% -> 12%
where the time goes in v8:
time: 56.2 us; the launch traced here: 56 us
  starting transfers between devices  34 us (60%)
  waiting for transfers between devices  11.4 us (20%)
  Pallas kernels  9.73 us (17%)
  between operations  0.8 us (1%)
    ppermute x10, starting transfers between devices, shifted(): lax.ppermute(block, axis, [(i, (i + by) % count) for i in range(count)])  13.5 us
    all_to_all x1, starting transfers between devices, on_device(): got = lax.all_to_all(packed, ('lat', 'rad'), 0, 0, tiled=True)  12.1 us
    ppermute x10, waiting for transfers between devices, shifted(): lax.ppermute(block, axis, [(i, (i + by) % count) for i in range(count)])  10.8 us
    pallas_call x12, Pallas kernels, call(): pl.pallas_call(kernel, out_shape=[jax.ShapeDtypeStruct(shape, F32) for sh...  9.73 us
    ppermute x8, starting transfers between devices, swapped(): return lax.ppermute(block, axis, pairs)  8.42 us
  transfers between devices with their start and end apart: 19, of which 8 were waited for; matrix products, arithmetic and copies ran while one was open for 0% of the time, Pallas kernels for 12%

profile of v8, /device:TPU:1, one launch (start us, length us, event | category | flops | bytes accessed | tf_op | source)
XLA Modules:
  0.0 56.0 jit_solution(3715604907550944954)
XLA Ops:
  0.6 1.6 %shard_map.96 = f32[11,2,8,128]{3,2,1,0:T(8,128)} custom-call(f32[3,4,16,128]{3,2,1,0:T(8,128)} %cur.5, f32[3,4,16,128]{3,2,1,0:T(8,128)} %prv.5, f32[4,4,16,128]{3,2,1,0:T(8,128)} %mod.5, f32[1,4,16,128]{3,2,1,0:T(8,128)} %bitcast.5), custom_call_target="tpu_custom_call" | custom-call | bytes 3000000 | tf_op jit(solution)/shard_map/pallas_call | solution.py:384
  2.2 3.8 %collective-permute-start = (f32[11,2,8,128]{3,2,1,0:T(8,128)}, f32[11,2,8,128]{3,2,1,0:T(8,128)S(1)}, u32[]{:S(2)}, u32[]{:S(2)}) collective-permute-start(f32[11,2,8,128]{3,2,1,0:T(8,128)} %shard_map.96), channel_id=1, source_target_pairs={{0,8},{8,16},{16,24},{24,32},{32,40},{40,48},{48,56},{56,0},{1,9},... | collective-permute-start | bytes 270344 | tf_op jit(solution)/shard_map/ppermute | solution.py:399
  6.1 2.8 %shard_map.95 = (f32[64,1,256]{2,1,0:T(1,128)}, f32[11,2,8,128]{3,2,1,0:T(8,128)}) custom-call(s32[1,128]{1,0:T(1,128)} %bitcast.8, s32[1,128]{1,0:T(1,128)} %bitcast.9, s32[1,128]{1,0:T(1,128)} %bitcast.10, f32[3,128,512]{2,1,0:T(8,128)} %bitcast.7, f32[3,4,16,128]{3,2,1,0:T(8,128)} %cur.5, f32[3,4,16,128]{3,2,1,0:T(8,128)} %prv.5, f32[4,4,16,128]{3,2,1,0:T(8,128)} %mod.5, ...), custom_call_target="tpu_custom_call" | custom-call | bytes 6000000 | tf_op jit(solution)/shard_map/pallas_call | solution.py:384
  8.9 2.3 %collective-permute-start.1 = (f32[11,2,8,128]{3,2,1,0:T(8,128)}, f32[11,2,8,128]{3,2,1,0:T(8,128)S(1)}, u32[]{:S(2)}, u32[]{:S(2)}) collective-permute-start(f32[11,2,8,128]{3,2,1,0:T(8,128)} %get-tuple-element.31), channel_id=1, source_target_pairs={{0,56},{8,0},{16,8},{24,16},{32,24},{40,32},{48,40},{56,48},{1,57}... | collective-permute-start | bytes 270344 | tf_op jit(solution)/shard_map/ppermute | solution.py:399
  11.2 12.1 %all-to-all-start = ((f32[64,1,256]{2,1,0:T(1,128)}), f32[64,1,256]{2,1,0:T(1,128)S(1)}, u32[]{:S(2)}, u32[]{:S(2)}) async-start(f32[64,1,256]{2,1,0:T(1,128)} %get-tuple-element.30), calls=%async_computation | async-start | bytes 131072 | tf_op jit(solution)/shard_map/all_to_all | solution.py:442
  23.7 1.1 %collective-permute-start.2 = (f32[5,24,128]{2,1,0:T(8,128)S(1)}, f32[5,24,128]{2,1,0:T(8,128)S(1)}, u32[]{:S(2)}, u32[]{:S(2)}) collective-permute-start(f32[5,24,128]{2,1,0:T(8,128)S(1)} %get-tuple-element.36), channel_id=1, source_target_pairs={{0,1},{1,0},{2,3},{3,2},{4,5},{5,4},{6,7},{7,6},{8,9},{9,8},{10,11... | collective-permute-start | bytes 184328 | tf_op jit(solution)/shard_map/ppermute | solution.py:405
  24.8 2.4 %collective-permute-start.3 = (f32[5,24,128]{2,1,0:T(8,128)S(1)}, f32[5,24,128]{2,1,0:T(8,128)S(1)}, u32[]{:S(2)}, u32[]{:S(2)}) collective-permute-start(f32[5,24,128]{2,1,0:T(8,128)S(1)} %get-tuple-element.37), channel_id=1, source_target_pairs={{0,7},{1,2},{2,1},{3,4},{4,3},{5,6},{6,5},{7,0},{8,15},{9,10},{10,... | collective-permute-start | bytes 184328 | tf_op jit(solution)/shard_map/ppermute | solution.py:405
  27.2 2.6 %collective-permute-start.4 = (f32[8,128]{1,0:T(8,128)S(1)}, f32[8,128]{1,0:T(8,128)S(1)}, u32[]{:S(2)}, u32[]{:S(2)}) collective-permute-start(f32[8,128]{1,0:T(8,128)S(1)} %get-tuple-element.38), channel_id=1, source_target_pairs={{0,64},{64,128},{128,192},{192,0},{1,65},{65,129},{129,193},{193,1... | collective-permute-start | bytes 12296 | tf_op jit(solution)/shard_map/ppermute | solution.py:399
  29.8 0.8 %collective-permute-done.4.at_left = f32[8,128]{1,0:T(8,128)S(1)} collective-permute-done((f32[8,128]{1,0:T(8,128)S(1)}, f32[8,128]{1,0:T(8,128)S(1)}, u32[]{:S(2)}, u32[]{:S(2)}) %collective-permute-start.4) | collective-permute-done | bytes 4128 | tf_op jit(solution)/shard_map/ppermute | solution.py:399
  30.5 2.6 %collective-permute-done.5.at_right = f32[8,128]{1,0:T(8,128)S(1)} collective-permute-done((f32[8,128]{1,0:T(8,128)S(1)}, f32[8,128]{1,0:T(8,128)S(1)}, u32[]{:S(2)}, u32[]{:S(2)}) %collective-permute-start.5) | collective-permute-done | bytes 4128 | tf_op jit(solution)/shard_map/ppermute | solution.py:399
  33.1 0.6 %shard_map.98 = (f32[2,5,24,128]{3,2,1,0:T(8,128)S(1)}, f32[3,4,24,128]{3,2,1,0:T(8,128)S(1)}, f32[3,4,24,128]{3,2,1,0:T(8,128)S(1)}, f32[3,4,24,128]{3,2,1,0:T(8,128)S(1)}, f32[3,4,24,128]{3,2,1,0:T(8,128)S(1)}) custom-call(f32[3,4,24,128]{3,2,1,0:T(8,128)S(1)} %get-tuple-element.32.u.refs_1_, f32[3,4,24,128]{3,2,1,0:T(8,128)S(1)} %get-tuple-element.33.v, ...), custom_call_target="tpu_custom_call" | custom-call | bytes 3000000 | tf_op jit(solution)/shard_map/pallas_call | solution.py:384
  33.8 0.5 all-to-all-done.got
  34.3 0.7 %shard_map.99 = (f32[3,4,24,128]{3,2,1,0:T(8,128)S(1)}, f32[3,24,128]{2,1,0:T(8,128)S(1)}, f32[3,24,128]{2,1,0:T(8,128)S(1)}, f32[8,128]{1,0:T(8,128)S(1)}, f32[8,128]{1,0:T(8,128)S(1)}) custom-call(f32[64,1,256]{2,1,0:T(1,128)S(1)} %all-to-all-done.got, f32[3,4,24,128]{3,2,1,0:T(8,128)S(1)} %get-tuple-element.40.free, ...), custom_call_target="tpu_custom_call" | custom-call | bytes 3000000 | tf_op jit(solution)/shard_map/pallas_call | solution.py:384
  35.0 0.8 %collective-permute-start.7 = (f32[3,24,128]{2,1,0:T(8,128)S(1)}, f32[3,24,128]{2,1,0:T(8,128)S(1)}, u32[]{:S(2)}, u32[]{:S(2)}) collective-permute-start(f32[3,24,128]{2,1,0:T(8,128)S(1)} %get-tuple-element.43), channel_id=1, source_target_pairs={{0,7},{1,2},{2,1},{3,4},{4,3},{5,6},{6,5},{7,0},{8,15},{9,10},{10,... | collective-permute-start | bytes 110600 | tf_op jit(solution)/shard_map/ppermute | solution.py:405
  36.2 3.5 %collective-permute-start.8 = (f32[8,128]{1,0:T(8,128)S(1)}, f32[8,128]{1,0:T(8,128)S(1)}, u32[]{:S(2)}, u32[]{:S(2)}) collective-permute-start(f32[8,128]{1,0:T(8,128)S(1)} %get-tuple-element.44), channel_id=1, source_target_pairs={{0,64},{64,128},{128,192},{192,0},{1,65},{65,129},{129,193},{193,1... | collective-permute-start | bytes 12296 | tf_op jit(solution)/shard_map/ppermute | solution.py:399
  39.7 1.3 %shard_map.100.refs_3_.sources = f32[3,3,4,24,128]{4,3,2,1,0:T(8,128)S(1)} custom-call(f32[64,1,256]{2,1,0:T(1,128)S(1)} %all-to-all-done.got, f32[4,24,128]{2,1,0:T(8,128)S(1)} %get-tuple-element.35.c.refs_2_), custom_call_target="tpu_custom_call" | custom-call | bytes 9000000 | tf_op jit(solution)/shard_map/pallas_call | solution.py:384
  41.1 1.7 %collective-permute-done.9.refs_6_.refs_7_ = f32[8,128]{1,0:T(8,128)S(1)} collective-permute-done((f32[8,128]{1,0:T(8,128)S(1)}, f32[8,128]{1,0:T(8,128)S(1)}, u32[]{:S(2)}, u32[]{:S(2)}) %collective-permute-start.9) | collective-permute-done | bytes 4128 | tf_op jit(solution)/shard_map/ppermute | solution.py:399
  42.9 1.9 %collective-permute-start.11 = (f32[3,24,128]{2,1,0:T(8,128)S(1)}, f32[3,24,128]{2,1,0:T(8,128)S(1)}, u32[]{:S(2)}, u32[]{:S(2)}) collective-permute-start(f32[3,24,128]{2,1,0:T(8,128)S(1)} %shard_map.101.refs_12_), channel_id=1, source_target_pairs={{0,7},{1,2},{2,1},{3,4},{4,3},{5,6},{6,5},{7,0},{8,15},{9,10},{10,... | collective-permute-start | bytes 110600 | tf_op jit(solution)/shard_map/ppermute | solution.py:405
  46.0 0.7 %collective-permute-done.12.refs_5_.refs_6_ = f32[8,128]{1,0:T(8,128)S(1)} collective-permute-done((f32[8,128]{1,0:T(8,128)S(1)}, f32[8,128]{1,0:T(8,128)S(1)}, u32[]{:S(2)}, u32[]{:S(2)}) %collective-permute-start.12) | collective-permute-done | bytes 4128 | tf_op jit(solution)/shard_map/ppermute | solution.py:399
  46.6 2.2 %collective-permute-done.13.refs_6_.refs_7_ = f32[8,128]{1,0:T(8,128)S(1)} collective-permute-done((f32[8,128]{1,0:T(8,128)S(1)}, f32[8,128]{1,0:T(8,128)S(1)}, u32[]{:S(2)}, u32[]{:S(2)}) %collective-permute-start.13) | collective-permute-done | bytes 4128 | tf_op jit(solution)/shard_map/ppermute | solution.py:399
  49.0 1.8 %collective-permute-start.15 = (f32[3,24,128]{2,1,0:T(8,128)S(1)}, f32[3,24,128]{2,1,0:T(8,128)S(1)}, u32[]{:S(2)}, u32[]{:S(2)}) collective-permute-start(f32[3,24,128]{2,1,0:T(8,128)S(1)} %shard_map.103.refs_12_), channel_id=1, source_target_pairs={{0,7},{1,2},{2,1},{3,4},{4,3},{5,6},{6,5},{7,0},{8,15},{9,10},{10,... | collective-permute-start | bytes 110600 | tf_op jit(solution)/shard_map/ppermute | solution.py:405
  52.0 0.7 %collective-permute-done.16.refs_5_.at_left = f32[8,128]{1,0:T(8,128)S(1)} collective-permute-done((f32[8,128]{1,0:T(8,128)S(1)}, f32[8,128]{1,0:T(8,128)S(1)}, u32[]{:S(2)}, u32[]{:S(2)}) %collective-permute-start.16) | collective-permute-done | bytes 4128 | tf_op jit(solution)/shard_map/ppermute | solution.py:399
  52.6 2.3 %collective-permute-done.17.refs_6_.at_right = f32[8,128]{1,0:T(8,128)S(1)} collective-permute-done((f32[8,128]{1,0:T(8,128)S(1)}, f32[8,128]{1,0:T(8,128)S(1)}, u32[]{:S(2)}, u32[]{:S(2)}) %collective-permute-start.17) | collective-permute-done | bytes 4128 | tf_op jit(solution)/shard_map/ppermute | solution.py:399
  55.1 0.9 %shard_map.106 = (f32[3,4,16,128]{3,2,1,0:T(8,128)}, f32[3,4,16,128]{3,2,1,0:T(8,128)}) custom-call(f32[3,4,24,128]{3,2,1,0:T(8,128)S(1)} %get-tuple-element.54.refs_0_.u, f32[3,4,24,128]{3,2,1,0:T(8,128)S(1)} %get-tuple-element.50.refs_0_.refs_1_.v, f32[4,24,128]{2,1,0:T(8,128)S(1)} %get-tuple-element.35.c.refs_2_, ...), custom_call_target="tpu_custom_call" | custom-call | bytes 3000000 | tf_op jit(solution)/shard_map/pallas_call | solution.py:384
  (34 shorter events, 3.5 us)
Async XLA Ops:
  2.2 21.1 %collective-permute-start = (f32[11,2,8,128]{3,2,1,0:T(8,128)}, f32[11,2,8,128]{3,2,1,0:T(8,128)S(1)}, u32[]{:S(2)}, u32[]{:S(2)}) collective-permute-start(f32[11,2,8,128]{3,2,1,0:T(8,128)} %shard_map.96), channel_id=1, source_target_pairs={{0,8},{8,16},{16,24},{24,32},{32,40},{40,48},{48,56},{56,0},{1,9},... | collective-permute-start | bytes 270344 | tf_op jit(solution)/shard_map/ppermute | solution.py:399
  6.0 17.3 %copy-start.1 = (f32[3,4,16,128]{3,2,1,0:T(8,128)S(1)}, f32[3,4,16,128]{3,2,1,0:T(8,128)}, u32[]{:S(2)}) copy-start(f32[3,4,16,128]{3,2,1,0:T(8,128)} %cur.5) | copy-start | bytes 294916
  6.0 17.3 %copy-start.2 = (f32[3,4,16,128]{3,2,1,0:T(8,128)S(1)}, f32[3,4,16,128]{3,2,1,0:T(8,128)}, u32[]{:S(2)}) copy-start(f32[3,4,16,128]{3,2,1,0:T(8,128)} %prv.5) | copy-start | bytes 294916
  6.1 17.3 %copy-start.3 = (f32[4,16,128]{2,1,0:T(8,128)S(1)}, f32[4,16,128]{2,1,0:T(8,128)}, u32[]{:S(2)}) copy-start(f32[4,16,128]{2,1,0:T(8,128)} %den.1) | copy-start | bytes 98308
  8.9 14.5 %copy-start = (f32[4,4,16,128]{3,2,1,0:T(8,128)S(1)}, f32[4,4,16,128]{3,2,1,0:T(8,128)}, u32[]{:S(2)}) copy-start(f32[4,4,16,128]{3,2,1,0:T(8,128)} %mod.5) | copy-start | bytes 393220
  8.9 14.4 %collective-permute-start.1 = (f32[11,2,8,128]{3,2,1,0:T(8,128)}, f32[11,2,8,128]{3,2,1,0:T(8,128)S(1)}, u32[]{:S(2)}, u32[]{:S(2)}) collective-permute-start(f32[11,2,8,128]{3,2,1,0:T(8,128)} %get-tuple-element.31), channel_id=1, source_target_pairs={{0,56},{8,0},{16,8},{24,16},{32,24},{40,32},{48,40},{56,48},{1,57}... | collective-permute-start | bytes 270344 | tf_op jit(solution)/shard_map/ppermute | solution.py:399
  11.2 23.1 %all-to-all-start = ((f32[64,1,256]{2,1,0:T(1,128)}), f32[64,1,256]{2,1,0:T(1,128)S(1)}, u32[]{:S(2)}, u32[]{:S(2)}) async-start(f32[64,1,256]{2,1,0:T(1,128)} %get-tuple-element.30), calls=%async_computation | async-start | bytes 131072 | tf_op jit(solution)/shard_map/all_to_all | solution.py:442
  23.7 9.5 %collective-permute-start.2 = (f32[5,24,128]{2,1,0:T(8,128)S(1)}, f32[5,24,128]{2,1,0:T(8,128)S(1)}, u32[]{:S(2)}, u32[]{:S(2)}) collective-permute-start(f32[5,24,128]{2,1,0:T(8,128)S(1)} %get-tuple-element.36), channel_id=1, source_target_pairs={{0,1},{1,0},{2,3},{3,2},{4,5},{5,4},{6,7},{7,6},{8,9},{9,8},{10,11... | collective-permute-start | bytes 184328 | tf_op jit(solution)/shard_map/ppermute | solution.py:405
  24.8 8.4 %collective-permute-start.3 = (f32[5,24,128]{2,1,0:T(8,128)S(1)}, f32[5,24,128]{2,1,0:T(8,128)S(1)}, u32[]{:S(2)}, u32[]{:S(2)}) collective-permute-start(f32[5,24,128]{2,1,0:T(8,128)S(1)} %get-tuple-element.37), channel_id=1, source_target_pairs={{0,7},{1,2},{2,1},{3,4},{4,3},{5,6},{6,5},{7,0},{8,15},{9,10},{10,... | collective-permute-start | bytes 184328 | tf_op jit(solution)/shard_map/ppermute | solution.py:405
  27.2 3.4 %collective-permute-start.4 = (f32[8,128]{1,0:T(8,128)S(1)}, f32[8,128]{1,0:T(8,128)S(1)}, u32[]{:S(2)}, u32[]{:S(2)}) collective-permute-start(f32[8,128]{1,0:T(8,128)S(1)} %get-tuple-element.38), channel_id=1, source_target_pairs={{0,64},{64,128},{128,192},{192,0},{1,65},{65,129},{129,193},{193,1... | collective-permute-start | bytes 12296 | tf_op jit(solution)/shard_map/ppermute | solution.py:399
  29.8 3.3 %collective-permute-start.5 = (f32[8,128]{1,0:T(8,128)S(1)}, f32[8,128]{1,0:T(8,128)S(1)}, u32[]{:S(2)}, u32[]{:S(2)}) collective-permute-start(f32[8,128]{1,0:T(8,128)S(1)} %get-tuple-element.39), channel_id=1, source_target_pairs={{0,192},{64,0},{128,64},{192,128},{1,193},{65,1},{129,65},{193,129... | collective-permute-start | bytes 12296 | tf_op jit(solution)/shard_map/ppermute | solution.py:399
  35.0 7.7 %collective-permute-start.7 = (f32[3,24,128]{2,1,0:T(8,128)S(1)}, f32[3,24,128]{2,1,0:T(8,128)S(1)}, u32[]{:S(2)}, u32[]{:S(2)}) collective-permute-start(f32[3,24,128]{2,1,0:T(8,128)S(1)} %get-tuple-element.43), channel_id=1, source_target_pairs={{0,7},{1,2},{2,1},{3,4},{4,3},{5,6},{6,5},{7,0},{8,15},{9,10},{10,... | collective-permute-start | bytes 110600 | tf_op jit(solution)/shard_map/ppermute | solution.py:405
  35.8 9.0 %collective-permute-start.6 = (f32[3,24,128]{2,1,0:T(8,128)S(1)}, f32[3,24,128]{2,1,0:T(8,128)S(1)}, u32[]{:S(2)}, u32[]{:S(2)}) collective-permute-start(f32[3,24,128]{2,1,0:T(8,128)S(1)} %get-tuple-element.42), channel_id=1, source_target_pairs={{0,1},{1,0},{2,3},{3,2},{4,5},{5,4},{6,7},{7,6},{8,9},{9,8},{10,11... | collective-permute-start | bytes 110600 | tf_op jit(solution)/shard_map/ppermute | solution.py:405
  36.2 4.9 %collective-permute-start.8 = (f32[8,128]{1,0:T(8,128)S(1)}, f32[8,128]{1,0:T(8,128)S(1)}, u32[]{:S(2)}, u32[]{:S(2)}) collective-permute-start(f32[8,128]{1,0:T(8,128)S(1)} %get-tuple-element.44), channel_id=1, source_target_pairs={{0,64},{64,128},{128,192},{192,0},{1,65},{65,129},{129,193},{193,1... | collective-permute-start | bytes 12296 | tf_op jit(solution)/shard_map/ppermute | solution.py:399
  39.7 3.0 %collective-permute-start.9 = (f32[8,128]{1,0:T(8,128)S(1)}, f32[8,128]{1,0:T(8,128)S(1)}, u32[]{:S(2)}, u32[]{:S(2)}) collective-permute-start(f32[8,128]{1,0:T(8,128)S(1)} %get-tuple-element.45), channel_id=1, source_target_pairs={{0,192},{64,0},{128,64},{192,128},{1,193},{65,1},{129,65},{193,129... | collective-permute-start | bytes 12296 | tf_op jit(solution)/shard_map/ppermute | solution.py:399
  42.9 6.0 %collective-permute-start.11 = (f32[3,24,128]{2,1,0:T(8,128)S(1)}, f32[3,24,128]{2,1,0:T(8,128)S(1)}, u32[]{:S(2)}, u32[]{:S(2)}) collective-permute-start(f32[3,24,128]{2,1,0:T(8,128)S(1)} %shard_map.101.refs_12_), channel_id=1, source_target_pairs={{0,7},{1,2},{2,1},{3,4},{4,3},{5,6},{6,5},{7,0},{8,15},{9,10},{10,... | collective-permute-start | bytes 110600 | tf_op jit(solution)/shard_map/ppermute | solution.py:405
  45.3 5.5 %collective-permute-start.10 = (f32[3,24,128]{2,1,0:T(8,128)S(1)}, f32[3,24,128]{2,1,0:T(8,128)S(1)}, u32[]{:S(2)}, u32[]{:S(2)}) collective-permute-start(f32[3,24,128]{2,1,0:T(8,128)S(1)} %get-tuple-element.51), channel_id=1, source_target_pairs={{0,1},{1,0},{2,3},{3,2},{4,5},{5,4},{6,7},{7,6},{8,9},{9,8},{10,11... | collective-permute-start | bytes 110600 | tf_op jit(solution)/shard_map/ppermute | solution.py:405
  45.4 1.2 %collective-permute-start.12 = (f32[8,128]{1,0:T(8,128)S(1)}, f32[8,128]{1,0:T(8,128)S(1)}, u32[]{:S(2)}, u32[]{:S(2)}) collective-permute-start(f32[8,128]{1,0:T(8,128)S(1)} %get-tuple-element.52), channel_id=1, source_target_pairs={{0,64},{64,128},{128,192},{192,0},{1,65},{65,129},{129,193},{193,1... | collective-permute-start | bytes 12296 | tf_op jit(solution)/shard_map/ppermute | solution.py:399
  45.6 3.3 %collective-permute-start.13 = (f32[8,128]{1,0:T(8,128)S(1)}, f32[8,128]{1,0:T(8,128)S(1)}, u32[]{:S(2)}, u32[]{:S(2)}) collective-permute-start(f32[8,128]{1,0:T(8,128)S(1)} %get-tuple-element.53), channel_id=1, source_target_pairs={{0,192},{64,0},{128,64},{192,128},{1,193},{65,1},{129,65},{193,129... | collective-permute-start | bytes 12296 | tf_op jit(solution)/shard_map/ppermute | solution.py:399
  49.0 5.9 %collective-permute-start.15 = (f32[3,24,128]{2,1,0:T(8,128)S(1)}, f32[3,24,128]{2,1,0:T(8,128)S(1)}, u32[]{:S(2)}, u32[]{:S(2)}) collective-permute-start(f32[3,24,128]{2,1,0:T(8,128)S(1)} %shard_map.103.refs_12_), channel_id=1, source_target_pairs={{0,7},{1,2},{2,1},{3,4},{4,3},{5,6},{6,5},{7,0},{8,15},{9,10},{10,... | collective-permute-start | bytes 110600 | tf_op jit(solution)/shard_map/ppermute | solution.py:405
  51.3 3.8 %collective-permute-start.14 = (f32[3,24,128]{2,1,0:T(8,128)S(1)}, f32[3,24,128]{2,1,0:T(8,128)S(1)}, u32[]{:S(2)}, u32[]{:S(2)}) collective-permute-start(f32[3,24,128]{2,1,0:T(8,128)S(1)} %get-tuple-element.55), channel_id=1, source_target_pairs={{0,1},{1,0},{2,3},{3,2},{4,5},{5,4},{6,7},{7,6},{8,9},{9,8},{10,11... | collective-permute-start | bytes 110600 | tf_op jit(solution)/shard_map/ppermute | solution.py:405
  51.4 1.2 %collective-permute-start.16 = (f32[8,128]{1,0:T(8,128)S(1)}, f32[8,128]{1,0:T(8,128)S(1)}, u32[]{:S(2)}, u32[]{:S(2)}) collective-permute-start(f32[8,128]{1,0:T(8,128)S(1)} %get-tuple-element.56), channel_id=1, source_target_pairs={{0,64},{64,128},{128,192},{192,0},{1,65},{65,129},{129,193},{193,1... | collective-permute-start | bytes 12296 | tf_op jit(solution)/shard_map/ppermute | solution.py:399
  51.8 3.1 %collective-permute-start.17 = (f32[8,128]{1,0:T(8,128)S(1)}, f32[8,128]{1,0:T(8,128)S(1)}, u32[]{:S(2)}, u32[]{:S(2)}) collective-permute-start(f32[8,128]{1,0:T(8,128)S(1)} %get-tuple-element.57), channel_id=1, source_target_pairs={{0,192},{64,0},{128,64},{192,128},{1,193},{65,1},{129,65},{193,129... | collective-permute-start | bytes 12296 | tf_op jit(solution)/shard_map/ppermute | solution.py:399

commit v9 on v8

--- a/solution.py
+++ b/solution.py
@@ -363,19 +363,51 @@
     put_rest(following, *rest)
 
 
-def last_kernel(
-    u, v, c, sources, even, odd, at_left, at_right, ar, al, au, ad, made, final, before_final
-):
-    lows, highs = radial_ends(even, odd, 3)
-    for k in range(3):
+def base_kernel(u, v, c, sources, ar, al, base, before_final):
+    for k in range(3):
+        i, jl = TABLE[k][0] // 2, TABLE[k][1] - 1
         for r in range(CR):
-            total = force(k, r, u, lows, highs, at_left, at_right, ar, al, au, ad)
-            value = 2.0 * u[k, r] - v[k, r] + c[r] * total + sources[STEPS - 2, k, r]
-            final[k, r] = value[:CL]
-            before_final[k, r] = u[k, r, 0:CL, :]
+            here = u[k, r]
+            flux = al[jl, r] * (pltpu.roll(here, ROWS - 1, 0) - here)
+            total = flux - pltpu.roll(flux, 1, 0)
+            if r < CR - 1:
+                total = total + ar[i, r + 1] * (u[k, r + 1] - here)
+            if r > 0:
+                total = total - ar[i, r] * (here - u[k, r - 1])
+            value = 2.0 * here - v[k, r] + c[r] * total + sources[STEPS - 2, k, r]
+            base[k, r] = value[:CL]
+            before_final[k, r] = here[:CL]
+
+
+def end_kernel(u, c, odd, ar, out):
     lead, _ = end_layers()
-    for k in range(3):
-        final[k, lead] = made[k, 0:CL, :]
+    rad, downwards = lax.axis_index("rad"), rad_is_even()
+    joined = jnp.where(downwards, rad > 0, rad < lax.axis_size("rad") - 1)
+    face = jnp.where(downwards, 0, CR)
+    for k in range(3):
+        outer = jnp.where(joined, odd[k, 0:CL, :], 0.0)
+        coefficient = c[lead, 0:CL, :] * ar[TABLE[k][0] // 2, face, 0:CL, :]
+        out[k] = coefficient * (outer - u[k, lead, 0:CL, :])
+
+
+def last_kernel(u, c, base, even, made, at_left, at_right, ar, au, ad, final):
+    lane = iota((CL, CE), 1)
+    for k in range(3):
+        je = TABLE[k][2] - 1
+        for r in range(CR):
+            here = u[k, r, 0:CL, :]
+            right, left = column(at_right, 0, k, r)[:CL], column(at_left, 0, k, r)[:CL]
+            after = jnp.where(lane == CE - 1, right, pltpu.roll(here, CE - 1, 1))
+            before = jnp.where(lane == 0, left, pltpu.roll(here, 1, 1))
+            total = au[je, r, 0:CL, :] * (after - here) + ad[je, r, 0:CL, :] * (before - here)
+            final[k, r] = base[k, r] + c[r, 0:CL, :] * total
+    lead, rest = end_layers()
+    face = jnp.where(rad_is_even(), CR, 0)
+    for k in range(3):
+        coefficient = c[rest, 0:CL, :] * ar[TABLE[k][0] // 2, face, 0:CL, :]
+        flux = coefficient * (even[k, 0:CL, :] - u[k, rest, 0:CL, :])
+        final[k, rest] = final[k, rest] + flux
+        final[k, lead] = final[k, lead] + made[k]
 
 
 def call(kernel, outs, args, scratch=(), hbm=0, us=1.0):
@@ -471,6 +503,15 @@
     for t in range(1, STEPS):
         even = swapped(even, "rad", 0)
         at_left, at_right = swap_columns(*ends)
+        if t == STEPS - 1:
+            ar, al, au, ad = coefficients
+            own = (3, CR, CL, CE)
+            base, before_final = call(base_kernel, [own, own], (u, v, c, sources, ar, al))
+            (made,) = call(end_kernel, [(3, CL, CE)], (u, c, odd, ar), us=0.3)
+            (final,) = call(
+                last_kernel, [own], (u, c, base, even, made, at_left, at_right, ar, au, ad)
+            )
+            return final, before_final
         before = (u, v, c, sources)
         after = (at_left, at_right, *coefficients)
 
@@ -481,9 +522,6 @@
             step_kernel(t, *refs)
 
         (made,) = call(lead, [layer], before + (odd,) + after)
-        if t == STEPS - 1:
-            args = before + (even, odd) + after + (made,)
-            return tuple(call(last_kernel, [(3, CR, CL, CE)] * 2, args))
         next_odd = swapped(made, "rad", 1)
         following, even, *ends = call(
             step, [wide, layer] + columns, before + (even, odd) + after + (made,)

time: 56.2 us -> 56 us (level)
  waiting for transfers between devices: 11.4 us -> 10.7 us
  Pallas kernels: 9.73 us -> 10.3 us
    ppermute x10, waiting for transfers between devices: 10.8 us -> 9.14 us  [shifted(): lax.ppermute(block, axis, [(i, (i + by) % count) for i in range(count)])]
    ppermute x8, waiting for transfers between devices: 0.02 us -> 1.01 us  [swapped(): return lax.ppermute(block, axis, pairs)]
    pallas_call x12 -> x13, Pallas kernels: 9.73 us -> 10.3 us  [call(): pl.pallas_call(kernel, out_shape=[jax.ShapeDtypeStruct(shape, F32) for sh...]
  transfers between devices with their start and end apart: 19 -> 19, of which waited for: 8 -> 8; matrix products, arithmetic and copies ran while one was open for 0% -> 0% of each run, Pallas kernels for 12% -> 13%
where the time goes in v9:
time: 56 us; the launch traced here: 55.8 us
  starting transfers between devices  34 us (61%)
  waiting for transfers between devices  10.7 us (19%)
  Pallas kernels  10.3 us (18%)
  between operations  0.81 us (1%)
    ppermute x10, starting transfers between devices, shifted(): lax.ppermute(block, axis, [(i, (i + by) % count) for i in range(count)])  13.5 us
    all_to_all x1, starting transfers between devices, on_device(): got = lax.all_to_all(packed, ('lat', 'rad'), 0, 0, tiled=True)  12.1 us
    pallas_call x13, Pallas kernels, call(): pl.pallas_call(kernel, out_shape=[jax.ShapeDtypeStruct(shape, F32) for sh...  10.3 us
    ppermute x10, waiting for transfers between devices, shifted(): lax.ppermute(block, axis, [(i, (i + by) % count) for i in range(count)])  9.14 us
    ppermute x8, starting transfers between devices, swapped(): return lax.ppermute(block, axis, pairs)  8.43 us
  transfers between devices with their start and end apart: 19, of which 8 were waited for; matrix products, arithmetic and copies ran while one was open for 0% of the time, Pallas kernels for 13%

profile of v9, /device:TPU:1, one launch (start us, length us, event | category | flops | bytes accessed | tf_op | source)
XLA Modules:
  0.0 55.8 jit_solution(16577958956230882542)
XLA Ops:
  0.6 1.6 %shard_map.96 = f32[11,2,8,128]{3,2,1,0:T(8,128)} custom-call(f32[3,4,16,128]{3,2,1,0:T(8,128)} %cur.5, f32[3,4,16,128]{3,2,1,0:T(8,128)} %prv.5, f32[4,4,16,128]{3,2,1,0:T(8,128)} %mod.5, f32[1,4,16,128]{3,2,1,0:T(8,128)} %bitcast.5), custom_call_target="tpu_custom_call" | custom-call | bytes 3000000 | tf_op jit(solution)/shard_map/pallas_call | solution.py:416
  2.2 3.8 %collective-permute-start = (f32[11,2,8,128]{3,2,1,0:T(8,128)}, f32[11,2,8,128]{3,2,1,0:T(8,128)S(1)}, u32[]{:S(2)}, u32[]{:S(2)}) collective-permute-start(f32[11,2,8,128]{3,2,1,0:T(8,128)} %shard_map.96), channel_id=1, source_target_pairs={{0,8},{8,16},{16,24},{24,32},{32,40},{40,48},{48,56},{56,0},{1,9},... | collective-permute-start | bytes 270344 | tf_op jit(solution)/shard_map/ppermute | solution.py:431
  6.1 2.8 %shard_map.95 = (f32[64,1,256]{2,1,0:T(1,128)}, f32[11,2,8,128]{3,2,1,0:T(8,128)}) custom-call(s32[1,128]{1,0:T(1,128)} %bitcast.8, s32[1,128]{1,0:T(1,128)} %bitcast.9, s32[1,128]{1,0:T(1,128)} %bitcast.10, f32[3,128,512]{2,1,0:T(8,128)} %bitcast.7, f32[3,4,16,128]{3,2,1,0:T(8,128)} %cur.5, f32[3,4,16,128]{3,2,1,0:T(8,128)} %prv.5, f32[4,4,16,128]{3,2,1,0:T(8,128)} %mod.5, ...), custom_call_target="tpu_custom_call" | custom-call | bytes 6000000 | tf_op jit(solution)/shard_map/pallas_call | solution.py:416
  8.9 2.3 %collective-permute-start.1 = (f32[11,2,8,128]{3,2,1,0:T(8,128)}, f32[11,2,8,128]{3,2,1,0:T(8,128)S(1)}, u32[]{:S(2)}, u32[]{:S(2)}) collective-permute-start(f32[11,2,8,128]{3,2,1,0:T(8,128)} %get-tuple-element.33), channel_id=1, source_target_pairs={{0,56},{8,0},{16,8},{24,16},{32,24},{40,32},{48,40},{56,48},{1,57}... | collective-permute-start | bytes 270344 | tf_op jit(solution)/shard_map/ppermute | solution.py:431
  11.2 12.1 %all-to-all-start = ((f32[64,1,256]{2,1,0:T(1,128)}), f32[64,1,256]{2,1,0:T(1,128)S(1)}, u32[]{:S(2)}, u32[]{:S(2)}) async-start(f32[64,1,256]{2,1,0:T(1,128)} %get-tuple-element.32), calls=%async_computation | async-start | bytes 131072 | tf_op jit(solution)/shard_map/all_to_all | solution.py:474
  23.7 1.1 %collective-permute-start.2 = (f32[5,24,128]{2,1,0:T(8,128)S(1)}, f32[5,24,128]{2,1,0:T(8,128)S(1)}, u32[]{:S(2)}, u32[]{:S(2)}) collective-permute-start(f32[5,24,128]{2,1,0:T(8,128)S(1)} %get-tuple-element.38), channel_id=1, source_target_pairs={{0,1},{1,0},{2,3},{3,2},{4,5},{5,4},{6,7},{7,6},{8,9},{9,8},{10,11... | collective-permute-start | bytes 184328 | tf_op jit(solution)/shard_map/ppermute | solution.py:437
  24.8 2.4 %collective-permute-start.3 = (f32[5,24,128]{2,1,0:T(8,128)S(1)}, f32[5,24,128]{2,1,0:T(8,128)S(1)}, u32[]{:S(2)}, u32[]{:S(2)}) collective-permute-start(f32[5,24,128]{2,1,0:T(8,128)S(1)} %get-tuple-element.39), channel_id=1, source_target_pairs={{0,7},{1,2},{2,1},{3,4},{4,3},{5,6},{6,5},{7,0},{8,15},{9,10},{10,... | collective-permute-start | bytes 184328 | tf_op jit(solution)/shard_map/ppermute | solution.py:437
  27.2 2.6 %collective-permute-start.4 = (f32[8,128]{1,0:T(8,128)S(1)}, f32[8,128]{1,0:T(8,128)S(1)}, u32[]{:S(2)}, u32[]{:S(2)}) collective-permute-start(f32[8,128]{1,0:T(8,128)S(1)} %get-tuple-element.40), channel_id=1, source_target_pairs={{0,64},{64,128},{128,192},{192,0},{1,65},{65,129},{129,193},{193,1... | collective-permute-start | bytes 12296 | tf_op jit(solution)/shard_map/ppermute | solution.py:431
  29.8 0.8 %collective-permute-done.4.at_left = f32[8,128]{1,0:T(8,128)S(1)} collective-permute-done((f32[8,128]{1,0:T(8,128)S(1)}, f32[8,128]{1,0:T(8,128)S(1)}, u32[]{:S(2)}, u32[]{:S(2)}) %collective-permute-start.4) | collective-permute-done | bytes 4128 | tf_op jit(solution)/shard_map/ppermute | solution.py:431
  30.6 2.6 %collective-permute-done.5.at_right = f32[8,128]{1,0:T(8,128)S(1)} collective-permute-done((f32[8,128]{1,0:T(8,128)S(1)}, f32[8,128]{1,0:T(8,128)S(1)}, u32[]{:S(2)}, u32[]{:S(2)}) %collective-permute-start.5) | collective-permute-done | bytes 4128 | tf_op jit(solution)/shard_map/ppermute | solution.py:431
  33.1 0.6 %shard_map.98 = (f32[2,5,24,128]{3,2,1,0:T(8,128)S(1)}, f32[3,4,24,128]{3,2,1,0:T(8,128)S(1)}, f32[3,4,24,128]{3,2,1,0:T(8,128)S(1)}, f32[3,4,24,128]{3,2,1,0:T(8,128)S(1)}, f32[3,4,24,128]{3,2,1,0:T(8,128)S(1)}) custom-call(f32[3,4,24,128]{3,2,1,0:T(8,128)S(1)} %get-tuple-element.34.u.refs_1_, f32[3,4,24,128]{3,2,1,0:T(8,128)S(1)} %get-tuple-element.35.v, ...), custom_call_target="tpu_custom_call" | custom-call | bytes 3000000 | tf_op jit(solution)/shard_map/pallas_call | solution.py:416
  34.3 0.7 %shard_map.99 = (f32[3,4,24,128]{3,2,1,0:T(8,128)S(1)}, f32[3,24,128]{2,1,0:T(8,128)S(1)}, f32[3,24,128]{2,1,0:T(8,128)S(1)}, f32[8,128]{1,0:T(8,128)S(1)}, f32[8,128]{1,0:T(8,128)S(1)}) custom-call(f32[64,1,256]{2,1,0:T(1,128)S(1)} %all-to-all-done.got, f32[3,4,24,128]{3,2,1,0:T(8,128)S(1)} %get-tuple-element.42.free, ...), custom_call_target="tpu_custom_call" | custom-call | bytes 3000000 | tf_op jit(solution)/shard_map/pallas_call | solution.py:416
  35.1 0.8 %collective-permute-start.7 = (f32[3,24,128]{2,1,0:T(8,128)S(1)}, f32[3,24,128]{2,1,0:T(8,128)S(1)}, u32[]{:S(2)}, u32[]{:S(2)}) collective-permute-start(f32[3,24,128]{2,1,0:T(8,128)S(1)} %get-tuple-element.45), channel_id=1, source_target_pairs={{0,7},{1,2},{2,1},{3,4},{4,3},{5,6},{6,5},{7,0},{8,15},{9,10},{10,... | collective-permute-start | bytes 110600 | tf_op jit(solution)/shard_map/ppermute | solution.py:437
  36.2 3.5 %collective-permute-start.8 = (f32[8,128]{1,0:T(8,128)S(1)}, f32[8,128]{1,0:T(8,128)S(1)}, u32[]{:S(2)}, u32[]{:S(2)}) collective-permute-start(f32[8,128]{1,0:T(8,128)S(1)} %get-tuple-element.46), channel_id=1, source_target_pairs={{0,64},{64,128},{128,192},{192,0},{1,65},{65,129},{129,193},{193,1... | collective-permute-start | bytes 12296 | tf_op jit(solution)/shard_map/ppermute | solution.py:431
  39.7 1.3 %shard_map.100.refs_3_.sources = f32[3,3,4,24,128]{4,3,2,1,0:T(8,128)S(1)} custom-call(f32[64,1,256]{2,1,0:T(1,128)S(1)} %all-to-all-done.got, f32[4,24,128]{2,1,0:T(8,128)S(1)} %get-tuple-element.37.c.refs_2_), custom_call_target="tpu_custom_call" | custom-call | bytes 9000000 | tf_op jit(solution)/shard_map/pallas_call | solution.py:416
  41.1 1.7 %collective-permute-done.9.refs_6_.refs_7_ = f32[8,128]{1,0:T(8,128)S(1)} collective-permute-done((f32[8,128]{1,0:T(8,128)S(1)}, f32[8,128]{1,0:T(8,128)S(1)}, u32[]{:S(2)}, u32[]{:S(2)}) %collective-permute-start.9) | collective-permute-done | bytes 4128 | tf_op jit(solution)/shard_map/ppermute | solution.py:431
  42.9 1.9 %collective-permute-start.11 = (f32[3,24,128]{2,1,0:T(8,128)S(1)}, f32[3,24,128]{2,1,0:T(8,128)S(1)}, u32[]{:S(2)}, u32[]{:S(2)}) collective-permute-start(f32[3,24,128]{2,1,0:T(8,128)S(1)} %shard_map.101.refs_12_), channel_id=1, source_target_pairs={{0,7},{1,2},{2,1},{3,4},{4,3},{5,6},{6,5},{7,0},{8,15},{9,10},{10,... | collective-permute-start | bytes 110600 | tf_op jit(solution)/shard_map/ppermute | solution.py:437
  46.0 0.7 %collective-permute-done.12.refs_5_.refs_6_ = f32[8,128]{1,0:T(8,128)S(1)} collective-permute-done((f32[8,128]{1,0:T(8,128)S(1)}, f32[8,128]{1,0:T(8,128)S(1)}, u32[]{:S(2)}, u32[]{:S(2)}) %collective-permute-start.12) | collective-permute-done | bytes 4128 | tf_op jit(solution)/shard_map/ppermute | solution.py:431
  46.6 2.2 %collective-permute-done.13.refs_6_.refs_7_ = f32[8,128]{1,0:T(8,128)S(1)} collective-permute-done((f32[8,128]{1,0:T(8,128)S(1)}, f32[8,128]{1,0:T(8,128)S(1)}, u32[]{:S(2)}, u32[]{:S(2)}) %collective-permute-start.13) | collective-permute-done | bytes 4128 | tf_op jit(solution)/shard_map/ppermute | solution.py:431
  49.0 1.8 %collective-permute-start.15 = (f32[3,24,128]{2,1,0:T(8,128)S(1)}, f32[3,24,128]{2,1,0:T(8,128)S(1)}, u32[]{:S(2)}, u32[]{:S(2)}) collective-permute-start(f32[3,24,128]{2,1,0:T(8,128)S(1)} %shard_map.103.refs_12_), channel_id=1, source_target_pairs={{0,7},{1,2},{2,1},{3,4},{4,3},{5,6},{6,5},{7,0},{8,15},{9,10},{10,... | collective-permute-start | bytes 110600 | tf_op jit(solution)/shard_map/ppermute | solution.py:437
  52.0 0.7 %shard_map.105 = (f32[3,4,16,128]{3,2,1,0:T(8,128)S(1)}, f32[3,4,16,128]{3,2,1,0:T(8,128)}) custom-call(f32[3,4,24,128]{3,2,1,0:T(8,128)S(1)} %get-tuple-element.56.u, f32[3,4,24,128]{3,2,1,0:T(8,128)S(1)} %get-tuple-element.52.refs_0_.v, f32[4,24,128]{2,1,0:T(8,128)S(1)} %get-tuple-element.37.c.refs_2_, ...), custom_call_target="tpu_custom_call" | custom-call | bytes 3000000 | tf_op jit(solution)/shard_map/pallas_call | solution.py:416
  52.7 1.0 %collective-permute-done.15.odd = f32[3,24,128]{2,1,0:T(8,128)S(1)} collective-permute-done((f32[3,24,128]{2,1,0:T(8,128)S(1)}, f32[3,24,128]{2,1,0:T(8,128)S(1)}, u32[]{:S(2)}, u32[]{:S(2)}) %collective-permute-start.15) | collective-permute-done | bytes 36896 | tf_op jit(solution)/shard_map/ppermute | solution.py:437
  53.7 1.2 %collective-permute-done.17.at_right = f32[8,128]{1,0:T(8,128)S(1)} collective-permute-done((f32[8,128]{1,0:T(8,128)S(1)}, f32[8,128]{1,0:T(8,128)S(1)}, u32[]{:S(2)}, u32[]{:S(2)}) %collective-permute-start.17) | collective-permute-done | bytes 4128 | tf_op jit(solution)/shard_map/ppermute | solution.py:431
  54.9 0.9 %shard_map.107 = f32[3,4,16,128]{3,2,1,0:T(8,128)} custom-call(f32[3,4,24,128]{3,2,1,0:T(8,128)S(1)} %get-tuple-element.56.u, f32[4,24,128]{2,1,0:T(8,128)S(1)} %get-tuple-element.37.c.refs_2_, f32[3,4,16,128]{3,2,1,0:T(8,128)S(1)} %get-tuple-element.57.base, f32[3,24,128]{2,1,0:T(8,128)S(1)} %collective-permute-done.14.even, ...), custom_call_target="tpu_custom_call" | custom-call | bytes 3000000 | tf_op jit(solution)/shard_map/pallas_call | solution.py:416
  (35 shorter events, 3.9 us)
Async XLA Ops:
  2.2 21.1 %collective-permute-start = (f32[11,2,8,128]{3,2,1,0:T(8,128)}, f32[11,2,8,128]{3,2,1,0:T(8,128)S(1)}, u32[]{:S(2)}, u32[]{:S(2)}) collective-permute-start(f32[11,2,8,128]{3,2,1,0:T(8,128)} %shard_map.96), channel_id=1, source_target_pairs={{0,8},{8,16},{16,24},{24,32},{32,40},{40,48},{48,56},{56,0},{1,9},... | collective-permute-start | bytes 270344 | tf_op jit(solution)/shard_map/ppermute | solution.py:431
  6.0 17.3 %copy-start.1 = (f32[3,4,16,128]{3,2,1,0:T(8,128)S(1)}, f32[3,4,16,128]{3,2,1,0:T(8,128)}, u32[]{:S(2)}) copy-start(f32[3,4,16,128]{3,2,1,0:T(8,128)} %cur.5) | copy-start | bytes 294916
  6.0 17.3 %copy-start.2 = (f32[3,4,16,128]{3,2,1,0:T(8,128)S(1)}, f32[3,4,16,128]{3,2,1,0:T(8,128)}, u32[]{:S(2)}) copy-start(f32[3,4,16,128]{3,2,1,0:T(8,128)} %prv.5) | copy-start | bytes 294916
  6.1 17.3 %copy-start.3 = (f32[4,16,128]{2,1,0:T(8,128)S(1)}, f32[4,16,128]{2,1,0:T(8,128)}, u32[]{:S(2)}) copy-start(f32[4,16,128]{2,1,0:T(8,128)} %den.1) | copy-start | bytes 98308
  8.9 14.5 %copy-start = (f32[4,4,16,128]{3,2,1,0:T(8,128)S(1)}, f32[4,4,16,128]{3,2,1,0:T(8,128)}, u32[]{:S(2)}) copy-start(f32[4,4,16,128]{3,2,1,0:T(8,128)} %mod.5) | copy-start | bytes 393220
  8.9 14.4 %collective-permute-start.1 = (f32[11,2,8,128]{3,2,1,0:T(8,128)}, f32[11,2,8,128]{3,2,1,0:T(8,128)S(1)}, u32[]{:S(2)}, u32[]{:S(2)}) collective-permute-start(f32[11,2,8,128]{3,2,1,0:T(8,128)} %get-tuple-element.33), channel_id=1, source_target_pairs={{0,56},{8,0},{16,8},{24,16},{32,24},{40,32},{48,40},{56,48},{1,57}... | collective-permute-start | bytes 270344 | tf_op jit(solution)/shard_map/ppermute | solution.py:431
  11.2 23.1 %all-to-all-start = ((f32[64,1,256]{2,1,0:T(1,128)}), f32[64,1,256]{2,1,0:T(1,128)S(1)}, u32[]{:S(2)}, u32[]{:S(2)}) async-start(f32[64,1,256]{2,1,0:T(1,128)} %get-tuple-element.32), calls=%async_computation | async-start | bytes 131072 | tf_op jit(solution)/shard_map/all_to_all | solution.py:474
  23.7 9.5 %collective-permute-start.2 = (f32[5,24,128]{2,1,0:T(8,128)S(1)}, f32[5,24,128]{2,1,0:T(8,128)S(1)}, u32[]{:S(2)}, u32[]{:S(2)}) collective-permute-start(f32[5,24,128]{2,1,0:T(8,128)S(1)} %get-tuple-element.38), channel_id=1, source_target_pairs={{0,1},{1,0},{2,3},{3,2},{4,5},{5,4},{6,7},{7,6},{8,9},{9,8},{10,11... | collective-permute-start | bytes 184328 | tf_op jit(solution)/shard_map/ppermute | solution.py:437
  24.8 8.4 %collective-permute-start.3 = (f32[5,24,128]{2,1,0:T(8,128)S(1)}, f32[5,24,128]{2,1,0:T(8,128)S(1)}, u32[]{:S(2)}, u32[]{:S(2)}) collective-permute-start(f32[5,24,128]{2,1,0:T(8,128)S(1)} %get-tuple-element.39), channel_id=1, source_target_pairs={{0,7},{1,2},{2,1},{3,4},{4,3},{5,6},{6,5},{7,0},{8,15},{9,10},{10,... | collective-permute-start | bytes 184328 | tf_op jit(solution)/shard_map/ppermute | solution.py:437
  27.2 3.4 %collective-permute-start.4 = (f32[8,128]{1,0:T(8,128)S(1)}, f32[8,128]{1,0:T(8,128)S(1)}, u32[]{:S(2)}, u32[]{:S(2)}) collective-permute-start(f32[8,128]{1,0:T(8,128)S(1)} %get-tuple-element.40), channel_id=1, source_target_pairs={{0,64},{64,128},{128,192},{192,0},{1,65},{65,129},{129,193},{193,1... | collective-permute-start | bytes 12296 | tf_op jit(solution)/shard_map/ppermute | solution.py:431
  29.8 3.3 %collective-permute-start.5 = (f32[8,128]{1,0:T(8,128)S(1)}, f32[8,128]{1,0:T(8,128)S(1)}, u32[]{:S(2)}, u32[]{:S(2)}) collective-permute-start(f32[8,128]{1,0:T(8,128)S(1)} %get-tuple-element.41), channel_id=1, source_target_pairs={{0,192},{64,0},{128,64},{192,128},{1,193},{65,1},{129,65},{193,129... | collective-permute-start | bytes 12296 | tf_op jit(solution)/shard_map/ppermute | solution.py:431
  35.1 7.7 %collective-permute-start.7 = (f32[3,24,128]{2,1,0:T(8,128)S(1)}, f32[3,24,128]{2,1,0:T(8,128)S(1)}, u32[]{:S(2)}, u32[]{:S(2)}) collective-permute-start(f32[3,24,128]{2,1,0:T(8,128)S(1)} %get-tuple-element.45), channel_id=1, source_target_pairs={{0,7},{1,2},{2,1},{3,4},{4,3},{5,6},{6,5},{7,0},{8,15},{9,10},{10,... | collective-permute-start | bytes 110600 | tf_op jit(solution)/shard_map/ppermute | solution.py:437
  35.8 9.0 %collective-permute-start.6 = (f32[3,24,128]{2,1,0:T(8,128)S(1)}, f32[3,24,128]{2,1,0:T(8,128)S(1)}, u32[]{:S(2)}, u32[]{:S(2)}) collective-permute-start(f32[3,24,128]{2,1,0:T(8,128)S(1)} %get-tuple-element.44), channel_id=1, source_target_pairs={{0,1},{1,0},{2,3},{3,2},{4,5},{5,4},{6,7},{7,6},{8,9},{9,8},{10,11... | collective-permute-start | bytes 110600 | tf_op jit(solution)/shard_map/ppermute | solution.py:437
  36.2 4.9 %collective-permute-start.8 = (f32[8,128]{1,0:T(8,128)S(1)}, f32[8,128]{1,0:T(8,128)S(1)}, u32[]{:S(2)}, u32[]{:S(2)}) collective-permute-start(f32[8,128]{1,0:T(8,128)S(1)} %get-tuple-element.46), channel_id=1, source_target_pairs={{0,64},{64,128},{128,192},{192,0},{1,65},{65,129},{129,193},{193,1... | collective-permute-start | bytes 12296 | tf_op jit(solution)/shard_map/ppermute | solution.py:431
  39.7 3.0 %collective-permute-start.9 = (f32[8,128]{1,0:T(8,128)S(1)}, f32[8,128]{1,0:T(8,128)S(1)}, u32[]{:S(2)}, u32[]{:S(2)}) collective-permute-start(f32[8,128]{1,0:T(8,128)S(1)} %get-tuple-element.47), channel_id=1, source_target_pairs={{0,192},{64,0},{128,64},{192,128},{1,193},{65,1},{129,65},{193,129... | collective-permute-start | bytes 12296 | tf_op jit(solution)/shard_map/ppermute | solution.py:431
  42.9 6.0 %collective-permute-start.11 = (f32[3,24,128]{2,1,0:T(8,128)S(1)}, f32[3,24,128]{2,1,0:T(8,128)S(1)}, u32[]{:S(2)}, u32[]{:S(2)}) collective-permute-start(f32[3,24,128]{2,1,0:T(8,128)S(1)} %shard_map.101.refs_12_), channel_id=1, source_target_pairs={{0,7},{1,2},{2,1},{3,4},{4,3},{5,6},{6,5},{7,0},{8,15},{9,10},{10,... | collective-permute-start | bytes 110600 | tf_op jit(solution)/shard_map/ppermute | solution.py:437
  45.3 5.5 %collective-permute-start.10 = (f32[3,24,128]{2,1,0:T(8,128)S(1)}, f32[3,24,128]{2,1,0:T(8,128)S(1)}, u32[]{:S(2)}, u32[]{:S(2)}) collective-permute-start(f32[3,24,128]{2,1,0:T(8,128)S(1)} %get-tuple-element.53), channel_id=1, source_target_pairs={{0,1},{1,0},{2,3},{3,2},{4,5},{5,4},{6,7},{7,6},{8,9},{9,8},{10,11... | collective-permute-start | bytes 110600 | tf_op jit(solution)/shard_map/ppermute | solution.py:437
  45.4 1.2 %collective-permute-start.12 = (f32[8,128]{1,0:T(8,128)S(1)}, f32[8,128]{1,0:T(8,128)S(1)}, u32[]{:S(2)}, u32[]{:S(2)}) collective-permute-start(f32[8,128]{1,0:T(8,128)S(1)} %get-tuple-element.54), channel_id=1, source_target_pairs={{0,64},{64,128},{128,192},{192,0},{1,65},{65,129},{129,193},{193,1... | collective-permute-start | bytes 12296 | tf_op jit(solution)/shard_map/ppermute | solution.py:431
  45.6 3.3 %collective-permute-start.13 = (f32[8,128]{1,0:T(8,128)S(1)}, f32[8,128]{1,0:T(8,128)S(1)}, u32[]{:S(2)}, u32[]{:S(2)}) collective-permute-start(f32[8,128]{1,0:T(8,128)S(1)} %get-tuple-element.55), channel_id=1, source_target_pairs={{0,192},{64,0},{128,64},{192,128},{1,193},{65,1},{129,65},{193,129... | collective-permute-start | bytes 12296 | tf_op jit(solution)/shard_map/ppermute | solution.py:431
  49.0 4.6 %collective-permute-start.15 = (f32[3,24,128]{2,1,0:T(8,128)S(1)}, f32[3,24,128]{2,1,0:T(8,128)S(1)}, u32[]{:S(2)}, u32[]{:S(2)}) collective-permute-start(f32[3,24,128]{2,1,0:T(8,128)S(1)} %shard_map.103.refs_12_), channel_id=1, source_target_pairs={{0,7},{1,2},{2,1},{3,4},{4,3},{5,6},{6,5},{7,0},{8,15},{9,10},{10,... | collective-permute-start | bytes 110600 | tf_op jit(solution)/shard_map/ppermute | solution.py:437
  51.3 3.6 %collective-permute-start.14 = (f32[3,24,128]{2,1,0:T(8,128)S(1)}, f32[3,24,128]{2,1,0:T(8,128)S(1)}, u32[]{:S(2)}, u32[]{:S(2)}) collective-permute-start(f32[3,24,128]{2,1,0:T(8,128)S(1)} %get-tuple-element.58), channel_id=1, source_target_pairs={{0,1},{1,0},{2,3},{3,2},{4,5},{5,4},{6,7},{7,6},{8,9},{9,8},{10,11... | collective-permute-start | bytes 110600 | tf_op jit(solution)/shard_map/ppermute | solution.py:437
  51.4 2.3 %collective-permute-start.16 = (f32[8,128]{1,0:T(8,128)S(1)}, f32[8,128]{1,0:T(8,128)S(1)}, u32[]{:S(2)}, u32[]{:S(2)}) collective-permute-start(f32[8,128]{1,0:T(8,128)S(1)} %get-tuple-element.59), channel_id=1, source_target_pairs={{0,64},{64,128},{128,192},{192,0},{1,65},{65,129},{129,193},{193,1... | collective-permute-start | bytes 12296 | tf_op jit(solution)/shard_map/ppermute | solution.py:431
  51.8 3.1 %collective-permute-start.17 = (f32[8,128]{1,0:T(8,128)S(1)}, f32[8,128]{1,0:T(8,128)S(1)}, u32[]{:S(2)}, u32[]{:S(2)}) collective-permute-start(f32[8,128]{1,0:T(8,128)S(1)} %get-tuple-element.60), channel_id=1, source_target_pairs={{0,192},{64,0},{128,64},{192,128},{1,193},{65,1},{129,65},{193,129... | collective-permute-start | bytes 12296 | tf_op jit(solution)/shard_map/ppermute | solution.py:431

commit v10 on v8

--- a/solution.py
+++ b/solution.py
@@ -259,6 +259,13 @@
         lows.append(jnp.where(rad > 0, low, 0.0))
         highs.append(jnp.where(rad < lax.axis_size("rad") - 1, high, 0.0))
     return lows, highs
+
+
+def joined_kernel(odd, out):
+    rad = lax.axis_index("rad")
+    joined = jnp.where(rad_is_even(), rad > 0, rad < lax.axis_size("rad") - 1)
+    for k in range(odd.shape[0]):
+        out[k] = jnp.where(joined, odd[k], 0.0)
 
 
 def prepare_kernel(u, v, m, c, even, odd, at_left, at_right, ar, al, au, ad, following):
@@ -447,10 +454,12 @@
         + [(5, ROWS, CE), (5, ROWS, CE), (8, CE), (8, CE)],
         (current, previous, moduli, density, from_low, from_high),
     )
+    even, odd = swapped(even, "rad", 0), swapped(odd, "rad", 1)
+    (odd,) = call(joined_kernel, [(5, ROWS, CE)], (odd,), us=0.3)
     *coefficients, free = call(
         prepare_kernel,
         [(2, CR + 1, ROWS, CE), wide, wide, wide, wide],
-        (u, v, m, c, swapped(even, "rad", 0), swapped(odd, "rad", 1), *swap_columns(*ends)),
+        (u, v, m, c, even, odd, *swap_columns(*ends)),
     )
     cells, lanes = CR * ROWS, 3 * SLOTS * 128
     first, even, odd, *ends = call(

time: 56.2 us -> 56.2 us (level)
  waiting for transfers between devices: 11.4 us -> 12.6 us
  starting transfers between devices: 34 us -> 32.9 us
    all_to_all x1, waiting for transfers between devices: 0.53 us -> 1.76 us  [on_device(): got = lax.all_to_all(packed, ('lat', 'rad'), 0, 0, tiled=True)]
    ppermute x10, starting transfers between devices: 13.5 us -> 12.6 us  [shifted(): lax.ppermute(block, axis, [(i, (i + by) % count) for i in range(count)])]
    pallas_call x12 -> x13, Pallas kernels: 9.73 us -> 9.73 us  [call(): pl.pallas_call(kernel, out_shape=[jax.ShapeDtypeStruct(shape, F32) for sh...]
where the time goes in v10:
time: 56.2 us; the launch traced here: 56 us
  starting transfers between devices  32.9 us (59%)
  waiting for transfers between devices  12.6 us (22%)
  Pallas kernels  9.73 us (17%)
  between operations  0.81 us (1%)
    ppermute x10, starting transfers between devices, shifted(): lax.ppermute(block, axis, [(i, (i + by) % count) for i in range(count)])  12.6 us
    all_to_all x1, starting transfers between devices, on_device(): got = lax.all_to_all(packed, ('lat', 'rad'), 0, 0, tiled=True)  12.1 us
    ppermute x10, waiting for transfers between devices, shifted(): lax.ppermute(block, axis, [(i, (i + by) % count) for i in range(count)])  10.8 us
    pallas_call x13, Pallas kernels, call(): pl.pallas_call(kernel, out_shape=[jax.ShapeDtypeStruct(shape, F32) for sh...  9.73 us
    ppermute x8, starting transfers between devices, swapped(): return lax.ppermute(block, axis, pairs)  8.15 us
    all_to_all x1, waiting for transfers between devices, on_device(): got = lax.all_to_all(packed, ('lat', 'rad'), 0, 0, tiled=True)  1.76 us
  transfers between devices with their start and end apart: 19, of which 8 were waited for; matrix products, arithmetic and copies ran while one was open for 0% of the time, Pallas kernels for 12%

profile of v10, /device:TPU:1, one launch (start us, length us, event | category | flops | bytes accessed | tf_op | source)
XLA Modules:
  0.0 56.0 jit_solution(3155304217185536973)
XLA Ops:
  0.6 1.6 %shard_map.96 = f32[11,2,8,128]{3,2,1,0:T(8,128)} custom-call(f32[3,4,16,128]{3,2,1,0:T(8,128)} %cur.5, f32[3,4,16,128]{3,2,1,0:T(8,128)} %prv.5, f32[4,4,16,128]{3,2,1,0:T(8,128)} %mod.5, f32[1,4,16,128]{3,2,1,0:T(8,128)} %bitcast.5), custom_call_target="tpu_custom_call" | custom-call | bytes 3000000 | tf_op jit(solution)/shard_map/pallas_call | solution.py:391
  2.2 3.8 %collective-permute-start = (f32[11,2,8,128]{3,2,1,0:T(8,128)}, f32[11,2,8,128]{3,2,1,0:T(8,128)S(1)}, u32[]{:S(2)}, u32[]{:S(2)}) collective-permute-start(f32[11,2,8,128]{3,2,1,0:T(8,128)} %shard_map.96), channel_id=1, source_target_pairs={{0,8},{8,16},{16,24},{24,32},{32,40},{40,48},{48,56},{56,0},{1,9},... | collective-permute-start | bytes 270344 | tf_op jit(solution)/shard_map/ppermute | solution.py:406
  6.1 2.8 %shard_map.95 = (f32[64,1,256]{2,1,0:T(1,128)}, f32[11,2,8,128]{3,2,1,0:T(8,128)}) custom-call(s32[1,128]{1,0:T(1,128)} %bitcast.8, s32[1,128]{1,0:T(1,128)} %bitcast.9, s32[1,128]{1,0:T(1,128)} %bitcast.10, f32[3,128,512]{2,1,0:T(8,128)} %bitcast.7, f32[3,4,16,128]{3,2,1,0:T(8,128)} %cur.5, f32[3,4,16,128]{3,2,1,0:T(8,128)} %prv.5, f32[4,4,16,128]{3,2,1,0:T(8,128)} %mod.5, ...), custom_call_target="tpu_custom_call" | custom-call | bytes 6000000 | tf_op jit(solution)/shard_map/pallas_call | solution.py:391
  8.9 2.3 %collective-permute-start.1 = (f32[11,2,8,128]{3,2,1,0:T(8,128)}, f32[11,2,8,128]{3,2,1,0:T(8,128)S(1)}, u32[]{:S(2)}, u32[]{:S(2)}) collective-permute-start(f32[11,2,8,128]{3,2,1,0:T(8,128)} %get-tuple-element.31), channel_id=1, source_target_pairs={{0,56},{8,0},{16,8},{24,16},{32,24},{40,32},{48,40},{56,48},{1,57}... | collective-permute-start | bytes 270344 | tf_op jit(solution)/shard_map/ppermute | solution.py:406
  11.2 12.1 %all-to-all-start = ((f32[64,1,256]{2,1,0:T(1,128)}), f32[64,1,256]{2,1,0:T(1,128)S(1)}, u32[]{:S(2)}, u32[]{:S(2)}) async-start(f32[64,1,256]{2,1,0:T(1,128)} %get-tuple-element.30), calls=%async_computation | async-start | bytes 131072 | tf_op jit(solution)/shard_map/all_to_all | solution.py:449
  23.7 2.3 %collective-permute-start.3 = (f32[5,24,128]{2,1,0:T(8,128)S(1)}, f32[5,24,128]{2,1,0:T(8,128)S(1)}, u32[]{:S(2)}, u32[]{:S(2)}) collective-permute-start(f32[5,24,128]{2,1,0:T(8,128)S(1)} %get-tuple-element.37), channel_id=1, source_target_pairs={{0,7},{1,2},{2,1},{3,4},{4,3},{5,6},{6,5},{7,0},{8,15},{9,10},{10,... | collective-permute-start | bytes 184328 | tf_op jit(solution)/shard_map/ppermute | solution.py:412
  26.0 2.6 %collective-permute-start.4 = (f32[8,128]{1,0:T(8,128)S(1)}, f32[8,128]{1,0:T(8,128)S(1)}, u32[]{:S(2)}, u32[]{:S(2)}) collective-permute-start(f32[8,128]{1,0:T(8,128)S(1)} %get-tuple-element.38), channel_id=1, source_target_pairs={{0,64},{64,128},{128,192},{192,0},{1,65},{65,129},{129,193},{193,1... | collective-permute-start | bytes 12296 | tf_op jit(solution)/shard_map/ppermute | solution.py:406
  28.6 0.7 %collective-permute-done.4.at_left = f32[8,128]{1,0:T(8,128)S(1)} collective-permute-done((f32[8,128]{1,0:T(8,128)S(1)}, f32[8,128]{1,0:T(8,128)S(1)}, u32[]{:S(2)}, u32[]{:S(2)}) %collective-permute-start.4) | collective-permute-done | bytes 4128 | tf_op jit(solution)/shard_map/ppermute | solution.py:406
  29.3 2.6 %collective-permute-done.5.at_right = f32[8,128]{1,0:T(8,128)S(1)} collective-permute-done((f32[8,128]{1,0:T(8,128)S(1)}, f32[8,128]{1,0:T(8,128)S(1)}, u32[]{:S(2)}, u32[]{:S(2)}) %collective-permute-start.5) | collective-permute-done | bytes 4128 | tf_op jit(solution)/shard_map/ppermute | solution.py:406
  31.9 0.6 %shard_map.99 = (f32[2,5,24,128]{3,2,1,0:T(8,128)S(1)}, f32[3,4,24,128]{3,2,1,0:T(8,128)S(1)}, f32[3,4,24,128]{3,2,1,0:T(8,128)S(1)}, f32[3,4,24,128]{3,2,1,0:T(8,128)S(1)}, f32[3,4,24,128]{3,2,1,0:T(8,128)S(1)}) custom-call(f32[3,4,24,128]{3,2,1,0:T(8,128)S(1)} %get-tuple-element.32.u.refs_1_, f32[3,4,24,128]{3,2,1,0:T(8,128)S(1)} %get-tuple-element.33.v, ...), custom_call_target="tpu_custom_call" | custom-call | bytes 3000000 | tf_op jit(solution)/shard_map/pallas_call | solution.py:391
  32.5 1.8 %all-to-all-done.got = f32[64,1,256]{2,1,0:T(1,128)S(1)} async-done(((f32[64,1,256]{2,1,0:T(1,128)}), f32[64,1,256]{2,1,0:T(1,128)S(1)}, u32[]{:S(2)}, u32[]{:S(2)}) %all-to-all-start) | async-done | bytes 65568 | tf_op jit(solution)/shard_map/all_to_all | solution.py:449
  34.3 0.7 %shard_map.100 = (f32[3,4,24,128]{3,2,1,0:T(8,128)S(1)}, f32[3,24,128]{2,1,0:T(8,128)S(1)}, f32[3,24,128]{2,1,0:T(8,128)S(1)}, f32[8,128]{1,0:T(8,128)S(1)}, f32[8,128]{1,0:T(8,128)S(1)}) custom-call(f32[64,1,256]{2,1,0:T(1,128)S(1)} %all-to-all-done.got, f32[3,4,24,128]{3,2,1,0:T(8,128)S(1)} %get-tuple-element.40.free, ...), custom_call_target="tpu_custom_call" | custom-call | bytes 3000000 | tf_op jit(solution)/shard_map/pallas_call | solution.py:391
  35.0 0.7 %collective-permute-start.7 = (f32[3,24,128]{2,1,0:T(8,128)S(1)}, f32[3,24,128]{2,1,0:T(8,128)S(1)}, u32[]{:S(2)}, u32[]{:S(2)}) collective-permute-start(f32[3,24,128]{2,1,0:T(8,128)S(1)} %get-tuple-element.43), channel_id=1, source_target_pairs={{0,7},{1,2},{2,1},{3,4},{4,3},{5,6},{6,5},{7,0},{8,15},{9,10},{10,... | collective-permute-start | bytes 110600 | tf_op jit(solution)/shard_map/ppermute | solution.py:412
  35.8 1.2 %collective-permute-start.6 = (f32[3,24,128]{2,1,0:T(8,128)S(1)}, f32[3,24,128]{2,1,0:T(8,128)S(1)}, u32[]{:S(2)}, u32[]{:S(2)}) collective-permute-start(f32[3,24,128]{2,1,0:T(8,128)S(1)} %get-tuple-element.42), channel_id=1, source_target_pairs={{0,1},{1,0},{2,3},{3,2},{4,5},{5,4},{6,7},{7,6},{8,9},{9,8},{10,11... | collective-permute-start | bytes 110600 | tf_op jit(solution)/shard_map/ppermute | solution.py:412
  37.0 2.7 %collective-permute-start.8 = (f32[8,128]{1,0:T(8,128)S(1)}, f32[8,128]{1,0:T(8,128)S(1)}, u32[]{:S(2)}, u32[]{:S(2)}) collective-permute-start(f32[8,128]{1,0:T(8,128)S(1)} %get-tuple-element.44), channel_id=1, source_target_pairs={{0,64},{64,128},{128,192},{192,0},{1,65},{65,129},{129,193},{193,1... | collective-permute-start | bytes 12296 | tf_op jit(solution)/shard_map/ppermute | solution.py:406
  39.7 1.3 %shard_map.101.refs_3_.sources = f32[3,3,4,24,128]{4,3,2,1,0:T(8,128)S(1)} custom-call(f32[64,1,256]{2,1,0:T(1,128)S(1)} %all-to-all-done.got, f32[4,24,128]{2,1,0:T(8,128)S(1)} %get-tuple-element.35.c.refs_2_), custom_call_target="tpu_custom_call" | custom-call | bytes 9000000 | tf_op jit(solution)/shard_map/pallas_call | solution.py:391
  41.0 1.7 %collective-permute-done.9.refs_6_.refs_7_ = f32[8,128]{1,0:T(8,128)S(1)} collective-permute-done((f32[8,128]{1,0:T(8,128)S(1)}, f32[8,128]{1,0:T(8,128)S(1)}, u32[]{:S(2)}, u32[]{:S(2)}) %collective-permute-start.9) | collective-permute-done | bytes 4128 | tf_op jit(solution)/shard_map/ppermute | solution.py:406
  42.8 2.0 %collective-permute-start.11 = (f32[3,24,128]{2,1,0:T(8,128)S(1)}, f32[3,24,128]{2,1,0:T(8,128)S(1)}, u32[]{:S(2)}, u32[]{:S(2)}) collective-permute-start(f32[3,24,128]{2,1,0:T(8,128)S(1)} %shard_map.102.refs_12_), channel_id=1, source_target_pairs={{0,7},{1,2},{2,1},{3,4},{4,3},{5,6},{6,5},{7,0},{8,15},{9,10},{10,... | collective-permute-start | bytes 110600 | tf_op jit(solution)/shard_map/ppermute | solution.py:412
  46.0 0.7 %collective-permute-done.12.refs_5_.refs_6_ = f32[8,128]{1,0:T(8,128)S(1)} collective-permute-done((f32[8,128]{1,0:T(8,128)S(1)}, f32[8,128]{1,0:T(8,128)S(1)}, u32[]{:S(2)}, u32[]{:S(2)}) %collective-permute-start.12) | collective-permute-done | bytes 4128 | tf_op jit(solution)/shard_map/ppermute | solution.py:406
  46.7 2.2 %collective-permute-done.13.refs_6_.refs_7_ = f32[8,128]{1,0:T(8,128)S(1)} collective-permute-done((f32[8,128]{1,0:T(8,128)S(1)}, f32[8,128]{1,0:T(8,128)S(1)}, u32[]{:S(2)}, u32[]{:S(2)}) %collective-permute-start.13) | collective-permute-done | bytes 4128 | tf_op jit(solution)/shard_map/ppermute | solution.py:406
  49.1 1.8 %collective-permute-start.15 = (f32[3,24,128]{2,1,0:T(8,128)S(1)}, f32[3,24,128]{2,1,0:T(8,128)S(1)}, u32[]{:S(2)}, u32[]{:S(2)}) collective-permute-start(f32[3,24,128]{2,1,0:T(8,128)S(1)} %shard_map.104.refs_12_), channel_id=1, source_target_pairs={{0,7},{1,2},{2,1},{3,4},{4,3},{5,6},{6,5},{7,0},{8,15},{9,10},{10,... | collective-permute-start | bytes 110600 | tf_op jit(solution)/shard_map/ppermute | solution.py:412
  52.0 0.7 %collective-permute-done.16.refs_5_.at_left = f32[8,128]{1,0:T(8,128)S(1)} collective-permute-done((f32[8,128]{1,0:T(8,128)S(1)}, f32[8,128]{1,0:T(8,128)S(1)}, u32[]{:S(2)}, u32[]{:S(2)}) %collective-permute-start.16) | collective-permute-done | bytes 4128 | tf_op jit(solution)/shard_map/ppermute | solution.py:406
  52.7 2.2 %collective-permute-done.17.refs_6_.at_right = f32[8,128]{1,0:T(8,128)S(1)} collective-permute-done((f32[8,128]{1,0:T(8,128)S(1)}, f32[8,128]{1,0:T(8,128)S(1)}, u32[]{:S(2)}, u32[]{:S(2)}) %collective-permute-start.17) | collective-permute-done | bytes 4128 | tf_op jit(solution)/shard_map/ppermute | solution.py:406
  55.1 0.9 %shard_map.107 = (f32[3,4,16,128]{3,2,1,0:T(8,128)}, f32[3,4,16,128]{3,2,1,0:T(8,128)}) custom-call(f32[3,4,24,128]{3,2,1,0:T(8,128)S(1)} %get-tuple-element.54.refs_0_.u, f32[3,4,24,128]{3,2,1,0:T(8,128)S(1)} %get-tuple-element.50.refs_0_.refs_1_.v, f32[4,24,128]{2,1,0:T(8,128)S(1)} %get-tuple-element.35.c.refs_2_, ...), custom_call_target="tpu_custom_call" | custom-call | bytes 3000000 | tf_op jit(solution)/shard_map/pallas_call | solution.py:391
  (35 shorter events, 3.1 us)
Async XLA Ops:
  2.2 21.1 %collective-permute-start = (f32[11,2,8,128]{3,2,1,0:T(8,128)}, f32[11,2,8,128]{3,2,1,0:T(8,128)S(1)}, u32[]{:S(2)}, u32[]{:S(2)}) collective-permute-start(f32[11,2,8,128]{3,2,1,0:T(8,128)} %shard_map.96), channel_id=1, source_target_pairs={{0,8},{8,16},{16,24},{24,32},{32,40},{40,48},{48,56},{56,0},{1,9},... | collective-permute-start | bytes 270344 | tf_op jit(solution)/shard_map/ppermute | solution.py:406
  6.0 17.3 %copy-start.1 = (f32[3,4,16,128]{3,2,1,0:T(8,128)S(1)}, f32[3,4,16,128]{3,2,1,0:T(8,128)}, u32[]{:S(2)}) copy-start(f32[3,4,16,128]{3,2,1,0:T(8,128)} %cur.5) | copy-start | bytes 294916
  6.0 17.3 %copy-start.2 = (f32[3,4,16,128]{3,2,1,0:T(8,128)S(1)}, f32[3,4,16,128]{3,2,1,0:T(8,128)}, u32[]{:S(2)}) copy-start(f32[3,4,16,128]{3,2,1,0:T(8,128)} %prv.5) | copy-start | bytes 294916
  6.1 17.3 %copy-start.3 = (f32[4,16,128]{2,1,0:T(8,128)S(1)}, f32[4,16,128]{2,1,0:T(8,128)}, u32[]{:S(2)}) copy-start(f32[4,16,128]{2,1,0:T(8,128)} %den.1) | copy-start | bytes 98308
  8.9 14.5 %copy-start = (f32[4,4,16,128]{3,2,1,0:T(8,128)S(1)}, f32[4,4,16,128]{3,2,1,0:T(8,128)}, u32[]{:S(2)}) copy-start(f32[4,4,16,128]{3,2,1,0:T(8,128)} %mod.5) | copy-start | bytes 393220
  8.9 14.4 %collective-permute-start.1 = (f32[11,2,8,128]{3,2,1,0:T(8,128)}, f32[11,2,8,128]{3,2,1,0:T(8,128)S(1)}, u32[]{:S(2)}, u32[]{:S(2)}) collective-permute-start(f32[11,2,8,128]{3,2,1,0:T(8,128)} %get-tuple-element.31), channel_id=1, source_target_pairs={{0,56},{8,0},{16,8},{24,16},{32,24},{40,32},{48,40},{56,48},{1,57}... | collective-permute-start | bytes 270344 | tf_op jit(solution)/shard_map/ppermute | solution.py:406
  11.2 23.1 %all-to-all-start = ((f32[64,1,256]{2,1,0:T(1,128)}), f32[64,1,256]{2,1,0:T(1,128)S(1)}, u32[]{:S(2)}, u32[]{:S(2)}) async-start(f32[64,1,256]{2,1,0:T(1,128)} %get-tuple-element.30), calls=%async_computation | async-start | bytes 131072 | tf_op jit(solution)/shard_map/all_to_all | solution.py:449
  23.7 4.9 %collective-permute-start.3 = (f32[5,24,128]{2,1,0:T(8,128)S(1)}, f32[5,24,128]{2,1,0:T(8,128)S(1)}, u32[]{:S(2)}, u32[]{:S(2)}) collective-permute-start(f32[5,24,128]{2,1,0:T(8,128)S(1)} %get-tuple-element.37), channel_id=1, source_target_pairs={{0,7},{1,2},{2,1},{3,4},{4,3},{5,6},{6,5},{7,0},{8,15},{9,10},{10,... | collective-permute-start | bytes 184328 | tf_op jit(solution)/shard_map/ppermute | solution.py:412
  26.0 5.9 %collective-permute-start.2 = (f32[5,24,128]{2,1,0:T(8,128)S(1)}, f32[5,24,128]{2,1,0:T(8,128)S(1)}, u32[]{:S(2)}, u32[]{:S(2)}) collective-permute-start(f32[5,24,128]{2,1,0:T(8,128)S(1)} %get-tuple-element.36), channel_id=1, source_target_pairs={{0,1},{1,0},{2,3},{3,2},{4,5},{5,4},{6,7},{7,6},{8,9},{9,8},{10,11... | collective-permute-start | bytes 184328 | tf_op jit(solution)/shard_map/ppermute | solution.py:412
  26.0 3.4 %collective-permute-start.4 = (f32[8,128]{1,0:T(8,128)S(1)}, f32[8,128]{1,0:T(8,128)S(1)}, u32[]{:S(2)}, u32[]{:S(2)}) collective-permute-start(f32[8,128]{1,0:T(8,128)S(1)} %get-tuple-element.38), channel_id=1, source_target_pairs={{0,64},{64,128},{128,192},{192,0},{1,65},{65,129},{129,193},{193,1... | collective-permute-start | bytes 12296 | tf_op jit(solution)/shard_map/ppermute | solution.py:406
  28.6 3.3 %collective-permute-start.5 = (f32[8,128]{1,0:T(8,128)S(1)}, f32[8,128]{1,0:T(8,128)S(1)}, u32[]{:S(2)}, u32[]{:S(2)}) collective-permute-start(f32[8,128]{1,0:T(8,128)S(1)} %get-tuple-element.39), channel_id=1, source_target_pairs={{0,192},{64,0},{128,64},{192,128},{1,193},{65,1},{129,65},{193,129... | collective-permute-start | bytes 12296 | tf_op jit(solution)/shard_map/ppermute | solution.py:406
  35.0 7.7 %collective-permute-start.7 = (f32[3,24,128]{2,1,0:T(8,128)S(1)}, f32[3,24,128]{2,1,0:T(8,128)S(1)}, u32[]{:S(2)}, u32[]{:S(2)}) collective-permute-start(f32[3,24,128]{2,1,0:T(8,128)S(1)} %get-tuple-element.43), channel_id=1, source_target_pairs={{0,7},{1,2},{2,1},{3,4},{4,3},{5,6},{6,5},{7,0},{8,15},{9,10},{10,... | collective-permute-start | bytes 110600 | tf_op jit(solution)/shard_map/ppermute | solution.py:412
  35.8 9.0 %collective-permute-start.6 = (f32[3,24,128]{2,1,0:T(8,128)S(1)}, f32[3,24,128]{2,1,0:T(8,128)S(1)}, u32[]{:S(2)}, u32[]{:S(2)}) collective-permute-start(f32[3,24,128]{2,1,0:T(8,128)S(1)} %get-tuple-element.42), channel_id=1, source_target_pairs={{0,1},{1,0},{2,3},{3,2},{4,5},{5,4},{6,7},{7,6},{8,9},{9,8},{10,11... | collective-permute-start | bytes 110600 | tf_op jit(solution)/shard_map/ppermute | solution.py:412
  37.0 4.0 %collective-permute-start.8 = (f32[8,128]{1,0:T(8,128)S(1)}, f32[8,128]{1,0:T(8,128)S(1)}, u32[]{:S(2)}, u32[]{:S(2)}) collective-permute-start(f32[8,128]{1,0:T(8,128)S(1)} %get-tuple-element.44), channel_id=1, source_target_pairs={{0,64},{64,128},{128,192},{192,0},{1,65},{65,129},{129,193},{193,1... | collective-permute-start | bytes 12296 | tf_op jit(solution)/shard_map/ppermute | solution.py:406
  39.7 3.0 %collective-permute-start.9 = (f32[8,128]{1,0:T(8,128)S(1)}, f32[8,128]{1,0:T(8,128)S(1)}, u32[]{:S(2)}, u32[]{:S(2)}) collective-permute-start(f32[8,128]{1,0:T(8,128)S(1)} %get-tuple-element.45), channel_id=1, source_target_pairs={{0,192},{64,0},{128,64},{192,128},{1,193},{65,1},{129,65},{193,129... | collective-permute-start | bytes 12296 | tf_op jit(solution)/shard_map/ppermute | solution.py:406
  42.8 6.1 %collective-permute-start.11 = (f32[3,24,128]{2,1,0:T(8,128)S(1)}, f32[3,24,128]{2,1,0:T(8,128)S(1)}, u32[]{:S(2)}, u32[]{:S(2)}) collective-permute-start(f32[3,24,128]{2,1,0:T(8,128)S(1)} %shard_map.102.refs_12_), channel_id=1, source_target_pairs={{0,7},{1,2},{2,1},{3,4},{4,3},{5,6},{6,5},{7,0},{8,15},{9,10},{10,... | collective-permute-start | bytes 110600 | tf_op jit(solution)/shard_map/ppermute | solution.py:412
  45.3 5.5 %collective-permute-start.10 = (f32[3,24,128]{2,1,0:T(8,128)S(1)}, f32[3,24,128]{2,1,0:T(8,128)S(1)}, u32[]{:S(2)}, u32[]{:S(2)}) collective-permute-start(f32[3,24,128]{2,1,0:T(8,128)S(1)} %get-tuple-element.51), channel_id=1, source_target_pairs={{0,1},{1,0},{2,3},{3,2},{4,5},{5,4},{6,7},{7,6},{8,9},{9,8},{10,11... | collective-permute-start | bytes 110600 | tf_op jit(solution)/shard_map/ppermute | solution.py:412
  45.4 1.2 %collective-permute-start.12 = (f32[8,128]{1,0:T(8,128)S(1)}, f32[8,128]{1,0:T(8,128)S(1)}, u32[]{:S(2)}, u32[]{:S(2)}) collective-permute-start(f32[8,128]{1,0:T(8,128)S(1)} %get-tuple-element.52), channel_id=1, source_target_pairs={{0,64},{64,128},{128,192},{192,0},{1,65},{65,129},{129,193},{193,1... | collective-permute-start | bytes 12296 | tf_op jit(solution)/shard_map/ppermute | solution.py:406
  45.7 3.3 %collective-permute-start.13 = (f32[8,128]{1,0:T(8,128)S(1)}, f32[8,128]{1,0:T(8,128)S(1)}, u32[]{:S(2)}, u32[]{:S(2)}) collective-permute-start(f32[8,128]{1,0:T(8,128)S(1)} %get-tuple-element.53), channel_id=1, source_target_pairs={{0,192},{64,0},{128,64},{192,128},{1,193},{65,1},{129,65},{193,129... | collective-permute-start | bytes 12296 | tf_op jit(solution)/shard_map/ppermute | solution.py:406
  49.1 5.9 %collective-permute-start.15 = (f32[3,24,128]{2,1,0:T(8,128)S(1)}, f32[3,24,128]{2,1,0:T(8,128)S(1)}, u32[]{:S(2)}, u32[]{:S(2)}) collective-permute-start(f32[3,24,128]{2,1,0:T(8,128)S(1)} %shard_map.104.refs_12_), channel_id=1, source_target_pairs={{0,7},{1,2},{2,1},{3,4},{4,3},{5,6},{6,5},{7,0},{8,15},{9,10},{10,... | collective-permute-start | bytes 110600 | tf_op jit(solution)/shard_map/ppermute | solution.py:412
  51.3 3.7 %collective-permute-start.14 = (f32[3,24,128]{2,1,0:T(8,128)S(1)}, f32[3,24,128]{2,1,0:T(8,128)S(1)}, u32[]{:S(2)}, u32[]{:S(2)}) collective-permute-start(f32[3,24,128]{2,1,0:T(8,128)S(1)} %get-tuple-element.55), channel_id=1, source_target_pairs={{0,1},{1,0},{2,3},{3,2},{4,5},{5,4},{6,7},{7,6},{8,9},{9,8},{10,11... | collective-permute-start | bytes 110600 | tf_op jit(solution)/shard_map/ppermute | solution.py:412
  51.4 1.2 %collective-permute-start.16 = (f32[8,128]{1,0:T(8,128)S(1)}, f32[8,128]{1,0:T(8,128)S(1)}, u32[]{:S(2)}, u32[]{:S(2)}) collective-permute-start(f32[8,128]{1,0:T(8,128)S(1)} %get-tuple-element.56), channel_id=1, source_target_pairs={{0,64},{64,128},{128,192},{192,0},{1,65},{65,129},{129,193},{193,1... | collective-permute-start | bytes 12296 | tf_op jit(solution)/shard_map/ppermute | solution.py:406
  51.7 3.2 %collective-permute-start.17 = (f32[8,128]{1,0:T(8,128)S(1)}, f32[8,128]{1,0:T(8,128)S(1)}, u32[]{:S(2)}, u32[]{:S(2)}) collective-permute-start(f32[8,128]{1,0:T(8,128)S(1)} %get-tuple-element.57), channel_id=1, source_target_pairs={{0,192},{64,0},{128,64},{192,128},{1,193},{65,1},{129,65},{193,129... | collective-permute-start | bytes 12296 | tf_op jit(solution)/shard_map/ppermute | solution.py:406

commit v11 on v8

--- a/solution.py
+++ b/solution.py
@@ -69,16 +69,22 @@
     return lead, CR - 1 - lead
 
 
+def whole(layer):
+    if layer.shape[0] == ROWS:
+        return layer
+    return jnp.concatenate([layer, jnp.zeros((ROWS - layer.shape[0], CE), F32)], axis=0)
+
+
 def keep_lead(u_ref, made):
     lead, _ = end_layers()
     for k in range(3):
-        u_ref[k, lead] = made[k]
+        u_ref[k, lead, : made.shape[1], :] = made[k]
 
 
 def put_rest(u_ref, even_ref, left_ref, right_ref):
     _, rest = end_layers()
     for k in range(3):
-        even_ref[k] = u_ref[k, rest]
+        even_ref[k] = u_ref[k, rest, : even_ref.shape[1], :]
     left_ref[...] = jnp.zeros_like(left_ref)
     right_ref[...] = jnp.zeros_like(right_ref)
     put_columns(tiles_of(u_ref, 3), left_ref, right_ref, 0)
@@ -254,8 +260,8 @@
     rad, is_even = lax.axis_index("rad"), rad_is_even()
     lows, highs = [], []
     for k in range(count):
-        low = jnp.where(is_even, odd[k], even[k])
-        high = jnp.where(is_even, even[k], odd[k])
+        low = jnp.where(is_even, whole(odd[k]), whole(even[k]))
+        high = jnp.where(is_even, whole(even[k]), whole(odd[k]))
         lows.append(jnp.where(rad > 0, low, 0.0))
         highs.append(jnp.where(rad < lax.axis_size("rad") - 1, high, 0.0))
     return lows, highs
@@ -345,10 +351,11 @@
     outer_face, inner_face = jnp.where(downwards, 0, CR), jnp.where(downwards, 1, CR - 1)
     for k in range(3):
         i, here = TABLE[k][0] // 2, u[k, lead]
-        outer = jnp.where(joined, odd[k], 0.0)
+        outer = jnp.where(joined, whole(odd[k]), 0.0)
         total = ar[i, outer_face] * (outer - here) + ar[i, inner_face] * (u[k, inner] - here)
         total = total + level(k, lead, here, at_left, at_right, al, au, ad)
-        out[k] = 2.0 * here - v[k, lead] + c[lead] * total + sources[t - 1, k, lead]
+        value = 2.0 * here - v[k, lead] + c[lead] * total + sources[t - 1, k, lead]
+        out[k] = value[: out.shape[1]]
 
 
 def step_kernel(
@@ -480,6 +487,8 @@
         def step(*refs, t=t):
             step_kernel(t, *refs)
 
+        if t == STEPS - 2:
+            layer = (3, CL, CE)
         (made,) = call(lead, [layer], before + (odd,) + after)
         if t == STEPS - 1:
             args = before + (even, odd) + after + (made,)

time: 56.2 us -> 56.1 us (level)
  no operation moved by 1% of the time
where the time goes in v11:
time: 56.1 us; the launch traced here: 55.9 us
  starting transfers between devices  34 us (61%)
  waiting for transfers between devices  11.3 us (20%)
  Pallas kernels  9.68 us (17%)
  between operations  0.8 us (1%)
    ppermute x10, starting transfers between devices, shifted(): lax.ppermute(block, axis, [(i, (i + by) % count) for i in range(count)])  13.5 us
    all_to_all x1, starting transfers between devices, on_device(): got = lax.all_to_all(packed, ('lat', 'rad'), 0, 0, tiled=True)  12.1 us
    ppermute x10, waiting for transfers between devices, shifted(): lax.ppermute(block, axis, [(i, (i + by) % count) for i in range(count)])  10.8 us
    pallas_call x12, Pallas kernels, call(): pl.pallas_call(kernel, out_shape=[jax.ShapeDtypeStruct(shape, F32) for sh...  9.68 us
    ppermute x8, starting transfers between devices, swapped(): return lax.ppermute(block, axis, pairs)  8.42 us
  transfers between devices with their start and end apart: 19, of which 8 were waited for; matrix products, arithmetic and copies ran while one was open for 0% of the time, Pallas kernels for 12%

profile of v11, /device:TPU:1, one launch (start us, length us, event | category | flops | bytes accessed | tf_op | source)
XLA Modules:
  0.0 55.9 jit_solution(12100086090033513169)
XLA Ops:
  0.6 1.6 %shard_map.96 = f32[11,2,8,128]{3,2,1,0:T(8,128)} custom-call(f32[3,4,16,128]{3,2,1,0:T(8,128)} %cur.5, f32[3,4,16,128]{3,2,1,0:T(8,128)} %prv.5, f32[4,4,16,128]{3,2,1,0:T(8,128)} %mod.5, f32[1,4,16,128]{3,2,1,0:T(8,128)} %bitcast.5), custom_call_target="tpu_custom_call" | custom-call | bytes 3000000 | tf_op jit(solution)/shard_map/pallas_call | solution.py:391
  2.2 3.8 %collective-permute-start = (f32[11,2,8,128]{3,2,1,0:T(8,128)}, f32[11,2,8,128]{3,2,1,0:T(8,128)S(1)}, u32[]{:S(2)}, u32[]{:S(2)}) collective-permute-start(f32[11,2,8,128]{3,2,1,0:T(8,128)} %shard_map.96), channel_id=1, source_target_pairs={{0,8},{8,16},{16,24},{24,32},{32,40},{40,48},{48,56},{56,0},{1,9},... | collective-permute-start | bytes 270344 | tf_op jit(solution)/shard_map/ppermute | solution.py:406
  6.1 2.8 %shard_map.95 = (f32[64,1,256]{2,1,0:T(1,128)}, f32[11,2,8,128]{3,2,1,0:T(8,128)}) custom-call(s32[1,128]{1,0:T(1,128)} %bitcast.8, s32[1,128]{1,0:T(1,128)} %bitcast.9, s32[1,128]{1,0:T(1,128)} %bitcast.10, f32[3,128,512]{2,1,0:T(8,128)} %bitcast.7, f32[3,4,16,128]{3,2,1,0:T(8,128)} %cur.5, f32[3,4,16,128]{3,2,1,0:T(8,128)} %prv.5, f32[4,4,16,128]{3,2,1,0:T(8,128)} %mod.5, ...), custom_call_target="tpu_custom_call" | custom-call | bytes 6000000 | tf_op jit(solution)/shard_map/pallas_call | solution.py:391
  8.9 2.3 %collective-permute-start.1 = (f32[11,2,8,128]{3,2,1,0:T(8,128)}, f32[11,2,8,128]{3,2,1,0:T(8,128)S(1)}, u32[]{:S(2)}, u32[]{:S(2)}) collective-permute-start(f32[11,2,8,128]{3,2,1,0:T(8,128)} %get-tuple-element.31), channel_id=1, source_target_pairs={{0,56},{8,0},{16,8},{24,16},{32,24},{40,32},{48,40},{56,48},{1,57}... | collective-permute-start | bytes 270344 | tf_op jit(solution)/shard_map/ppermute | solution.py:406
  11.2 12.1 %all-to-all-start = ((f32[64,1,256]{2,1,0:T(1,128)}), f32[64,1,256]{2,1,0:T(1,128)S(1)}, u32[]{:S(2)}, u32[]{:S(2)}) async-start(f32[64,1,256]{2,1,0:T(1,128)} %get-tuple-element.30), calls=%async_computation | async-start | bytes 131072 | tf_op jit(solution)/shard_map/all_to_all | solution.py:449
  23.7 1.1 %collective-permute-start.2 = (f32[5,24,128]{2,1,0:T(8,128)S(1)}, f32[5,24,128]{2,1,0:T(8,128)S(1)}, u32[]{:S(2)}, u32[]{:S(2)}) collective-permute-start(f32[5,24,128]{2,1,0:T(8,128)S(1)} %get-tuple-element.36), channel_id=1, source_target_pairs={{0,1},{1,0},{2,3},{3,2},{4,5},{5,4},{6,7},{7,6},{8,9},{9,8},{10,11... | collective-permute-start | bytes 184328 | tf_op jit(solution)/shard_map/ppermute | solution.py:412
  24.8 2.4 %collective-permute-start.3 = (f32[5,24,128]{2,1,0:T(8,128)S(1)}, f32[5,24,128]{2,1,0:T(8,128)S(1)}, u32[]{:S(2)}, u32[]{:S(2)}) collective-permute-start(f32[5,24,128]{2,1,0:T(8,128)S(1)} %get-tuple-element.37), channel_id=1, source_target_pairs={{0,7},{1,2},{2,1},{3,4},{4,3},{5,6},{6,5},{7,0},{8,15},{9,10},{10,... | collective-permute-start | bytes 184328 | tf_op jit(solution)/shard_map/ppermute | solution.py:412
  27.2 2.6 %collective-permute-start.4 = (f32[8,128]{1,0:T(8,128)S(1)}, f32[8,128]{1,0:T(8,128)S(1)}, u32[]{:S(2)}, u32[]{:S(2)}) collective-permute-start(f32[8,128]{1,0:T(8,128)S(1)} %get-tuple-element.38), channel_id=1, source_target_pairs={{0,64},{64,128},{128,192},{192,0},{1,65},{65,129},{129,193},{193,1... | collective-permute-start | bytes 12296 | tf_op jit(solution)/shard_map/ppermute | solution.py:406
  29.8 0.8 %collective-permute-done.4.at_left = f32[8,128]{1,0:T(8,128)S(1)} collective-permute-done((f32[8,128]{1,0:T(8,128)S(1)}, f32[8,128]{1,0:T(8,128)S(1)}, u32[]{:S(2)}, u32[]{:S(2)}) %collective-permute-start.4) | collective-permute-done | bytes 4128 | tf_op jit(solution)/shard_map/ppermute | solution.py:406
  30.5 2.6 %collective-permute-done.5.at_right = f32[8,128]{1,0:T(8,128)S(1)} collective-permute-done((f32[8,128]{1,0:T(8,128)S(1)}, f32[8,128]{1,0:T(8,128)S(1)}, u32[]{:S(2)}, u32[]{:S(2)}) %collective-permute-start.5) | collective-permute-done | bytes 4128 | tf_op jit(solution)/shard_map/ppermute | solution.py:406
  33.1 0.6 %shard_map.98 = (f32[2,5,24,128]{3,2,1,0:T(8,128)S(1)}, f32[3,4,24,128]{3,2,1,0:T(8,128)S(1)}, f32[3,4,24,128]{3,2,1,0:T(8,128)S(1)}, f32[3,4,24,128]{3,2,1,0:T(8,128)S(1)}, f32[3,4,24,128]{3,2,1,0:T(8,128)S(1)}) custom-call(f32[3,4,24,128]{3,2,1,0:T(8,128)S(1)} %get-tuple-element.32.u.refs_1_, f32[3,4,24,128]{3,2,1,0:T(8,128)S(1)} %get-tuple-element.33.v, ...), custom_call_target="tpu_custom_call" | custom-call | bytes 3000000 | tf_op jit(solution)/shard_map/pallas_call | solution.py:391
  33.8 0.5 all-to-all-done.got
  34.3 0.7 %shard_map.99 = (f32[3,4,24,128]{3,2,1,0:T(8,128)S(1)}, f32[3,24,128]{2,1,0:T(8,128)S(1)}, f32[3,24,128]{2,1,0:T(8,128)S(1)}, f32[8,128]{1,0:T(8,128)S(1)}, f32[8,128]{1,0:T(8,128)S(1)}) custom-call(f32[64,1,256]{2,1,0:T(1,128)S(1)} %all-to-all-done.got, f32[3,4,24,128]{3,2,1,0:T(8,128)S(1)} %get-tuple-element.40.free, ...), custom_call_target="tpu_custom_call" | custom-call | bytes 3000000 | tf_op jit(solution)/shard_map/pallas_call | solution.py:391
  35.0 0.8 %collective-permute-start.7 = (f32[3,24,128]{2,1,0:T(8,128)S(1)}, f32[3,24,128]{2,1,0:T(8,128)S(1)}, u32[]{:S(2)}, u32[]{:S(2)}) collective-permute-start(f32[3,24,128]{2,1,0:T(8,128)S(1)} %get-tuple-element.43), channel_id=1, source_target_pairs={{0,7},{1,2},{2,1},{3,4},{4,3},{5,6},{6,5},{7,0},{8,15},{9,10},{10,... | collective-permute-start | bytes 110600 | tf_op jit(solution)/shard_map/ppermute | solution.py:412
  36.2 3.5 %collective-permute-start.8 = (f32[8,128]{1,0:T(8,128)S(1)}, f32[8,128]{1,0:T(8,128)S(1)}, u32[]{:S(2)}, u32[]{:S(2)}) collective-permute-start(f32[8,128]{1,0:T(8,128)S(1)} %get-tuple-element.44), channel_id=1, source_target_pairs={{0,64},{64,128},{128,192},{192,0},{1,65},{65,129},{129,193},{193,1... | collective-permute-start | bytes 12296 | tf_op jit(solution)/shard_map/ppermute | solution.py:406
  39.7 1.3 %shard_map.100.refs_3_.sources = f32[3,3,4,24,128]{4,3,2,1,0:T(8,128)S(1)} custom-call(f32[64,1,256]{2,1,0:T(1,128)S(1)} %all-to-all-done.got, f32[4,24,128]{2,1,0:T(8,128)S(1)} %get-tuple-element.35.c.refs_2_), custom_call_target="tpu_custom_call" | custom-call | bytes 9000000 | tf_op jit(solution)/shard_map/pallas_call | solution.py:391
  41.1 1.7 %collective-permute-done.9.refs_6_.refs_7_ = f32[8,128]{1,0:T(8,128)S(1)} collective-permute-done((f32[8,128]{1,0:T(8,128)S(1)}, f32[8,128]{1,0:T(8,128)S(1)}, u32[]{:S(2)}, u32[]{:S(2)}) %collective-permute-start.9) | collective-permute-done | bytes 4128 | tf_op jit(solution)/shard_map/ppermute | solution.py:406
  42.9 1.9 %collective-permute-start.11 = (f32[3,24,128]{2,1,0:T(8,128)S(1)}, f32[3,24,128]{2,1,0:T(8,128)S(1)}, u32[]{:S(2)}, u32[]{:S(2)}) collective-permute-start(f32[3,24,128]{2,1,0:T(8,128)S(1)} %shard_map.101.refs_12_), channel_id=1, source_target_pairs={{0,7},{1,2},{2,1},{3,4},{4,3},{5,6},{6,5},{7,0},{8,15},{9,10},{10,... | collective-permute-start | bytes 110600 | tf_op jit(solution)/shard_map/ppermute | solution.py:412
  46.0 0.7 %collective-permute-done.12.refs_5_.refs_6_ = f32[8,128]{1,0:T(8,128)S(1)} collective-permute-done((f32[8,128]{1,0:T(8,128)S(1)}, f32[8,128]{1,0:T(8,128)S(1)}, u32[]{:S(2)}, u32[]{:S(2)}) %collective-permute-start.12) | collective-permute-done | bytes 4128 | tf_op jit(solution)/shard_map/ppermute | solution.py:406
  46.6 2.2 %collective-permute-done.13.refs_6_.refs_7_ = f32[8,128]{1,0:T(8,128)S(1)} collective-permute-done((f32[8,128]{1,0:T(8,128)S(1)}, f32[8,128]{1,0:T(8,128)S(1)}, u32[]{:S(2)}, u32[]{:S(2)}) %collective-permute-start.13) | collective-permute-done | bytes 4128 | tf_op jit(solution)/shard_map/ppermute | solution.py:406
  49.0 1.8 %collective-permute-start.15 = (f32[3,16,128]{2,1,0:T(8,128)S(1)}, f32[3,16,128]{2,1,0:T(8,128)S(1)}, u32[]{:S(2)}, u32[]{:S(2)}) collective-permute-start(f32[3,16,128]{2,1,0:T(8,128)S(1)} %shard_map.103.refs_12_), channel_id=1, source_target_pairs={{0,7},{1,2},{2,1},{3,4},{4,3},{5,6},{6,5},{7,0},{8,15},{9,10},{10,... | collective-permute-start | bytes 73736 | tf_op jit(solution)/shard_map/ppermute | solution.py:412
  51.9 0.7 %collective-permute-done.16.refs_5_.at_left = f32[8,128]{1,0:T(8,128)S(1)} collective-permute-done((f32[8,128]{1,0:T(8,128)S(1)}, f32[8,128]{1,0:T(8,128)S(1)}, u32[]{:S(2)}, u32[]{:S(2)}) %collective-permute-start.16) | collective-permute-done | bytes 4128 | tf_op jit(solution)/shard_map/ppermute | solution.py:406
  52.6 2.2 %collective-permute-done.17.refs_6_.at_right = f32[8,128]{1,0:T(8,128)S(1)} collective-permute-done((f32[8,128]{1,0:T(8,128)S(1)}, f32[8,128]{1,0:T(8,128)S(1)}, u32[]{:S(2)}, u32[]{:S(2)}) %collective-permute-start.17) | collective-permute-done | bytes 4128 | tf_op jit(solution)/shard_map/ppermute | solution.py:406
  54.9 0.9 %shard_map.106 = (f32[3,4,16,128]{3,2,1,0:T(8,128)}, f32[3,4,16,128]{3,2,1,0:T(8,128)}) custom-call(f32[3,4,24,128]{3,2,1,0:T(8,128)S(1)} %get-tuple-element.54.refs_0_.u, f32[3,4,24,128]{3,2,1,0:T(8,128)S(1)} %get-tuple-element.50.refs_0_.refs_1_.v, f32[4,24,128]{2,1,0:T(8,128)S(1)} %get-tuple-element.35.c.refs_2_, ...), custom_call_target="tpu_custom_call" | custom-call | bytes 3000000 | tf_op jit(solution)/shard_map/pallas_call | solution.py:391
  (34 shorter events, 3.4 us)
Async XLA Ops:
  2.2 21.1 %collective-permute-start = (f32[11,2,8,128]{3,2,1,0:T(8,128)}, f32[11,2,8,128]{3,2,1,0:T(8,128)S(1)}, u32[]{:S(2)}, u32[]{:S(2)}) collective-permute-start(f32[11,2,8,128]{3,2,1,0:T(8,128)} %shard_map.96), channel_id=1, source_target_pairs={{0,8},{8,16},{16,24},{24,32},{32,40},{40,48},{48,56},{56,0},{1,9},... | collective-permute-start | bytes 270344 | tf_op jit(solution)/shard_map/ppermute | solution.py:406
  6.0 17.3 %copy-start.1 = (f32[3,4,16,128]{3,2,1,0:T(8,128)S(1)}, f32[3,4,16,128]{3,2,1,0:T(8,128)}, u32[]{:S(2)}) copy-start(f32[3,4,16,128]{3,2,1,0:T(8,128)} %cur.5) | copy-start | bytes 294916
  6.0 17.3 %copy-start.2 = (f32[3,4,16,128]{3,2,1,0:T(8,128)S(1)}, f32[3,4,16,128]{3,2,1,0:T(8,128)}, u32[]{:S(2)}) copy-start(f32[3,4,16,128]{3,2,1,0:T(8,128)} %prv.5) | copy-start | bytes 294916
  6.1 17.3 %copy-start.3 = (f32[4,16,128]{2,1,0:T(8,128)S(1)}, f32[4,16,128]{2,1,0:T(8,128)}, u32[]{:S(2)}) copy-start(f32[4,16,128]{2,1,0:T(8,128)} %den.1) | copy-start | bytes 98308
  8.9 14.5 %copy-start = (f32[4,4,16,128]{3,2,1,0:T(8,128)S(1)}, f32[4,4,16,128]{3,2,1,0:T(8,128)}, u32[]{:S(2)}) copy-start(f32[4,4,16,128]{3,2,1,0:T(8,128)} %mod.5) | copy-start | bytes 393220
  8.9 14.4 %collective-permute-start.1 = (f32[11,2,8,128]{3,2,1,0:T(8,128)}, f32[11,2,8,128]{3,2,1,0:T(8,128)S(1)}, u32[]{:S(2)}, u32[]{:S(2)}) collective-permute-start(f32[11,2,8,128]{3,2,1,0:T(8,128)} %get-tuple-element.31), channel_id=1, source_target_pairs={{0,56},{8,0},{16,8},{24,16},{32,24},{40,32},{48,40},{56,48},{1,57}... | collective-permute-start | bytes 270344 | tf_op jit(solution)/shard_map/ppermute | solution.py:406
  11.2 23.1 %all-to-all-start = ((f32[64,1,256]{2,1,0:T(1,128)}), f32[64,1,256]{2,1,0:T(1,128)S(1)}, u32[]{:S(2)}, u32[]{:S(2)}) async-start(f32[64,1,256]{2,1,0:T(1,128)} %get-tuple-element.30), calls=%async_computation | async-start | bytes 131072 | tf_op jit(solution)/shard_map/all_to_all | solution.py:449
  23.7 9.5 %collective-permute-start.2 = (f32[5,24,128]{2,1,0:T(8,128)S(1)}, f32[5,24,128]{2,1,0:T(8,128)S(1)}, u32[]{:S(2)}, u32[]{:S(2)}) collective-permute-start(f32[5,24,128]{2,1,0:T(8,128)S(1)} %get-tuple-element.36), channel_id=1, source_target_pairs={{0,1},{1,0},{2,3},{3,2},{4,5},{5,4},{6,7},{7,6},{8,9},{9,8},{10,11... | collective-permute-start | bytes 184328 | tf_op jit(solution)/shard_map/ppermute | solution.py:412
  24.8 8.4 %collective-permute-start.3 = (f32[5,24,128]{2,1,0:T(8,128)S(1)}, f32[5,24,128]{2,1,0:T(8,128)S(1)}, u32[]{:S(2)}, u32[]{:S(2)}) collective-permute-start(f32[5,24,128]{2,1,0:T(8,128)S(1)} %get-tuple-element.37), channel_id=1, source_target_pairs={{0,7},{1,2},{2,1},{3,4},{4,3},{5,6},{6,5},{7,0},{8,15},{9,10},{10,... | collective-permute-start | bytes 184328 | tf_op jit(solution)/shard_map/ppermute | solution.py:412
  27.2 3.4 %collective-permute-start.4 = (f32[8,128]{1,0:T(8,128)S(1)}, f32[8,128]{1,0:T(8,128)S(1)}, u32[]{:S(2)}, u32[]{:S(2)}) collective-permute-start(f32[8,128]{1,0:T(8,128)S(1)} %get-tuple-element.38), channel_id=1, source_target_pairs={{0,64},{64,128},{128,192},{192,0},{1,65},{65,129},{129,193},{193,1... | collective-permute-start | bytes 12296 | tf_op jit(solution)/shard_map/ppermute | solution.py:406
  29.8 3.3 %collective-permute-start.5 = (f32[8,128]{1,0:T(8,128)S(1)}, f32[8,128]{1,0:T(8,128)S(1)}, u32[]{:S(2)}, u32[]{:S(2)}) collective-permute-start(f32[8,128]{1,0:T(8,128)S(1)} %get-tuple-element.39), channel_id=1, source_target_pairs={{0,192},{64,0},{128,64},{192,128},{1,193},{65,1},{129,65},{193,129... | collective-permute-start | bytes 12296 | tf_op jit(solution)/shard_map/ppermute | solution.py:406
  35.0 7.7 %collective-permute-start.7 = (f32[3,24,128]{2,1,0:T(8,128)S(1)}, f32[3,24,128]{2,1,0:T(8,128)S(1)}, u32[]{:S(2)}, u32[]{:S(2)}) collective-permute-start(f32[3,24,128]{2,1,0:T(8,128)S(1)} %get-tuple-element.43), channel_id=1, source_target_pairs={{0,7},{1,2},{2,1},{3,4},{4,3},{5,6},{6,5},{7,0},{8,15},{9,10},{10,... | collective-permute-start | bytes 110600 | tf_op jit(solution)/shard_map/ppermute | solution.py:412
  35.8 9.0 %collective-permute-start.6 = (f32[3,24,128]{2,1,0:T(8,128)S(1)}, f32[3,24,128]{2,1,0:T(8,128)S(1)}, u32[]{:S(2)}, u32[]{:S(2)}) collective-permute-start(f32[3,24,128]{2,1,0:T(8,128)S(1)} %get-tuple-element.42), channel_id=1, source_target_pairs={{0,1},{1,0},{2,3},{3,2},{4,5},{5,4},{6,7},{7,6},{8,9},{9,8},{10,11... | collective-permute-start | bytes 110600 | tf_op jit(solution)/shard_map/ppermute | solution.py:412
  36.2 4.9 %collective-permute-start.8 = (f32[8,128]{1,0:T(8,128)S(1)}, f32[8,128]{1,0:T(8,128)S(1)}, u32[]{:S(2)}, u32[]{:S(2)}) collective-permute-start(f32[8,128]{1,0:T(8,128)S(1)} %get-tuple-element.44), channel_id=1, source_target_pairs={{0,64},{64,128},{128,192},{192,0},{1,65},{65,129},{129,193},{193,1... | collective-permute-start | bytes 12296 | tf_op jit(solution)/shard_map/ppermute | solution.py:406
  39.7 3.0 %collective-permute-start.9 = (f32[8,128]{1,0:T(8,128)S(1)}, f32[8,128]{1,0:T(8,128)S(1)}, u32[]{:S(2)}, u32[]{:S(2)}) collective-permute-start(f32[8,128]{1,0:T(8,128)S(1)} %get-tuple-element.45), channel_id=1, source_target_pairs={{0,192},{64,0},{128,64},{192,128},{1,193},{65,1},{129,65},{193,129... | collective-permute-start | bytes 12296 | tf_op jit(solution)/shard_map/ppermute | solution.py:406
  42.9 6.0 %collective-permute-start.11 = (f32[3,24,128]{2,1,0:T(8,128)S(1)}, f32[3,24,128]{2,1,0:T(8,128)S(1)}, u32[]{:S(2)}, u32[]{:S(2)}) collective-permute-start(f32[3,24,128]{2,1,0:T(8,128)S(1)} %shard_map.101.refs_12_), channel_id=1, source_target_pairs={{0,7},{1,2},{2,1},{3,4},{4,3},{5,6},{6,5},{7,0},{8,15},{9,10},{10,... | collective-permute-start | bytes 110600 | tf_op jit(solution)/shard_map/ppermute | solution.py:412
  45.3 5.5 %collective-permute-start.10 = (f32[3,24,128]{2,1,0:T(8,128)S(1)}, f32[3,24,128]{2,1,0:T(8,128)S(1)}, u32[]{:S(2)}, u32[]{:S(2)}) collective-permute-start(f32[3,24,128]{2,1,0:T(8,128)S(1)} %get-tuple-element.51), channel_id=1, source_target_pairs={{0,1},{1,0},{2,3},{3,2},{4,5},{5,4},{6,7},{7,6},{8,9},{9,8},{10,11... | collective-permute-start | bytes 110600 | tf_op jit(solution)/shard_map/ppermute | solution.py:412
  45.4 1.2 %collective-permute-start.12 = (f32[8,128]{1,0:T(8,128)S(1)}, f32[8,128]{1,0:T(8,128)S(1)}, u32[]{:S(2)}, u32[]{:S(2)}) collective-permute-start(f32[8,128]{1,0:T(8,128)S(1)} %get-tuple-element.52), channel_id=1, source_target_pairs={{0,64},{64,128},{128,192},{192,0},{1,65},{65,129},{129,193},{193,1... | collective-permute-start | bytes 12296 | tf_op jit(solution)/shard_map/ppermute | solution.py:406
  45.6 3.3 %collective-permute-start.13 = (f32[8,128]{1,0:T(8,128)S(1)}, f32[8,128]{1,0:T(8,128)S(1)}, u32[]{:S(2)}, u32[]{:S(2)}) collective-permute-start(f32[8,128]{1,0:T(8,128)S(1)} %get-tuple-element.53), channel_id=1, source_target_pairs={{0,192},{64,0},{128,64},{192,128},{1,193},{65,1},{129,65},{193,129... | collective-permute-start | bytes 12296 | tf_op jit(solution)/shard_map/ppermute | solution.py:406
  49.0 5.8 %collective-permute-start.15 = (f32[3,16,128]{2,1,0:T(8,128)S(1)}, f32[3,16,128]{2,1,0:T(8,128)S(1)}, u32[]{:S(2)}, u32[]{:S(2)}) collective-permute-start(f32[3,16,128]{2,1,0:T(8,128)S(1)} %shard_map.103.refs_12_), channel_id=1, source_target_pairs={{0,7},{1,2},{2,1},{3,4},{4,3},{5,6},{6,5},{7,0},{8,15},{9,10},{10,... | collective-permute-start | bytes 73736 | tf_op jit(solution)/shard_map/ppermute | solution.py:412
  51.2 3.7 %collective-permute-start.14 = (f32[3,16,128]{2,1,0:T(8,128)S(1)}, f32[3,16,128]{2,1,0:T(8,128)S(1)}, u32[]{:S(2)}, u32[]{:S(2)}) collective-permute-start(f32[3,16,128]{2,1,0:T(8,128)S(1)} %get-tuple-element.55), channel_id=1, source_target_pairs={{0,1},{1,0},{2,3},{3,2},{4,5},{5,4},{6,7},{7,6},{8,9},{9,8},{10,11... | collective-permute-start | bytes 73736 | tf_op jit(solution)/shard_map/ppermute | solution.py:412
  51.4 1.2 %collective-permute-start.16 = (f32[8,128]{1,0:T(8,128)S(1)}, f32[8,128]{1,0:T(8,128)S(1)}, u32[]{:S(2)}, u32[]{:S(2)}) collective-permute-start(f32[8,128]{1,0:T(8,128)S(1)} %get-tuple-element.56), channel_id=1, source_target_pairs={{0,64},{64,128},{128,192},{192,0},{1,65},{65,129},{129,193},{193,1... | collective-permute-start | bytes 12296 | tf_op jit(solution)/shard_map/ppermute | solution.py:406
  51.8 3.0 %collective-permute-start.17 = (f32[8,128]{1,0:T(8,128)S(1)}, f32[8,128]{1,0:T(8,128)S(1)}, u32[]{:S(2)}, u32[]{:S(2)}) collective-permute-start(f32[8,128]{1,0:T(8,128)S(1)} %get-tuple-element.57), channel_id=1, source_target_pairs={{0,192},{64,0},{128,64},{192,128},{1,193},{65,1},{129,65},{193,129... | collective-permute-start | bytes 12296 | tf_op jit(solution)/shard_map/ppermute | solution.py:406

commit v12 on v9

--- a/solution.py
+++ b/solution.py
@@ -259,6 +259,13 @@
         lows.append(jnp.where(rad > 0, low, 0.0))
         highs.append(jnp.where(rad < lax.axis_size("rad") - 1, high, 0.0))
     return lows, highs
+
+
+def joined_kernel(odd, out):
+    rad = lax.axis_index("rad")
+    joined = jnp.where(rad_is_even(), rad > 0, rad < lax.axis_size("rad") - 1)
+    for k in range(odd.shape[0]):
+        out[k] = jnp.where(joined, odd[k], 0.0)
 
 
 def prepare_kernel(u, v, m, c, even, odd, at_left, at_right, ar, al, au, ad, following):
@@ -479,10 +486,12 @@
         + [(5, ROWS, CE), (5, ROWS, CE), (8, CE), (8, CE)],
         (current, previous, moduli, density, from_low, from_high),
     )
+    even, odd = swapped(even, "rad", 0), swapped(odd, "rad", 1)
+    (odd,) = call(joined_kernel, [(5, ROWS, CE)], (odd,), us=0.3)
     *coefficients, free = call(
         prepare_kernel,
         [(2, CR + 1, ROWS, CE), wide, wide, wide, wide],
-        (u, v, m, c, swapped(even, "rad", 0), swapped(odd, "rad", 1), *swap_columns(*ends)),
+        (u, v, m, c, even, odd, *swap_columns(*ends)),
     )
     cells, lanes = CR * ROWS, 3 * SLOTS * 128
     first, even, odd, *ends = call(

time: 56 us -> 56.1 us (level)
  waiting for transfers between devices: 10.7 us -> 11.9 us
  starting transfers between devices: 34 us -> 32.9 us
    all_to_all x1, waiting for transfers between devices: 0.55 us -> 1.75 us  [on_device(): got = lax.all_to_all(packed, ('lat', 'rad'), 0, 0, tiled=True)]
    ppermute x10, starting transfers between devices: 13.5 us -> 12.6 us  [shifted(): lax.ppermute(block, axis, [(i, (i + by) % count) for i in range(count)])]
    pallas_call x13 -> x14, Pallas kernels: 10.3 us -> 10.3 us  [call(): pl.pallas_call(kernel, out_shape=[jax.ShapeDtypeStruct(shape, F32) for sh...]
where the time goes in v12:
time: 56.1 us; the launch traced here: 55.8 us
  starting transfers between devices  32.9 us (59%)
  waiting for transfers between devices  11.9 us (21%)
  Pallas kernels  10.3 us (18%)
  between operations  0.81 us (1%)
    ppermute x10, starting transfers between devices, shifted(): lax.ppermute(block, axis, [(i, (i + by) % count) for i in range(count)])  12.6 us
    all_to_all x1, starting transfers between devices, on_device(): got = lax.all_to_all(packed, ('lat', 'rad'), 0, 0, tiled=True)  12.1 us
    pallas_call x14, Pallas kernels, call(): pl.pallas_call(kernel, out_shape=[jax.ShapeDtypeStruct(shape, F32) for sh...  10.3 us
    ppermute x10, waiting for transfers between devices, shifted(): lax.ppermute(block, axis, [(i, (i + by) % count) for i in range(count)])  9.1 us
    ppermute x8, starting transfers between devices, swapped(): return lax.ppermute(block, axis, pairs)  8.15 us
    all_to_all x1, waiting for transfers between devices, on_device(): got = lax.all_to_all(packed, ('lat', 'rad'), 0, 0, tiled=True)  1.75 us
  transfers between devices with their start and end apart: 19, of which 8 were waited for; matrix products, arithmetic and copies ran while one was open for 0% of the time, Pallas kernels for 13%

profile of v12, /device:TPU:1, one launch (start us, length us, event | category | flops | bytes accessed | tf_op | source)
XLA Modules:
  0.0 55.8 jit_solution(11091926951095499388)
XLA Ops:
  0.6 1.6 %shard_map.96 = f32[11,2,8,128]{3,2,1,0:T(8,128)} custom-call(f32[3,4,16,128]{3,2,1,0:T(8,128)} %cur.5, f32[3,4,16,128]{3,2,1,0:T(8,128)} %prv.5, f32[4,4,16,128]{3,2,1,0:T(8,128)} %mod.5, f32[1,4,16,128]{3,2,1,0:T(8,128)} %bitcast.5), custom_call_target="tpu_custom_call" | custom-call | bytes 3000000 | tf_op jit(solution)/shard_map/pallas_call | solution.py:423
  2.2 3.8 %collective-permute-start = (f32[11,2,8,128]{3,2,1,0:T(8,128)}, f32[11,2,8,128]{3,2,1,0:T(8,128)S(1)}, u32[]{:S(2)}, u32[]{:S(2)}) collective-permute-start(f32[11,2,8,128]{3,2,1,0:T(8,128)} %shard_map.96), channel_id=1, source_target_pairs={{0,8},{8,16},{16,24},{24,32},{32,40},{40,48},{48,56},{56,0},{1,9},... | collective-permute-start | bytes 270344 | tf_op jit(solution)/shard_map/ppermute | solution.py:438
  6.1 2.8 %shard_map.95 = (f32[64,1,256]{2,1,0:T(1,128)}, f32[11,2,8,128]{3,2,1,0:T(8,128)}) custom-call(s32[1,128]{1,0:T(1,128)} %bitcast.8, s32[1,128]{1,0:T(1,128)} %bitcast.9, s32[1,128]{1,0:T(1,128)} %bitcast.10, f32[3,128,512]{2,1,0:T(8,128)} %bitcast.7, f32[3,4,16,128]{3,2,1,0:T(8,128)} %cur.5, f32[3,4,16,128]{3,2,1,0:T(8,128)} %prv.5, f32[4,4,16,128]{3,2,1,0:T(8,128)} %mod.5, ...), custom_call_target="tpu_custom_call" | custom-call | bytes 6000000 | tf_op jit(solution)/shard_map/pallas_call | solution.py:423
  8.9 2.3 %collective-permute-start.1 = (f32[11,2,8,128]{3,2,1,0:T(8,128)}, f32[11,2,8,128]{3,2,1,0:T(8,128)S(1)}, u32[]{:S(2)}, u32[]{:S(2)}) collective-permute-start(f32[11,2,8,128]{3,2,1,0:T(8,128)} %get-tuple-element.33), channel_id=1, source_target_pairs={{0,56},{8,0},{16,8},{24,16},{32,24},{40,32},{48,40},{56,48},{1,57}... | collective-permute-start | bytes 270344 | tf_op jit(solution)/shard_map/ppermute | solution.py:438
  11.2 12.1 %all-to-all-start = ((f32[64,1,256]{2,1,0:T(1,128)}), f32[64,1,256]{2,1,0:T(1,128)S(1)}, u32[]{:S(2)}, u32[]{:S(2)}) async-start(f32[64,1,256]{2,1,0:T(1,128)} %get-tuple-element.32), calls=%async_computation | async-start | bytes 131072 | tf_op jit(solution)/shard_map/all_to_all | solution.py:481
  23.7 2.3 %collective-permute-start.3 = (f32[5,24,128]{2,1,0:T(8,128)S(1)}, f32[5,24,128]{2,1,0:T(8,128)S(1)}, u32[]{:S(2)}, u32[]{:S(2)}) collective-permute-start(f32[5,24,128]{2,1,0:T(8,128)S(1)} %get-tuple-element.39), channel_id=1, source_target_pairs={{0,7},{1,2},{2,1},{3,4},{4,3},{5,6},{6,5},{7,0},{8,15},{9,10},{10,... | collective-permute-start | bytes 184328 | tf_op jit(solution)/shard_map/ppermute | solution.py:444
  26.0 2.6 %collective-permute-start.4 = (f32[8,128]{1,0:T(8,128)S(1)}, f32[8,128]{1,0:T(8,128)S(1)}, u32[]{:S(2)}, u32[]{:S(2)}) collective-permute-start(f32[8,128]{1,0:T(8,128)S(1)} %get-tuple-element.40), channel_id=1, source_target_pairs={{0,64},{64,128},{128,192},{192,0},{1,65},{65,129},{129,193},{193,1... | collective-permute-start | bytes 12296 | tf_op jit(solution)/shard_map/ppermute | solution.py:438
  28.6 0.7 %collective-permute-done.4.at_left = f32[8,128]{1,0:T(8,128)S(1)} collective-permute-done((f32[8,128]{1,0:T(8,128)S(1)}, f32[8,128]{1,0:T(8,128)S(1)}, u32[]{:S(2)}, u32[]{:S(2)}) %collective-permute-start.4) | collective-permute-done | bytes 4128 | tf_op jit(solution)/shard_map/ppermute | solution.py:438
  29.3 2.6 %collective-permute-done.5.at_right = f32[8,128]{1,0:T(8,128)S(1)} collective-permute-done((f32[8,128]{1,0:T(8,128)S(1)}, f32[8,128]{1,0:T(8,128)S(1)}, u32[]{:S(2)}, u32[]{:S(2)}) %collective-permute-start.5) | collective-permute-done | bytes 4128 | tf_op jit(solution)/shard_map/ppermute | solution.py:438
  32.6 1.8 %all-to-all-done.got = f32[64,1,256]{2,1,0:T(1,128)S(1)} async-done(((f32[64,1,256]{2,1,0:T(1,128)}), f32[64,1,256]{2,1,0:T(1,128)S(1)}, u32[]{:S(2)}, u32[]{:S(2)}) %all-to-all-start) | async-done | bytes 65568 | tf_op jit(solution)/shard_map/all_to_all | solution.py:481
  34.3 0.7 %shard_map.100 = (f32[3,4,24,128]{3,2,1,0:T(8,128)S(1)}, f32[3,24,128]{2,1,0:T(8,128)S(1)}, f32[3,24,128]{2,1,0:T(8,128)S(1)}, f32[8,128]{1,0:T(8,128)S(1)}, f32[8,128]{1,0:T(8,128)S(1)}) custom-call(f32[64,1,256]{2,1,0:T(1,128)S(1)} %all-to-all-done.got, f32[3,4,24,128]{3,2,1,0:T(8,128)S(1)} %get-tuple-element.42.free, ...), custom_call_target="tpu_custom_call" | custom-call | bytes 3000000 | tf_op jit(solution)/shard_map/pallas_call | solution.py:423
  35.0 0.7 %collective-permute-start.7 = (f32[3,24,128]{2,1,0:T(8,128)S(1)}, f32[3,24,128]{2,1,0:T(8,128)S(1)}, u32[]{:S(2)}, u32[]{:S(2)}) collective-permute-start(f32[3,24,128]{2,1,0:T(8,128)S(1)} %get-tuple-element.45), channel_id=1, source_target_pairs={{0,7},{1,2},{2,1},{3,4},{4,3},{5,6},{6,5},{7,0},{8,15},{9,10},{10,... | collective-permute-start | bytes 110600 | tf_op jit(solution)/shard_map/ppermute | solution.py:444
  35.8 1.2 %collective-permute-start.6 = (f32[3,24,128]{2,1,0:T(8,128)S(1)}, f32[3,24,128]{2,1,0:T(8,128)S(1)}, u32[]{:S(2)}, u32[]{:S(2)}) collective-permute-start(f32[3,24,128]{2,1,0:T(8,128)S(1)} %get-tuple-element.44), channel_id=1, source_target_pairs={{0,1},{1,0},{2,3},{3,2},{4,5},{5,4},{6,7},{7,6},{8,9},{9,8},{10,11... | collective-permute-start | bytes 110600 | tf_op jit(solution)/shard_map/ppermute | solution.py:444
  37.0 2.7 %collective-permute-start.8 = (f32[8,128]{1,0:T(8,128)S(1)}, f32[8,128]{1,0:T(8,128)S(1)}, u32[]{:S(2)}, u32[]{:S(2)}) collective-permute-start(f32[8,128]{1,0:T(8,128)S(1)} %get-tuple-element.46), channel_id=1, source_target_pairs={{0,64},{64,128},{128,192},{192,0},{1,65},{65,129},{129,193},{193,1... | collective-permute-start | bytes 12296 | tf_op jit(solution)/shard_map/ppermute | solution.py:438
  39.7 1.3 %shard_map.101.refs_3_.sources = f32[3,3,4,24,128]{4,3,2,1,0:T(8,128)S(1)} custom-call(f32[64,1,256]{2,1,0:T(1,128)S(1)} %all-to-all-done.got, f32[4,24,128]{2,1,0:T(8,128)S(1)} %get-tuple-element.37.c.refs_2_), custom_call_target="tpu_custom_call" | custom-call | bytes 9000000 | tf_op jit(solution)/shard_map/pallas_call | solution.py:423
  41.0 1.7 %collective-permute-done.9.refs_6_.refs_7_ = f32[8,128]{1,0:T(8,128)S(1)} collective-permute-done((f32[8,128]{1,0:T(8,128)S(1)}, f32[8,128]{1,0:T(8,128)S(1)}, u32[]{:S(2)}, u32[]{:S(2)}) %collective-permute-start.9) | collective-permute-done | bytes 4128 | tf_op jit(solution)/shard_map/ppermute | solution.py:438
  42.9 2.0 %collective-permute-start.11 = (f32[3,24,128]{2,1,0:T(8,128)S(1)}, f32[3,24,128]{2,1,0:T(8,128)S(1)}, u32[]{:S(2)}, u32[]{:S(2)}) collective-permute-start(f32[3,24,128]{2,1,0:T(8,128)S(1)} %shard_map.102.refs_12_), channel_id=1, source_target_pairs={{0,7},{1,2},{2,1},{3,4},{4,3},{5,6},{6,5},{7,0},{8,15},{9,10},{10,... | collective-permute-start | bytes 110600 | tf_op jit(solution)/shard_map/ppermute | solution.py:444
  46.0 0.7 %collective-permute-done.12.refs_5_.refs_6_ = f32[8,128]{1,0:T(8,128)S(1)} collective-permute-done((f32[8,128]{1,0:T(8,128)S(1)}, f32[8,128]{1,0:T(8,128)S(1)}, u32[]{:S(2)}, u32[]{:S(2)}) %collective-permute-start.12) | collective-permute-done | bytes 4128 | tf_op jit(solution)/shard_map/ppermute | solution.py:438
  46.7 2.2 %collective-permute-done.13.refs_6_.refs_7_ = f32[8,128]{1,0:T(8,128)S(1)} collective-permute-done((f32[8,128]{1,0:T(8,128)S(1)}, f32[8,128]{1,0:T(8,128)S(1)}, u32[]{:S(2)}, u32[]{:S(2)}) %collective-permute-start.13) | collective-permute-done | bytes 4128 | tf_op jit(solution)/shard_map/ppermute | solution.py:438
  49.1 1.8 %collective-permute-start.15 = (f32[3,24,128]{2,1,0:T(8,128)S(1)}, f32[3,24,128]{2,1,0:T(8,128)S(1)}, u32[]{:S(2)}, u32[]{:S(2)}) collective-permute-start(f32[3,24,128]{2,1,0:T(8,128)S(1)} %shard_map.104.refs_12_), channel_id=1, source_target_pairs={{0,7},{1,2},{2,1},{3,4},{4,3},{5,6},{6,5},{7,0},{8,15},{9,10},{10,... | collective-permute-start | bytes 110600 | tf_op jit(solution)/shard_map/ppermute | solution.py:444
  52.0 0.7 %shard_map.106 = (f32[3,4,16,128]{3,2,1,0:T(8,128)S(1)}, f32[3,4,16,128]{3,2,1,0:T(8,128)}) custom-call(f32[3,4,24,128]{3,2,1,0:T(8,128)S(1)} %get-tuple-element.56.u, f32[3,4,24,128]{3,2,1,0:T(8,128)S(1)} %get-tuple-element.52.refs_0_.v, f32[4,24,128]{2,1,0:T(8,128)S(1)} %get-tuple-element.37.c.refs_2_, ...), custom_call_target="tpu_custom_call" | custom-call | bytes 3000000 | tf_op jit(solution)/shard_map/pallas_call | solution.py:423
  52.7 1.0 %collective-permute-done.15.odd = f32[3,24,128]{2,1,0:T(8,128)S(1)} collective-permute-done((f32[3,24,128]{2,1,0:T(8,128)S(1)}, f32[3,24,128]{2,1,0:T(8,128)S(1)}, u32[]{:S(2)}, u32[]{:S(2)}) %collective-permute-start.15) | collective-permute-done | bytes 36896 | tf_op jit(solution)/shard_map/ppermute | solution.py:444
  53.7 1.2 %collective-permute-done.17.at_right = f32[8,128]{1,0:T(8,128)S(1)} collective-permute-done((f32[8,128]{1,0:T(8,128)S(1)}, f32[8,128]{1,0:T(8,128)S(1)}, u32[]{:S(2)}, u32[]{:S(2)}) %collective-permute-start.17) | collective-permute-done | bytes 4128 | tf_op jit(solution)/shard_map/ppermute | solution.py:438
  54.9 0.9 %shard_map.108 = f32[3,4,16,128]{3,2,1,0:T(8,128)} custom-call(f32[3,4,24,128]{3,2,1,0:T(8,128)S(1)} %get-tuple-element.56.u, f32[4,24,128]{2,1,0:T(8,128)S(1)} %get-tuple-element.37.c.refs_2_, f32[3,4,16,128]{3,2,1,0:T(8,128)S(1)} %get-tuple-element.57.base, f32[3,24,128]{2,1,0:T(8,128)S(1)} %collective-permute-done.14.even, ...), custom_call_target="tpu_custom_call" | custom-call | bytes 3000000 | tf_op jit(solution)/shard_map/pallas_call | solution.py:423
  (36 shorter events, 3.6 us)
Async XLA Ops:
  2.2 21.1 %collective-permute-start = (f32[11,2,8,128]{3,2,1,0:T(8,128)}, f32[11,2,8,128]{3,2,1,0:T(8,128)S(1)}, u32[]{:S(2)}, u32[]{:S(2)}) collective-permute-start(f32[11,2,8,128]{3,2,1,0:T(8,128)} %shard_map.96), channel_id=1, source_target_pairs={{0,8},{8,16},{16,24},{24,32},{32,40},{40,48},{48,56},{56,0},{1,9},... | collective-permute-start | bytes 270344 | tf_op jit(solution)/shard_map/ppermute | solution.py:438
  6.0 17.3 %copy-start.1 = (f32[3,4,16,128]{3,2,1,0:T(8,128)S(1)}, f32[3,4,16,128]{3,2,1,0:T(8,128)}, u32[]{:S(2)}) copy-start(f32[3,4,16,128]{3,2,1,0:T(8,128)} %cur.5) | copy-start | bytes 294916
  6.0 17.3 %copy-start.2 = (f32[3,4,16,128]{3,2,1,0:T(8,128)S(1)}, f32[3,4,16,128]{3,2,1,0:T(8,128)}, u32[]{:S(2)}) copy-start(f32[3,4,16,128]{3,2,1,0:T(8,128)} %prv.5) | copy-start | bytes 294916
  6.1 17.3 %copy-start.3 = (f32[4,16,128]{2,1,0:T(8,128)S(1)}, f32[4,16,128]{2,1,0:T(8,128)}, u32[]{:S(2)}) copy-start(f32[4,16,128]{2,1,0:T(8,128)} %den.1) | copy-start | bytes 98308
  8.9 14.5 %copy-start = (f32[4,4,16,128]{3,2,1,0:T(8,128)S(1)}, f32[4,4,16,128]{3,2,1,0:T(8,128)}, u32[]{:S(2)}) copy-start(f32[4,4,16,128]{3,2,1,0:T(8,128)} %mod.5) | copy-start | bytes 393220
  8.9 14.4 %collective-permute-start.1 = (f32[11,2,8,128]{3,2,1,0:T(8,128)}, f32[11,2,8,128]{3,2,1,0:T(8,128)S(1)}, u32[]{:S(2)}, u32[]{:S(2)}) collective-permute-start(f32[11,2,8,128]{3,2,1,0:T(8,128)} %get-tuple-element.33), channel_id=1, source_target_pairs={{0,56},{8,0},{16,8},{24,16},{32,24},{40,32},{48,40},{56,48},{1,57}... | collective-permute-start | bytes 270344 | tf_op jit(solution)/shard_map/ppermute | solution.py:438
  11.2 23.1 %all-to-all-start = ((f32[64,1,256]{2,1,0:T(1,128)}), f32[64,1,256]{2,1,0:T(1,128)S(1)}, u32[]{:S(2)}, u32[]{:S(2)}) async-start(f32[64,1,256]{2,1,0:T(1,128)} %get-tuple-element.32), calls=%async_computation | async-start | bytes 131072 | tf_op jit(solution)/shard_map/all_to_all | solution.py:481
  23.7 4.9 %collective-permute-start.3 = (f32[5,24,128]{2,1,0:T(8,128)S(1)}, f32[5,24,128]{2,1,0:T(8,128)S(1)}, u32[]{:S(2)}, u32[]{:S(2)}) collective-permute-start(f32[5,24,128]{2,1,0:T(8,128)S(1)} %get-tuple-element.39), channel_id=1, source_target_pairs={{0,7},{1,2},{2,1},{3,4},{4,3},{5,6},{6,5},{7,0},{8,15},{9,10},{10,... | collective-permute-start | bytes 184328 | tf_op jit(solution)/shard_map/ppermute | solution.py:444
  26.0 5.9 %collective-permute-start.2 = (f32[5,24,128]{2,1,0:T(8,128)S(1)}, f32[5,24,128]{2,1,0:T(8,128)S(1)}, u32[]{:S(2)}, u32[]{:S(2)}) collective-permute-start(f32[5,24,128]{2,1,0:T(8,128)S(1)} %get-tuple-element.38), channel_id=1, source_target_pairs={{0,1},{1,0},{2,3},{3,2},{4,5},{5,4},{6,7},{7,6},{8,9},{9,8},{10,11... | collective-permute-start | bytes 184328 | tf_op jit(solution)/shard_map/ppermute | solution.py:444
  26.0 3.4 %collective-permute-start.4 = (f32[8,128]{1,0:T(8,128)S(1)}, f32[8,128]{1,0:T(8,128)S(1)}, u32[]{:S(2)}, u32[]{:S(2)}) collective-permute-start(f32[8,128]{1,0:T(8,128)S(1)} %get-tuple-element.40), channel_id=1, source_target_pairs={{0,64},{64,128},{128,192},{192,0},{1,65},{65,129},{129,193},{193,1... | collective-permute-start | bytes 12296 | tf_op jit(solution)/shard_map/ppermute | solution.py:438
  28.6 3.3 %collective-permute-start.5 = (f32[8,128]{1,0:T(8,128)S(1)}, f32[8,128]{1,0:T(8,128)S(1)}, u32[]{:S(2)}, u32[]{:S(2)}) collective-permute-start(f32[8,128]{1,0:T(8,128)S(1)} %get-tuple-element.41), channel_id=1, source_target_pairs={{0,192},{64,0},{128,64},{192,128},{1,193},{65,1},{129,65},{193,129... | collective-permute-start | bytes 12296 | tf_op jit(solution)/shard_map/ppermute | solution.py:438
  35.0 7.7 %collective-permute-start.7 = (f32[3,24,128]{2,1,0:T(8,128)S(1)}, f32[3,24,128]{2,1,0:T(8,128)S(1)}, u32[]{:S(2)}, u32[]{:S(2)}) collective-permute-start(f32[3,24,128]{2,1,0:T(8,128)S(1)} %get-tuple-element.45), channel_id=1, source_target_pairs={{0,7},{1,2},{2,1},{3,4},{4,3},{5,6},{6,5},{7,0},{8,15},{9,10},{10,... | collective-permute-start | bytes 110600 | tf_op jit(solution)/shard_map/ppermute | solution.py:444
  35.8 9.0 %collective-permute-start.6 = (f32[3,24,128]{2,1,0:T(8,128)S(1)}, f32[3,24,128]{2,1,0:T(8,128)S(1)}, u32[]{:S(2)}, u32[]{:S(2)}) collective-permute-start(f32[3,24,128]{2,1,0:T(8,128)S(1)} %get-tuple-element.44), channel_id=1, source_target_pairs={{0,1},{1,0},{2,3},{3,2},{4,5},{5,4},{6,7},{7,6},{8,9},{9,8},{10,11... | collective-permute-start | bytes 110600 | tf_op jit(solution)/shard_map/ppermute | solution.py:444
  37.0 4.0 %collective-permute-start.8 = (f32[8,128]{1,0:T(8,128)S(1)}, f32[8,128]{1,0:T(8,128)S(1)}, u32[]{:S(2)}, u32[]{:S(2)}) collective-permute-start(f32[8,128]{1,0:T(8,128)S(1)} %get-tuple-element.46), channel_id=1, source_target_pairs={{0,64},{64,128},{128,192},{192,0},{1,65},{65,129},{129,193},{193,1... | collective-permute-start | bytes 12296 | tf_op jit(solution)/shard_map/ppermute | solution.py:438
  39.7 3.0 %collective-permute-start.9 = (f32[8,128]{1,0:T(8,128)S(1)}, f32[8,128]{1,0:T(8,128)S(1)}, u32[]{:S(2)}, u32[]{:S(2)}) collective-permute-start(f32[8,128]{1,0:T(8,128)S(1)} %get-tuple-element.47), channel_id=1, source_target_pairs={{0,192},{64,0},{128,64},{192,128},{1,193},{65,1},{129,65},{193,129... | collective-permute-start | bytes 12296 | tf_op jit(solution)/shard_map/ppermute | solution.py:438
  42.9 6.1 %collective-permute-start.11 = (f32[3,24,128]{2,1,0:T(8,128)S(1)}, f32[3,24,128]{2,1,0:T(8,128)S(1)}, u32[]{:S(2)}, u32[]{:S(2)}) collective-permute-start(f32[3,24,128]{2,1,0:T(8,128)S(1)} %shard_map.102.refs_12_), channel_id=1, source_target_pairs={{0,7},{1,2},{2,1},{3,4},{4,3},{5,6},{6,5},{7,0},{8,15},{9,10},{10,... | collective-permute-start | bytes 110600 | tf_op jit(solution)/shard_map/ppermute | solution.py:444
  45.3 5.5 %collective-permute-start.10 = (f32[3,24,128]{2,1,0:T(8,128)S(1)}, f32[3,24,128]{2,1,0:T(8,128)S(1)}, u32[]{:S(2)}, u32[]{:S(2)}) collective-permute-start(f32[3,24,128]{2,1,0:T(8,128)S(1)} %get-tuple-element.53), channel_id=1, source_target_pairs={{0,1},{1,0},{2,3},{3,2},{4,5},{5,4},{6,7},{7,6},{8,9},{9,8},{10,11... | collective-permute-start | bytes 110600 | tf_op jit(solution)/shard_map/ppermute | solution.py:444
  45.5 1.2 %collective-permute-start.12 = (f32[8,128]{1,0:T(8,128)S(1)}, f32[8,128]{1,0:T(8,128)S(1)}, u32[]{:S(2)}, u32[]{:S(2)}) collective-permute-start(f32[8,128]{1,0:T(8,128)S(1)} %get-tuple-element.54), channel_id=1, source_target_pairs={{0,64},{64,128},{128,192},{192,0},{1,65},{65,129},{129,193},{193,1... | collective-permute-start | bytes 12296 | tf_op jit(solution)/shard_map/ppermute | solution.py:438
  45.7 3.3 %collective-permute-start.13 = (f32[8,128]{1,0:T(8,128)S(1)}, f32[8,128]{1,0:T(8,128)S(1)}, u32[]{:S(2)}, u32[]{:S(2)}) collective-permute-start(f32[8,128]{1,0:T(8,128)S(1)} %get-tuple-element.55), channel_id=1, source_target_pairs={{0,192},{64,0},{128,64},{192,128},{1,193},{65,1},{129,65},{193,129... | collective-permute-start | bytes 12296 | tf_op jit(solution)/shard_map/ppermute | solution.py:438
  49.1 4.6 %collective-permute-start.15 = (f32[3,24,128]{2,1,0:T(8,128)S(1)}, f32[3,24,128]{2,1,0:T(8,128)S(1)}, u32[]{:S(2)}, u32[]{:S(2)}) collective-permute-start(f32[3,24,128]{2,1,0:T(8,128)S(1)} %shard_map.104.refs_12_), channel_id=1, source_target_pairs={{0,7},{1,2},{2,1},{3,4},{4,3},{5,6},{6,5},{7,0},{8,15},{9,10},{10,... | collective-permute-start | bytes 110600 | tf_op jit(solution)/shard_map/ppermute | solution.py:444
  51.4 3.6 %collective-permute-start.14 = (f32[3,24,128]{2,1,0:T(8,128)S(1)}, f32[3,24,128]{2,1,0:T(8,128)S(1)}, u32[]{:S(2)}, u32[]{:S(2)}) collective-permute-start(f32[3,24,128]{2,1,0:T(8,128)S(1)} %get-tuple-element.58), channel_id=1, source_target_pairs={{0,1},{1,0},{2,3},{3,2},{4,5},{5,4},{6,7},{7,6},{8,9},{9,8},{10,11... | collective-permute-start | bytes 110600 | tf_op jit(solution)/shard_map/ppermute | solution.py:444
  51.5 2.3 %collective-permute-start.16 = (f32[8,128]{1,0:T(8,128)S(1)}, f32[8,128]{1,0:T(8,128)S(1)}, u32[]{:S(2)}, u32[]{:S(2)}) collective-permute-start(f32[8,128]{1,0:T(8,128)S(1)} %get-tuple-element.59), channel_id=1, source_target_pairs={{0,64},{64,128},{128,192},{192,0},{1,65},{65,129},{129,193},{193,1... | collective-permute-start | bytes 12296 | tf_op jit(solution)/shard_map/ppermute | solution.py:438
  51.7 3.2 %collective-permute-start.17 = (f32[8,128]{1,0:T(8,128)S(1)}, f32[8,128]{1,0:T(8,128)S(1)}, u32[]{:S(2)}, u32[]{:S(2)}) collective-permute-start(f32[8,128]{1,0:T(8,128)S(1)} %get-tuple-element.60), channel_id=1, source_target_pairs={{0,192},{64,0},{128,64},{192,128},{1,193},{65,1},{129,65},{193,129... | collective-permute-start | bytes 12296 | tf_op jit(solution)/shard_map/ppermute | solution.py:438
